TPU v7x, 32 devices: a whole 2x2x4 slice. The times are simulated.
32 devices in a mesh: illum: 2 (over x), row: 4 (over y, core), col: 4 (over z).
Axes of the slice: x: 2, y: 2, z: 4, core: 2. Of those that a mesh axis runs over, the one named last changes fastest.
Arguments:
- phase_delay: float32 [2, 512, 4096], P(None, ('row', 'illum'), 'col'), may hold values from -1 to 1
- angles: int32 [2, 2], P('illum'), may hold values from -8 to 8
- measured: bfloat16 [2, 2, 512, 4096], P(None, 'illum', 'row', 'col'), may hold values from -120 to 120, as said below
Outputs:
- phase_grad: float32 [2, 512, 4096], P(None, ('row', 'illum'), 'col')
Inputs may be any that keep to these rules, and one draw needn't show every extreme that they name: Real and imaginary parts of a measured field, with scales that vary over rows and columns.
All inputs are finite; a program needn't handle non-finite values.
Results may differ from a plain program's by a relative error of at most 0.0003.
Values sent between devices are 32-bit elements; how exact they have to be, the bound alone decides.
No kernel may reach another device: no remote copies, remote signals or barrier semaphores. Data moves between devices by JAX's collectives and lax.ppermute only.
A program may use at most 64 MiB of HBM per device.

v0:
```python
import math

import jax
import jax.numpy as jnp
from jax import lax
from jax.sharding import PartitionSpec as P

SWEEPS = 2


beta_step = 0.5
eps_energy = 1e-06


def with_halo(x, sides, width):
    for axis, dim in sides:
        peers, length = (lax.axis_size(axis), x.shape[dim])
        up = [(i, (i + 1) % peers) for i in range(peers - 1)]
        down = [(j, i) for i, j in up]
        last = lax.slice_in_dim(x, length - width, length, axis=dim)
        first = lax.slice_in_dim(x, 0, width, axis=dim)
        before = lax.ppermute(last, axis, up)
        after = lax.ppermute(first, axis, down)
        x = jnp.concatenate([before, x, after], axis=dim)
    return x


def neighbour_sum(padded):
    return (
        padded[..., 2:, 1:-1]
        + padded[..., :-2, 1:-1]
        + padded[..., 1:-1, 2:]
        + padded[..., 1:-1, :-2]
    )


def exchange_rims(wave_field):
    return with_halo(wave_field, (("row", 2), ("col", 3)), 1)


def propagate(wave_field, direction):
    beta_sign = direction * beta_step
    divisor = 1.0 + 16.0 * beta_sign * beta_sign
    beside_all = neighbour_sum(exchange_rims(wave_field))
    real_part, imag_part = (wave_field[0], wave_field[1])
    rhs_real = real_part + 4.0 * beta_sign * imag_part - beta_sign * beside_all[1]
    rhs_imag = imag_part - 4.0 * beta_sign * real_part + beta_sign * beside_all[0]
    for sweep in range(SWEEPS):
        if sweep > 0:
            beside_all = neighbour_sum(exchange_rims(jnp.stack([real_part, imag_part])))
        total_real = rhs_real - beta_sign * beside_all[1]
        total_imag = rhs_imag + beta_sign * beside_all[0]
        real_part = (total_real + 4.0 * beta_sign * total_imag) / divisor
        imag_part = (total_imag - 4.0 * beta_sign * total_real) / divisor
    return jnp.stack([real_part, imag_part])


def per_device(phase_delay, angles, measured):
    illum_count = lax.axis_size("illum")
    stripe = phase_delay.shape[1]
    rows_tile = stripe * illum_count
    cols_tile = measured.shape[3]
    total_rows = rows_tile * lax.axis_size("row")
    total_cols = cols_tile * lax.axis_size("col")
    row_ids = lax.axis_index("row") * rows_tile + lax.iota(jnp.int32, rows_tile)
    col_ids = lax.axis_index("col") * cols_tile + lax.iota(jnp.int32, cols_tile)

    def advance(field_now, direction):
        return propagate(field_now, direction)

    along_x = angles[:, 0:1] * row_ids[None, :] % total_rows
    along_y = angles[:, 1:2] * col_ids[None, :] % total_cols
    angle_phase = (
        2.0
        * math.pi
        * (
            along_x.astype(jnp.float32)[:, :, None] / total_rows
            + along_y.astype(jnp.float32)[:, None, :] / total_cols
        )
    )
    wave_field = jnp.stack([jnp.cos(angle_phase), jnp.sin(angle_phase)])
    target = measured.astype(jnp.float32)
    energy = (
        lax.psum(jnp.sum(target * target, axis=(0, 2, 3)), ("row", "col"))
        / (total_rows * total_cols)
        + eps_energy
    )
    all_planes = lax.all_gather(phase_delay, "illum", axis=1, tiled=True)
    stored = []
    for depth_index in range(phase_delay.shape[0]):
        phase_plane = all_planes[depth_index]
        cosine = jnp.cos(phase_plane)
        sine_part = jnp.sin(phase_plane)
        modulated = jnp.stack(
            [
                wave_field[0] * cosine - wave_field[1] * sine_part,
                wave_field[0] * sine_part + wave_field[1] * cosine,
            ]
        )
        stored.append((modulated, cosine, sine_part))
        wave_field = advance(modulated, 1.0)
    adjoint_wave = 2.0 * (wave_field - target) / energy[None, :, None, None]
    slice_grads = [None] * len(stored)
    for depth_index in reversed(range(len(stored))):
        modulated, cosine, sine_part = stored[depth_index]
        adjoint_wave = advance(adjoint_wave, -1.0)
        slice_grads[depth_index] = jnp.sum(
            adjoint_wave[1] * modulated[0] - adjoint_wave[0] * modulated[1], axis=0
        )
        if depth_index > 0:
            adjoint_wave = jnp.stack(
                [
                    adjoint_wave[0] * cosine + adjoint_wave[1] * sine_part,
                    adjoint_wave[1] * cosine - adjoint_wave[0] * sine_part,
                ]
            )
    local_grads = jnp.stack(slice_grads)
    summed = lax.psum(local_grads, "illum")
    return lax.dynamic_slice_in_dim(summed, lax.axis_index("illum") * stripe, stripe, 1)


def solution(mesh):
    placed = (P(None, ("row", "illum"), "col"), P("illum", None), P(None, "illum", "row", "col"))
    return jax.shard_map(
        per_device,
        mesh=mesh,
        in_specs=placed,
        out_specs=P(None, ("row", "illum"), "col"),
        check_vma=False,
    )
```

profile of v0, /device:TPU:0, one launch (start us, length us, event | category | flops | bytes accessed | tf_op | source)
XLA Modules:
  0.0 278.1 jit_solution(14714277182653705812)
XLA Ops:
  9.8 23.1 %all-gather.2.cloned.1.call-done = f32[2,128,1024]{2,1,0:T(8,128)} async-done(((f32[2,64,1024]{2,1,0:T(8,128)}), f32[2,128,1024]{2,1,0:T(8,128)}) %all-gather.2.cloned.1.call-update) | async-done | bytes 1048592 | tf_op jit(solution)/shard_map/all_gather | solution.py:88
  32.9 4.8 %fusion.64 = (f32[1,1,128,1024]{3,2,1,0:T(8,128)S(1)}, f32[1,1,128,1024]{3,2,1,0:T(8,128)S(1)}) fusion(f32[2,128,1024]{2,1,0:T(8,128)} %all-gather.2.cloned.1.call-done, f32[1024]{0:T(1024)S(1)} %fusion.60, f32[128]{0:T(128)S(1)} %fusion.62), kind=kLoop, calls=%fused_computation.267 | loop fusion | flops 1048576 | bytes 1577472 | tf_op jit(solution)/shard_map/stack | solution.py:94
  37.8 1.7 collective-permute-start.1
  39.5 1.3 collective-permute-start
  40.8 3.0 %collective-permute-done = f32[2,1,1,1024]{3,2,1,0:T(1,128)S(1)} collective-permute-done((f32[2,1,1,1024]{3,2,1,0:T(1,128)S(1)}, f32[2,1,1,1024]{3,2,1,0:T(1,128)S(1)}, u32[]{:S(2)}, u32[]{:S(2)}) %collective-permute-start) | collective-permute-done | bytes 8224 | tf_op jit(solution)/shard_map/ppermute | solution.py:23
  44.0 1.3 collective-permute-start.2
  45.3 4.7 %collective-permute-start.3 = (f32[2,1,130,1]{3,2,1,0:T(8,128)S(1)}, f32[2,1,130,1]{3,2,1,0:T(8,128)S(1)}, u32[]{:S(2)}, u32[]{:S(2)}) collective-permute-start(f32[2,1,130,1]{3,2,1,0:T(8,128)S(1)} %get-tuple-element.37), channel_id=1, source_target_pairs={{0,1},{1,2},{2,3},{4,5},{5,6},{6,7},{8,9},{9,10},{10,11},{12,13},{... | collective-permute-start | bytes 3128 | tf_op jit(solution)/shard_map/ppermute | solution.py:22
  50.9 1.9 collective-permute-done.3
  53.6 4.2 %multiply_bitcast_fusion.7 = (f32[1,1,128,1024]{3,2,1,0:T(8,128)S(1)}, f32[1,1,128,1024]{3,2,1,0:T(8,128)S(1)}) fusion(f32[2,1,128,1024]{3,2,1,0:T(8,128)S(1)} %fusion.24, f32[2,128,1024]{2,1,0:T(8,128)S(1)} %copy-done, f32[1024]{0:T(1024)S(1)} %fusion.60, f32[128]{0:T(128)S(1)} %fusion.62), kind=kLoop, calls=%fused_computation.191 | loop fusion | flops 3145728 | bytes 2626048 | tf_op jit(solution)/shard_map/stack | solution.py:50
  57.8 3.2 %collective-permute-start.5 = (f32[2,1,1,1024]{3,2,1,0:T(1,128)S(1)}, f32[2,1,1,1024]{3,2,1,0:T(1,128)S(1)}, u32[]{:S(2)}, u32[]{:S(2)}) collective-permute-start(f32[2,1,1,1024]{3,2,1,0:T(1,128)S(1)} %get-tuple-element.54), channel_id=1, source_target_pairs={{0,4},{4,8},{8,12},{1,5},{5,9},{9,13},{2,6},{6,10},{10,14},{3,7},{... | collective-permute-start | bytes 24584 | tf_op jit(solution)/shard_map/ppermute | solution.py:22
  61.0 1.3 collective-permute-start.4
  62.3 2.1 collective-permute-done.4
  65.8 5.0 %collective-permute-start.7 = (f32[2,1,130,1]{3,2,1,0:T(8,128)S(1)}, f32[2,1,130,1]{3,2,1,0:T(8,128)S(1)}, u32[]{:S(2)}, u32[]{:S(2)}) collective-permute-start(f32[2,1,130,1]{3,2,1,0:T(8,128)S(1)} %get-tuple-element.35), channel_id=1, source_target_pairs={{0,1},{1,2},{2,3},{4,5},{5,6},{6,7},{8,9},{9,10},{10,11},{12,13},{... | collective-permute-start | bytes 3128 | tf_op jit(solution)/shard_map/ppermute | solution.py:22
  71.9 1.5 collective-permute-done.7
  74.1 6.1 %multiply_subtract_fusion.3 = (f32[1,128,1024]{2,1,0:T(8,128)S(1)}, f32[1,128,1024]{2,1,0:T(8,128)S(1)}) fusion(f32[2,128,1024]{2,1,0:T(8,128)S(1)} %copy-done, f32[2,1,128,1024]{3,2,1,0:T(8,128)S(1)} %fusion.21, f32[2,1,128,1024]{3,2,1,0:T(8,128)S(1)} %fusion.24, f32[1024]{0:T(1024)S(1)} %fusion.60, f32[128]{0:T(128)S(1)} %fusion.62), kind=kLoop, calls=%fused_computation.187 | loop fusion | flops 4194304 | bytes 4198912 | tf_op jit(solution)/shard_map/sub | solution.py:96
  80.2 3.5 %collective-permute-start.9 = (f32[2,1,1,1024]{3,2,1,0:T(1,128)S(1)}, f32[2,1,1,1024]{3,2,1,0:T(1,128)S(1)}, u32[]{:S(2)}, u32[]{:S(2)}) collective-permute-start(f32[2,1,1,1024]{3,2,1,0:T(1,128)S(1)} %get-tuple-element.52), channel_id=1, source_target_pairs={{0,4},{4,8},{8,12},{1,5},{5,9},{9,13},{2,6},{6,10},{10,14},{3,7},{... | collective-permute-start | bytes 24584 | tf_op jit(solution)/shard_map/ppermute | solution.py:22
  83.7 1.3 collective-permute-start.8
  85.0 2.1 collective-permute-done.8
  87.3 1.3 collective-permute-start.10
  88.6 5.0 %collective-permute-start.11 = (f32[2,1,130,1]{3,2,1,0:T(8,128)S(1)}, f32[2,1,130,1]{3,2,1,0:T(8,128)S(1)}, u32[]{:S(2)}, u32[]{:S(2)}) collective-permute-start(f32[2,1,130,1]{3,2,1,0:T(8,128)S(1)} %get-tuple-element.33), channel_id=1, source_target_pairs={{0,1},{1,2},{2,3},{4,5},{5,6},{6,7},{8,9},{9,10},{10,11},{12,13},{... | collective-permute-start | bytes 3128 | tf_op jit(solution)/shard_map/ppermute | solution.py:22
  94.7 1.5 collective-permute-done.11
  98.1 3.5 %collective-permute-start.13 = (f32[2,1,1,1024]{3,2,1,0:T(1,128)S(1)}, f32[2,1,1,1024]{3,2,1,0:T(1,128)S(1)}, u32[]{:S(2)}, u32[]{:S(2)}) collective-permute-start(f32[2,1,1,1024]{3,2,1,0:T(1,128)S(1)} %get-tuple-element.50), channel_id=1, source_target_pairs={{0,4},{4,8},{8,12},{1,5},{5,9},{9,13},{2,6},{6,10},{10,14},{3,7},{... | collective-permute-start | bytes 24584 | tf_op jit(solution)/shard_map/ppermute | solution.py:22
  101.6 1.4 collective-permute-start.12
  103.0 2.1 collective-permute-done.12
  107.2 5.0 %collective-permute-start.15 = (f32[2,1,130,1]{3,2,1,0:T(8,128)}, f32[2,1,130,1]{3,2,1,0:T(8,128)S(1)}, u32[]{:S(2)}, u32[]{:S(2)}) collective-permute-start(f32[2,1,130,1]{3,2,1,0:T(8,128)} %get-tuple-element.31), channel_id=1, source_target_pairs={{0,1},{1,2},{2,3},{4,5},{5,6},{6,7},{8,9},{9,10},{10,11},{12,13},{... | collective-permute-start | bytes 3128 | tf_op jit(solution)/shard_map/ppermute | solution.py:22
  113.2 32.3 %psum.14 = f32[1]{0:T(128)} all-reduce(f32[1]{0:T(128)} %bitcast.20), channel_id=1, replica_groups=mesh['illum'=2,'row'=4,'col'=4] {'row','col'}, use_global_device_ids=true, to_apply=%region_1.2 | all-reduce | flops 1 | bytes 8 | tf_op jit(solution)/shard_map/psum | solution.py:84
  151.2 5.5 %collective-permute-done.16 = f32[2,1,1,1024]{3,2,1,0:T(1,128)S(1)} collective-permute-done((f32[2,1,1,1024]{3,2,1,0:T(1,128)S(1)}, f32[2,1,1,1024]{3,2,1,0:T(1,128)S(1)}, u32[]{:S(2)}, u32[]{:S(2)}) %collective-permute-start.16) | collective-permute-done | bytes 8224 | tf_op jit(solution)/shard_map/ppermute | solution.py:23
  156.7 1.3 collective-permute-start.18
  158.0 4.6 %collective-permute-start.19 = (f32[2,1,130,1]{3,2,1,0:T(8,128)S(1)}, f32[2,1,130,1]{3,2,1,0:T(8,128)S(1)}, u32[]{:S(2)}, u32[]{:S(2)}) collective-permute-start(f32[2,1,130,1]{3,2,1,0:T(8,128)S(1)} %get-tuple-element.29), channel_id=1, source_target_pairs={{0,1},{1,2},{2,3},{4,5},{5,6},{6,7},{8,9},{9,10},{10,11},{12,13},{... | collective-permute-start | bytes 3128 | tf_op jit(solution)/shard_map/ppermute | solution.py:22
  163.7 1.8 collective-permute-done.19
  166.5 3.2 %collective-permute-start.21 = (f32[2,1,1,1024]{3,2,1,0:T(1,128)S(1)}, f32[2,1,1,1024]{3,2,1,0:T(1,128)S(1)}, u32[]{:S(2)}, u32[]{:S(2)}) collective-permute-start(f32[2,1,1,1024]{3,2,1,0:T(1,128)S(1)} %get-tuple-element.46), channel_id=1, source_target_pairs={{0,4},{4,8},{8,12},{1,5},{5,9},{9,13},{2,6},{6,10},{10,14},{3,7},{... | collective-permute-start | bytes 24584 | tf_op jit(solution)/shard_map/ppermute | solution.py:22
  169.7 1.3 collective-permute-start.20
  171.0 2.1 collective-permute-done.20
  174.6 5.2 %collective-permute-start.23 = (f32[2,1,130,1]{3,2,1,0:T(8,128)S(1)}, f32[2,1,130,1]{3,2,1,0:T(8,128)S(1)}, u32[]{:S(2)}, u32[]{:S(2)}) collective-permute-start(f32[2,1,130,1]{3,2,1,0:T(8,128)S(1)} %get-tuple-element.27), channel_id=1, source_target_pairs={{0,1},{1,2},{2,3},{4,5},{5,6},{6,7},{8,9},{9,10},{10,11},{12,13},{... | collective-permute-start | bytes 3128 | tf_op jit(solution)/shard_map/ppermute | solution.py:22
  180.7 1.5 collective-permute-done.23
  182.8 2.3 multiply_add_fusion
  185.1 2.1 multiply_subtract_fusion.2
  187.3 3.5 %collective-permute-start.25 = (f32[2,1,1,1024]{3,2,1,0:T(1,128)S(1)}, f32[2,1,1,1024]{3,2,1,0:T(1,128)S(1)}, u32[]{:S(2)}, u32[]{:S(2)}) collective-permute-start(f32[2,1,1,1024]{3,2,1,0:T(1,128)S(1)} %get-tuple-element.42), channel_id=1, source_target_pairs={{0,4},{4,8},{8,12},{1,5},{5,9},{9,13},{2,6},{6,10},{10,14},{3,7},{... | collective-permute-start | bytes 24584 | tf_op jit(solution)/shard_map/ppermute | solution.py:22
  192.1 2.1 collective-permute-done.24
  195.6 5.0 %collective-permute-start.27 = (f32[2,1,130,1]{3,2,1,0:T(8,128)S(1)}, f32[2,1,130,1]{3,2,1,0:T(8,128)S(1)}, u32[]{:S(2)}, u32[]{:S(2)}) collective-permute-start(f32[2,1,130,1]{3,2,1,0:T(8,128)S(1)} %get-tuple-element.25), channel_id=1, source_target_pairs={{0,1},{1,2},{2,3},{4,5},{5,6},{6,7},{8,9},{9,10},{10,11},{12,13},{... | collective-permute-start | bytes 3128 | tf_op jit(solution)/shard_map/ppermute | solution.py:22
  201.7 1.5 collective-permute-done.27
  204.5 3.5 %collective-permute-start.29 = (f32[2,1,1,1024]{3,2,1,0:T(1,128)S(1)}, f32[2,1,1,1024]{3,2,1,0:T(1,128)S(1)}, u32[]{:S(2)}, u32[]{:S(2)}) collective-permute-start(f32[2,1,1,1024]{3,2,1,0:T(1,128)S(1)} %get-tuple-element.40), channel_id=1, source_target_pairs={{0,4},{4,8},{8,12},{1,5},{5,9},{9,13},{2,6},{6,10},{10,14},{3,7},{... | collective-permute-start | bytes 24584 | tf_op jit(solution)/shard_map/ppermute | solution.py:22
  209.3 2.1 collective-permute-done.28
  212.8 5.0 %collective-permute-start.31 = (f32[2,1,130,1]{3,2,1,0:T(8,128)S(1)}, f32[2,1,130,1]{3,2,1,0:T(8,128)S(1)}, u32[]{:S(2)}, u32[]{:S(2)}) collective-permute-start(f32[2,1,130,1]{3,2,1,0:T(8,128)S(1)} %get-tuple-element.23), channel_id=1, source_target_pairs={{0,1},{1,2},{2,3},{4,5},{5,6},{6,7},{8,9},{9,10},{10,11},{12,13},{... | collective-permute-start | bytes 3128 | tf_op jit(solution)/shard_map/ppermute | solution.py:22
  218.9 1.5 collective-permute-done.31
  221.1 4.1 %multiply_subtract_fusion.1 = f32[1,128,1024]{2,1,0:T(8,128)S(1)} fusion(f32[1,128,1024]{2,1,0:T(8,128)S(1)} %get-tuple-element.7, f32[2,1,128,1024]{3,2,1,0:T(8,128)S(1)} %fusion.3, f32[1,128,1024]{2,1,0:T(8,128)S(1)} %get-tuple-element.6, f32[2,128,1024]{2,1,0:T(8,128)S(1)} %copy-done, f32[1024]{0:T(1024)S(1)} %fusion.60, f32[128]{0:T(128)S(1)} %fusion.62), kind=kLoop, calls=%fused_computation.169 | loop fusion | flops 2752512 | bytes 3150336 | tf_op jit(solution)/shard_map/sub | solution.py:108
  226.3 43.1 %all-reduce.2.cloned.1.call-done = f32[2,128,1024]{2,1,0:T(8,128)} async-done(((f32[2,128,1024]{2,1,0:T(8,128)}), f32[2,128,1024]{2,1,0:T(8,128)}) %all-reduce.2.cloned.1.call-update) | async-done | bytes 1048592 | tf_op jit(solution)/shard_map/psum | solution.py:118
  269.4 1.9 constant_dynamic-slice_fusion
  (82 shorter events, 35.1 us)
Async XLA Ops:
  6.5 26.4 %all-gather.2.cloned.1.call-start = ((), (), s32[]{:S(2)}) async-start(), calls=%async_computation | async-start | bytes 1572864 | tf_op jit(solution)/shard_map/all_gather | solution.py:88
  7.3 262.1 %all-reduce.2.cloned.1.call-start = ((), (), s32[]{:S(2)}) async-start(), calls=%async_computation.1 | async-start | bytes 2097152 | tf_op jit(solution)/shard_map/psum | solution.py:118
  7.3 0.7 copy-start.7
  37.8 3.0 %collective-permute-start.1 = (f32[2,1,1,1024]{3,2,1,0:T(1,128)S(1)}, f32[2,1,1,1024]{3,2,1,0:T(1,128)S(1)}, u32[]{:S(2)}, u32[]{:S(2)}) collective-permute-start(f32[2,1,1,1024]{3,2,1,0:T(1,128)S(1)} %get-tuple-element.56), channel_id=1, source_target_pairs={{0,4},{4,8},{8,12},{1,5},{5,9},{9,13},{2,6},{6,10},{10,14},{3,7},{... | collective-permute-start | bytes 24584 | tf_op jit(solution)/shard_map/ppermute | solution.py:22
  39.5 4.3 %collective-permute-start = (f32[2,1,1,1024]{3,2,1,0:T(1,128)S(1)}, f32[2,1,1,1024]{3,2,1,0:T(1,128)S(1)}, u32[]{:S(2)}, u32[]{:S(2)}) collective-permute-start(f32[2,1,1,1024]{3,2,1,0:T(1,128)S(1)} %get-tuple-element.57), channel_id=1, source_target_pairs={{4,0},{8,4},{12,8},{5,1},{9,5},{13,9},{6,2},{10,6},{14,10},{7,3},{... | collective-permute-start | bytes 24584 | tf_op jit(solution)/shard_map/ppermute | solution.py:23
  44.0 6.9 %collective-permute-start.2 = (f32[2,1,130,1]{3,2,1,0:T(8,128)S(1)}, f32[2,1,130,1]{3,2,1,0:T(8,128)S(1)}, u32[]{:S(2)}, u32[]{:S(2)}) collective-permute-start(f32[2,1,130,1]{3,2,1,0:T(8,128)S(1)} %get-tuple-element.36), channel_id=1, source_target_pairs={{1,0},{2,1},{3,2},{5,4},{6,5},{7,6},{9,8},{10,9},{11,10},{13,12},{... | collective-permute-start | bytes 3128 | tf_op jit(solution)/shard_map/ppermute | solution.py:23
  45.3 8.3 %copy-start = (f32[2,128,1024]{2,1,0:T(8,128)S(1)}, f32[2,128,1024]{2,1,0:T(8,128)}, u32[]{:S(2)}) copy-start(f32[2,128,1024]{2,1,0:T(8,128)} %all-gather.2.cloned.1.call-done) | copy-start | bytes 3145732
  45.3 7.6 %collective-permute-start.3 = (f32[2,1,130,1]{3,2,1,0:T(8,128)S(1)}, f32[2,1,130,1]{3,2,1,0:T(8,128)S(1)}, u32[]{:S(2)}, u32[]{:S(2)}) collective-permute-start(f32[2,1,130,1]{3,2,1,0:T(8,128)S(1)} %get-tuple-element.37), channel_id=1, source_target_pairs={{0,1},{1,2},{2,3},{4,5},{5,6},{6,7},{8,9},{9,10},{10,11},{12,13},{... | collective-permute-start | bytes 3128 | tf_op jit(solution)/shard_map/ppermute | solution.py:22
  57.8 4.5 %collective-permute-start.5 = (f32[2,1,1,1024]{3,2,1,0:T(1,128)S(1)}, f32[2,1,1,1024]{3,2,1,0:T(1,128)S(1)}, u32[]{:S(2)}, u32[]{:S(2)}) collective-permute-start(f32[2,1,1,1024]{3,2,1,0:T(1,128)S(1)} %get-tuple-element.54), channel_id=1, source_target_pairs={{0,4},{4,8},{8,12},{1,5},{5,9},{9,13},{2,6},{6,10},{10,14},{3,7},{... | collective-permute-start | bytes 24584 | tf_op jit(solution)/shard_map/ppermute | solution.py:22
  61.0 3.4 %collective-permute-start.4 = (f32[2,1,1,1024]{3,2,1,0:T(1,128)S(1)}, f32[2,1,1,1024]{3,2,1,0:T(1,128)S(1)}, u32[]{:S(2)}, u32[]{:S(2)}) collective-permute-start(f32[2,1,1,1024]{3,2,1,0:T(1,128)S(1)} %get-tuple-element.55), channel_id=1, source_target_pairs={{4,0},{8,4},{12,8},{5,1},{9,5},{13,9},{6,2},{10,6},{14,10},{7,3},{... | collective-permute-start | bytes 24584 | tf_op jit(solution)/shard_map/ppermute | solution.py:23
  64.5 7.4 %collective-permute-start.6 = (f32[2,1,130,1]{3,2,1,0:T(8,128)S(1)}, f32[2,1,130,1]{3,2,1,0:T(8,128)S(1)}, u32[]{:S(2)}, u32[]{:S(2)}) collective-permute-start(f32[2,1,130,1]{3,2,1,0:T(8,128)S(1)} %get-tuple-element.34), channel_id=1, source_target_pairs={{1,0},{2,1},{3,2},{5,4},{6,5},{7,6},{9,8},{10,9},{11,10},{13,12},{... | collective-permute-start | bytes 3128 | tf_op jit(solution)/shard_map/ppermute | solution.py:23
  65.8 7.6 %collective-permute-start.7 = (f32[2,1,130,1]{3,2,1,0:T(8,128)S(1)}, f32[2,1,130,1]{3,2,1,0:T(8,128)S(1)}, u32[]{:S(2)}, u32[]{:S(2)}) collective-permute-start(f32[2,1,130,1]{3,2,1,0:T(8,128)S(1)} %get-tuple-element.35), channel_id=1, source_target_pairs={{0,1},{1,2},{2,3},{4,5},{5,6},{6,7},{8,9},{9,10},{10,11},{12,13},{... | collective-permute-start | bytes 3128 | tf_op jit(solution)/shard_map/ppermute | solution.py:22
  80.2 4.8 %collective-permute-start.9 = (f32[2,1,1,1024]{3,2,1,0:T(1,128)S(1)}, f32[2,1,1,1024]{3,2,1,0:T(1,128)S(1)}, u32[]{:S(2)}, u32[]{:S(2)}) collective-permute-start(f32[2,1,1,1024]{3,2,1,0:T(1,128)S(1)} %get-tuple-element.52), channel_id=1, source_target_pairs={{0,4},{4,8},{8,12},{1,5},{5,9},{9,13},{2,6},{6,10},{10,14},{3,7},{... | collective-permute-start | bytes 24584 | tf_op jit(solution)/shard_map/ppermute | solution.py:22
  83.7 3.4 %collective-permute-start.8 = (f32[2,1,1,1024]{3,2,1,0:T(1,128)S(1)}, f32[2,1,1,1024]{3,2,1,0:T(1,128)S(1)}, u32[]{:S(2)}, u32[]{:S(2)}) collective-permute-start(f32[2,1,1,1024]{3,2,1,0:T(1,128)S(1)} %get-tuple-element.53), channel_id=1, source_target_pairs={{4,0},{8,4},{12,8},{5,1},{9,5},{13,9},{6,2},{10,6},{14,10},{7,3},{... | collective-permute-start | bytes 24584 | tf_op jit(solution)/shard_map/ppermute | solution.py:23
  87.3 7.4 %collective-permute-start.10 = (f32[2,1,130,1]{3,2,1,0:T(8,128)S(1)}, f32[2,1,130,1]{3,2,1,0:T(8,128)S(1)}, u32[]{:S(2)}, u32[]{:S(2)}) collective-permute-start(f32[2,1,130,1]{3,2,1,0:T(8,128)S(1)} %get-tuple-element.32), channel_id=1, source_target_pairs={{1,0},{2,1},{3,2},{5,4},{6,5},{7,6},{9,8},{10,9},{11,10},{13,12},{... | collective-permute-start | bytes 3128 | tf_op jit(solution)/shard_map/ppermute | solution.py:23
  88.6 7.6 %collective-permute-start.11 = (f32[2,1,130,1]{3,2,1,0:T(8,128)S(1)}, f32[2,1,130,1]{3,2,1,0:T(8,128)S(1)}, u32[]{:S(2)}, u32[]{:S(2)}) collective-permute-start(f32[2,1,130,1]{3,2,1,0:T(8,128)S(1)} %get-tuple-element.33), channel_id=1, source_target_pairs={{0,1},{1,2},{2,3},{4,5},{5,6},{6,7},{8,9},{9,10},{10,11},{12,13},{... | collective-permute-start | bytes 3128 | tf_op jit(solution)/shard_map/ppermute | solution.py:22
  97.1 0.8 copy-start.1
  97.1 1.0 copy-start.3
  98.1 4.9 %collective-permute-start.13 = (f32[2,1,1,1024]{3,2,1,0:T(1,128)S(1)}, f32[2,1,1,1024]{3,2,1,0:T(1,128)S(1)}, u32[]{:S(2)}, u32[]{:S(2)}) collective-permute-start(f32[2,1,1,1024]{3,2,1,0:T(1,128)S(1)} %get-tuple-element.50), channel_id=1, source_target_pairs={{0,4},{4,8},{8,12},{1,5},{5,9},{9,13},{2,6},{6,10},{10,14},{3,7},{... | collective-permute-start | bytes 24584 | tf_op jit(solution)/shard_map/ppermute | solution.py:22
  101.6 10.6 %copy-start.5 = (bf16[2,1,128,1024]{3,2,1,0:T(8,128)(2,1)S(1)}, bf16[2,1,128,1024]{3,2,1,0:T(8,128)(2,1)}, u32[]{:S(2)}) copy-start(bf16[2,1,128,1024]{3,2,1,0:T(8,128)(2,1)} %param.5) | copy-start | bytes 1572868
  101.6 3.6 %collective-permute-start.12 = (f32[2,1,1,1024]{3,2,1,0:T(1,128)S(1)}, f32[2,1,1,1024]{3,2,1,0:T(1,128)S(1)}, u32[]{:S(2)}, u32[]{:S(2)}) collective-permute-start(f32[2,1,1,1024]{3,2,1,0:T(1,128)S(1)} %get-tuple-element.51), channel_id=1, source_target_pairs={{4,0},{8,4},{12,8},{5,1},{9,5},{13,9},{6,2},{10,6},{14,10},{7,3},{... | collective-permute-start | bytes 24584 | tf_op jit(solution)/shard_map/ppermute | solution.py:23
  105.9 40.2 %collective-permute-start.14 = (f32[2,1,130,1]{3,2,1,0:T(8,128)}, f32[2,1,130,1]{3,2,1,0:T(8,128)S(1)}, u32[]{:S(2)}, u32[]{:S(2)}) collective-permute-start(f32[2,1,130,1]{3,2,1,0:T(8,128)} %get-tuple-element.30), channel_id=1, source_target_pairs={{1,0},{2,1},{3,2},{5,4},{6,5},{7,6},{9,8},{10,9},{11,10},{13,12},{... | collective-permute-start | bytes 3128 | tf_op jit(solution)/shard_map/ppermute | solution.py:23
  107.2 39.0 %collective-permute-start.15 = (f32[2,1,130,1]{3,2,1,0:T(8,128)}, f32[2,1,130,1]{3,2,1,0:T(8,128)S(1)}, u32[]{:S(2)}, u32[]{:S(2)}) collective-permute-start(f32[2,1,130,1]{3,2,1,0:T(8,128)} %get-tuple-element.31), channel_id=1, source_target_pairs={{0,1},{1,2},{2,3},{4,5},{5,6},{6,7},{8,9},{9,10},{10,11},{12,13},{... | collective-permute-start | bytes 3128 | tf_op jit(solution)/shard_map/ppermute | solution.py:22
  146.1 1.0 copy-start.2
  146.1 1.2 copy-start.4
  147.3 1.0 copy-start.6
  148.6 2.6 collective-permute-start.17
  149.9 6.8 %collective-permute-start.16 = (f32[2,1,1,1024]{3,2,1,0:T(1,128)S(1)}, f32[2,1,1,1024]{3,2,1,0:T(1,128)S(1)}, u32[]{:S(2)}, u32[]{:S(2)}) collective-permute-start(f32[2,1,1,1024]{3,2,1,0:T(1,128)S(1)} %get-tuple-element.49), channel_id=1, source_target_pairs={{4,0},{8,4},{12,8},{5,1},{9,5},{13,9},{6,2},{10,6},{14,10},{7,3},{... | collective-permute-start | bytes 24584 | tf_op jit(solution)/shard_map/ppermute | solution.py:23
  156.7 6.9 %collective-permute-start.18 = (f32[2,1,130,1]{3,2,1,0:T(8,128)S(1)}, f32[2,1,130,1]{3,2,1,0:T(8,128)S(1)}, u32[]{:S(2)}, u32[]{:S(2)}) collective-permute-start(f32[2,1,130,1]{3,2,1,0:T(8,128)S(1)} %get-tuple-element.28), channel_id=1, source_target_pairs={{1,0},{2,1},{3,2},{5,4},{6,5},{7,6},{9,8},{10,9},{11,10},{13,12},{... | collective-permute-start | bytes 3128 | tf_op jit(solution)/shard_map/ppermute | solution.py:23
  158.0 7.4 %collective-permute-start.19 = (f32[2,1,130,1]{3,2,1,0:T(8,128)S(1)}, f32[2,1,130,1]{3,2,1,0:T(8,128)S(1)}, u32[]{:S(2)}, u32[]{:S(2)}) collective-permute-start(f32[2,1,130,1]{3,2,1,0:T(8,128)S(1)} %get-tuple-element.29), channel_id=1, source_target_pairs={{0,1},{1,2},{2,3},{4,5},{5,6},{6,7},{8,9},{9,10},{10,11},{12,13},{... | collective-permute-start | bytes 3128 | tf_op jit(solution)/shard_map/ppermute | solution.py:22
  166.5 4.5 %collective-permute-start.21 = (f32[2,1,1,1024]{3,2,1,0:T(1,128)S(1)}, f32[2,1,1,1024]{3,2,1,0:T(1,128)S(1)}, u32[]{:S(2)}, u32[]{:S(2)}) collective-permute-start(f32[2,1,1,1024]{3,2,1,0:T(1,128)S(1)} %get-tuple-element.46), channel_id=1, source_target_pairs={{0,4},{4,8},{8,12},{1,5},{5,9},{9,13},{2,6},{6,10},{10,14},{3,7},{... | collective-permute-start | bytes 24584 | tf_op jit(solution)/shard_map/ppermute | solution.py:22
  169.7 3.4 %collective-permute-start.20 = (f32[2,1,1,1024]{3,2,1,0:T(1,128)S(1)}, f32[2,1,1,1024]{3,2,1,0:T(1,128)S(1)}, u32[]{:S(2)}, u32[]{:S(2)}) collective-permute-start(f32[2,1,1,1024]{3,2,1,0:T(1,128)S(1)} %get-tuple-element.47), channel_id=1, source_target_pairs={{4,0},{8,4},{12,8},{5,1},{9,5},{13,9},{6,2},{10,6},{14,10},{7,3},{... | collective-permute-start | bytes 24584 | tf_op jit(solution)/shard_map/ppermute | solution.py:23
  173.3 7.4 %collective-permute-start.22 = (f32[2,1,130,1]{3,2,1,0:T(8,128)S(1)}, f32[2,1,130,1]{3,2,1,0:T(8,128)S(1)}, u32[]{:S(2)}, u32[]{:S(2)}) collective-permute-start(f32[2,1,130,1]{3,2,1,0:T(8,128)S(1)} %get-tuple-element.26), channel_id=1, source_target_pairs={{1,0},{2,1},{3,2},{5,4},{6,5},{7,6},{9,8},{10,9},{11,10},{13,12},{... | collective-permute-start | bytes 3128 | tf_op jit(solution)/shard_map/ppermute | solution.py:23
  174.6 7.6 %collective-permute-start.23 = (f32[2,1,130,1]{3,2,1,0:T(8,128)S(1)}, f32[2,1,130,1]{3,2,1,0:T(8,128)S(1)}, u32[]{:S(2)}, u32[]{:S(2)}) collective-permute-start(f32[2,1,130,1]{3,2,1,0:T(8,128)S(1)} %get-tuple-element.27), channel_id=1, source_target_pairs={{0,1},{1,2},{2,3},{4,5},{5,6},{6,7},{8,9},{9,10},{10,11},{12,13},{... | collective-permute-start | bytes 3128 | tf_op jit(solution)/shard_map/ppermute | solution.py:22
  187.3 4.8 %collective-permute-start.25 = (f32[2,1,1,1024]{3,2,1,0:T(1,128)S(1)}, f32[2,1,1,1024]{3,2,1,0:T(1,128)S(1)}, u32[]{:S(2)}, u32[]{:S(2)}) collective-permute-start(f32[2,1,1,1024]{3,2,1,0:T(1,128)S(1)} %get-tuple-element.42), channel_id=1, source_target_pairs={{0,4},{4,8},{8,12},{1,5},{5,9},{9,13},{2,6},{6,10},{10,14},{3,7},{... | collective-permute-start | bytes 24584 | tf_op jit(solution)/shard_map/ppermute | solution.py:22
  190.7 3.4 %collective-permute-start.24 = (f32[2,1,1,1024]{3,2,1,0:T(1,128)S(1)}, f32[2,1,1,1024]{3,2,1,0:T(1,128)S(1)}, u32[]{:S(2)}, u32[]{:S(2)}) collective-permute-start(f32[2,1,1,1024]{3,2,1,0:T(1,128)S(1)} %get-tuple-element.43), channel_id=1, source_target_pairs={{4,0},{8,4},{12,8},{5,1},{9,5},{13,9},{6,2},{10,6},{14,10},{7,3},{... | collective-permute-start | bytes 24584 | tf_op jit(solution)/shard_map/ppermute | solution.py:23
  194.3 7.4 %collective-permute-start.26 = (f32[2,1,130,1]{3,2,1,0:T(8,128)S(1)}, f32[2,1,130,1]{3,2,1,0:T(8,128)S(1)}, u32[]{:S(2)}, u32[]{:S(2)}) collective-permute-start(f32[2,1,130,1]{3,2,1,0:T(8,128)S(1)} %get-tuple-element.24), channel_id=1, source_target_pairs={{1,0},{2,1},{3,2},{5,4},{6,5},{7,6},{9,8},{10,9},{11,10},{13,12},{... | collective-permute-start | bytes 3128 | tf_op jit(solution)/shard_map/ppermute | solution.py:23
  195.6 7.6 %collective-permute-start.27 = (f32[2,1,130,1]{3,2,1,0:T(8,128)S(1)}, f32[2,1,130,1]{3,2,1,0:T(8,128)S(1)}, u32[]{:S(2)}, u32[]{:S(2)}) collective-permute-start(f32[2,1,130,1]{3,2,1,0:T(8,128)S(1)} %get-tuple-element.25), channel_id=1, source_target_pairs={{0,1},{1,2},{2,3},{4,5},{5,6},{6,7},{8,9},{9,10},{10,11},{12,13},{... | collective-permute-start | bytes 3128 | tf_op jit(solution)/shard_map/ppermute | solution.py:22
  204.5 4.8 %collective-permute-start.29 = (f32[2,1,1,1024]{3,2,1,0:T(1,128)S(1)}, f32[2,1,1,1024]{3,2,1,0:T(1,128)S(1)}, u32[]{:S(2)}, u32[]{:S(2)}) collective-permute-start(f32[2,1,1,1024]{3,2,1,0:T(1,128)S(1)} %get-tuple-element.40), channel_id=1, source_target_pairs={{0,4},{4,8},{8,12},{1,5},{5,9},{9,13},{2,6},{6,10},{10,14},{3,7},{... | collective-permute-start | bytes 24584 | tf_op jit(solution)/shard_map/ppermute | solution.py:22
  208.0 3.4 %collective-permute-start.28 = (f32[2,1,1,1024]{3,2,1,0:T(1,128)S(1)}, f32[2,1,1,1024]{3,2,1,0:T(1,128)S(1)}, u32[]{:S(2)}, u32[]{:S(2)}) collective-permute-start(f32[2,1,1,1024]{3,2,1,0:T(1,128)S(1)} %get-tuple-element.41), channel_id=1, source_target_pairs={{4,0},{8,4},{12,8},{5,1},{9,5},{13,9},{6,2},{10,6},{14,10},{7,3},{... | collective-permute-start | bytes 24584 | tf_op jit(solution)/shard_map/ppermute | solution.py:23
  211.5 7.4 %collective-permute-start.30 = (f32[2,1,130,1]{3,2,1,0:T(8,128)S(1)}, f32[2,1,130,1]{3,2,1,0:T(8,128)S(1)}, u32[]{:S(2)}, u32[]{:S(2)}) collective-permute-start(f32[2,1,130,1]{3,2,1,0:T(8,128)S(1)} %get-tuple-element.22), channel_id=1, source_target_pairs={{1,0},{2,1},{3,2},{5,4},{6,5},{7,6},{9,8},{10,9},{11,10},{13,12},{... | collective-permute-start | bytes 3128 | tf_op jit(solution)/shard_map/ppermute | solution.py:23
  212.8 7.6 %collective-permute-start.31 = (f32[2,1,130,1]{3,2,1,0:T(8,128)S(1)}, f32[2,1,130,1]{3,2,1,0:T(8,128)S(1)}, u32[]{:S(2)}, u32[]{:S(2)}) collective-permute-start(f32[2,1,130,1]{3,2,1,0:T(8,128)S(1)} %get-tuple-element.23), channel_id=1, source_target_pairs={{0,1},{1,2},{2,3},{4,5},{5,6},{6,7},{8,9},{9,10},{10,11},{12,13},{... | collective-permute-start | bytes 3128 | tf_op jit(solution)/shard_map/ppermute | solution.py:22
Sparse Core Ops, SparseCore 0:
  8.9 23.9 all-gather.1
  226.4 42.9 all-reduce.1
where the time goes:
time: 279 us; the launch traced here: 278 us
  waiting for transfers between devices  107 us (38%)
  starting transfers between devices  83.6 us (30%)
  other arithmetic  35.8 us (13%)
  blocking collectives  32.3 us (12%)
  between operations  14.7 us (5%)
  local copies, waits for them, and re-layouts  5.17 us (2%)
    ppermute x16, starting transfers between devices, with_halo(): before = lax.ppermute(last, axis, up)  62.8 us
    psum x1, waiting for transfers between devices, per_device(): summed = lax.psum(local_grads, 'illum')  43.1 us
    psum x1, blocking collectives, per_device(): lax.psum(jnp.sum(target * target, axis=(0, 2, 3)), ('row', 'col'))  32.3 us
    ppermute x16, waiting for transfers between devices, with_halo(): after = lax.ppermute(first, axis, down)  28.5 us
    all_gather x1, waiting for transfers between devices, per_device(): all_planes = lax.all_gather(phase_delay, 'illum', axis=1, tiled=True)  23.1 us
    ppermute x16, starting transfers between devices, with_halo(): after = lax.ppermute(first, axis, down)  20.8 us
    ppermute x16, waiting for transfers between devices, with_halo(): before = lax.ppermute(last, axis, up)  11.2 us
    sub x1, other arithmetic, per_device(): wave_field[0] * cosine - wave_field[1] * sine_part  6.09 us
  transfers between devices with their start and end apart: 34, of which 24 were waited for; matrix products, arithmetic and copies ran while one was open for 1% of the time, Pallas kernels for 0%

commit v1 on v0

v1 whole, which is shorter than its diff:
```python
import functools
import math

import jax
import jax.numpy as jnp
from jax import lax
from jax.experimental import pallas as pl
from jax.experimental.pallas import tpu as pltpu
from jax.sharding import PartitionSpec as P

EPS_ENERGY = 1e-06
RIM = 8
REACH = 4
LANES = 128
F32 = jnp.float32


def sine_cosine(x):
    y = x * x
    s = -2.5052108385441718e-08
    for c in (2.7557319223985893e-06, -1.9841269841269841e-04, 8.333333333333333e-03, -1.6666666666666666e-01):
        s = s * y + c
    c_ = -2.7557319223985888e-07
    for c in (2.48015873015873e-05, -1.3888888888888889e-03, 4.1666666666666664e-02, -0.5, 1.0):
        c_ = c_ * y + c
    return x + x * y * s, c_


def sine_cosine_of_turns(turns):
    quarters = 4.0 * (turns - jnp.floor(turns))
    nearest = jnp.floor(quarters + 0.5)
    s, c = sine_cosine((quarters - nearest) * (0.5 * math.pi))
    odd = (nearest == 1.0) | (nearest == 3.0)
    s, c = jnp.where(odd, c, s), jnp.where(odd, s, c)
    s = jnp.where((nearest == 2.0) | (nearest == 3.0), -s, s)
    c = jnp.where((nearest == 1.0) | (nearest == 2.0), -c, c)
    return s, c


def lane_ids(shape):
    return lax.broadcasted_iota(jnp.int32, shape, len(shape) - 1)


class Tile:
    def __init__(self, stripe, tiles, top, bottom, rim_lanes):
        self.stripe, self.tiles = stripe, tiles
        self.rows = stripe + 2 * RIM
        self.top, self.bottom, self.rim_lanes = top, bottom, rim_lanes
        step = 32 if stripe % 32 == 0 else 8
        self.inner = [(2 * RIM + r, step, None) for r in range(0, stripe, step)]
        self.blocks = [(RIM, RIM, top)] + self.inner + [(2 * RIM + stripe, RIM, bottom)]

    def sweep(self, body, blocks):
        def one(t, last):
            left = jnp.where(t == 0, self.tiles - 1, t - 1) if not last else self.tiles - 2
            right = t + 1 if not last else 0
            for first, count, factor in blocks:
                mask = (lambda x: x) if factor is None else (lambda x, f=factor: x * f)
                if last:
                    mask = lambda x, m=mask: m(x) * self.rim_lanes
                body(t, left, right, pl.ds(first, count), mask)

        def step(t, carry):
            one(t, False)
            return carry

        lax.fori_loop(0, self.tiles - 1, step, 0)
        one(self.tiles - 1, True)


def beside(ref, t, left, right, rows):
    above = pl.ds(rows.start - 1, rows.size)
    below = pl.ds(rows.start + 1, rows.size)
    here = ref[t, rows, :]
    lane = lane_ids(here.shape)
    west = pltpu.roll(jnp.where(lane == LANES - 1, ref[left, rows, :], here), 1, 1)
    east = pltpu.roll(jnp.where(lane == 0, ref[right, rows, :], here), LANES - 1, 1)
    return here, (ref[t, above, :] + ref[t, below, :]) + (west + east)


def first_half(tile, field, half, sign, blocks):
    fr, fi = field
    hr, hi = half

    def body(t, left, right, rows, mask):
        real, beside_real = beside(fr, t, left, right, rows)
        imag, beside_imag = beside(fi, t, left, right, rows)
        hr[t, rows, :] = mask(beside_real + (2.0 * sign) * imag)
        hi[t, rows, :] = mask(beside_imag - (2.0 * sign) * real)

    tile.sweep(body, blocks)


def second_half(tile, field, half, blocks, use):
    fr, fi = field
    hr, hi = half

    def body(t, left, right, rows, mask):
        _, beside_real = beside(hr, t, left, right, rows)
        _, beside_imag = beside(hi, t, left, right, rows)
        use(t, rows, mask, 0.1 * beside_real - fr[t, rows, :], 0.1 * beside_imag - fi[t, rows, :])

    tile.sweep(body, blocks)


def gradient_kernel(sizes, place_ref, angles_ref, scale_ref, phase_ref, target_ref, out_ref,
                    c0, s0, c1, s1, w0r, w0i, w1r, w1i, gr, gi, hr, hi, row_r, row_i, col_r, col_i):
    stripe, tiles, illums, total_rows, total_cols = sizes
    row_first, col_first = place_ref[0], place_ref[1]
    width = (tiles - 1) * LANES
    top = jnp.where(row_first == 0, 0.0, 1.0).astype(F32)
    bottom = jnp.where(row_first + stripe == total_rows, 0.0, 1.0).astype(F32)
    lane = lane_ids((1, LANES))
    in_west = (lane >= LANES - RIM) & (col_first > 0)
    in_east = (lane < RIM) & (col_first + width < total_cols)
    rim_lanes = jnp.where(in_west | in_east, 1.0, 0.0).astype(F32)
    tile = Tile(stripe, tiles, top, bottom, rim_lanes)
    rows_all = tile.rows
    span = pl.ds(RIM, rows_all)

    for ref in (w0r, w0i, w1r, w1i, gr, gi, hr, hi):
        ref[:, 0:RIM, :] = jnp.zeros((tiles, RIM, LANES), F32)
        ref[:, rows_all + RIM :, :] = jnp.zeros((tiles, RIM, LANES), F32)
    out_ref[...] = jnp.zeros(out_ref.shape, F32)

    def trig(t, carry):
        here = pl.ds(pl.multiple_of(t * LANES, LANES), LANES)
        for k, (c, s) in enumerate(((c0, s0), (c1, s1))):
            s[t, span, :], c[t, span, :] = sine_cosine(phase_ref[k, :, here])
        return carry

    lax.fori_loop(0, tiles, trig, 0)

    def illum(j, carry):
        tilt_x, tilt_y = angles_ref[j, 0].astype(F32), angles_ref[j, 1].astype(F32)
        scale = scale_ref[j]
        ids = lax.broadcasted_iota(jnp.int32, (rows_all, LANES), 0) + (row_first - RIM)
        s, c = sine_cosine_of_turns(ids.astype(F32) * tilt_x / total_rows)
        row_r[...] = (-7.0 * c - 24.0 * s) * 0.04
        row_i[...] = (-7.0 * s + 24.0 * c) * 0.04
        at = lax.broadcasted_iota(jnp.int32, (col_r.shape[0], LANES), 0)
        on = lane_ids((col_r.shape[0], LANES))
        ids = col_first + at * LANES + on
        ids = jnp.where((at >= tiles - 1) & (on >= LANES // 2), col_first - LANES + on, ids)
        col_i[...], col_r[...] = sine_cosine_of_turns(ids.astype(F32) * tilt_y / total_cols)

        def start(t, left, right, rows, mask):
            ar, ai = row_r[pl.ds(rows.start - RIM, rows.size), :], row_i[pl.ds(rows.start - RIM, rows.size), :]
            br, bi = col_r[pl.ds(t, 1), :], col_i[pl.ds(t, 1), :]
            ur, ui = ar * br - ai * bi, ar * bi + ai * br
            c, s = c0[t, rows, :], s0[t, rows, :]
            w0r[t, rows, :] = mask(ur * c - ui * s)
            w0i[t, rows, :] = mask(ur * s + ui * c)

        tile.sweep(start, tile.blocks)
        first_half(tile, (w0r, w0i), (hr, hi), 1.0, tile.blocks)

        def modulate(t, rows, mask, ur, ui):
            c, s = c1[t, rows, :], s1[t, rows, :]
            w1r[t, rows, :] = mask(ur * c - ui * s)
            w1i[t, rows, :] = mask(ur * s + ui * c)

        second_half(tile, (w0r, w0i), (hr, hi), tile.blocks, modulate)
        first_half(tile, (w1r, w1i), (hr, hi), 1.0, tile.blocks)

        def residual(t, rows, mask, ur, ui):
            here = pl.ds(t * LANES if isinstance(t, int) else pl.multiple_of(t * LANES, LANES), LANES)
            at = pl.ds(rows.start - RIM, rows.size)
            gr[t, rows, :] = mask(ur - target_ref[j, 0, at, here])
            gi[t, rows, :] = mask(ui - target_ref[j, 1, at, here])

        second_half(tile, (w1r, w1i), (hr, hi), tile.blocks, residual)
        first_half(tile, (gr, gi), (hr, hi), -1.0, tile.blocks)

        def put(k, t, rows, value):
            here = pl.ds(t * LANES if isinstance(t, int) else pl.multiple_of(t * LANES, LANES), LANES)
            at = pl.ds(rows.start - 2 * RIM, rows.size)
            out_ref[k, at, here] = out_ref[k, at, here] + scale * value

        def back(t, rows, mask, ur, ui):
            if not isinstance(t, int) and 2 * RIM <= rows.start < 2 * RIM + stripe:
                put(1, t, rows, ui * w1r[t, rows, :] - ur * w1i[t, rows, :])
            c, s = c1[t, rows, :], s1[t, rows, :]
            gr[t, rows, :] = mask(ur * c + ui * s)
            gi[t, rows, :] = mask(ui * c - ur * s)

        second_half(tile, (gr, gi), (hr, hi), tile.blocks, back)
        first_half(tile, (gr, gi), (hr, hi), -1.0, tile.blocks)

        def last(t, rows, mask, ur, ui):
            if not isinstance(t, int):
                put(0, t, rows, ui * w0r[t, rows, :] - ur * w0i[t, rows, :])

        second_half(tile, (gr, gi), (hr, hi), tile.inner, last)
        return carry

    lax.fori_loop(0, illums, illum, 0)


def halo(x, axis, dim, width, index_of=None):
    peers = lax.axis_size(axis)
    up = [(i, i + 1) for i in range(peers - 1)]
    before = lax.ppermute(lax.slice_in_dim(x, x.shape[dim] - width, x.shape[dim], axis=dim), axis, up)
    after = lax.ppermute(lax.slice_in_dim(x, 0, width, axis=dim), axis, [(j, i) for i, j in up])
    return before, after


def with_column_rims(x, width):
    before, after = halo(x, "col", x.ndim - 1, width)
    gap = jnp.zeros(x.shape[:-1] + (LANES - 2 * width,), x.dtype)
    return jnp.concatenate([x, after, gap, before], axis=-1)


def stripe_halo(x, width):
    illums, rows = lax.axis_size("illum"), lax.axis_size("row")
    where = [(s % illums) * rows + s // illums for s in range(illums * rows)]
    up = [(where[s], where[s + 1]) for s in range(illums * rows - 1)]
    before = lax.ppermute(x[:, -width:], ("illum", "row"), up)
    after = lax.ppermute(x[:, :width], ("illum", "row"), [(b, a) for a, b in up])
    return jnp.concatenate([before, x, after], axis=1)


def per_device(phase_delay, angles, measured):
    illums = lax.axis_size("illum")
    slices, stripe, width = phase_delay.shape
    tile_rows = measured.shape[2]
    total_rows, total_cols = tile_rows * lax.axis_size("row"), width * lax.axis_size("col")
    tiles = width // LANES + 1
    row_first = lax.axis_index("row") * tile_rows + lax.axis_index("illum") * stripe
    col_first = lax.axis_index("col") * width

    target = measured[:, 0].astype(F32)
    energy = lax.psum(jnp.sum(target * target).reshape(1), ("row", "col"))
    energies = lax.all_gather(energy, "illum", tiled=True) / (total_rows * total_cols) + EPS_ENERGY
    tilts = lax.all_gather(angles, "illum", tiled=True)

    phase = with_column_rims(stripe_halo(phase_delay, RIM), RIM)
    above, below = halo(target, "row", 1, REACH)
    target = with_column_rims(jnp.concatenate([above, target, below], axis=1), REACH)
    windows = jnp.stack([target[:, i * stripe : (i + 1) * stripe + 2 * REACH] for i in range(illums)])
    windows = lax.all_to_all(windows, "illum", 0, 0, tiled=True)
    windows = jnp.pad(windows, ((0, 0), (0, 0), (RIM - REACH, RIM - REACH), (0, 0)))

    field = pltpu.VMEM((tiles, stripe + 4 * RIM, LANES), F32)
    rows_all = stripe + 2 * RIM
    return pl.pallas_call(
        functools.partial(gradient_kernel, (stripe, tiles, illums, total_rows, total_cols)),
        out_shape=jax.ShapeDtypeStruct(phase_delay.shape, F32),
        in_specs=[pl.BlockSpec(memory_space=pltpu.SMEM)] * 3 + [pl.BlockSpec(memory_space=pltpu.VMEM)] * 2,
        out_specs=pl.BlockSpec(memory_space=pltpu.VMEM),
        scratch_shapes=[field] * 12
        + [pltpu.VMEM((rows_all, LANES), F32)] * 2
        + [pltpu.VMEM((-(-tiles // 8) * 8, LANES), F32)] * 2,
        compiler_params=pltpu.CompilerParams(vmem_limit_bytes=48 * 2**20),
    )(jnp.stack([row_first, col_first]), tilts, 2.0 / energies, phase, windows)


def solution(mesh):
    placed = (P(None, ("row", "illum"), "col"), P("illum", None), P(None, "illum", "row", "col"))
    return jax.shard_map(
        per_device,
        mesh=mesh,
        in_specs=placed,
        out_specs=P(None, ("row", "illum"), "col"),
        check_vma=False,
    )
```

time: 279 us -> 106 us (0.38)
  the two profiles are of different devices: /device:TPU:0 before, /device:TPU:12 now
where the time goes in v1:
time: 106 us
  blocking collectives  46.7 us (44%)
  starting transfers between devices  26.7 us (25%)
  Pallas kernels  18.8 us (18%)
  waiting for transfers between devices  6.25 us (6%)
  local copies, waits for them, and re-layouts  3.62 us (3%)
  other arithmetic  3.6 us (3%)
    psum x1, blocking collectives, per_device(): energy = lax.psum(jnp.sum(target * target).reshape(1), ('row', 'col'))  31 us
    pallas_call x1, Pallas kernels, per_device(): pl.pallas_call(functools.partial(gradient_kernel, (stripe, tiles, illums,...  18.8 us
    all_gather x1, blocking collectives, per_device(): tilts = lax.all_gather(angles, 'illum', tiled=True)  10.8 us
    ppermute x3, starting transfers between devices, halo(): lax.ppermute(lax.slice_in_dim(x, 0, width, axis=dim), axis, [(j, i) for i...  10 us
    ppermute x3, starting transfers between devices, halo(): lax.ppermute(lax.slice_in_dim(x, x.shape[dim] - width, x.shape[dim], axis...  7.76 us
    unnamed x1, blocking collectives  4.94 us
    ppermute x3, waiting for transfers between devices, halo(): lax.ppermute(lax.slice_in_dim(x, x.shape[dim] - width, x.shape[dim], axis...  4.17 us
    all_to_all x1, starting transfers between devices, per_device(): windows = lax.all_to_all(windows, 'illum', 0, 0, tiled=True)  3.63 us
  transfers between devices with their start and end apart: 9, of which 2 were waited for; matrix products, arithmetic and copies ran while one was open for 6% of the time, Pallas kernels for 0%

profile of v1, /device:TPU:12, one launch (start us, length us, event | category | flops | bytes accessed | tf_op | source)
XLA Modules:
  0.0 105.9 jit_solution(9638655574216007610)
XLA Ops:
  0.0 0.0 copy-start.3
  0.0 0.0 copy-start
  0.0 0.0 copy-start.1
  0.0 1.2 %bitcast_convert_fusion = f32[2,128,1024]{2,1,0:T(8,128)S(1)} fusion(bf16[2,1,128,1024]{3,2,1,0:T(8,128)(2,1)} %param.5), kind=kLoop, calls=%fused_computation.5 | loop fusion | flops 262144 | bytes 1572864 | tf_op jit(solution)/shard_map/convert_element_type | solution.py:232
  1.3 1.9 %collective-permute-start.4 = (f32[2,4,1024]{2,1,0:T(4,128)S(1)}, f32[2,4,1024]{2,1,0:T(4,128)S(1)}, u32[]{:S(2)}, u32[]{:S(2)}) collective-permute-start(f32[2,4,1024]{2,1,0:T(4,128)S(1)} %get-tuple-element.9), channel_id=1, source_target_pairs={{0,4},{4,8},{8,12},{1,5},{5,9},{9,13},{2,6},{6,10},{10,14},{3,7},{... | collective-permute-start | bytes 98312 | tf_op jit(solution)/shard_map/ppermute | solution.py:203
  3.2 3.6 %collective-permute-start.5 = (f32[2,4,1024]{2,1,0:T(4,128)S(1)}, f32[2,4,1024]{2,1,0:T(4,128)S(1)}, u32[]{:S(2)}, u32[]{:S(2)}) collective-permute-start(f32[2,4,1024]{2,1,0:T(4,128)S(1)} %get-tuple-element.10), channel_id=1, source_target_pairs={{4,0},{8,4},{12,8},{5,1},{9,5},{13,9},{6,2},{10,6},{14,10},{7,3},{... | collective-permute-start | bytes 98312 | tf_op jit(solution)/shard_map/ppermute | solution.py:204
  6.8 0.0 copy-done.1
  6.9 0.6 fusion.3
  7.5 3.4 %collective-permute-start = (f32[2,8,1024]{2,1,0:T(8,128)}, f32[2,8,1024]{2,1,0:T(8,128)S(1)}, u32[]{:S(2)}, u32[]{:S(2)}) collective-permute-start(f32[2,8,1024]{2,1,0:T(8,128)} %get-tuple-element.14), channel_id=1, source_target_pairs={{0,16},{16,4},{4,20},{20,8},{8,24},{24,12},{12,28},{1,17},{17,5},{... | collective-permute-start | bytes 196616 | tf_op jit(solution)/shard_map/ppermute | solution.py:218
  10.9 0.0 copy-done
  10.9 0.9 multiply_reduce_fusion
  11.8 31.0 %psum.7 = f32[1]{0:T(128)} all-reduce(f32[1]{0:T(128)} %bitcast.6), channel_id=1, replica_groups=mesh['illum'=2,'row'=4,'col'=4] {'row','col'}, use_global_device_ids=true, to_apply=%region_1.0 | all-reduce | flops 1 | bytes 8 | tf_op jit(solution)/shard_map/psum | solution.py:233
  42.8 0.0 copy-done.3
  42.8 0.6 dynamic-slice
  43.5 1.4 %dynamic-update-slice = f32[2]{0:T(128)S(1)} dynamic-update-slice(f32[2]{0:T(128)S(1)} %broadcast.15, f32[1]{0:T(128)} %psum.7, u32[]{:T(128)} %bitcast.7) | dynamic-update-slice | bytes 12
  44.8 1.9 %collective-permute-start.1 = (f32[2,8,1024]{2,1,0:T(8,128)S(1)}, f32[2,8,1024]{2,1,0:T(8,128)S(1)}, u32[]{:S(2)}, u32[]{:S(2)}) collective-permute-start(f32[2,8,1024]{2,1,0:T(8,128)S(1)} %get-tuple-element.13), channel_id=1, source_target_pairs={{16,0},{4,16},{20,4},{8,20},{24,8},{12,24},{28,12},{17,1},{5,17},{... | collective-permute-start | bytes 196616 | tf_op jit(solution)/shard_map/ppermute | solution.py:219
  46.8 4.9 %all-reduce.1 = f32[2]{0:T(128)S(1)} all-reduce(f32[2]{0:T(128)S(1)} %dynamic-update-slice), channel_id=1, replica_groups=mesh['illum'=2,'row'=4,'col'=4] {'illum'}, use_global_device_ids=true, to_apply=%add.1 | all-reduce | flops 2 | bytes 16
  51.7 0.0 collective-permute-done.4
  51.7 0.0 collective-permute-done.5
  51.7 0.2 pad_maximum_fusion.1
  51.9 0.1 fusion
  52.0 4.4 %collective-permute-start.6 = (f32[2,136,4]{2,1,0:T(8,128)S(1)}, f32[2,136,4]{2,1,0:T(8,128)S(1)}, u32[]{:S(2)}, u32[]{:S(2)}) collective-permute-start(f32[2,136,4]{2,1,0:T(8,128)S(1)} %get-tuple-element.8), channel_id=1, source_target_pairs={{1,0},{2,1},{3,2},{5,4},{6,5},{7,6},{9,8},{10,9},{11,10},{13,12},{... | collective-permute-start | bytes 13064 | tf_op jit(solution)/shard_map/ppermute | solution.py:204
  56.4 1.9 %collective-permute-start.7 = (f32[2,136,4]{2,1,0:T(8,128)S(1)}, f32[2,136,4]{2,1,0:T(8,128)S(1)}, u32[]{:S(2)}, u32[]{:S(2)}) collective-permute-start(f32[2,136,4]{2,1,0:T(8,128)S(1)} %get-tuple-element.7), channel_id=1, source_target_pairs={{0,1},{1,2},{2,3},{4,5},{5,6},{6,7},{8,9},{9,10},{10,11},{12,13},{... | collective-permute-start | bytes 13064 | tf_op jit(solution)/shard_map/ppermute | solution.py:203
  58.4 2.1 %collective-permute-done.6 = f32[2,136,4]{2,1,0:T(8,128)S(1)} collective-permute-done((f32[2,136,4]{2,1,0:T(8,128)S(1)}, f32[2,136,4]{2,1,0:T(8,128)S(1)}, u32[]{:S(2)}, u32[]{:S(2)}) %collective-permute-start.6) | collective-permute-done | bytes 4384 | tf_op jit(solution)/shard_map/ppermute | solution.py:204
  60.5 4.2 %collective-permute-done.7 = f32[2,136,4]{2,1,0:T(8,128)S(1)} collective-permute-done((f32[2,136,4]{2,1,0:T(8,128)S(1)}, f32[2,136,4]{2,1,0:T(8,128)S(1)}, u32[]{:S(2)}, u32[]{:S(2)}) %collective-permute-start.7) | collective-permute-done | bytes 4384 | tf_op jit(solution)/shard_map/ppermute | solution.py:203
  64.6 0.4 concatenate.15
  65.0 0.1 slice_bitcast_fusion.1
  65.1 1.2 %pad_maximum_fusion = f32[2,2,72,1152]{3,2,1,0:T(8,128)} fusion(f32[1,2,72,1152]{3,2,1,0:T(8,128)S(1)} %get-tuple-element.6, f32[1,2,72,1152]{3,2,1,0:T(8,128)S(1)} %get-tuple-element.5), kind=kLoop, calls=%fused_computation | loop fusion | flops 331776 | bytes 2654208 | tf_op jit(solution)/shard_map/stack | solution.py:240
  66.3 3.6 %all-to-all-start = ((f32[2,2,72,1152]{3,2,1,0:T(8,128)}), f32[2,2,72,1152]{3,2,1,0:T(8,128)S(1)}, u32[]{:S(2)}, u32[]{:S(2)}) async-start(f32[2,2,72,1152]{3,2,1,0:T(8,128)} %pad_maximum_fusion), calls=%async_computation | async-start | bytes 2654208 | tf_op jit(solution)/shard_map/all_to_all | solution.py:241
  69.9 0.0 copy-start.2
  69.9 0.0 collective-permute-done
  70.0 0.0 collective-permute-done.1
  70.0 0.1 fusion.2
  70.1 1.9 %collective-permute-start.2 = (f32[2,80,8]{2,1,0:T(8,128)S(1)}, f32[2,80,8]{2,1,0:T(8,128)S(1)}, u32[]{:S(2)}, u32[]{:S(2)}) collective-permute-start(f32[2,80,8]{2,1,0:T(8,128)S(1)} %get-tuple-element.12), channel_id=1, source_target_pairs={{1,0},{2,1},{3,2},{5,4},{6,5},{7,6},{9,8},{10,9},{11,10},{13,12},{... | collective-permute-start | bytes 15368 | tf_op jit(solution)/shard_map/ppermute | solution.py:204
  72.1 3.9 %collective-permute-start.3 = (f32[2,80,8]{2,1,0:T(8,128)S(1)}, f32[2,80,8]{2,1,0:T(8,128)S(1)}, u32[]{:S(2)}, u32[]{:S(2)}) collective-permute-start(f32[2,80,8]{2,1,0:T(8,128)S(1)} %get-tuple-element.11), channel_id=1, source_target_pairs={{0,1},{1,2},{2,3},{4,5},{5,6},{6,7},{8,9},{9,10},{10,11},{12,13},{... | collective-permute-start | bytes 15368 | tf_op jit(solution)/shard_map/ppermute | solution.py:203
  76.0 0.1 pad_add_fusion.place_ref
  76.1 0.0 copy-done.2
  76.1 10.8 %all-gather = s32[2,1,2]{2,1,0:T(1,128)S(1)} all-gather(s32[1,1,2]{2,1,0:T(1,128)S(1)} %bitcast.18), channel_id=1, replica_groups=mesh['illum'=2,'row'=4,'col'=4] {'illum'}, dimensions={0}, use_global_device_ids=true | all-gather | bytes 24 | tf_op jit(solution)/shard_map/all_gather | solution.py:235
  86.9 0.0 collective-permute-done.2
  86.9 0.0 collective-permute-done.3
  86.9 0.1 concatenate.13.phase_ref
  87.0 0.0 all-to-all-done
  87.0 0.1 pad.4.target_ref
  87.1 18.8 %shard_map.37 = f32[2,64,1024]{2,1,0:T(8,128)} custom-call(s32[2]{0:T(128)S(1)} %pad_add_fusion.place_ref, s32[2,2]{1,0:T(2,128)S(1)} %bitcast.17, f32[2]{0:T(128)S(1)} %add_divide_fusion.scale_ref, f32[2,80,1152]{2,1,0:T(8,128)S(1)} %concatenate.13.phase_ref, f32[2,2,80,1152]{3,2,1,0:T(8,128)S(1)} %pad.4.target_ref), custom_call_target="tpu_custom_call" | custom-call | tf_op jit(solution)/shard_map/pallas_call | solution.py:246
  (8 shorter events, 0.1 us)
Async XLA Ops:
  0.0 42.8 %copy-start.3 = (u32[32]{0:T(128)S(1)}, u32[32]{0:T(128)}, u32[]{:S(2)}) copy-start(u32[32]{0:T(128)} %constant.38) | copy-start | bytes 388
  0.0 10.9 %copy-start = (bf16[2,1,128,1024]{3,2,1,0:T(8,128)(2,1)S(1)}, bf16[2,1,128,1024]{3,2,1,0:T(8,128)(2,1)}, u32[]{:S(2)}) copy-start(bf16[2,1,128,1024]{3,2,1,0:T(8,128)(2,1)} %param.5) | copy-start | bytes 1572868
  0.0 6.8 %copy-start.1 = (f32[2,64,1024]{2,1,0:T(8,128)S(1)}, f32[2,64,1024]{2,1,0:T(8,128)}, u32[]{:S(2)}) copy-start(f32[2,64,1024]{2,1,0:T(8,128)} %param.3) | copy-start | bytes 1572868
  1.3 50.4 %collective-permute-start.4 = (f32[2,4,1024]{2,1,0:T(4,128)S(1)}, f32[2,4,1024]{2,1,0:T(4,128)S(1)}, u32[]{:S(2)}, u32[]{:S(2)}) collective-permute-start(f32[2,4,1024]{2,1,0:T(4,128)S(1)} %get-tuple-element.9), channel_id=1, source_target_pairs={{0,4},{4,8},{8,12},{1,5},{5,9},{9,13},{2,6},{6,10},{10,14},{3,7},{... | collective-permute-start | bytes 98312 | tf_op jit(solution)/shard_map/ppermute | solution.py:203
  3.2 48.5 %collective-permute-start.5 = (f32[2,4,1024]{2,1,0:T(4,128)S(1)}, f32[2,4,1024]{2,1,0:T(4,128)S(1)}, u32[]{:S(2)}, u32[]{:S(2)}) collective-permute-start(f32[2,4,1024]{2,1,0:T(4,128)S(1)} %get-tuple-element.10), channel_id=1, source_target_pairs={{4,0},{8,4},{12,8},{5,1},{9,5},{13,9},{6,2},{10,6},{14,10},{7,3},{... | collective-permute-start | bytes 98312 | tf_op jit(solution)/shard_map/ppermute | solution.py:204
  7.5 62.4 %collective-permute-start = (f32[2,8,1024]{2,1,0:T(8,128)}, f32[2,8,1024]{2,1,0:T(8,128)S(1)}, u32[]{:S(2)}, u32[]{:S(2)}) collective-permute-start(f32[2,8,1024]{2,1,0:T(8,128)} %get-tuple-element.14), channel_id=1, source_target_pairs={{0,16},{16,4},{4,20},{20,8},{8,24},{24,12},{12,28},{1,17},{17,5},{... | collective-permute-start | bytes 196616 | tf_op jit(solution)/shard_map/ppermute | solution.py:218
  44.8 25.2 %collective-permute-start.1 = (f32[2,8,1024]{2,1,0:T(8,128)S(1)}, f32[2,8,1024]{2,1,0:T(8,128)S(1)}, u32[]{:S(2)}, u32[]{:S(2)}) collective-permute-start(f32[2,8,1024]{2,1,0:T(8,128)S(1)} %get-tuple-element.13), channel_id=1, source_target_pairs={{16,0},{4,16},{20,4},{8,20},{24,8},{12,24},{28,12},{17,1},{5,17},{... | collective-permute-start | bytes 196616 | tf_op jit(solution)/shard_map/ppermute | solution.py:219
  52.0 8.5 %collective-permute-start.6 = (f32[2,136,4]{2,1,0:T(8,128)S(1)}, f32[2,136,4]{2,1,0:T(8,128)S(1)}, u32[]{:S(2)}, u32[]{:S(2)}) collective-permute-start(f32[2,136,4]{2,1,0:T(8,128)S(1)} %get-tuple-element.8), channel_id=1, source_target_pairs={{1,0},{2,1},{3,2},{5,4},{6,5},{7,6},{9,8},{10,9},{11,10},{13,12},{... | collective-permute-start | bytes 13064 | tf_op jit(solution)/shard_map/ppermute | solution.py:204
  56.4 8.2 %collective-permute-start.7 = (f32[2,136,4]{2,1,0:T(8,128)S(1)}, f32[2,136,4]{2,1,0:T(8,128)S(1)}, u32[]{:S(2)}, u32[]{:S(2)}) collective-permute-start(f32[2,136,4]{2,1,0:T(8,128)S(1)} %get-tuple-element.7), channel_id=1, source_target_pairs={{0,1},{1,2},{2,3},{4,5},{5,6},{6,7},{8,9},{9,10},{10,11},{12,13},{... | collective-permute-start | bytes 13064 | tf_op jit(solution)/shard_map/ppermute | solution.py:203
  66.3 20.7 %all-to-all-start = ((f32[2,2,72,1152]{3,2,1,0:T(8,128)}), f32[2,2,72,1152]{3,2,1,0:T(8,128)S(1)}, u32[]{:S(2)}, u32[]{:S(2)}) async-start(f32[2,2,72,1152]{3,2,1,0:T(8,128)} %pad_maximum_fusion), calls=%async_computation | async-start | bytes 2654208 | tf_op jit(solution)/shard_map/all_to_all | solution.py:241
  69.9 6.1 %copy-start.2 = (s32[1,2]{1,0:T(1,128)S(1)}, s32[1,2]{1,0:T(1,128)}, u32[]{:S(2)}) copy-start(s32[1,2]{1,0:T(1,128)} %param.4) | copy-start | bytes 28
  70.1 16.7 %collective-permute-start.2 = (f32[2,80,8]{2,1,0:T(8,128)S(1)}, f32[2,80,8]{2,1,0:T(8,128)S(1)}, u32[]{:S(2)}, u32[]{:S(2)}) collective-permute-start(f32[2,80,8]{2,1,0:T(8,128)S(1)} %get-tuple-element.12), channel_id=1, source_target_pairs={{1,0},{2,1},{3,2},{5,4},{6,5},{7,6},{9,8},{10,9},{11,10},{13,12},{... | collective-permute-start | bytes 15368 | tf_op jit(solution)/shard_map/ppermute | solution.py:204
  72.1 14.8 %collective-permute-start.3 = (f32[2,80,8]{2,1,0:T(8,128)S(1)}, f32[2,80,8]{2,1,0:T(8,128)S(1)}, u32[]{:S(2)}, u32[]{:S(2)}) collective-permute-start(f32[2,80,8]{2,1,0:T(8,128)S(1)} %get-tuple-element.11), channel_id=1, source_target_pairs={{0,1},{1,2},{2,3},{4,5},{5,6},{6,7},{8,9},{9,10},{10,11},{12,13},{... | collective-permute-start | bytes 15368 | tf_op jit(solution)/shard_map/ppermute | solution.py:203

commit v2 on v1

--- a/solution.py
+++ b/solution.py
@@ -51,21 +51,15 @@
         self.blocks = [(RIM, RIM, top)] + self.inner + [(2 * RIM + stripe, RIM, bottom)]
 
     def sweep(self, body, blocks):
-        def one(t, last):
-            left = jnp.where(t == 0, self.tiles - 1, t - 1) if not last else self.tiles - 2
-            right = t + 1 if not last else 0
+        for t in range(self.tiles):
+            last = t == self.tiles - 1
             for first, count, factor in blocks:
-                mask = (lambda x: x) if factor is None else (lambda x, f=factor: x * f)
-                if last:
-                    mask = lambda x, m=mask: m(x) * self.rim_lanes
-                body(t, left, right, pl.ds(first, count), mask)
-
-        def step(t, carry):
-            one(t, False)
-            return carry
-
-        lax.fori_loop(0, self.tiles - 1, step, 0)
-        one(self.tiles - 1, True)
+
+                def mask(x, factor=factor, last=last):
+                    x = x if factor is None else x * factor
+                    return x * self.rim_lanes if last else x
+
+                body(t, (t - 1) % self.tiles, (t + 1) % self.tiles, pl.ds(first, count), mask)
 
 
 def beside(ref, t, left, right, rows):
@@ -103,98 +97,496 @@
     tile.sweep(body, blocks)
 
 
+def blank_rims(refs, tile):
+    for ref in refs:
+        for first in (0, tile.rows + RIM):
+            ref[:, first : first + RIM, :] = jnp.zeros((tile.tiles, RIM, LANES), F32)
+
+
+def incident_tables(tile, tilts, row_first, col_first, total_rows, total_cols, tables):
+    row_r, row_i, col_r, col_i = tables
+    ids = lax.broadcasted_iota(jnp.int32, (tile.rows, LANES), 0) + (row_first - RIM)
+    s, c = sine_cosine_of_turns(ids.astype(F32) * tilts[0] / total_rows)
+    row_r[...] = (-7.0 * c - 24.0 * s) * 0.04
+    row_i[...] = (-7.0 * s + 24.0 * c) * 0.04
+    at = lax.broadcasted_iota(jnp.int32, col_r.shape, 0)
+    on = lane_ids(col_r.shape)
+    ids = col_first + at * LANES + on
+    ids = jnp.where((at >= tile.tiles - 1) & (on >= LANES // 2), col_first - LANES + on, ids)
+    col_i[...], col_r[...] = sine_cosine_of_turns(ids.astype(F32) * tilts[1] / total_cols)
+
+
+def enter(tile, tables, trig, field):
+    row_r, row_i, col_r, col_i = tables
+    fr, fi = field
+
+    def start(t, left, right, rows, mask):
+        at = pl.ds(rows.start - RIM, rows.size)
+        ar, ai = row_r[at, :], row_i[at, :]
+        br, bi = col_r[t : t + 1, :], col_i[t : t + 1, :]
+        ur, ui = ar * br - ai * bi, ar * bi + ai * br
+        c, s = trig[0][t, rows, :], trig[1][t, rows, :]
+        fr[t, rows, :] = mask(ur * c - ui * s)
+        fi[t, rows, :] = mask(ur * s + ui * c)
+
+    tile.sweep(start, tile.blocks)
+
+
+def modulate_into(trig, field):
+    def use(t, rows, mask, ur, ui):
+        c, s = trig[0][t, rows, :], trig[1][t, rows, :]
+        field[0][t, rows, :] = mask(ur * c - ui * s)
+        field[1][t, rows, :] = mask(ur * s + ui * c)
+
+    return use
+
+
+def backward(tile, adjoint, half, w0, w1, trig1, put):
+    gr, gi = adjoint
+    own_tiles = tile.tiles - 1
+    inner = [first for first, _, _ in tile.inner]
+
+    def back(t, rows, mask, ur, ui):
+        if t < own_tiles and rows.start in inner:
+            put(1, t, rows, ui * w1[0][t, rows, :] - ur * w1[1][t, rows, :])
+        c, s = trig1[0][t, rows, :], trig1[1][t, rows, :]
+        gr[t, rows, :] = mask(ur * c + ui * s)
+        gi[t, rows, :] = mask(ui * c - ur * s)
+
+    def last(t, rows, mask, ur, ui):
+        if t < own_tiles:
+            put(0, t, rows, ui * w0[0][t, rows, :] - ur * w0[1][t, rows, :])
+
+    first_half(tile, adjoint, half, -1.0, tile.blocks)
+    second_half(tile, adjoint, half, tile.blocks, back)
+    first_half(tile, adjoint, half, -1.0, tile.blocks)
+    second_half(tile, adjoint, half, tile.inner, last)
+
+
+def own_columns(t):
+    return slice(t * LANES, (t + 1) * LANES)
+
+
+def own_rows(rows):
+    return slice(rows.start - 2 * RIM, rows.start - 2 * RIM + rows.size)
+
+
 def gradient_kernel(sizes, place_ref, angles_ref, scale_ref, phase_ref, target_ref, out_ref,
                     c0, s0, c1, s1, w0r, w0i, w1r, w1i, gr, gi, hr, hi, row_r, row_i, col_r, col_i):
     stripe, tiles, illums, total_rows, total_cols = sizes
     row_first, col_first = place_ref[0], place_ref[1]
+    tile = Tile(stripe, tiles, *edges_of(row_first, col_first, stripe, tiles, total_rows, total_cols))
+    blank_rims((w0r, w0i, w1r, w1i, gr, gi, hr, hi), tile)
+    out_ref[...] = jnp.zeros(out_ref.shape, F32)
+    span = slice(RIM, RIM + tile.rows)
+    for t in range(tiles):
+        for k, (c, s) in enumerate(((c0, s0), (c1, s1))):
+            s[t, span, :], c[t, span, :] = sine_cosine(phase_ref[k, :, own_columns(t)])
+    tables, half = (row_r, row_i, col_r, col_i), (hr, hi)
+
+    def illum(j, carry):
+        tilts = angles_ref[j, 0].astype(F32), angles_ref[j, 1].astype(F32)
+        incident_tables(tile, tilts, row_first, col_first, total_rows, total_cols, tables)
+        enter(tile, tables, (c0, s0), (w0r, w0i))
+        first_half(tile, (w0r, w0i), half, 1.0, tile.blocks)
+        second_half(tile, (w0r, w0i), half, tile.blocks, modulate_into((c1, s1), (w1r, w1i)))
+        first_half(tile, (w1r, w1i), half, 1.0, tile.blocks)
+
+        def residual(t, rows, mask, ur, ui):
+            at = slice(rows.start - RIM, rows.start - RIM + rows.size)
+            gr[t, rows, :] = mask(ur - target_ref[j, 0, at, own_columns(t)])
+            gi[t, rows, :] = mask(ui - target_ref[j, 1, at, own_columns(t)])
+
+        second_half(tile, (w1r, w1i), half, tile.blocks, residual)
+
+        def put(k, t, rows, value):
+            at = (k, own_rows(rows), own_columns(t))
+            out_ref[at] = out_ref[at] + scale_ref[j] * value
+
+        backward(tile, (gr, gi), half, (w0r, w0i), (w1r, w1i), (c1, s1), put)
+        return carry
+
+    lax.fori_loop(0, illums, illum, 0)
+
+
+def edges_of(row_first, col_first, stripe, tiles, total_rows, total_cols):
     width = (tiles - 1) * LANES
     top = jnp.where(row_first == 0, 0.0, 1.0).astype(F32)
     bottom = jnp.where(row_first + stripe == total_rows, 0.0, 1.0).astype(F32)
     lane = lane_ids((1, LANES))
     in_west = (lane >= LANES - RIM) & (col_first > 0)
     in_east = (lane < RIM) & (col_first + width < total_cols)
-    rim_lanes = jnp.where(in_west | in_east, 1.0, 0.0).astype(F32)
-    tile = Tile(stripe, tiles, top, bottom, rim_lanes)
-    rows_all = tile.rows
-    span = pl.ds(RIM, rows_all)
-
-    for ref in (w0r, w0i, w1r, w1i, gr, gi, hr, hi):
-        ref[:, 0:RIM, :] = jnp.zeros((tiles, RIM, LANES), F32)
-        ref[:, rows_all + RIM :, :] = jnp.zeros((tiles, RIM, LANES), F32)
-    out_ref[...] = jnp.zeros(out_ref.shape, F32)
-
-    def trig(t, carry):
-        here = pl.ds(pl.multiple_of(t * LANES, LANES), LANES)
+    return top, bottom, jnp.where(in_west | in_east, 1.0, 0.0).astype(F32)
+
+
+def pack_rows(real, imag, low):
+    first = lax.broadcasted_iota(jnp.int32, real.shape, 0) < 4
+    if low:
+        return jnp.where(first, real, pltpu.roll(imag, 4, 0))
+    return jnp.where(first, pltpu.roll(real, 4, 0), imag)
+
+
+def unpack_rows(packed, low):
+    turned = pltpu.roll(packed, 4, 0)
+    return (packed, turned) if low else (turned, packed)
+
+
+def edge_blocks(measured_ref, first):
+    base = first // 16 * 16
+    at = first - base
+    return [measured_ref[p, 0, base : base + 16, :].astype(F32)[at : at + 8] for p in range(2)]
+
+
+def energy_kernel(place_ref, tilt_ref, measured_ref, note_ref):
+    rows, cols = measured_ref.shape[2:]
+    total = jnp.zeros((8, cols), F32)
+    for p in range(2):
+        for r in range(0, rows, 16):
+            x = measured_ref[p, 0, r : r + 16, :].astype(F32)
+            x = x * x
+            total = total + (x[:8] + x[8:])
+    energy = jnp.sum(jnp.sum(total, axis=1, keepdims=True), axis=0, keepdims=True)
+    lane = lane_ids((8, LANES))
+    note = jnp.where(lane == place_ref[0] * 4 + place_ref[1], energy, 0.0)
+    note = jnp.where(lane == 16, tilt_ref[0, 0].astype(F32), note)
+    note_ref[...] = jnp.where(lane == 17, tilt_ref[0, 1].astype(F32), note)
+
+
+def send_kernel(place_ref, phase_ref, measured_ref, swap_ref, along_ref, same_ref):
+    stripe, width = phase_ref.shape[1:]
+    rows = 2 * stripe
+
+    def fill(other, near, low, phase_from, along, along_low, same, same_low):
+        for p in range(2):
+            for r in range(0, stripe, 16):
+                swap_ref[p * stripe + r : p * stripe + r + 16, :] = measured_ref[p, 0, other + r : other + r + 16, :].astype(F32)
+        swap_ref[rows:, :] = pack_rows(*edge_blocks(measured_ref, near), low)
+        for k in range(2):
+            along_ref[:, k * width : (k + 1) * width] = phase_ref[k, phase_from : phase_from + 8, :]
+        along_ref[:, 2 * width :] = pack_rows(*edge_blocks(measured_ref, along), along_low)
+        same_ref[...] = pack_rows(*edge_blocks(measured_ref, same), same_low)
+
+    @pl.when(place_ref[0] == 0)
+    def _():
+        fill(stripe, stripe - 8, False, 0, 0, True, rows - 8, False)
+
+    @pl.when(place_ref[0] == 1)
+    def _():
+        fill(0, stripe, True, stripe - 8, rows - 8, False, 0, True)
+
+
+def partner_kernel(place_ref, phase_ref, note_ref, core_note_ref, partner_ref, known_ref):
+    stripe, width = phase_ref.shape[1:]
+    for which, first in ((0, stripe - 8), (1, 0)):
+
+        @pl.when(place_ref[0] == which)
+        def _():
+            for k in range(2):
+                partner_ref[:, k * width : (k + 1) * width] = phase_ref[k, first : first + 8, :]
+
+    lane = lane_ids((8, LANES))
+    known = jnp.where(lane < 16, jnp.maximum(note_ref[...], core_note_ref[...]), note_ref[...])
+    partner_ref[:, 2 * width :] = known
+    known_ref[...] = known
+
+
+def same_kernel(packed_ref, known_ref, partner_ref, same_ref):
+    width = packed_ref.shape[1]
+    same_ref[:, :width] = packed_ref[...]
+    same_ref[:, width:] = jnp.maximum(known_ref[...], partner_ref[:, 2 * width :])
+
+
+def rim_pack_kernel(place_ref, phase_ref, measured_ref, known_ref, partner_ref, along_ref, same_ref, out_ref):
+    stripe, width = phase_ref.shape[1:]
+    rows = 2 * stripe
+    low_illum = place_ref[0] == 0
+    col, cols = place_ref[2], out_ref.shape[0]
+    lane = lane_ids((8, LANES))
+    known = jnp.maximum(jnp.maximum(known_ref[...], partner_ref[:, 2 * width :]), same_ref[:, width:])
+    for c in range(cols):
+        out_ref[c, out_ref.shape[1] - 8 :, :] = known
+
+    for east in (True, False):
+        edge = slice(width - LANES, width) if east else slice(0, LANES)
+        base = LANES - RIM if east else 0
+
+        @pl.when(col < cols - 1 if east else col > 0)
+        def _():
+            to = col + 1 if east else col - 1
+            groups = []
+            for j in range(stripe // 8 + 2):
+                items = []
+                for k in range(2):
+                    tile = slice(k * width + edge.start, k * width + edge.stop)
+                    if j == 0:
+                        items.append(jnp.where(low_illum, along_ref[:, tile], partner_ref[:, tile]))
+                    elif j == stripe // 8 + 1:
+                        items.append(jnp.where(low_illum, partner_ref[:, tile], along_ref[:, tile]))
+                    else:
+                        items.append(phase_ref[k, 8 * (j - 1) : 8 * j, edge])
+                groups.append(items)
+            while len(groups) < rows // 8 + 1:
+                groups.append([None, None])
+            for r in range(0, rows, 16):
+                both = [measured_ref[p, 0, r : r + 16, edge].astype(F32) for p in range(2)]
+                for h in range(2):
+                    groups[r // 8 + h] += [b[8 * h : 8 * h + 8] for b in both]
+            groups[rows // 8] += [same_ref[:, edge], along_ref[:, 2 * width + edge.start : 2 * width + edge.stop]]
+            for g in range(0, len(groups), 4):
+                acc = jnp.zeros((8, LANES), F32)
+                for q, items in enumerate(groups[g : g + 4]):
+                    for k, item in enumerate(items):
+                        if item is not None:
+                            slot = 4 * q + k
+                            shift = (8 * slot - base) % LANES
+                            moved = pltpu.roll(item, shift, 1) if shift else item
+                            acc = jnp.where((lane >= 8 * slot) & (lane < 8 * slot + 8), moved, acc)
+                out_ref[to, 2 * g : 2 * g + 8, :] = acc
+
+
+def rim_unpack_kernel(place_ref, got_ref, phase_rim_ref, rim_ref, relay_ref):
+    cols, depth = got_ref.shape[:2]
+    stripe = phase_rim_ref.shape[1] - 2 * RIM
+    rows = 2 * stripe
+    col = place_ref[2]
+    west, east = jnp.maximum(col - 1, 0), jnp.minimum(col + 1, cols - 1)
+    lane = lane_ids((8, LANES))
+    in_west = (lane >= LANES - RIM) & (col > 0)
+    in_east = (lane < RIM) & (col < cols - 1)
+    for g in range(0, rows // 8 + 1, 4):
+        a, b = got_ref[west, 2 * g : 2 * g + 8, :], got_ref[east, 2 * g : 2 * g + 8, :]
+        for j in range(g, min(g + 4, rows // 8 + 1)):
+            for k in range(4):
+                if k < 2 and j >= stripe // 8 + 2:
+                    continue
+                slot = 4 * (j - g) + k
+                from_west = pltpu.roll(a, (LANES - RIM - 8 * slot) % LANES, 1)
+                from_east = pltpu.roll(b, (-8 * slot) % LANES, 1) if slot else b
+                item = jnp.where(in_west, from_west, jnp.where(in_east, from_east, 0.0))
+                (phase_rim_ref if k < 2 else rim_ref)[k % 2, 8 * j : 8 * j + 8, :] = item
+    for which, other, near in ((0, stripe, stripe - 8), (1, 0, stripe)):
+
+        @pl.when(place_ref[0] == which)
+        def _():
+            for r in range(0, stripe, 8):
+                at = slice(other + r, other + r + 8)
+                relay_ref[r : r + 8, :] = rim_ref[0, at, :] + pltpu.roll(rim_ref[1, at, :], LANES // 2, 1)
+            at = slice(near, near + 8)
+            relay_ref[stripe : stripe + 8, :] = rim_ref[0, at, :] + pltpu.roll(rim_ref[1, at, :], LANES // 2, 1)
+
+    total = got_ref[0, depth - 8 :, :]
+    for c in range(1, cols):
+        total = total + got_ref[c, depth - 8 :, :]
+    relay_ref[stripe + 8 :, :] = total
+
+
+def tile_of(place_ref, sizes):
+    stripe, tiles, total_rows, total_cols = sizes
+    row_first = (place_ref[1] * 2 + place_ref[0]) * stripe
+    col_first = place_ref[2] * (tiles - 1) * LANES
+    edges = edges_of(row_first, col_first, stripe, tiles, total_rows, total_cols)
+    return Tile(stripe, tiles, *edges), row_first, col_first
+
+
+def fill_target(tile, target, low_illum, middle, near, far):
+    end = 2 * RIM + tile.stripe
+    for t in range(tile.tiles):
+        beside_rows, packed = near(t), far(t)
+        for part, ref in enumerate(target):
+            for r in range(0, tile.stripe, 16):
+                ref[t, 2 * RIM + r : 2 * RIM + r + 16, :] = middle(part, t, r)
+            ref[t, RIM : 2 * RIM, :] = jnp.where(low_illum, unpack_rows(packed, False)[part], beside_rows[part])
+            ref[t, end : end + RIM, :] = jnp.where(low_illum, beside_rows[part], unpack_rows(packed, True)[part])
+
+
+def forward_kernel(sizes, place_ref, phase_ref, measured_ref, known_ref, partner_ref, along_ref, same_ref, phase_rim_ref, rim_ref,
+                   own_ref, o0r, o0i, o1r, o1i, o2r, o2i, c1, s1,
+                   c0, s0, w0r, w0i, w1r, w1i, gr, gi, hr, hi, mr, mi, row_r, row_i, col_r, col_i):
+    stripe, tiles, total_rows, total_cols = sizes
+    tile, row_first, col_first = tile_of(place_ref, sizes)
+    width = (tiles - 1) * LANES
+    low_illum = place_ref[0] == 0
+    blank_rims((w0r, w0i, w1r, w1i, gr, gi, hr, hi, o0r, o0i, o1r, o1i), tile)
+
+    for t in range(tiles):
         for k, (c, s) in enumerate(((c0, s0), (c1, s1))):
-            s[t, span, :], c[t, span, :] = sine_cosine(phase_ref[k, :, here])
-        return carry
-
-    lax.fori_loop(0, tiles, trig, 0)
-
-    def illum(j, carry):
-        tilt_x, tilt_y = angles_ref[j, 0].astype(F32), angles_ref[j, 1].astype(F32)
-        scale = scale_ref[j]
-        ids = lax.broadcasted_iota(jnp.int32, (rows_all, LANES), 0) + (row_first - RIM)
-        s, c = sine_cosine_of_turns(ids.astype(F32) * tilt_x / total_rows)
-        row_r[...] = (-7.0 * c - 24.0 * s) * 0.04
-        row_i[...] = (-7.0 * s + 24.0 * c) * 0.04
-        at = lax.broadcasted_iota(jnp.int32, (col_r.shape[0], LANES), 0)
-        on = lane_ids((col_r.shape[0], LANES))
-        ids = col_first + at * LANES + on
-        ids = jnp.where((at >= tiles - 1) & (on >= LANES // 2), col_first - LANES + on, ids)
-        col_i[...], col_r[...] = sine_cosine_of_turns(ids.astype(F32) * tilt_y / total_cols)
-
-        def start(t, left, right, rows, mask):
-            ar, ai = row_r[pl.ds(rows.start - RIM, rows.size), :], row_i[pl.ds(rows.start - RIM, rows.size), :]
-            br, bi = col_r[pl.ds(t, 1), :], col_i[pl.ds(t, 1), :]
-            ur, ui = ar * br - ai * bi, ar * bi + ai * br
-            c, s = c0[t, rows, :], s0[t, rows, :]
-            w0r[t, rows, :] = mask(ur * c - ui * s)
-            w0i[t, rows, :] = mask(ur * s + ui * c)
-
-        tile.sweep(start, tile.blocks)
-        first_half(tile, (w0r, w0i), (hr, hi), 1.0, tile.blocks)
-
-        def modulate(t, rows, mask, ur, ui):
-            c, s = c1[t, rows, :], s1[t, rows, :]
-            w1r[t, rows, :] = mask(ur * c - ui * s)
-            w1i[t, rows, :] = mask(ur * s + ui * c)
-
-        second_half(tile, (w0r, w0i), (hr, hi), tile.blocks, modulate)
-        first_half(tile, (w1r, w1i), (hr, hi), 1.0, tile.blocks)
-
-        def residual(t, rows, mask, ur, ui):
-            here = pl.ds(t * LANES if isinstance(t, int) else pl.multiple_of(t * LANES, LANES), LANES)
-            at = pl.ds(rows.start - RIM, rows.size)
-            gr[t, rows, :] = mask(ur - target_ref[j, 0, at, here])
-            gi[t, rows, :] = mask(ui - target_ref[j, 1, at, here])
-
-        second_half(tile, (w1r, w1i), (hr, hi), tile.blocks, residual)
-        first_half(tile, (gr, gi), (hr, hi), -1.0, tile.blocks)
-
-        def put(k, t, rows, value):
-            here = pl.ds(t * LANES if isinstance(t, int) else pl.multiple_of(t * LANES, LANES), LANES)
-            at = pl.ds(rows.start - 2 * RIM, rows.size)
-            out_ref[k, at, here] = out_ref[k, at, here] + scale * value
-
-        def back(t, rows, mask, ur, ui):
-            if not isinstance(t, int) and 2 * RIM <= rows.start < 2 * RIM + stripe:
-                put(1, t, rows, ui * w1r[t, rows, :] - ur * w1i[t, rows, :])
-            c, s = c1[t, rows, :], s1[t, rows, :]
-            gr[t, rows, :] = mask(ur * c + ui * s)
-            gi[t, rows, :] = mask(ui * c - ur * s)
-
-        second_half(tile, (gr, gi), (hr, hi), tile.blocks, back)
-        first_half(tile, (gr, gi), (hr, hi), -1.0, tile.blocks)
-
-        def last(t, rows, mask, ur, ui):
-            if not isinstance(t, int):
-                put(0, t, rows, ui * w0r[t, rows, :] - ur * w0i[t, rows, :])
-
-        second_half(tile, (gr, gi), (hr, hi), tile.inner, last)
-        return carry
-
-    lax.fori_loop(0, illums, illum, 0)
+            if t < tiles - 1:
+                at = own_columns(t + k * (tiles - 1))
+                far, near = along_ref[:, at], partner_ref[:, at]
+                here = [(RIM, jnp.where(low_illum, far, near)), (2 * RIM + stripe, jnp.where(low_illum, near, far))]
+                here += [(2 * RIM + r, phase_ref[k, r : r + 16, own_columns(t)]) for r in range(0, stripe, 16)]
+            else:
+                here = [(RIM + r, phase_rim_ref[k, r : r + 16, :]) for r in range(0, tile.rows, 16)]
+            for first, x in here:
+                s[t, first : first + x.shape[0], :], c[t, first : first + x.shape[0], :] = sine_cosine(x)
+
+    mine = place_ref[0] * stripe
+    near_base = pl.multiple_of(stripe - 16 * place_ref[0], 16)
+    near_rim = pl.multiple_of(stripe - 8 * place_ref[0], 8)
+
+    def middle(part, t, r):
+        at = pl.ds(pl.multiple_of(mine + r, 16), 16)
+        if t < tiles - 1:
+            return measured_ref[part, 0, at, own_columns(t)].astype(F32)
+        return rim_ref[part, at, :]
+
+    def near(t):
+        if t < tiles - 1:
+            both = [measured_ref[part, 0, pl.ds(near_base, 16), own_columns(t)].astype(F32) for part in range(2)]
+            return [jnp.where(low_illum, x[:8], x[8:]) for x in both]
+        return [rim_ref[part, pl.ds(near_rim, 8), :] for part in range(2)]
+
+    def far(t):
+        return same_ref[:, own_columns(t)] if t < tiles - 1 else rim_ref[0, 2 * stripe :, :]
+
+    fill_target(tile, (mr, mi), low_illum, middle, near, far)
+
+    lane = lane_ids((8, LANES))
+
+    def tilts(note):
+        return [jnp.sum(jnp.where(lane == n, note, 0.0)[:1], axis=1, keepdims=True) for n in (16, 17)]
+
+    tables, half = (row_r, row_i, col_r, col_i), (hr, hi)
+    trig0, trig1 = (c0, s0), (c1, s1)
+
+    def forward(note, w0, w1, use):
+        incident_tables(tile, tilts(note), row_first, col_first, total_rows, total_cols, tables)
+        enter(tile, tables, trig0, w0)
+        first_half(tile, w0, half, 1.0, tile.blocks)
+        second_half(tile, w0, half, tile.blocks, modulate_into(trig1, w1))
+        first_half(tile, w1, half, 1.0, tile.blocks)
+        second_half(tile, w1, half, tile.blocks, use)
+
+    def keep(t, rows, mask, ur, ui):
+        o2r[t, rows, :] = ur
+        o2i[t, rows, :] = ui
+
+    def residual(t, rows, mask, ur, ui):
+        gr[t, rows, :] = mask(ur - mr[t, rows, :])
+        gi[t, rows, :] = mask(ui - mi[t, rows, :])
+
+    def put(k, t, rows, value):
+        own_ref[k, own_rows(rows), own_columns(t)] = value
+
+    forward(partner_ref[:, 2 * width :], (o0r, o0i), (o1r, o1i), keep)
+    forward(known_ref[...], (w0r, w0i), (w1r, w1i), residual)
+    backward(tile, (gr, gi), half, (w0r, w0i), (w1r, w1i), trig1, put)
+
+
+def finish_kernel(sizes, place_ref, own_ref, swap_ref, along_ref, rim_ref, relay_ref, partner_relay_ref,
+                  w0r, w0i, w1r, w1i, ur_ref, ui_ref, c1, s1, out_ref, gr, gi, hr, hi, mr, mi):
+    stripe, tiles, total_rows, total_cols = sizes
+    tile, _, _ = tile_of(place_ref, sizes)
+    width = (tiles - 1) * LANES
+    low_illum = place_ref[0] == 0
+    blank_rims((gr, gi, hr, hi), tile)
+
+    lane = lane_ids((8, LANES))
+    sums = jnp.maximum(relay_ref[stripe + 8 :, :], partner_relay_ref[stripe + 8 :, :])
+    scales = []
+    for which in range(2):
+        here = jnp.where((lane >= 4 * which) & (lane < 4 * which + 4), sums, 0.0)
+        energy = jnp.sum(here[:1], axis=1, keepdims=True) / (total_rows * total_cols) + EPS_ENERGY
+        scales.append(2.0 / energy)
+    mine = jnp.where(low_illum, scales[0], scales[1])
+    others = jnp.where(low_illum, scales[1], scales[0])
+
+    def middle(part, t, r):
+        if t < tiles - 1:
+            return swap_ref[part * stripe + r : part * stripe + r + 16, own_columns(t)]
+        x = partner_relay_ref[r : r + 16, :]
+        return pltpu.roll(x, LANES // 2, 1) if part else x
+
+    def near(t):
+        if t < tiles - 1:
+            packed = swap_ref[2 * stripe :, own_columns(t)]
+            high, low = unpack_rows(packed, False), unpack_rows(packed, True)
+            return [jnp.where(low_illum, low[part], high[part]) for part in range(2)]
+        x = partner_relay_ref[stripe : stripe + 8, :]
+        return [x, pltpu.roll(x, LANES // 2, 1)]
+
+    def far(t):
+        return along_ref[:, own_columns(t + 2 * (tiles - 1))] if t < tiles - 1 else rim_ref[1, 2 * stripe :, :]
+
+    fill_target(tile, (mr, mi), low_illum, middle, near, far)
+
+    def residual(t, left, right, rows, mask):
+        gr[t, rows, :] = mask(ur_ref[t, rows, :] - mr[t, rows, :])
+        gi[t, rows, :] = mask(ui_ref[t, rows, :] - mi[t, rows, :])
+
+    tile.sweep(residual, tile.blocks)
+
+    def put(k, t, rows, value):
+        at = (k, own_rows(rows), own_columns(t))
+        out_ref[at] = own_ref[at] * mine + value * others
+
+    backward(tile, (gr, gi), (hr, hi), (w0r, w0i), (w1r, w1i), (c1, s1), put)
+
+
+def call(kernel, outs, *args, scratch=(), scalars=1, flops=0):
+    shapes = [jax.ShapeDtypeStruct(shape, F32) for shape in outs]
+    return pl.pallas_call(
+        kernel,
+        out_shape=shapes,
+        in_specs=[pl.BlockSpec(memory_space=pltpu.SMEM)] * scalars
+        + [pl.BlockSpec(memory_space=pltpu.VMEM)] * (len(args) - scalars),
+        out_specs=[pl.BlockSpec(memory_space=pltpu.VMEM)] * len(outs),
+        scratch_shapes=[pltpu.VMEM(shape, F32) for shape in scratch],
+        compiler_params=pltpu.CompilerParams(vmem_limit_bytes=32 * 2**20),
+        cost_estimate=pl.CostEstimate(flops=flops, bytes_accessed=2**20, transcendentals=0),
+    )(*args)
+
+
+def paired(phase_delay, angles, measured):
+    slices, stripe, width = phase_delay.shape
+    rows, cols = lax.axis_size("row"), lax.axis_size("col")
+    tiles = width // LANES + 1
+    sizes = (stripe, tiles, 2 * stripe * rows, width * cols)
+    place = jnp.stack([lax.axis_index("illum"), lax.axis_index("row"), lax.axis_index("col")])
+    swap = [(0, 1), (1, 0)]
+    along = []
+    for r in range(rows - 1):
+        along += [(rows + r, r + 1), (r + 1, rows + r)]
+    same = [(r, (r + 1) % rows) for r in range(rows)] + [(rows + (r + 1) % rows, rows + r) for r in range(rows)]
+
+    (note,) = call(energy_kernel, [(8, LANES)], place, angles, measured, scalars=2)
+    core_note = lax.ppermute(note, "row", [(r, r ^ 1) for r in range(rows)])
+    swap_out, along_out, same_packed = call(
+        send_kernel, [(2 * stripe + 8, width), (8, 3 * width), (8, width)], place, phase_delay, measured
+    )
+    partner_out, known = call(partner_kernel, [(8, 2 * width + LANES), (8, LANES)], place, phase_delay, note, core_note)
+    partner_in = lax.ppermute(partner_out, "illum", swap)
+    along_in = lax.ppermute(along_out, ("illum", "row"), along)
+    swap_in = lax.ppermute(swap_out, "illum", swap)
+    (same_out,) = call(same_kernel, [(8, width + LANES)], same_packed, known, partner_in, scalars=0)
+    same_in = lax.ppermute(same_out, ("illum", "row"), same)
+    depth = 8 * (-(-(stripe // 4 + 1) // 4)) + 8
+    (rims_out,) = call(
+        rim_pack_kernel, [(cols, depth, LANES)], place, phase_delay, measured, known, partner_in, along_in, same_in
+    )
+    rims_in = lax.all_to_all(rims_out, "col", 0, 0, tiled=True)
+    phase_rim, rim, relay = call(
+        rim_unpack_kernel,
+        [(2, stripe + 2 * RIM, LANES), (2, 2 * stripe + 8, LANES), (stripe + 16, LANES)],
+        place, rims_in,
+    )
+    partner_relay = lax.ppermute(relay, "illum", swap)
+
+    field = (tiles, stripe + 4 * RIM, LANES)
+    tables = [(stripe + 2 * RIM, LANES)] * 2 + [(-(-tiles // 8) * 8, LANES)] * 2
+    own, *kept = call(
+        functools.partial(forward_kernel, sizes),
+        [phase_delay.shape] + [field] * 8,
+        place, phase_delay, measured, known, partner_in, along_in, same_in, phase_rim, rim,
+        scratch=[field] * 12 + tables, flops=10**9,
+    )
+    (out,) = call(
+        functools.partial(finish_kernel, sizes),
+        [phase_delay.shape],
+        place, own, swap_in, along_in, rim, relay, partner_relay, *kept,
+        scratch=[field] * 6,
+    )
+    return out
 
 
 def halo(x, axis, dim, width, index_of=None):
@@ -222,6 +614,8 @@
 
 def per_device(phase_delay, angles, measured):
     illums = lax.axis_size("illum")
+    if illums == 2 and lax.axis_size("row") == 4:
+        return paired(phase_delay, angles, measured)
     slices, stripe, width = phase_delay.shape
     tile_rows = measured.shape[2]
     total_rows, total_cols = tile_rows * lax.axis_size("row"), width * lax.axis_size("col")

time: 106 us -> 46.5 us (0.44)
  the two profiles are of different devices: /device:TPU:12 before, /device:TPU:0 now
where the time goes in v2:
time: 46.5 us; the launch traced here: 46.3 us
  waiting for transfers between devices  15.9 us (34%)
  Pallas kernels  12.9 us (28%)
  blocking collectives  11 us (24%)
  starting transfers between devices  4.15 us (9%)
  local copies, waits for them, and re-layouts  2.1 us (5%)
    pallas_call x8, Pallas kernels, call(): pl.pallas_call(kernel, out_shape=shapes, in_specs=[pl.BlockSpec(memory_sp...  12.9 us
    ppermute x1, waiting for transfers between devices, paired(): partner_in = lax.ppermute(partner_out, 'illum', swap)  11.4 us
    all_to_all x1, blocking collectives, paired(): rims_in = lax.all_to_all(rims_out, 'col', 0, 0, tiled=True)  11 us
    ppermute x1, waiting for transfers between devices, paired(): same_in = lax.ppermute(same_out, ('illum', 'row'), same)  3.37 us
    ppermute x1, starting transfers between devices, paired(): swap_in = lax.ppermute(swap_out, 'illum', swap)  3 us
    unnamed x10, local copies, waits for them, and re-layouts  2.1 us
    ppermute x1, waiting for transfers between devices, paired(): core_note = lax.ppermute(note, 'row', [(r, r ^ 1) for r in range(rows)])  1.16 us
  transfers between devices with their start and end apart: 6, of which 3 were waited for; matrix products, arithmetic and copies ran while one was open for 0% of the time, Pallas kernels for 20%

profile of v2, /device:TPU:0, one launch (start us, length us, event | category | flops | bytes accessed | tf_op | source)
XLA Modules:
  0.0 46.3 jit_solution(7472002241374450197)
XLA Ops:
  0.0 0.1 pad_add_fusion.place_ref
  0.1 0.0 copy-start
  0.1 1.0 %copy-done = f32[2,64,1024]{2,1,0:T(8,128)S(1)} copy-done((f32[2,64,1024]{2,1,0:T(8,128)S(1)}, f32[2,64,1024]{2,1,0:T(8,128)}, u32[]{:S(2)}) %copy-start) | copy-done | bytes 524312
  1.1 0.0 copy-start.2
  1.1 1.0 %copy-done.2 = bf16[2,1,128,1024]{3,2,1,0:T(8,128)(2,1)S(1)} copy-done((bf16[2,1,128,1024]{3,2,1,0:T(8,128)(2,1)S(1)}, bf16[2,1,128,1024]{3,2,1,0:T(8,128)(2,1)}, u32[]{:S(2)}) %copy-start.2) | copy-done | bytes 524312
  2.2 0.0 copy-start.3
  2.2 0.0 copy-start.4
  2.2 0.6 %shard_map.39 = (f32[136,1024]{1,0:T(8,128)S(1)}, f32[8,3072]{1,0:T(8,128)S(1)}, f32[8,1024]{1,0:T(8,128)S(1)}) custom-call(s32[3]{0:T(128)S(1)} %pad_add_fusion.place_ref, f32[2,64,1024]{2,1,0:T(8,128)S(1)} %copy-done, bf16[2,1,128,1024]{3,2,1,0:T(8,128)(2,1)S(1)} %copy-done.2), custom_call_target="tpu_custom_call" | custom-call | bytes 1048576 | tf_op jit(solution)/shard_map/pallas_call | solution.py:528
  2.8 0.0 copy-start.1
  2.8 3.0 %collective-permute-start.4 = (f32[136,1024]{1,0:T(8,128)S(1)}, f32[136,1024]{1,0:T(8,128)S(1)}, u32[]{:S(2)}, u32[]{:S(2)}) collective-permute-start(f32[136,1024]{1,0:T(8,128)S(1)} %get-tuple-element.29), channel_id=1, source_target_pairs={{0,16},{16,0},{1,17},{17,1},{2,18},{18,2},{3,19},{19,3},{4,20},{20... | collective-permute-start | bytes 1671176 | tf_op jit(solution)/shard_map/ppermute | solution.py:560
  5.8 0.0 copy-done.3
  5.8 0.0 copy-done.4
  5.8 0.7 %shard_map.37.note_ref = f32[8,128]{1,0:T(8,128)S(1)} custom-call(s32[3]{0:T(128)S(1)} %pad_add_fusion.place_ref, s32[1,2]{1,0:T(1,128)S(1)} %copy-done.4, bf16[2,1,128,1024]{3,2,1,0:T(8,128)(2,1)S(1)} %copy-done.3), custom_call_target="tpu_custom_call" | custom-call | bytes 1048576 | tf_op jit(solution)/shard_map/pallas_call | solution.py:528
  6.5 0.0 collective-permute-start
  6.5 1.2 %collective-permute-done.core_note_ref = f32[8,128]{1,0:T(8,128)S(1)} collective-permute-done((f32[8,128]{1,0:T(8,128)S(1)}, f32[8,128]{1,0:T(8,128)S(1)}, u32[]{:S(2)}, u32[]{:S(2)}) %collective-permute-start) | collective-permute-done | bytes 4128 | tf_op jit(solution)/shard_map/ppermute | solution.py:553
  7.7 0.0 copy-done.1
  7.7 0.6 %shard_map.38 = (f32[8,2176]{1,0:T(8,128)S(1)}, f32[8,128]{1,0:T(8,128)S(1)}) custom-call(s32[3]{0:T(128)S(1)} %pad_add_fusion.place_ref, f32[2,64,1024]{2,1,0:T(8,128)S(1)} %copy-done.1, f32[8,128]{1,0:T(8,128)S(1)} %shard_map.37.note_ref, f32[8,128]{1,0:T(8,128)S(1)} %collective-permute-done.core_note_ref), custom_call_target="tpu_custom_call" | custom-call | bytes 1048576 | tf_op jit(solution)/shard_map/pallas_call | solution.py:528
  8.3 0.4 collective-permute-start.1
  8.7 0.7 %collective-permute-start.2 = (f32[8,3072]{1,0:T(8,128)S(1)}, f32[8,3072]{1,0:T(8,128)S(1)}, u32[]{:S(2)}, u32[]{:S(2)}) collective-permute-start(f32[8,3072]{1,0:T(8,128)S(1)} %get-tuple-element.24), channel_id=1, source_target_pairs={{16,4},{4,16},{20,8},{8,20},{24,12},{12,24},{17,5},{5,17},{21,9},{... | collective-permute-start | bytes 294920 | tf_op jit(solution)/shard_map/ppermute | solution.py:559
  9.3 11.4 %collective-permute-done.1.partner_ref = f32[8,2176]{1,0:T(8,128)S(1)} collective-permute-done((f32[8,2176]{1,0:T(8,128)S(1)}, f32[8,2176]{1,0:T(8,128)S(1)}, u32[]{:S(2)}, u32[]{:S(2)}) %collective-permute-start.1) | collective-permute-done | bytes 69664 | tf_op jit(solution)/shard_map/ppermute | solution.py:558
  20.7 0.0 collective-permute-start.3
  20.7 0.0 collective-permute-done.2.along_ref
  20.8 3.4 %collective-permute-done.3.same_ref = f32[8,1152]{1,0:T(8,128)S(1)} collective-permute-done((f32[8,1152]{1,0:T(8,128)S(1)}, f32[8,1152]{1,0:T(8,128)S(1)}, u32[]{:S(2)}, u32[]{:S(2)}) %collective-permute-start.3) | collective-permute-done | bytes 36896 | tf_op jit(solution)/shard_map/ppermute | solution.py:562
  24.1 0.7 %shard_map.41 = f32[4,48,128]{2,1,0:T(8,128)S(1)} custom-call(s32[3]{0:T(128)S(1)} %pad_add_fusion.place_ref, f32[2,64,1024]{2,1,0:T(8,128)S(1)} %copy-done.1, bf16[2,1,128,1024]{3,2,1,0:T(8,128)(2,1)S(1)} %copy-done.3, f32[8,128]{1,0:T(8,128)S(1)} %get-tuple-element.22.known_ref, f32[8,2176]{1,0:T(8,128)S(1)} %collective-permute-done.1.partner_ref, ...), custom_call_target="tpu_custom_call" | custom-call | bytes 1048576 | tf_op jit(solution)/shard_map/pallas_call | solution.py:528
  24.8 11.0 %all_to_all.5.got_ref = f32[4,48,128]{2,1,0:T(8,128)S(1)} all-to-all(f32[4,48,128]{2,1,0:T(8,128)S(1)} %shard_map.41), channel_id=1, replica_groups=mesh['illum'=2,'row'=4,'col'=4] {'col'}, dimensions={0} | all-to-all | bytes 196608 | tf_op jit(solution)/shard_map/all_to_all | solution.py:567
  35.8 0.8 %shard_map.42 = (f32[2,80,128]{2,1,0:T(8,128)S(1)}, f32[2,136,128]{2,1,0:T(8,128)S(1)}, f32[80,128]{1,0:T(8,128)S(1)}) custom-call(s32[3]{0:T(128)S(1)} %pad_add_fusion.place_ref, f32[4,48,128]{2,1,0:T(8,128)S(1)} %all_to_all.5.got_ref), custom_call_target="tpu_custom_call" | custom-call | bytes 1048576 | tf_op jit(solution)/shard_map/pallas_call | solution.py:528
  36.6 0.1 collective-permute-start.5
  36.6 6.5 %shard_map.43 = (f32[2,64,1024]{2,1,0:T(8,128)S(1)}, f32[9,96,128]{2,1,0:T(8,128)S(1)}, f32[9,96,128]{2,1,0:T(8,128)S(1)}, f32[9,96,128]{2,1,0:T(8,128)S(1)}, f3...) custom-call(s32[3]{0:T(128)S(1)} %pad_add_fusion.place_ref, ...), custom_call_target="tpu_custom_call" | custom-call | flops 1000000000 | bytes 1048576 | tf_op jit(solution)/shard_map/pallas_call | solution.py:528
  43.1 0.0 collective-permute-done.5.partner_relay_ref
  43.1 0.0 collective-permute-done.4.swap_ref
  43.1 3.1 %shard_map.44 = f32[2,64,1024]{2,1,0:T(8,128)} custom-call(s32[3]{0:T(128)S(1)} %pad_add_fusion.place_ref, f32[2,64,1024]{2,1,0:T(8,128)S(1)} %get-tuple-element.28.own_ref, f32[136,1024]{1,0:T(8,128)S(1)} %collective-permute-done.4.swap_ref, f32[8,3072]{1,0:T(8,128)S(1)} %collective-permute-done.2.along_ref, f32[2,136,128]{2,1,0:T(8,128)S(1)} %get-tuple-element.27.rim_ref, ...), custom_call_target="tpu_custom_call" | custom-call | bytes 1048576 | tf_op jit(solution)/shard_map/pallas_call | solution.py:528
  (1 shorter events, 0.0 us)
Async XLA Ops:
  0.1 1.0 %copy-start = (f32[2,64,1024]{2,1,0:T(8,128)S(1)}, f32[2,64,1024]{2,1,0:T(8,128)}, u32[]{:S(2)}) copy-start(f32[2,64,1024]{2,1,0:T(8,128)} %phase_ref.7) | copy-start | bytes 1572868
  1.1 1.0 %copy-start.2 = (bf16[2,1,128,1024]{3,2,1,0:T(8,128)(2,1)S(1)}, bf16[2,1,128,1024]{3,2,1,0:T(8,128)(2,1)}, u32[]{:S(2)}) copy-start(bf16[2,1,128,1024]{3,2,1,0:T(8,128)(2,1)} %measured_ref.7) | copy-start | bytes 1572868
  2.2 3.6 %copy-start.3 = (bf16[2,1,128,1024]{3,2,1,0:T(8,128)(2,1)S(1)}, bf16[2,1,128,1024]{3,2,1,0:T(8,128)(2,1)}, u32[]{:S(2)}) copy-start(bf16[2,1,128,1024]{3,2,1,0:T(8,128)(2,1)} %measured_ref.7) | copy-start | bytes 1572868
  2.2 3.6 %copy-start.4 = (s32[1,2]{1,0:T(1,128)S(1)}, s32[1,2]{1,0:T(1,128)}, u32[]{:S(2)}) copy-start(s32[1,2]{1,0:T(1,128)} %tilt_ref.1) | copy-start | bytes 28
  2.8 4.9 %copy-start.1 = (f32[2,64,1024]{2,1,0:T(8,128)S(1)}, f32[2,64,1024]{2,1,0:T(8,128)}, u32[]{:S(2)}) copy-start(f32[2,64,1024]{2,1,0:T(8,128)} %phase_ref.7) | copy-start | bytes 1572868
  2.8 40.4 %collective-permute-start.4 = (f32[136,1024]{1,0:T(8,128)S(1)}, f32[136,1024]{1,0:T(8,128)S(1)}, u32[]{:S(2)}, u32[]{:S(2)}) collective-permute-start(f32[136,1024]{1,0:T(8,128)S(1)} %get-tuple-element.29), channel_id=1, source_target_pairs={{0,16},{16,0},{1,17},{17,1},{2,18},{18,2},{3,19},{19,3},{4,20},{20... | collective-permute-start | bytes 1671176 | tf_op jit(solution)/shard_map/ppermute | solution.py:560
  6.5 1.2 %collective-permute-start = (f32[8,128]{1,0:T(8,128)S(1)}, f32[8,128]{1,0:T(8,128)S(1)}, u32[]{:S(2)}, u32[]{:S(2)}) collective-permute-start(f32[8,128]{1,0:T(8,128)S(1)} %shard_map.37.note_ref), channel_id=1, source_target_pairs={{0,4},{4,0},{8,12},{12,8},{1,5},{5,1},{9,13},{13,9},{2,6},{6,2},{1... | collective-permute-start | bytes 12296 | tf_op jit(solution)/shard_map/ppermute | solution.py:553
  8.3 12.5 %collective-permute-start.1 = (f32[8,2176]{1,0:T(8,128)S(1)}, f32[8,2176]{1,0:T(8,128)S(1)}, u32[]{:S(2)}, u32[]{:S(2)}) collective-permute-start(f32[8,2176]{1,0:T(8,128)S(1)} %get-tuple-element.23), channel_id=1, source_target_pairs={{0,16},{16,0},{1,17},{17,1},{2,18},{18,2},{3,19},{19,3},{4,20},{20... | collective-permute-start | bytes 208904 | tf_op jit(solution)/shard_map/ppermute | solution.py:558
  8.7 12.1 %collective-permute-start.2 = (f32[8,3072]{1,0:T(8,128)S(1)}, f32[8,3072]{1,0:T(8,128)S(1)}, u32[]{:S(2)}, u32[]{:S(2)}) collective-permute-start(f32[8,3072]{1,0:T(8,128)S(1)} %get-tuple-element.24), channel_id=1, source_target_pairs={{16,4},{4,16},{20,8},{8,20},{24,12},{12,24},{17,5},{5,17},{21,9},{... | collective-permute-start | bytes 294920 | tf_op jit(solution)/shard_map/ppermute | solution.py:559
  20.7 3.4 %collective-permute-start.3 = (f32[8,1152]{1,0:T(8,128)S(1)}, f32[8,1152]{1,0:T(8,128)S(1)}, u32[]{:S(2)}, u32[]{:S(2)}) collective-permute-start(f32[8,1152]{1,0:T(8,128)S(1)} %shard_map.40), channel_id=1, source_target_pairs={{0,4},{4,8},{8,12},{12,0},{20,16},{24,20},{28,24},{16,28},{1,5},{5... | collective-permute-start | bytes 110600 | tf_op jit(solution)/shard_map/ppermute | solution.py:562
  36.6 6.6 %collective-permute-start.5 = (f32[80,128]{1,0:T(8,128)S(1)}, f32[80,128]{1,0:T(8,128)S(1)}, u32[]{:S(2)}, u32[]{:S(2)}) collective-permute-start(f32[80,128]{1,0:T(8,128)S(1)} %get-tuple-element.30.relay_ref), channel_id=1, source_target_pairs={{0,16},{16,0},{1,17},{17,1},{2,18},{18,2},{3,19},{19,3},{4,20},{20... | collective-permute-start | bytes 122888 | tf_op jit(solution)/shard_map/ppermute | solution.py:573

commit v3 on v2

v3 whole, which is shorter than its diff:
```python
import functools
import math

import jax
import jax.numpy as jnp
from jax import lax
from jax.experimental import pallas as pl
from jax.experimental.pallas import tpu as pltpu
from jax.sharding import PartitionSpec as P

EPS_ENERGY = 1e-06
RIM = 8
REACH = 4
LANES = 128
F32 = jnp.float32


def sine_cosine(x):
    y = x * x
    s = -2.5052108385441718e-08
    for c in (2.7557319223985893e-06, -1.9841269841269841e-04, 8.333333333333333e-03, -1.6666666666666666e-01):
        s = s * y + c
    c_ = -2.7557319223985888e-07
    for c in (2.48015873015873e-05, -1.3888888888888889e-03, 4.1666666666666664e-02, -0.5, 1.0):
        c_ = c_ * y + c
    return x + x * y * s, c_


def sine_cosine_of_turns(turns):
    quarters = 4.0 * (turns - jnp.floor(turns))
    nearest = jnp.floor(quarters + 0.5)
    s, c = sine_cosine((quarters - nearest) * (0.5 * math.pi))
    odd = (nearest == 1.0) | (nearest == 3.0)
    s, c = jnp.where(odd, c, s), jnp.where(odd, s, c)
    s = jnp.where((nearest == 2.0) | (nearest == 3.0), -s, s)
    c = jnp.where((nearest == 1.0) | (nearest == 2.0), -c, c)
    return s, c


def lane_ids(shape):
    return lax.broadcasted_iota(jnp.int32, shape, len(shape) - 1)


class Tile:
    def __init__(self, stripe, tiles, top, bottom, lanes=None, rim=None):
        self.stripe, self.tiles = stripe, tiles
        self.rows = stripe + 2 * RIM
        self.top, self.bottom, self.lanes, self.rim = top, bottom, lanes, rim
        self.owned = tiles - 1 if rim else tiles
        step = 32 if stripe % 32 == 0 else 8
        self.inner = [(2 * RIM + r, step, None) for r in range(0, stripe, step)]
        self.blocks = [(RIM, RIM, top)] + self.inner + [(2 * RIM + stripe, RIM, bottom)]

    def sweep(self, body, blocks):
        for t in range(self.tiles):
            for first, count, factor in blocks:

                def mask(x, factor=factor, lanes=self.lanes if t == self.rim else None):
                    x = x if factor is None else x * factor
                    return x if lanes is None else x * lanes

                body(t, (t - 1) % self.tiles, (t + 1) % self.tiles, pl.ds(first, count), mask)


def beside(ref, t, left, right, rows):
    above = pl.ds(rows.start - 1, rows.size)
    below = pl.ds(rows.start + 1, rows.size)
    here = ref[t, rows, :]
    lane = lane_ids(here.shape)
    west = pltpu.roll(here if left == t else jnp.where(lane == LANES - 1, ref[left, rows, :], here), 1, 1)
    east = pltpu.roll(here if right == t else jnp.where(lane == 0, ref[right, rows, :], here), LANES - 1, 1)
    return here, (ref[t, above, :] + ref[t, below, :]) + (west + east)


def first_half(tile, field, half, sign, blocks):
    fr, fi = field
    hr, hi = half

    def body(t, left, right, rows, mask):
        real, beside_real = beside(fr, t, left, right, rows)
        imag, beside_imag = beside(fi, t, left, right, rows)
        hr[t, rows, :] = mask(beside_real + (2.0 * sign) * imag)
        hi[t, rows, :] = mask(beside_imag - (2.0 * sign) * real)

    tile.sweep(body, blocks)


def second_half(tile, field, half, blocks, use):
    fr, fi = field
    hr, hi = half

    def body(t, left, right, rows, mask):
        _, beside_real = beside(hr, t, left, right, rows)
        _, beside_imag = beside(hi, t, left, right, rows)
        use(t, rows, mask, 0.1 * beside_real - fr[t, rows, :], 0.1 * beside_imag - fi[t, rows, :])

    tile.sweep(body, blocks)


def blank_rims(refs, tile):
    for ref in refs:
        for first in (0, tile.rows + RIM):
            ref[:, first : first + RIM, :] = jnp.zeros((tile.tiles, RIM, LANES), F32)


def rim_columns(tile, col_first, shape):
    at, on = lax.broadcasted_iota(jnp.int32, shape, 0), lane_ids(shape)
    return col_first + jnp.where((at >= tile.owned) & (on >= LANES // 2), on - LANES, at * LANES + on)


def incident_tables(tile, tilts, row_first, columns, total_rows, total_cols, tables):
    row_r, row_i, col_r, col_i = tables
    ids = lax.broadcasted_iota(jnp.int32, (tile.rows, LANES), 0) + (row_first - RIM)
    s, c = sine_cosine_of_turns(ids.astype(F32) * tilts[0] / total_rows)
    row_r[...] = (-7.0 * c - 24.0 * s) * 0.04
    row_i[...] = (-7.0 * s + 24.0 * c) * 0.04
    col_i[...], col_r[...] = sine_cosine_of_turns(columns.astype(F32) * tilts[1] / total_cols)


def enter(tile, tables, trig, field):
    row_r, row_i, col_r, col_i = tables
    fr, fi = field

    def start(t, left, right, rows, mask):
        at = pl.ds(rows.start - RIM, rows.size)
        ar, ai = row_r[at, :], row_i[at, :]
        br, bi = col_r[t : t + 1, :], col_i[t : t + 1, :]
        ur, ui = ar * br - ai * bi, ar * bi + ai * br
        c, s = trig[0][t, rows, :], trig[1][t, rows, :]
        fr[t, rows, :] = mask(ur * c - ui * s)
        fi[t, rows, :] = mask(ur * s + ui * c)

    tile.sweep(start, tile.blocks)


def modulate_into(trig, field):
    def use(t, rows, mask, ur, ui):
        c, s = trig[0][t, rows, :], trig[1][t, rows, :]
        field[0][t, rows, :] = mask(ur * c - ui * s)
        field[1][t, rows, :] = mask(ur * s + ui * c)

    return use


def backward(tile, adjoint, half, w0, w1, trig1, put):
    gr, gi = adjoint
    inner = [first for first, _, _ in tile.inner]

    def back(t, rows, mask, ur, ui):
        if t < tile.owned and rows.start in inner:
            put(1, t, rows, ui * w1[0][t, rows, :] - ur * w1[1][t, rows, :])
        c, s = trig1[0][t, rows, :], trig1[1][t, rows, :]
        gr[t, rows, :] = mask(ur * c + ui * s)
        gi[t, rows, :] = mask(ui * c - ur * s)

    def last(t, rows, mask, ur, ui):
        if t < tile.owned:
            put(0, t, rows, ui * w0[0][t, rows, :] - ur * w0[1][t, rows, :])

    first_half(tile, adjoint, half, -1.0, tile.blocks)
    second_half(tile, adjoint, half, tile.blocks, back)
    first_half(tile, adjoint, half, -1.0, tile.blocks)
    second_half(tile, adjoint, half, tile.inner, last)


def own_columns(t):
    return slice(t * LANES, (t + 1) * LANES)


def own_rows(rows):
    return slice(rows.start - 2 * RIM, rows.start - 2 * RIM + rows.size)


def gradient_kernel(sizes, place_ref, angles_ref, scale_ref, phase_ref, target_ref, out_ref,
                    c0, s0, c1, s1, w0r, w0i, w1r, w1i, gr, gi, hr, hi, row_r, row_i, col_r, col_i):
    stripe, tiles, illums, total_rows, total_cols = sizes
    row_first, col_first = place_ref[0], place_ref[1]
    edges = edges_of(row_first, col_first, stripe, tiles, total_rows, total_cols)
    tile = Tile(stripe, tiles, *edges, rim=tiles - 1)
    blank_rims((w0r, w0i, w1r, w1i, gr, gi, hr, hi), tile)
    out_ref[...] = jnp.zeros(out_ref.shape, F32)
    span = slice(RIM, RIM + tile.rows)
    for t in range(tiles):
        for k, (c, s) in enumerate(((c0, s0), (c1, s1))):
            s[t, span, :], c[t, span, :] = sine_cosine(phase_ref[k, :, own_columns(t)])
    tables, half = (row_r, row_i, col_r, col_i), (hr, hi)

    def illum(j, carry):
        tilts = angles_ref[j, 0].astype(F32), angles_ref[j, 1].astype(F32)
        incident_tables(tile, tilts, row_first, rim_columns(tile, col_first, col_r.shape), total_rows, total_cols, tables)
        enter(tile, tables, (c0, s0), (w0r, w0i))
        first_half(tile, (w0r, w0i), half, 1.0, tile.blocks)
        second_half(tile, (w0r, w0i), half, tile.blocks, modulate_into((c1, s1), (w1r, w1i)))
        first_half(tile, (w1r, w1i), half, 1.0, tile.blocks)

        def residual(t, rows, mask, ur, ui):
            at = slice(rows.start - RIM, rows.start - RIM + rows.size)
            gr[t, rows, :] = mask(ur - target_ref[j, 0, at, own_columns(t)])
            gi[t, rows, :] = mask(ui - target_ref[j, 1, at, own_columns(t)])

        second_half(tile, (w1r, w1i), half, tile.blocks, residual)

        def put(k, t, rows, value):
            at = (k, own_rows(rows), own_columns(t))
            out_ref[at] = out_ref[at] + scale_ref[j] * value

        backward(tile, (gr, gi), half, (w0r, w0i), (w1r, w1i), (c1, s1), put)
        return carry

    lax.fori_loop(0, illums, illum, 0)


def edges_of(row_first, col_first, stripe, tiles, total_rows, total_cols):
    width = (tiles - 1) * LANES
    top = jnp.where(row_first == 0, 0.0, 1.0).astype(F32)
    bottom = jnp.where(row_first + stripe == total_rows, 0.0, 1.0).astype(F32)
    lane = lane_ids((1, LANES))
    in_west = (lane >= LANES - RIM) & (col_first > 0)
    in_east = (lane < RIM) & (col_first + width < total_cols)
    return top, bottom, jnp.where(in_west | in_east, 1.0, 0.0).astype(F32)


def place():
    return lax.axis_index("illum"), lax.axis_index("row"), lax.axis_index("col")


def pack_rows(real, imag, low):
    first = lax.broadcasted_iota(jnp.int32, real.shape, 0) < 4
    if low:
        return jnp.where(first, real, pltpu.roll(imag, 4, 0))
    return jnp.where(first, pltpu.roll(real, 4, 0), imag)


def unpack_rows(packed, low):
    turned = pltpu.roll(packed, 4, 0)
    return (packed, turned) if low else (turned, packed)


def edge_blocks(measured_ref, first):
    base = first // 16 * 16
    at = first - base
    return [measured_ref[p, 0, base : base + 16, :].astype(F32)[at : at + 8] for p in range(2)]


def open_kernel(phase_ref, measured_ref, note_ref, along_ref, same_ref, held, edge, sems):
    stripe, width = phase_ref.shape[1:]
    rows = 2 * stripe
    illum, row, _ = place()
    first = pl.multiple_of(illum * (stripe - 8), 8)
    field_copy = pltpu.make_async_copy(measured_ref, held, sems.at[0])
    edge_copy = pltpu.make_async_copy(phase_ref.at[:, pl.ds(first, 8), :], edge, sems.at[1])
    edge_copy.start()
    field_copy.start()
    edge_copy.wait()
    for k in range(2):
        along_ref[:, k * width : (k + 1) * width] = edge[k]
    field_copy.wait()
    top, bottom = pack_rows(*edge_blocks(held, 0), True), pack_rows(*edge_blocks(held, rows - 8), False)
    along_ref[:, 2 * width :] = jnp.where(illum == 0, top, bottom)
    same_ref[...] = jnp.where(illum == 0, bottom, top)
    total = jnp.zeros((8, width), F32)
    for p in range(2):
        for r in range(0, rows, 16):
            x = held[p, 0, r : r + 16, :].astype(F32)
            x = x * x
            total = total + (x[:8] + x[8:])
    energy = jnp.sum(jnp.sum(total, axis=1, keepdims=True), axis=0, keepdims=True)
    note_ref[...] = jnp.where(lane_ids((8, LANES)) == illum * 4 + row, energy, 0.0)


def partner_kernel(phase_ref, angles_ref, note_ref, core_note_ref, partner_ref, known_ref):
    stripe, width = phase_ref.shape[1:]
    illum, _, _ = place()
    first = pl.multiple_of((1 - illum) * (stripe - 8), 8)
    for k in range(2):
        partner_ref[:, k * width : (k + 1) * width] = phase_ref[k, pl.ds(first, 8), :]
    lane = lane_ids((8, LANES))
    known = jnp.maximum(note_ref[...], core_note_ref[...])
    for n in range(2):
        known = jnp.where(lane == 16 + n, angles_ref[:, n : n + 1].astype(F32), known)
    partner_ref[:, 2 * width :] = known
    known_ref[...] = known


def swap_kernel(measured_ref, known_ref, swap_ref):
    stripe = measured_ref.shape[2] // 2
    illum, _, _ = place()
    other = pl.multiple_of((1 - illum) * stripe, 16)
    for p in range(2):
        for r in range(0, stripe, 16):
            at = pl.ds(pl.multiple_of(other + r, 16), 16)
            swap_ref[p * stripe + r : p * stripe + r + 16, :] = measured_ref[p, 0, at, :].astype(F32)
    above = pack_rows(*edge_blocks(measured_ref, stripe - 8), False)
    below = pack_rows(*edge_blocks(measured_ref, stripe), True)
    swap_ref[2 * stripe :, :] = jnp.where(illum == 0, above, below)


def same_kernel(packed_ref, known_ref, partner_ref, same_ref):
    width = packed_ref.shape[1]
    same_ref[:, :width] = packed_ref[...]
    same_ref[:, width:] = jnp.maximum(known_ref[...], partner_ref[:, 2 * width :])


def rim_pack_kernel(phase_ref, measured_ref, known_ref, partner_ref, along_ref, same_ref, out_ref):
    stripe, width = phase_ref.shape[1:]
    rows = 2 * stripe
    illum, _, col = place()
    low_illum = illum == 0
    cols = out_ref.shape[0]
    lane = lane_ids((8, LANES))
    known = jnp.maximum(jnp.maximum(known_ref[...], partner_ref[:, 2 * width :]), same_ref[:, width:])
    for c in range(cols):
        out_ref[c, out_ref.shape[1] - 8 :, :] = known

    for east in (True, False):
        edge = slice(width - LANES, width) if east else slice(0, LANES)
        base = LANES - RIM if east else 0

        @pl.when(col < cols - 1 if east else col > 0)
        def _():
            to = col + 1 if east else col - 1
            groups = []
            for j in range(stripe // 8 + 2):
                items = []
                for k in range(2):
                    tile = slice(k * width + edge.start, k * width + edge.stop)
                    if j == 0:
                        items.append(jnp.where(low_illum, along_ref[:, tile], partner_ref[:, tile]))
                    elif j == stripe // 8 + 1:
                        items.append(jnp.where(low_illum, partner_ref[:, tile], along_ref[:, tile]))
                    else:
                        items.append(phase_ref[k, 8 * (j - 1) : 8 * j, edge])
                groups.append(items)
            while len(groups) < rows // 8 + 1:
                groups.append([None, None])
            for r in range(0, rows, 16):
                both = [measured_ref[p, 0, r : r + 16, edge].astype(F32) for p in range(2)]
                for h in range(2):
                    groups[r // 8 + h] += [b[8 * h : 8 * h + 8] for b in both]
            groups[rows // 8] += [same_ref[:, edge], along_ref[:, 2 * width + edge.start : 2 * width + edge.stop]]
            for g in range(0, len(groups), 4):
                acc = jnp.zeros((8, LANES), F32)
                for q, items in enumerate(groups[g : g + 4]):
                    for k, item in enumerate(items):
                        if item is not None:
                            slot = 4 * q + k
                            shift = (8 * slot - base) % LANES
                            moved = pltpu.roll(item, shift, 1) if shift else item
                            acc = jnp.where((lane >= 8 * slot) & (lane < 8 * slot + 8), moved, acc)
                out_ref[to, 2 * g : 2 * g + 8, :] = acc


def rim_unpack_kernel(got_ref, phase_rim_ref, rim_ref, relay_ref):
    cols, depth = got_ref.shape[:2]
    stripe = phase_rim_ref.shape[1] - 2 * RIM
    rows = 2 * stripe
    illum, _, col = place()
    west, east = jnp.maximum(col - 1, 0), jnp.minimum(col + 1, cols - 1)
    lane = lane_ids((8, LANES))
    in_west = (lane >= LANES - RIM) & (col > 0)
    in_east = (lane < RIM) & (col < cols - 1)
    for g in range(0, rows // 8 + 1, 4):
        a, b = got_ref[west, 2 * g : 2 * g + 8, :], got_ref[east, 2 * g : 2 * g + 8, :]
        for j in range(g, min(g + 4, rows // 8 + 1)):
            for k in range(4):
                if k < 2 and j >= stripe // 8 + 2:
                    continue
                slot = 4 * (j - g) + k
                from_west = pltpu.roll(a, (LANES - RIM - 8 * slot) % LANES, 1)
                from_east = pltpu.roll(b, (-8 * slot) % LANES, 1) if slot else b
                item = jnp.where(in_west, from_west, jnp.where(in_east, from_east, 0.0))
                (phase_rim_ref if k < 2 else rim_ref)[k % 2, 8 * j : 8 * j + 8, :] = item
    other = pl.multiple_of((1 - illum) * stripe, 8)
    near = pl.multiple_of(stripe - 8 + 8 * illum, 8)
    for r in range(0, stripe + 8, 8):
        at = pl.ds(pl.multiple_of(other + r, 8) if r < stripe else near, 8)
        relay_ref[r : r + 8, :] = rim_ref[0, at, :] + pltpu.roll(rim_ref[1, at, :], LANES // 2, 1)
    total = got_ref[0, depth - 8 :, :]
    for c in range(1, cols):
        total = total + got_ref[c, depth - 8 :, :]
    relay_ref[stripe + 8 :, :] = total


def fill_target(tile, target, low_illum, middle, near, far):
    end = 2 * RIM + tile.stripe
    for t in range(tile.tiles):
        beside_rows, packed = near(t), far(t)
        for part, ref in enumerate(target):
            for r in range(0, tile.stripe, 16):
                ref[t, 2 * RIM + r : 2 * RIM + r + 16, :] = middle(part, t, r)
            ref[t, RIM : 2 * RIM, :] = jnp.where(low_illum, unpack_rows(packed, False)[part], beside_rows[part])
            ref[t, end : end + RIM, :] = jnp.where(low_illum, beside_rows[part], unpack_rows(packed, True)[part])


def fill_trig(tile, trig, low_illum, middle, near, far):
    for t in range(tile.tiles):
        for k, (c, s) in enumerate(trig):
            above, below = far(k, t), near(k, t)
            here = [(RIM, jnp.where(low_illum, above, below)), (2 * RIM + tile.stripe, jnp.where(low_illum, below, above))]
            here += [(2 * RIM + r, middle(k, t, r)) for r in range(0, tile.stripe, 16)]
            for first, x in here:
                s[t, first : first + x.shape[0], :], c[t, first : first + x.shape[0], :] = sine_cosine(x)


def tilts_of(note):
    lane = lane_ids(note.shape)
    return [jnp.sum(jnp.where(lane == n, note, 0.0)[:1], axis=1, keepdims=True) for n in (16, 17)]


def forward_both(tile, notes, columns, row_first, totals, trig, half, tables, fields, uses):
    for note, columns_of, (w0, w1), use in zip(notes, (columns, columns), fields, uses):
        incident_tables(tile, tilts_of(note), row_first, columns_of, *totals, tables)
        enter(tile, tables, trig[0], w0)
        first_half(tile, w0, half, 1.0, tile.blocks)
        second_half(tile, w0, half, tile.blocks, modulate_into(trig[1], w1))
        first_half(tile, w1, half, 1.0, tile.blocks)
        second_half(tile, w1, half, tile.blocks, use)


def keep_in(field):
    def use(t, rows, mask, ur, ui):
        field[0][t, rows, :] = ur
        field[1][t, rows, :] = ui

    return use


def residual_in(field, target):
    def use(t, rows, mask, ur, ui):
        field[0][t, rows, :] = mask(ur - target[0][t, rows, :])
        field[1][t, rows, :] = mask(ui - target[1][t, rows, :])

    return use


def residual_of(tile, field, exit_field, target):
    def body(t, left, right, rows, mask):
        for g, u, m in zip(field, exit_field, target):
            g[t, rows, :] = mask(u[t, rows, :] - m[t, rows, :])

    tile.sweep(body, tile.blocks)


def put_in(ref):
    def put(k, t, rows, value):
        ref[k, own_rows(rows), own_columns(t)] = value

    return put


def main_tile(sizes):
    stripe, tiles, total_rows, total_cols = sizes
    illum, row, col = place()
    row_first = (row * 2 + illum) * stripe
    top, bottom, _ = edges_of(row_first, 0, stripe, tiles + 1, total_rows, total_cols)
    return Tile(stripe, tiles, top, bottom), row_first, col * tiles * LANES


def patch_tile(sizes):
    stripe, tiles, total_rows, total_cols = sizes
    _, row_first, col_first = main_tile(sizes)
    width = tiles * LANES
    top, bottom, _ = edges_of(row_first, 0, stripe, tiles + 1, total_rows, total_cols)
    lane = lane_ids((1, LANES))
    held = (lane < 16) | ((lane >= 56) & (lane < 72))
    held = held | ((lane >= 72) & (lane < 80) & (col_first + width < total_cols))
    held = held | ((lane >= LANES - RIM) & (col_first > 0))
    columns = jnp.where(lane < 16, lane, jnp.where(lane < 80, lane - 72 + width, lane - LANES)) + col_first
    tile = Tile(stripe, 1, top, bottom, jnp.where(held, 1.0, 0.0).astype(F32), 0)
    return tile, row_first, jnp.broadcast_to(columns, (8, LANES))


def join_edges(west, east, rim):
    lane = lane_ids(west.shape)
    moved = pltpu.roll(jnp.where(lane < RIM, rim, east), 72, 1)
    return jnp.where(lane < 16, west, jnp.where(lane >= LANES - RIM, rim, moved))


def forward_kernel(sizes, phase_ref, measured_ref, known_ref, partner_ref, along_ref, same_ref,
                   own_ref, o0r, o0i, o1r, o1i, o2r, o2i, c1, s1,
                   c0, s0, w0r, w0i, w1r, w1i, gr, gi, hr, hi, mr, mi, row_r, row_i, col_r, col_i):
    stripe, tiles, total_rows, total_cols = sizes
    tile, row_first, col_first = main_tile(sizes)
    illum, _, _ = place()
    low_illum = illum == 0
    blank_rims((w0r, w0i, w1r, w1i, gr, gi, hr, hi, o0r, o0i, o1r, o1i), tile)
    trig = (c0, s0), (c1, s1)
    fill_trig(
        tile, trig, low_illum,
        lambda k, t, r: phase_ref[k, r : r + 16, own_columns(t)],
        lambda k, t: partner_ref[:, own_columns(t + k * tiles)],
        lambda k, t: along_ref[:, own_columns(t + k * tiles)],
    )
    mine = illum * stripe
    near_base = pl.multiple_of(stripe - 16 * illum, 16)

    def middle(part, t, r):
        return measured_ref[part, 0, pl.ds(pl.multiple_of(mine + r, 16), 16), own_columns(t)].astype(F32)

    def near(t):
        both = [measured_ref[part, 0, pl.ds(near_base, 16), own_columns(t)].astype(F32) for part in range(2)]
        return [jnp.where(low_illum, x[:8], x[8:]) for x in both]

    fill_target(tile, (mr, mi), low_illum, middle, near, lambda t: same_ref[:, own_columns(t)])
    half = hr, hi
    forward_both(
        tile, (partner_ref[:, 2 * tiles * LANES :], known_ref[...]), rim_columns(tile, col_first, col_r.shape), row_first,
        (total_rows, total_cols), trig, half, (row_r, row_i, col_r, col_i),
        (((o0r, o0i), (o1r, o1i)), ((w0r, w0i), (w1r, w1i))),
        (keep_in((o2r, o2i)), residual_in((gr, gi), (mr, mi))),
    )
    backward(tile, (gr, gi), half, (w0r, w0i), (w1r, w1i), trig[1], put_in(own_ref))


def other_near(swap_ref, stripe, low_illum, columns):
    packed = swap_ref[2 * stripe :, columns]
    high, low = unpack_rows(packed, False), unpack_rows(packed, True)
    return [jnp.where(low_illum, low[part], high[part]) for part in range(2)]


def other_kernel(sizes, swap_ref, along_ref, w0r, w0i, w1r, w1i, ur_ref, ui_ref, c1, s1, out_ref, gr, gi, hr, hi, mr, mi):
    stripe, tiles, _, _ = sizes
    tile, _, _ = main_tile(sizes)
    illum, _, _ = place()
    blank_rims((gr, gi, hr, hi), tile)
    fill_target(
        tile, (mr, mi), illum == 0,
        lambda part, t, r: swap_ref[part * stripe + r : part * stripe + r + 16, own_columns(t)],
        lambda t: other_near(swap_ref, stripe, illum == 0, own_columns(t)),
        lambda t: along_ref[:, own_columns(t + 2 * tiles)],
    )
    residual_of(tile, (gr, gi), (ur_ref, ui_ref), (mr, mi))
    backward(tile, (gr, gi), (hr, hi), (w0r, w0i), (w1r, w1i), (c1, s1), put_in(out_ref))


def patch_kernel(sizes, phase_ref, measured_ref, known_ref, partner_ref, along_ref, same_ref, phase_rim_ref, rim_ref,
                 own_ref, o0r, o0i, o1r, o1i, o2r, o2i, c1, s1,
                 c0, s0, w0r, w0i, w1r, w1i, gr, gi, hr, hi, mr, mi, row_r, row_i, col_r, col_i):
    stripe, tiles, total_rows, total_cols = sizes
    tile, row_first, columns = patch_tile(sizes)
    illum, _, _ = place()
    low_illum = illum == 0
    blank_rims((w0r, w0i, w1r, w1i, gr, gi, hr, hi, o0r, o0i, o1r, o1i), tile)
    trig = (c0, s0), (c1, s1)
    first, last = 0, tiles - 1

    def joined(get, rim):
        return join_edges(get(first), get(last), rim)

    end = stripe + RIM
    fill_trig(
        tile, trig, low_illum,
        lambda k, t, r: joined(lambda e: phase_ref[k, r : r + 16, own_columns(e)], phase_rim_ref[k, RIM + r : RIM + r + 16, :]),
        lambda k, t: joined(
            lambda e: partner_ref[:, own_columns(e + k * tiles)],
            jnp.where(low_illum, phase_rim_ref[k, end:, :], phase_rim_ref[k, :RIM, :]),
        ),
        lambda k, t: joined(
            lambda e: along_ref[:, own_columns(e + k * tiles)],
            jnp.where(low_illum, phase_rim_ref[k, :RIM, :], phase_rim_ref[k, end:, :]),
        ),
    )
    mine = illum * stripe
    near_base = pl.multiple_of(stripe - 16 * illum, 16)
    near_rim = pl.multiple_of(stripe - 8 * illum, 8)

    def middle(part, t, r):
        at = pl.ds(pl.multiple_of(mine + r, 16), 16)
        return joined(lambda e: measured_ref[part, 0, at, own_columns(e)].astype(F32), rim_ref[part, at, :])

    def near(t):
        def rows(part, e):
            x = measured_ref[part, 0, pl.ds(near_base, 16), own_columns(e)].astype(F32)
            return jnp.where(low_illum, x[:8], x[8:])

        return [joined(lambda e: rows(part, e), rim_ref[part, pl.ds(near_rim, 8), :]) for part in range(2)]

    def far(t):
        return joined(lambda e: same_ref[:, own_columns(e)], rim_ref[0, 2 * stripe :, :])

    fill_target(tile, (mr, mi), low_illum, middle, near, far)
    half = hr, hi
    forward_both(
        tile, (partner_ref[:, 2 * tiles * LANES :], known_ref[...]), columns, row_first,
        (total_rows, total_cols), trig, half, (row_r, row_i, col_r, col_i),
        (((o0r, o0i), (o1r, o1i)), ((w0r, w0i), (w1r, w1i))),
        (keep_in((o2r, o2i)), residual_in((gr, gi), (mr, mi))),
    )
    backward(tile, (gr, gi), half, (w0r, w0i), (w1r, w1i), trig[1], put_in(own_ref))


def finish_kernel(sizes, own_ref, other_ref, own_patch_ref, swap_ref, along_ref, rim_ref, relay_ref, partner_relay_ref,
                  w0r, w0i, w1r, w1i, ur_ref, ui_ref, c1, s1, out_ref, other_patch, gr, gi, hr, hi, mr, mi):
    stripe, tiles, total_rows, total_cols = sizes
    tile, _, _ = patch_tile(sizes)
    illum, _, _ = place()
    low_illum = illum == 0
    blank_rims((gr, gi, hr, hi), tile)

    lane = lane_ids((8, LANES))
    sums = jnp.maximum(relay_ref[stripe + 8 :, :], partner_relay_ref[stripe + 8 :, :])
    scales = []
    for which in range(2):
        here = jnp.where((lane >= 4 * which) & (lane < 4 * which + 4), sums, 0.0)
        energy = jnp.sum(here[:1], axis=1, keepdims=True) / (total_rows * total_cols) + EPS_ENERGY
        scales.append(2.0 / energy)
    mine = jnp.where(low_illum, scales[0], scales[1])
    others = jnp.where(low_illum, scales[1], scales[0])
    first, last = own_columns(0), own_columns(tiles - 1)

    def middle(part, t, r):
        rim = partner_relay_ref[r : r + 16, :]
        at = slice(part * stripe + r, part * stripe + r + 16)
        return join_edges(swap_ref[at, first], swap_ref[at, last], pltpu.roll(rim, LANES // 2, 1) if part else rim)

    def near(t):
        rim = partner_relay_ref[stripe : stripe + 8, :]
        rims = [rim, pltpu.roll(rim, LANES // 2, 1)]
        west, east = [other_near(swap_ref, stripe, low_illum, at) for at in (first, last)]
        return [join_edges(*x) for x in zip(west, east, rims)]

    def far(t):
        west, east = [along_ref[:, own_columns(e + 2 * tiles)] for e in (0, tiles - 1)]
        return join_edges(west, east, rim_ref[1, 2 * stripe :, :])

    fill_target(tile, (mr, mi), low_illum, middle, near, far)
    residual_of(tile, (gr, gi), (ur_ref, ui_ref), (mr, mi))
    backward(tile, (gr, gi), (hr, hi), (w0r, w0i), (w1r, w1i), (c1, s1), put_in(other_patch))

    for k in range(2):
        for t in range(tiles):
            out_ref[k, :, own_columns(t)] = own_ref[k, :, own_columns(t)] * mine + other_ref[k, :, own_columns(t)] * others
        patch = own_patch_ref[k] * mine + other_patch[k] * others
        on = lane_ids(patch.shape)
        out_ref[k, :, first] = jnp.where(on < RIM, patch, out_ref[k, :, first])
        out_ref[k, :, last] = jnp.where(on >= LANES - RIM, pltpu.roll(patch, 56, 1), out_ref[k, :, last])


def call(kernel, outs, *args, scratch=(), in_place=0, flops=0):
    return pl.pallas_call(
        kernel,
        out_shape=[jax.ShapeDtypeStruct(shape, F32) for shape in outs],
        in_specs=[pl.BlockSpec(memory_space=pl.ANY)] * in_place
        + [pl.BlockSpec(memory_space=pltpu.VMEM)] * (len(args) - in_place),
        out_specs=[pl.BlockSpec(memory_space=pltpu.VMEM)] * len(outs),
        scratch_shapes=[pltpu.VMEM(s, F32) if isinstance(s, tuple) else s for s in scratch],
        compiler_params=pltpu.CompilerParams(vmem_limit_bytes=24 * 2**20),
        cost_estimate=pl.CostEstimate(flops=flops, bytes_accessed=2**18, transcendentals=0),
    )(*args)


def paired(phase_delay, angles, measured):
    slices, stripe, width = phase_delay.shape
    rows, cols = lax.axis_size("row"), lax.axis_size("col")
    tiles = width // LANES
    sizes = (stripe, tiles, 2 * stripe * rows, width * cols)
    swap = [(0, 1), (1, 0)]
    along = []
    for r in range(rows - 1):
        along += [(rows + r, r + 1), (r + 1, rows + r)]
    same = [(r, (r + 1) % rows) for r in range(rows)] + [(rows + (r + 1) % rows, rows + r) for r in range(rows)]

    note, along_out, same_packed = call(
        open_kernel, [(8, LANES), (8, 3 * width), (8, width)], phase_delay, measured,
        scratch=[pltpu.VMEM(measured.shape, measured.dtype), (slices, 8, width), pltpu.SemaphoreType.DMA((2,))], in_place=2,
    )
    core_note = lax.ppermute(note, "row", [(r, r ^ 1) for r in range(rows)])
    along_in = lax.ppermute(along_out, ("illum", "row"), along)
    partner_out, known = call(partner_kernel, [(8, 2 * width + LANES), (8, LANES)], phase_delay, angles, note, core_note)
    partner_in = lax.ppermute(partner_out, "illum", swap)
    (swap_out,) = call(swap_kernel, [(2 * stripe + 8, width)], measured, known)
    swap_in = lax.ppermute(swap_out, "illum", swap)
    (same_out,) = call(same_kernel, [(8, width + LANES)], same_packed, known, partner_in)
    same_in = lax.ppermute(same_out, ("illum", "row"), same)
    depth = 8 * (-(-(stripe // 4 + 1) // 4)) + 8
    (rims_out,) = call(rim_pack_kernel, [(cols, depth, LANES)], phase_delay, measured, known, partner_in, along_in, same_in)
    rims_in = lax.all_to_all(rims_out, "col", 0, 0, tiled=True)

    def fields(count):
        return [(count, stripe + 4 * RIM, LANES)]

    def tables(count):
        return [(stripe + 2 * RIM, LANES)] * 2 + [(-(-count // 8) * 8, LANES)] * 2

    rows_in = phase_delay, measured, known, partner_in, along_in, same_in
    own, *kept = call(
        functools.partial(forward_kernel, sizes), [phase_delay.shape] + fields(tiles) * 8, *rows_in,
        scratch=fields(tiles) * 12 + tables(tiles), flops=6 * 10**9,
    )
    (other,) = call(
        functools.partial(other_kernel, sizes), [phase_delay.shape], swap_in, along_in, *kept,
        scratch=fields(tiles) * 6, flops=2 * 10**9,
    )
    phase_rim, rim, relay = call(
        rim_unpack_kernel, [(2, stripe + 2 * RIM, LANES), (2, 2 * stripe + 8, LANES), (stripe + 16, LANES)], rims_in
    )
    partner_relay = lax.ppermute(relay, "illum", swap)
    own_patch, *patch_kept = call(
        functools.partial(patch_kernel, sizes), [(slices, stripe, LANES)] + fields(1) * 8, *rows_in, phase_rim, rim,
        scratch=fields(1) * 12 + tables(1), flops=10**9,
    )
    (out,) = call(
        functools.partial(finish_kernel, sizes), [phase_delay.shape],
        own, other, own_patch, swap_in, along_in, rim, relay, partner_relay, *patch_kept,
        scratch=[(slices, stripe, LANES)] + fields(1) * 6,
    )
    return out


def halo(x, axis, dim, width, index_of=None):
    peers = lax.axis_size(axis)
    up = [(i, i + 1) for i in range(peers - 1)]
    before = lax.ppermute(lax.slice_in_dim(x, x.shape[dim] - width, x.shape[dim], axis=dim), axis, up)
    after = lax.ppermute(lax.slice_in_dim(x, 0, width, axis=dim), axis, [(j, i) for i, j in up])
    return before, after


def with_column_rims(x, width):
    before, after = halo(x, "col", x.ndim - 1, width)
    gap = jnp.zeros(x.shape[:-1] + (LANES - 2 * width,), x.dtype)
    return jnp.concatenate([x, after, gap, before], axis=-1)


def stripe_halo(x, width):
    illums, rows = lax.axis_size("illum"), lax.axis_size("row")
    where = [(s % illums) * rows + s // illums for s in range(illums * rows)]
    up = [(where[s], where[s + 1]) for s in range(illums * rows - 1)]
    before = lax.ppermute(x[:, -width:], ("illum", "row"), up)
    after = lax.ppermute(x[:, :width], ("illum", "row"), [(b, a) for a, b in up])
    return jnp.concatenate([before, x, after], axis=1)


def per_device(phase_delay, angles, measured):
    illums = lax.axis_size("illum")
    if illums == 2 and lax.axis_size("row") == 4:
        return paired(phase_delay, angles, measured)
    slices, stripe, width = phase_delay.shape
    tile_rows = measured.shape[2]
    total_rows, total_cols = tile_rows * lax.axis_size("row"), width * lax.axis_size("col")
    tiles = width // LANES + 1
    row_first = lax.axis_index("row") * tile_rows + lax.axis_index("illum") * stripe
    col_first = lax.axis_index("col") * width

    target = measured[:, 0].astype(F32)
    energy = lax.psum(jnp.sum(target * target).reshape(1), ("row", "col"))
    energies = lax.all_gather(energy, "illum", tiled=True) / (total_rows * total_cols) + EPS_ENERGY
    tilts = lax.all_gather(angles, "illum", tiled=True)

    phase = with_column_rims(stripe_halo(phase_delay, RIM), RIM)
    above, below = halo(target, "row", 1, REACH)
    target = with_column_rims(jnp.concatenate([above, target, below], axis=1), REACH)
    windows = jnp.stack([target[:, i * stripe : (i + 1) * stripe + 2 * REACH] for i in range(illums)])
    windows = lax.all_to_all(windows, "illum", 0, 0, tiled=True)
    windows = jnp.pad(windows, ((0, 0), (0, 0), (RIM - REACH, RIM - REACH), (0, 0)))

    field = pltpu.VMEM((tiles, stripe + 4 * RIM, LANES), F32)
    rows_all = stripe + 2 * RIM
    return pl.pallas_call(
        functools.partial(gradient_kernel, (stripe, tiles, illums, total_rows, total_cols)),
        out_shape=jax.ShapeDtypeStruct(phase_delay.shape, F32),
        in_specs=[pl.BlockSpec(memory_space=pltpu.SMEM)] * 3 + [pl.BlockSpec(memory_space=pltpu.VMEM)] * 2,
        out_specs=pl.BlockSpec(memory_space=pltpu.VMEM),
        scratch_shapes=[field] * 12
        + [pltpu.VMEM((rows_all, LANES), F32)] * 2
        + [pltpu.VMEM((-(-tiles // 8) * 8, LANES), F32)] * 2,
        compiler_params=pltpu.CompilerParams(vmem_limit_bytes=48 * 2**20),
    )(jnp.stack([row_first, col_first]), tilts, 2.0 / energies, phase, windows)


def solution(mesh):
    placed = (P(None, ("row", "illum"), "col"), P("illum", None), P(None, "illum", "row", "col"))
    return jax.shard_map(
        per_device,
        mesh=mesh,
        in_specs=placed,
        out_specs=P(None, ("row", "illum"), "col"),
        check_vma=False,
    )
```

time: 46.5 us -> 36 us (0.77)
  the two profiles are of different devices: /device:TPU:0 before, /device:TPU:1 now
where the time goes in v3:
time: 36 us; the launch traced here: 35.6 us
  starting transfers between devices  14.6 us (41%)
  Pallas kernels  10.8 us (30%)
  local copies, waits for them, and re-layouts  7.76 us (22%)
  waiting for transfers between devices  2.31 us (6%)
    pallas_call x10, Pallas kernels, call(): pl.pallas_call(kernel, out_shape=[jax.ShapeDtypeStruct(shape, F32) for sh...  10.8 us
    unnamed x38, local copies, waits for them, and re-layouts  7.76 us
    all_to_all x1, starting transfers between devices, paired(): rims_in = lax.all_to_all(rims_out, 'col', 0, 0, tiled=True)  4.85 us
    ppermute x1, starting transfers between devices, paired(): partner_relay = lax.ppermute(relay, 'illum', swap)  2.4 us
    ppermute x1, starting transfers between devices, paired(): partner_in = lax.ppermute(partner_out, 'illum', swap)  2.38 us
    ppermute x1, starting transfers between devices, paired(): same_in = lax.ppermute(same_out, ('illum', 'row'), same)  2.28 us
    ppermute x1, starting transfers between devices, paired(): along_in = lax.ppermute(along_out, ('illum', 'row'), along)  2.15 us
    ppermute x1, waiting for transfers between devices, paired(): core_note = lax.ppermute(note, 'row', [(r, r ^ 1) for r in range(rows)])  1.11 us
  transfers between devices with their start and end apart: 7, of which 3 were waited for; matrix products, arithmetic and copies ran while one was open for 0% of the time, Pallas kernels for 25%

profile of v3, /device:TPU:1, one launch (start us, length us, event | category | flops | bytes accessed | tf_op | source)
XLA Modules:
  0.0 35.6 jit_solution(13150736056044485140)
XLA Ops:
  0.0 0.0 copy-start
  0.0 1.0 %copy-done = f32[2,64,1024]{2,1,0:T(8,128)S(1)} copy-done((f32[2,64,1024]{2,1,0:T(8,128)S(1)}, f32[2,64,1024]{2,1,0:T(8,128)}, u32[]{:S(2)}) %copy-start) | copy-done | bytes 524312
  1.0 1.0 %copy-done.2 = bf16[2,1,128,1024]{3,2,1,0:T(8,128)(2,1)S(1)} copy-done((bf16[2,1,128,1024]{3,2,1,0:T(8,128)(2,1)S(1)}, bf16[2,1,128,1024]{3,2,1,0:T(8,128)(2,1)}, u32[]{:S(2)}) %copy-start.2) | copy-done | bytes 524312
  2.1 0.0 copy-start.4
  2.1 0.3 shard_map.37
  2.4 0.0 copy-start.3
  2.4 0.1 collective-permute-start
  2.5 1.1 %collective-permute-done.core_note_ref = f32[8,128]{1,0:T(8,128)S(1)} collective-permute-done((f32[8,128]{1,0:T(8,128)S(1)}, f32[8,128]{1,0:T(8,128)S(1)}, u32[]{:S(2)}, u32[]{:S(2)}) %collective-permute-start) | collective-permute-done | bytes 4128 | tf_op jit(solution)/shard_map/ppermute | solution.py:667
  3.6 0.0 copy-done.4
  3.6 0.1 shard_map.38
  3.7 2.4 %collective-permute-start.1 = (f32[8,2176]{1,0:T(8,128)S(1)}, f32[8,2176]{1,0:T(8,128)S(1)}, u32[]{:S(2)}, u32[]{:S(2)}) collective-permute-start(f32[8,2176]{1,0:T(8,128)S(1)} %get-tuple-element.33), channel_id=1, source_target_pairs={{0,16},{16,0},{1,17},{17,1},{2,18},{18,2},{3,19},{19,3},{4,20},{20... | collective-permute-start | bytes 208904 | tf_op jit(solution)/shard_map/ppermute | solution.py:670
  6.1 2.1 %collective-permute-start.2 = (f32[8,3072]{1,0:T(8,128)S(1)}, f32[8,3072]{1,0:T(8,128)S(1)}, u32[]{:S(2)}, u32[]{:S(2)}) collective-permute-start(f32[8,3072]{1,0:T(8,128)S(1)} %get-tuple-element.34), channel_id=1, source_target_pairs={{16,4},{4,16},{20,8},{8,20},{24,12},{12,24},{17,5},{5,17},{21,9},{... | collective-permute-start | bytes 294920 | tf_op jit(solution)/shard_map/ppermute | solution.py:668
  8.2 0.1 collective-permute-done.1.partner_ref
  8.4 2.3 %collective-permute-start.3 = (f32[8,1152]{1,0:T(8,128)S(1)}, f32[8,1152]{1,0:T(8,128)S(1)}, u32[]{:S(2)}, u32[]{:S(2)}) collective-permute-start(f32[8,1152]{1,0:T(8,128)S(1)} %shard_map.39), channel_id=1, source_target_pairs={{0,4},{4,8},{8,12},{12,0},{20,16},{24,20},{28,24},{16,28},{1,5},{5... | collective-permute-start | bytes 110600 | tf_op jit(solution)/shard_map/ppermute | solution.py:674
  10.7 0.0 copy-done.3
  10.7 0.4 %collective-permute-start.4 = (f32[136,1024]{1,0:T(8,128)S(1)}, f32[136,1024]{1,0:T(8,128)S(1)}, u32[]{:S(2)}, u32[]{:S(2)}) collective-permute-start(f32[136,1024]{1,0:T(8,128)S(1)} %shard_map.41), channel_id=1, source_target_pairs={{0,16},{16,0},{1,17},{17,1},{2,18},{18,2},{3,19},{19,3},{4,20},{20... | collective-permute-start | bytes 1671176 | tf_op jit(solution)/shard_map/ppermute | solution.py:672
  11.2 1.1 %collective-permute-done.2.along_ref = f32[8,3072]{1,0:T(8,128)S(1)} collective-permute-done((f32[8,3072]{1,0:T(8,128)S(1)}, f32[8,3072]{1,0:T(8,128)S(1)}, u32[]{:S(2)}, u32[]{:S(2)}) %collective-permute-start.2) | collective-permute-done | bytes 98336 | tf_op jit(solution)/shard_map/ppermute | solution.py:668
  12.2 0.0 collective-permute-done.3.same_ref
  12.2 0.0 copy-done.1
  12.2 0.7 %shard_map.43 = f32[4,48,128]{2,1,0:T(8,128)} custom-call(f32[2,64,1024]{2,1,0:T(8,128)S(1)} %copy-done.1, bf16[2,1,128,1024]{3,2,1,0:T(8,128)(2,1)S(1)} %copy-done.3, f32[8,128]{1,0:T(8,128)S(1)} %get-tuple-element.32.known_ref, f32[8,2176]{1,0:T(8,128)S(1)} %collective-permute-done.1.partner_ref, f32[8,3072]{1,0:T(8,128)S(1)} %collective-permute-done.2.along_ref, ...), custom_call_target="tpu_custom_call" | custom-call | bytes 262144 | tf_op jit(solution)/shard_map/pallas_call | solution.py:640
  13.0 4.9 %all-to-all-start = ((f32[4,48,128]{2,1,0:T(8,128)}), f32[4,48,128]{2,1,0:T(8,128)S(1)}, u32[]{:S(2)}, u32[]{:S(2)}) async-start(f32[4,48,128]{2,1,0:T(8,128)} %shard_map.43), calls=%async_computation | async-start | bytes 196608 | tf_op jit(solution)/shard_map/all_to_all | solution.py:677
  17.8 5.3 %shard_map.40 = (f32[2,64,1024]{2,1,0:T(8,128)S(1)}, f32[8,96,128]{2,1,0:T(8,128)S(1)}, f32[8,96,128]{2,1,0:T(8,128)S(1)}, f32[8,96,128]{2,1,0:T(8,128)S(1)}, f3...) custom-call(f32[2,64,1024]{2,1,0:T(8,128)S(1)} %copy-done.1, ...), custom_call_target="tpu_custom_call" | custom-call | flops 6000000000 | bytes 262144 | tf_op jit(solution)/shard_map/pallas_call | solution.py:640
  23.1 0.0 copy-start.5
  23.1 0.7 %copy-done.5 = f32[8,96,128]{2,1,0:T(8,128)} copy-done((f32[8,96,128]{2,1,0:T(8,128)}, f32[8,96,128]{2,1,0:T(8,128)S(1)}, u32[]{:S(2)}) %copy-start.5) | copy-done | bytes 393240
  23.9 0.8 %copy-done.7 = f32[8,96,128]{2,1,0:T(8,128)} copy-done((f32[8,96,128]{2,1,0:T(8,128)}, f32[8,96,128]{2,1,0:T(8,128)S(1)}, u32[]{:S(2)}) %copy-start.7) | copy-done | bytes 393240
  24.6 0.8 %copy-done.9 = f32[8,96,128]{2,1,0:T(8,128)} copy-done((f32[8,96,128]{2,1,0:T(8,128)}, f32[8,96,128]{2,1,0:T(8,128)S(1)}, u32[]{:S(2)}) %copy-start.9) | copy-done | bytes 393240
  25.4 0.8 %copy-done.11 = f32[8,96,128]{2,1,0:T(8,128)} copy-done((f32[8,96,128]{2,1,0:T(8,128)}, f32[8,96,128]{2,1,0:T(8,128)S(1)}, u32[]{:S(2)}) %copy-start.11) | copy-done | bytes 393240
  26.1 0.8 %copy-done.13 = f32[8,96,128]{2,1,0:T(8,128)} copy-done((f32[8,96,128]{2,1,0:T(8,128)}, f32[8,96,128]{2,1,0:T(8,128)S(1)}, u32[]{:S(2)}) %copy-start.13) | copy-done | bytes 393240
  26.9 0.8 %copy-done.15 = f32[8,96,128]{2,1,0:T(8,128)} copy-done((f32[8,96,128]{2,1,0:T(8,128)}, f32[8,96,128]{2,1,0:T(8,128)S(1)}, u32[]{:S(2)}) %copy-start.15) | copy-done | bytes 393240
  27.7 0.7 %copy-done.17 = f32[8,96,128]{2,1,0:T(8,128)} copy-done((f32[8,96,128]{2,1,0:T(8,128)}, f32[8,96,128]{2,1,0:T(8,128)S(1)}, u32[]{:S(2)}) %copy-start.17) | copy-done | bytes 393240
  28.4 0.0 all-to-all-done.got_ref
  28.4 0.2 shard_map.44
  28.6 2.4 %collective-permute-start.5 = (f32[80,128]{1,0:T(8,128)S(1)}, f32[80,128]{1,0:T(8,128)S(1)}, u32[]{:S(2)}, u32[]{:S(2)}) collective-permute-start(f32[80,128]{1,0:T(8,128)S(1)} %get-tuple-element.48.relay_ref), channel_id=1, source_target_pairs={{0,16},{16,0},{1,17},{17,1},{2,18},{18,2},{3,19},{19,3},{4,20},{20... | collective-permute-start | bytes 122888 | tf_op jit(solution)/shard_map/ppermute | solution.py:697
  31.0 0.0 copy-start.14
  31.0 0.0 copy-start.16
  31.1 0.0 copy-start.18
  31.1 1.2 %shard_map.45 = (f32[2,64,128]{2,1,0:T(8,128)S(1)}, f32[1,96,128]{2,1,0:T(8,128)S(1)}, f32[1,96,128]{2,1,0:T(8,128)S(1)}, f32[1,96,128]{2,1,0:T(8,128)S(1)}, f32...) custom-call(f32[2,64,1024]{2,1,0:T(8,128)S(1)} %copy-done.1, ...), custom_call_target="tpu_custom_call" | custom-call | flops 1000000000 | bytes 262144 | tf_op jit(solution)/shard_map/pallas_call | solution.py:640
  32.3 0.0 collective-permute-done.4.swap_ref
  32.3 0.0 copy-done.6
  32.3 0.0 copy-done.8
  32.4 0.0 copy-done.10
  32.4 0.0 copy-done.12
  32.4 0.1 copy-done.14
  32.5 0.1 copy-done.16
  32.6 0.1 copy-done.18
  32.7 1.5 %shard_map.42.other_ref = f32[2,64,1024]{2,1,0:T(8,128)S(1)} custom-call(f32[136,1024]{1,0:T(8,128)S(1)} %collective-permute-done.4.swap_ref, f32[8,3072]{1,0:T(8,128)S(1)} %collective-permute-done.2.along_ref, f32[8,96,128]{2,1,0:T(8,128)S(1)} %get-tuple-element.37.w0r, f32[8,96,128]{2,1,0:T(8,128)S(1)} %copy-done.6, f32[8,96,128]{2,1,0:T(8,128)S(1)} %copy-done.8, ...), custom_call_target="tpu_custom_call" | custom-call | flops 2000000000 | bytes 262144 | tf_op jit(solution)/shard_map/pallas_call | solution.py:640
  34.2 0.0 collective-permute-done.5.partner_relay_ref
  34.3 1.4 %shard_map.46 = f32[2,64,1024]{2,1,0:T(8,128)} custom-call(f32[2,64,1024]{2,1,0:T(8,128)S(1)} %get-tuple-element.36.own_ref, f32[2,64,1024]{2,1,0:T(8,128)S(1)} %shard_map.42.other_ref, f32[2,64,128]{2,1,0:T(8,128)S(1)} %get-tuple-element.47.own_patch_ref, f32[136,1024]{1,0:T(8,128)S(1)} %collective-permute-done.4.swap_ref, ...), custom_call_target="tpu_custom_call" | custom-call | bytes 262144 | tf_op jit(solution)/shard_map/pallas_call | solution.py:640
  (14 shorter events, 0.1 us)
Async XLA Ops:
  0.0 1.0 %copy-start = (f32[2,64,1024]{2,1,0:T(8,128)S(1)}, f32[2,64,1024]{2,1,0:T(8,128)}, u32[]{:S(2)}) copy-start(f32[2,64,1024]{2,1,0:T(8,128)} %phase_ref.9) | copy-start | bytes 1572868
  1.0 1.0 %copy-start.2 = (bf16[2,1,128,1024]{3,2,1,0:T(8,128)(2,1)S(1)}, bf16[2,1,128,1024]{3,2,1,0:T(8,128)(2,1)}, u32[]{:S(2)}) copy-start(bf16[2,1,128,1024]{3,2,1,0:T(8,128)(2,1)} %measured_ref.9) | copy-start | bytes 1572868
  2.1 1.5 %copy-start.4 = (s32[1,2]{1,0:T(1,128)S(1)}, s32[1,2]{1,0:T(1,128)}, u32[]{:S(2)}) copy-start(s32[1,2]{1,0:T(1,128)} %angles_ref.1) | copy-start | bytes 28
  2.4 8.3 %copy-start.3 = (bf16[2,1,128,1024]{3,2,1,0:T(8,128)(2,1)S(1)}, bf16[2,1,128,1024]{3,2,1,0:T(8,128)(2,1)}, u32[]{:S(2)}) copy-start(bf16[2,1,128,1024]{3,2,1,0:T(8,128)(2,1)} %measured_ref.9) | copy-start | bytes 1572868
  2.4 1.2 %collective-permute-start = (f32[8,128]{1,0:T(8,128)S(1)}, f32[8,128]{1,0:T(8,128)S(1)}, u32[]{:S(2)}, u32[]{:S(2)}) collective-permute-start(f32[8,128]{1,0:T(8,128)S(1)} %get-tuple-element.31.note_ref), channel_id=1, source_target_pairs={{0,4},{4,0},{8,12},{12,8},{1,5},{5,1},{9,13},{13,9},{2,6},{6,2},{1... | collective-permute-start | bytes 12296 | tf_op jit(solution)/shard_map/ppermute | solution.py:667
  3.7 4.7 %collective-permute-start.1 = (f32[8,2176]{1,0:T(8,128)S(1)}, f32[8,2176]{1,0:T(8,128)S(1)}, u32[]{:S(2)}, u32[]{:S(2)}) collective-permute-start(f32[8,2176]{1,0:T(8,128)S(1)} %get-tuple-element.33), channel_id=1, source_target_pairs={{0,16},{16,0},{1,17},{17,1},{2,18},{18,2},{3,19},{19,3},{4,20},{20... | collective-permute-start | bytes 208904 | tf_op jit(solution)/shard_map/ppermute | solution.py:670
  6.1 6.1 %collective-permute-start.2 = (f32[8,3072]{1,0:T(8,128)S(1)}, f32[8,3072]{1,0:T(8,128)S(1)}, u32[]{:S(2)}, u32[]{:S(2)}) collective-permute-start(f32[8,3072]{1,0:T(8,128)S(1)} %get-tuple-element.34), channel_id=1, source_target_pairs={{16,4},{4,16},{20,8},{8,20},{24,12},{12,24},{17,5},{5,17},{21,9},{... | collective-permute-start | bytes 294920 | tf_op jit(solution)/shard_map/ppermute | solution.py:668
  8.4 3.8 %copy-start.1 = (f32[2,64,1024]{2,1,0:T(8,128)S(1)}, f32[2,64,1024]{2,1,0:T(8,128)}, u32[]{:S(2)}) copy-start(f32[2,64,1024]{2,1,0:T(8,128)} %phase_ref.9) | copy-start | bytes 1572868
  8.4 3.8 %collective-permute-start.3 = (f32[8,1152]{1,0:T(8,128)S(1)}, f32[8,1152]{1,0:T(8,128)S(1)}, u32[]{:S(2)}, u32[]{:S(2)}) collective-permute-start(f32[8,1152]{1,0:T(8,128)S(1)} %shard_map.39), channel_id=1, source_target_pairs={{0,4},{4,8},{8,12},{12,0},{20,16},{24,20},{28,24},{16,28},{1,5},{5... | collective-permute-start | bytes 110600 | tf_op jit(solution)/shard_map/ppermute | solution.py:674
  10.7 21.6 %collective-permute-start.4 = (f32[136,1024]{1,0:T(8,128)S(1)}, f32[136,1024]{1,0:T(8,128)S(1)}, u32[]{:S(2)}, u32[]{:S(2)}) collective-permute-start(f32[136,1024]{1,0:T(8,128)S(1)} %shard_map.41), channel_id=1, source_target_pairs={{0,16},{16,0},{1,17},{17,1},{2,18},{18,2},{3,19},{19,3},{4,20},{20... | collective-permute-start | bytes 1671176 | tf_op jit(solution)/shard_map/ppermute | solution.py:672
  13.0 15.4 %all-to-all-start = ((f32[4,48,128]{2,1,0:T(8,128)}), f32[4,48,128]{2,1,0:T(8,128)S(1)}, u32[]{:S(2)}, u32[]{:S(2)}) async-start(f32[4,48,128]{2,1,0:T(8,128)} %shard_map.43), calls=%async_computation | async-start | bytes 196608 | tf_op jit(solution)/shard_map/all_to_all | solution.py:677
  23.1 0.7 %copy-start.5 = (f32[8,96,128]{2,1,0:T(8,128)}, f32[8,96,128]{2,1,0:T(8,128)S(1)}, u32[]{:S(2)}) copy-start(f32[8,96,128]{2,1,0:T(8,128)S(1)} %get-tuple-element.38.w0i) | copy-start | bytes 1179652
  23.9 0.8 %copy-start.7 = (f32[8,96,128]{2,1,0:T(8,128)}, f32[8,96,128]{2,1,0:T(8,128)S(1)}, u32[]{:S(2)}) copy-start(f32[8,96,128]{2,1,0:T(8,128)S(1)} %get-tuple-element.39.w1r) | copy-start | bytes 1179652
  24.6 0.8 %copy-start.9 = (f32[8,96,128]{2,1,0:T(8,128)}, f32[8,96,128]{2,1,0:T(8,128)S(1)}, u32[]{:S(2)}) copy-start(f32[8,96,128]{2,1,0:T(8,128)S(1)} %get-tuple-element.40.w1i) | copy-start | bytes 1179652
  25.4 0.8 %copy-start.11 = (f32[8,96,128]{2,1,0:T(8,128)}, f32[8,96,128]{2,1,0:T(8,128)S(1)}, u32[]{:S(2)}) copy-start(f32[8,96,128]{2,1,0:T(8,128)S(1)} %get-tuple-element.41.ur_ref) | copy-start | bytes 1179652
  26.1 0.8 %copy-start.13 = (f32[8,96,128]{2,1,0:T(8,128)}, f32[8,96,128]{2,1,0:T(8,128)S(1)}, u32[]{:S(2)}) copy-start(f32[8,96,128]{2,1,0:T(8,128)S(1)} %get-tuple-element.42.ui_ref) | copy-start | bytes 1179652
  26.9 0.8 %copy-start.15 = (f32[8,96,128]{2,1,0:T(8,128)}, f32[8,96,128]{2,1,0:T(8,128)S(1)}, u32[]{:S(2)}) copy-start(f32[8,96,128]{2,1,0:T(8,128)S(1)} %get-tuple-element.43.c1) | copy-start | bytes 1179652
  27.7 0.7 %copy-start.17 = (f32[8,96,128]{2,1,0:T(8,128)}, f32[8,96,128]{2,1,0:T(8,128)S(1)}, u32[]{:S(2)}) copy-start(f32[8,96,128]{2,1,0:T(8,128)S(1)} %get-tuple-element.44.s1) | copy-start | bytes 1179652
  28.6 5.6 %collective-permute-start.5 = (f32[80,128]{1,0:T(8,128)S(1)}, f32[80,128]{1,0:T(8,128)S(1)}, u32[]{:S(2)}, u32[]{:S(2)}) collective-permute-start(f32[80,128]{1,0:T(8,128)S(1)} %get-tuple-element.48.relay_ref), channel_id=1, source_target_pairs={{0,16},{16,0},{1,17},{17,1},{2,18},{18,2},{3,19},{19,3},{4,20},{20... | collective-permute-start | bytes 122888 | tf_op jit(solution)/shard_map/ppermute | solution.py:697
  31.0 1.3 %copy-start.6 = (f32[8,96,128]{2,1,0:T(8,128)S(1)}, f32[8,96,128]{2,1,0:T(8,128)}, u32[]{:S(2)}) copy-start(f32[8,96,128]{2,1,0:T(8,128)} %copy-done.5) | copy-start | bytes 1179652
  31.0 1.3 %copy-start.8 = (f32[8,96,128]{2,1,0:T(8,128)S(1)}, f32[8,96,128]{2,1,0:T(8,128)}, u32[]{:S(2)}) copy-start(f32[8,96,128]{2,1,0:T(8,128)} %copy-done.7) | copy-start | bytes 1179652
  31.0 1.3 %copy-start.10 = (f32[8,96,128]{2,1,0:T(8,128)S(1)}, f32[8,96,128]{2,1,0:T(8,128)}, u32[]{:S(2)}) copy-start(f32[8,96,128]{2,1,0:T(8,128)} %copy-done.9) | copy-start | bytes 1179652
  31.0 1.3 %copy-start.12 = (f32[8,96,128]{2,1,0:T(8,128)S(1)}, f32[8,96,128]{2,1,0:T(8,128)}, u32[]{:S(2)}) copy-start(f32[8,96,128]{2,1,0:T(8,128)} %copy-done.11) | copy-start | bytes 1179652
  31.0 1.5 %copy-start.14 = (f32[8,96,128]{2,1,0:T(8,128)S(1)}, f32[8,96,128]{2,1,0:T(8,128)}, u32[]{:S(2)}) copy-start(f32[8,96,128]{2,1,0:T(8,128)} %copy-done.13) | copy-start | bytes 1179652
  31.0 1.6 %copy-start.16 = (f32[8,96,128]{2,1,0:T(8,128)S(1)}, f32[8,96,128]{2,1,0:T(8,128)}, u32[]{:S(2)}) copy-start(f32[8,96,128]{2,1,0:T(8,128)} %copy-done.15) | copy-start | bytes 1179652
  31.1 1.7 %copy-start.18 = (f32[8,96,128]{2,1,0:T(8,128)S(1)}, f32[8,96,128]{2,1,0:T(8,128)}, u32[]{:S(2)}) copy-start(f32[8,96,128]{2,1,0:T(8,128)} %copy-done.17) | copy-start | bytes 1179652

commit v4 on v3

--- a/solution.py
+++ b/solution.py
@@ -51,50 +51,53 @@
         self.inner = [(2 * RIM + r, step, None) for r in range(0, stripe, step)]
         self.blocks = [(RIM, RIM, top)] + self.inner + [(2 * RIM + stripe, RIM, bottom)]
 
-    def sweep(self, body, blocks):
-        for t in range(self.tiles):
-            for first, count, factor in blocks:
+    def sweep(self, body, blocks, fields=()):
+        for first, count, factor in blocks:
+            rows = pl.ds(first, count)
+            held = {}
+
+            def load(ref, t, rows=rows, held=held):
+                key = id(ref), t % self.tiles
+                if key not in held:
+                    held[key] = ref[t % self.tiles, rows, :]
+                return held[key]
+
+            for t in range(self.tiles):
 
                 def mask(x, factor=factor, lanes=self.lanes if t == self.rim else None):
                     x = x if factor is None else x * factor
                     return x if lanes is None else x * lanes
 
-                body(t, (t - 1) % self.tiles, (t + 1) % self.tiles, pl.ds(first, count), mask)
-
-
-def beside(ref, t, left, right, rows):
-    above = pl.ds(rows.start - 1, rows.size)
-    below = pl.ds(rows.start + 1, rows.size)
-    here = ref[t, rows, :]
-    lane = lane_ids(here.shape)
-    west = pltpu.roll(here if left == t else jnp.where(lane == LANES - 1, ref[left, rows, :], here), 1, 1)
-    east = pltpu.roll(here if right == t else jnp.where(lane == 0, ref[right, rows, :], here), LANES - 1, 1)
-    return here, (ref[t, above, :] + ref[t, below, :]) + (west + east)
+                body(t, rows, mask, [self.beside(ref, t, rows, load) for ref in fields])
+
+    def beside(self, ref, t, rows, load):
+        above = pl.ds(rows.start - 1, rows.size)
+        below = pl.ds(rows.start + 1, rows.size)
+        here = load(ref, t)
+        west = east = here
+        if self.tiles > 1:
+            lane = lane_ids(here.shape)
+            west = jnp.where(lane == LANES - 1, load(ref, t - 1), here)
+            east = jnp.where(lane == 0, load(ref, t + 1), here)
+        west, east = pltpu.roll(west, 1, 1), pltpu.roll(east, LANES - 1, 1)
+        return here, (ref[t, above, :] + ref[t, below, :]) + (west + east)
 
 
 def first_half(tile, field, half, sign, blocks):
-    fr, fi = field
-    hr, hi = half
-
-    def body(t, left, right, rows, mask):
-        real, beside_real = beside(fr, t, left, right, rows)
-        imag, beside_imag = beside(fi, t, left, right, rows)
-        hr[t, rows, :] = mask(beside_real + (2.0 * sign) * imag)
-        hi[t, rows, :] = mask(beside_imag - (2.0 * sign) * real)
-
-    tile.sweep(body, blocks)
+    def body(t, rows, mask, sums):
+        (real, beside_real), (imag, beside_imag) = sums
+        half[0][t, rows, :] = mask(beside_real + (2.0 * sign) * imag)
+        half[1][t, rows, :] = mask(beside_imag - (2.0 * sign) * real)
+
+    tile.sweep(body, blocks, field)
 
 
 def second_half(tile, field, half, blocks, use):
-    fr, fi = field
-    hr, hi = half
-
-    def body(t, left, right, rows, mask):
-        _, beside_real = beside(hr, t, left, right, rows)
-        _, beside_imag = beside(hi, t, left, right, rows)
-        use(t, rows, mask, 0.1 * beside_real - fr[t, rows, :], 0.1 * beside_imag - fi[t, rows, :])
-
-    tile.sweep(body, blocks)
+    def body(t, rows, mask, sums):
+        (_, beside_real), (_, beside_imag) = sums
+        use(t, rows, mask, 0.1 * beside_real - field[0][t, rows, :], 0.1 * beside_imag - field[1][t, rows, :])
+
+    tile.sweep(body, blocks, half)
 
 
 def blank_rims(refs, tile):
@@ -121,7 +124,7 @@
     row_r, row_i, col_r, col_i = tables
     fr, fi = field
 
-    def start(t, left, right, rows, mask):
+    def start(t, rows, mask, _):
         at = pl.ds(rows.start - RIM, rows.size)
         ar, ai = row_r[at, :], row_i[at, :]
         br, bi = col_r[t : t + 1, :], col_i[t : t + 1, :]
@@ -242,22 +245,30 @@
     return [measured_ref[p, 0, base : base + 16, :].astype(F32)[at : at + 8] for p in range(2)]
 
 
-def open_kernel(phase_ref, measured_ref, note_ref, along_ref, same_ref, held, edge, sems):
+def open_kernel(phase_ref, measured_ref, tilt_ref, partner_ref, along_ref, same_ref, known_ref, held, edge, tilt, sems):
     stripe, width = phase_ref.shape[1:]
     rows = 2 * stripe
     illum, row, _ = place()
-    first = pl.multiple_of(illum * (stripe - 8), 8)
     field_copy = pltpu.make_async_copy(measured_ref, held, sems.at[0])
-    edge_copy = pltpu.make_async_copy(phase_ref.at[:, pl.ds(first, 8), :], edge, sems.at[1])
-    edge_copy.start()
+    tilt_copy = pltpu.make_async_copy(tilt_ref, tilt, sems.at[3])
+    edge_copies = [
+        pltpu.make_async_copy(phase_ref.at[:, pl.ds(first, 8), :], edge.at[e], sems.at[1 + e])
+        for e, first in enumerate((0, stripe - 8))
+    ]
+    for copy in edge_copies:
+        copy.start()
     field_copy.start()
-    edge_copy.wait()
+    tilt_copy.start()
+    for copy in edge_copies:
+        copy.wait()
     for k in range(2):
-        along_ref[:, k * width : (k + 1) * width] = edge[k]
+        top, bottom = edge[0, k], edge[1, k]
+        along_ref[:, k * width : (k + 1) * width] = jnp.where(illum == 0, top, bottom)
+        partner_ref[:, k * width : (k + 1) * width] = jnp.where(illum == 0, bottom, top)
     field_copy.wait()
     top, bottom = pack_rows(*edge_blocks(held, 0), True), pack_rows(*edge_blocks(held, rows - 8), False)
-    along_ref[:, 2 * width :] = jnp.where(illum == 0, top, bottom)
-    same_ref[...] = jnp.where(illum == 0, bottom, top)
+    along_ref[:, 2 * width : 3 * width] = jnp.where(illum == 0, top, bottom)
+    same_ref[:, :width] = jnp.where(illum == 0, bottom, top)
     total = jnp.zeros((8, width), F32)
     for p in range(2):
         for r in range(0, rows, 16):
@@ -265,24 +276,18 @@
             x = x * x
             total = total + (x[:8] + x[8:])
     energy = jnp.sum(jnp.sum(total, axis=1, keepdims=True), axis=0, keepdims=True)
-    note_ref[...] = jnp.where(lane_ids((8, LANES)) == illum * 4 + row, energy, 0.0)
-
-
-def partner_kernel(phase_ref, angles_ref, note_ref, core_note_ref, partner_ref, known_ref):
-    stripe, width = phase_ref.shape[1:]
-    illum, _, _ = place()
-    first = pl.multiple_of((1 - illum) * (stripe - 8), 8)
-    for k in range(2):
-        partner_ref[:, k * width : (k + 1) * width] = phase_ref[k, pl.ds(first, 8), :]
     lane = lane_ids((8, LANES))
-    known = jnp.maximum(note_ref[...], core_note_ref[...])
+    note = jnp.where(lane == illum * 4 + row, energy, 0.0)
+    along_ref[:, 3 * width :] = note
+    same_ref[:, width:] = note
+    tilt_copy.wait()
     for n in range(2):
-        known = jnp.where(lane == 16 + n, angles_ref[:, n : n + 1].astype(F32), known)
-    partner_ref[:, 2 * width :] = known
-    known_ref[...] = known
-
-
-def swap_kernel(measured_ref, known_ref, swap_ref):
+        note = jnp.where(lane == 16 + n, tilt[:, n : n + 1].astype(F32), note)
+    partner_ref[:, 2 * width :] = note
+    known_ref[...] = note
+
+
+def swap_kernel(measured_ref, partner_ref, swap_ref):
     stripe = measured_ref.shape[2] // 2
     illum, _, _ = place()
     other = pl.multiple_of((1 - illum) * stripe, 16)
@@ -295,12 +300,6 @@
     swap_ref[2 * stripe :, :] = jnp.where(illum == 0, above, below)
 
 
-def same_kernel(packed_ref, known_ref, partner_ref, same_ref):
-    width = packed_ref.shape[1]
-    same_ref[:, :width] = packed_ref[...]
-    same_ref[:, width:] = jnp.maximum(known_ref[...], partner_ref[:, 2 * width :])
-
-
 def rim_pack_kernel(phase_ref, measured_ref, known_ref, partner_ref, along_ref, same_ref, out_ref):
     stripe, width = phase_ref.shape[1:]
     rows = 2 * stripe
@@ -308,7 +307,8 @@
     low_illum = illum == 0
     cols = out_ref.shape[0]
     lane = lane_ids((8, LANES))
-    known = jnp.maximum(jnp.maximum(known_ref[...], partner_ref[:, 2 * width :]), same_ref[:, width:])
+    known = jnp.maximum(known_ref[...], partner_ref[:, 2 * width :])
+    known = jnp.maximum(jnp.maximum(known, same_ref[:, width:]), along_ref[:, 3 * width :])
     for c in range(cols):
         out_ref[c, out_ref.shape[1] - 8 :, :] = known
 
@@ -350,7 +350,7 @@
                 out_ref[to, 2 * g : 2 * g + 8, :] = acc
 
 
-def rim_unpack_kernel(got_ref, phase_rim_ref, rim_ref, relay_ref):
+def rim_unpack_kernel(got_ref, phase_rim_ref, rim_ref, relay_ref, sums_ref):
     cols, depth = got_ref.shape[:2]
     stripe = phase_rim_ref.shape[1] - 2 * RIM
     rows = 2 * stripe
@@ -378,7 +378,12 @@
     total = got_ref[0, depth - 8 :, :]
     for c in range(1, cols):
         total = total + got_ref[c, depth - 8 :, :]
-    relay_ref[stripe + 8 :, :] = total
+    sums_ref[...] = total
+
+
+def relay_kernel(relay_ref, sums_ref, core_sums_ref, out_ref):
+    out_ref[: relay_ref.shape[0], :] = relay_ref[...]
+    out_ref[relay_ref.shape[0] :, :] = jnp.maximum(sums_ref[...], core_sums_ref[...])
 
 
 def fill_target(tile, target, low_illum, middle, near, far):
@@ -434,7 +439,7 @@
 
 
 def residual_of(tile, field, exit_field, target):
-    def body(t, left, right, rows, mask):
+    def body(t, rows, mask, _):
         for g, u, m in zip(field, exit_field, target):
             g[t, rows, :] = mask(u[t, rows, :] - m[t, rows, :])
 
@@ -518,7 +523,7 @@
     return [jnp.where(low_illum, low[part], high[part]) for part in range(2)]
 
 
-def other_kernel(sizes, swap_ref, along_ref, w0r, w0i, w1r, w1i, ur_ref, ui_ref, c1, s1, out_ref, gr, gi, hr, hi, mr, mi):
+def other_kernel(sizes, swap_ref, along_ref, sums_ref, w0r, w0i, w1r, w1i, ur_ref, ui_ref, c1, s1, out_ref, gr, gi, hr, hi, mr, mi):
     stripe, tiles, _, _ = sizes
     tile, _, _ = main_tile(sizes)
     illum, _, _ = place()
@@ -636,15 +641,15 @@
         out_ref[k, :, last] = jnp.where(on >= LANES - RIM, pltpu.roll(patch, 56, 1), out_ref[k, :, last])
 
 
-def call(kernel, outs, *args, scratch=(), in_place=0, flops=0):
+def call(kernel, outs, *args, scratch=(), in_place=0, flops=0, mib=8):
     return pl.pallas_call(
         kernel,
         out_shape=[jax.ShapeDtypeStruct(shape, F32) for shape in outs],
-        in_specs=[pl.BlockSpec(memory_space=pl.ANY)] * in_place
+        in_specs=[pl.BlockSpec(memory_space=pltpu.HBM)] * in_place
         + [pl.BlockSpec(memory_space=pltpu.VMEM)] * (len(args) - in_place),
         out_specs=[pl.BlockSpec(memory_space=pltpu.VMEM)] * len(outs),
         scratch_shapes=[pltpu.VMEM(s, F32) if isinstance(s, tuple) else s for s in scratch],
-        compiler_params=pltpu.CompilerParams(vmem_limit_bytes=24 * 2**20),
+        compiler_params=pltpu.CompilerParams(vmem_limit_bytes=int(mib * 2**20)),
         cost_estimate=pl.CostEstimate(flops=flops, bytes_accessed=2**18, transcendentals=0),
     )(*args)
 
@@ -656,22 +661,23 @@
     sizes = (stripe, tiles, 2 * stripe * rows, width * cols)
     swap = [(0, 1), (1, 0)]
     along = []
-    for r in range(rows - 1):
-        along += [(rows + r, r + 1), (r + 1, rows + r)]
+    for r in range(rows):
+        along += [(rows + r, (r + 1) % rows), ((r + 1) % rows, rows + r)]
     same = [(r, (r + 1) % rows) for r in range(rows)] + [(rows + (r + 1) % rows, rows + r) for r in range(rows)]
 
-    note, along_out, same_packed = call(
-        open_kernel, [(8, LANES), (8, 3 * width), (8, width)], phase_delay, measured,
-        scratch=[pltpu.VMEM(measured.shape, measured.dtype), (slices, 8, width), pltpu.SemaphoreType.DMA((2,))], in_place=2,
-    )
-    core_note = lax.ppermute(note, "row", [(r, r ^ 1) for r in range(rows)])
+    partner_out, along_out, same_out, known = call(
+        open_kernel, [(8, 2 * width + LANES), (8, 3 * width + LANES), (8, width + LANES), (8, LANES)],
+        phase_delay, measured, angles, in_place=3, mib=62,
+        scratch=[
+            pltpu.VMEM(measured.shape, measured.dtype), (2, slices, 8, width),
+            pltpu.VMEM(angles.shape, angles.dtype), pltpu.SemaphoreType.DMA((4,)),
+        ],
+    )
     along_in = lax.ppermute(along_out, ("illum", "row"), along)
-    partner_out, known = call(partner_kernel, [(8, 2 * width + LANES), (8, LANES)], phase_delay, angles, note, core_note)
     partner_in = lax.ppermute(partner_out, "illum", swap)
-    (swap_out,) = call(swap_kernel, [(2 * stripe + 8, width)], measured, known)
+    same_in = lax.ppermute(same_out, ("illum", "row"), same)
+    (swap_out,) = call(swap_kernel, [(2 * stripe + 8, width)], measured, partner_in)
     swap_in = lax.ppermute(swap_out, "illum", swap)
-    (same_out,) = call(same_kernel, [(8, width + LANES)], same_packed, known, partner_in)
-    same_in = lax.ppermute(same_out, ("illum", "row"), same)
     depth = 8 * (-(-(stripe // 4 + 1) // 4)) + 8
     (rims_out,) = call(rim_pack_kernel, [(cols, depth, LANES)], phase_delay, measured, known, partner_in, along_in, same_in)
     rims_in = lax.all_to_all(rims_out, "col", 0, 0, tiled=True)
@@ -685,15 +691,17 @@
     rows_in = phase_delay, measured, known, partner_in, along_in, same_in
     own, *kept = call(
         functools.partial(forward_kernel, sizes), [phase_delay.shape] + fields(tiles) * 8, *rows_in,
-        scratch=fields(tiles) * 12 + tables(tiles), flops=6 * 10**9,
-    )
+        scratch=fields(tiles) * 12 + tables(tiles), flops=6 * 10**9, mib=16,
+    )
+    phase_rim, rim, relay, sums = call(
+        rim_unpack_kernel, [(2, stripe + 2 * RIM, LANES), (2, 2 * stripe + 8, LANES), (stripe + 8, LANES), (8, LANES)], rims_in
+    )
+    core_sums = lax.ppermute(sums, "row", [(r, r ^ 1) for r in range(rows)])
     (other,) = call(
-        functools.partial(other_kernel, sizes), [phase_delay.shape], swap_in, along_in, *kept,
-        scratch=fields(tiles) * 6, flops=2 * 10**9,
-    )
-    phase_rim, rim, relay = call(
-        rim_unpack_kernel, [(2, stripe + 2 * RIM, LANES), (2, 2 * stripe + 8, LANES), (stripe + 16, LANES)], rims_in
-    )
+        functools.partial(other_kernel, sizes), [phase_delay.shape], swap_in, along_in, sums, *kept,
+        scratch=fields(tiles) * 6, flops=2 * 10**9, mib=12,
+    )
+    (relay,) = call(relay_kernel, [(stripe + 16, LANES)], relay, sums, core_sums)
     partner_relay = lax.ppermute(relay, "illum", swap)
     own_patch, *patch_kept = call(
         functools.partial(patch_kernel, sizes), [(slices, stripe, LANES)] + fields(1) * 8, *rows_in, phase_rim, rim,

time: 36 us -> 36.1 us (level)
  the two profiles are of different devices: /device:TPU:1 before, /device:TPU:0 now
where the time goes in v4:
time: 36.1 us; the launch traced here: 35.8 us
  Pallas kernels  12.1 us (34%)
  starting transfers between devices  11.4 us (32%)
  local copies, waits for them, and re-layouts  6.12 us (17%)
  waiting for transfers between devices  6.01 us (17%)
    pallas_call x9, Pallas kernels, call(): pl.pallas_call(kernel, out_shape=[jax.ShapeDtypeStruct(shape, F32) for sh...  12.1 us
    unnamed x38, local copies, waits for them, and re-layouts  6.12 us
    all_to_all x1, starting transfers between devices, paired(): rims_in = lax.all_to_all(rims_out, 'col', 0, 0, tiled=True)  4.87 us
    ppermute x1, waiting for transfers between devices, paired(): partner_in = lax.ppermute(partner_out, 'illum', swap)  4.11 us
    ppermute x1, starting transfers between devices, paired(): along_in = lax.ppermute(along_out, ('illum', 'row'), along)  3.4 us
    ppermute x1, waiting for transfers between devices, paired(): partner_relay = lax.ppermute(relay, 'illum', swap)  1.89 us
    ppermute x1, starting transfers between devices, paired(): swap_in = lax.ppermute(swap_out, 'illum', swap)  1.51 us
    ppermute x1, starting transfers between devices, paired(): same_in = lax.ppermute(same_out, ('illum', 'row'), same)  0.93 us
  transfers between devices with their start and end apart: 7, of which 2 were waited for; matrix products, arithmetic and copies ran while one was open for 0% of the time, Pallas kernels for 24%

profile of v4, /device:TPU:0, one launch (start us, length us, event | category | flops | bytes accessed | tf_op | source)
XLA Modules:
  0.0 35.8 jit_solution(14313442215108186630)
XLA Ops:
  0.0 2.1 %shard_map.37 = (f32[8,2176]{1,0:T(8,128)}, f32[8,3200]{1,0:T(8,128)}, f32[8,1152]{1,0:T(8,128)}, f32[8,128]{1,0:T(8,128)}) custom-call(f32[2,64,1024]{2,1,0:T(8,128)} %phase_ref.7, bf16[2,1,128,1024]{3,2,1,0:T(8,128)(2,1)} %measured_ref.9, s32[1,2]{1,0:T(1,128)} %tilt_ref.1), custom_call_target="tpu_custom_call" | custom-call | bytes 262144 | tf_op jit(solution)/shard_map/pallas_call | solution.py:645
  2.1 3.4 %collective-permute-start.1 = (f32[8,3200]{1,0:T(8,128)}, f32[8,3200]{1,0:T(8,128)S(1)}, u32[]{:S(2)}, u32[]{:S(2)}) collective-permute-start(f32[8,3200]{1,0:T(8,128)} %get-tuple-element.33), channel_id=1, source_target_pairs={{16,4},{4,16},{20,8},{8,20},{24,12},{12,24},{28,0},{0,28},{17,5},{... | collective-permute-start | bytes 307208 | tf_op jit(solution)/shard_map/ppermute | solution.py:676
  5.5 0.0 collective-permute-start
  5.5 0.9 %collective-permute-start.2 = (f32[8,1152]{1,0:T(8,128)}, f32[8,1152]{1,0:T(8,128)S(1)}, u32[]{:S(2)}, u32[]{:S(2)}) collective-permute-start(f32[8,1152]{1,0:T(8,128)} %get-tuple-element.34), channel_id=1, source_target_pairs={{0,4},{4,8},{8,12},{12,0},{20,16},{24,20},{28,24},{16,28},{1,5},{5... | collective-permute-start | bytes 110600 | tf_op jit(solution)/shard_map/ppermute | solution.py:678
  6.4 4.1 %collective-permute-done.partner_ref = f32[8,2176]{1,0:T(8,128)S(1)} collective-permute-done((f32[8,2176]{1,0:T(8,128)}, f32[8,2176]{1,0:T(8,128)S(1)}, u32[]{:S(2)}, u32[]{:S(2)}) %collective-permute-start) | collective-permute-done | bytes 69664 | tf_op jit(solution)/shard_map/ppermute | solution.py:677
  10.6 0.0 copy-done
  10.6 1.5 %collective-permute-start.3 = (f32[136,1024]{1,0:T(8,128)S(1)}, f32[136,1024]{1,0:T(8,128)S(1)}, u32[]{:S(2)}, u32[]{:S(2)}) collective-permute-start(f32[136,1024]{1,0:T(8,128)S(1)} %shard_map.39), channel_id=1, source_target_pairs={{0,16},{16,0},{1,17},{17,1},{2,18},{18,2},{3,19},{19,3},{4,20},{20... | collective-permute-start | bytes 1671176 | tf_op jit(solution)/shard_map/ppermute | solution.py:680
  12.1 0.0 collective-permute-done.2.same_ref
  12.1 0.0 collective-permute-done.1.along_ref
  12.1 0.0 copy-done.1
  12.1 0.0 copy-done.2
  12.1 0.8 %shard_map.40 = f32[4,48,128]{2,1,0:T(8,128)} custom-call(f32[2,64,1024]{2,1,0:T(8,128)S(1)} %copy-done.1, bf16[2,1,128,1024]{3,2,1,0:T(8,128)(2,1)S(1)} %copy-done, f32[8,128]{1,0:T(8,128)S(1)} %copy-done.2, f32[8,2176]{1,0:T(8,128)S(1)} %collective-permute-done.partner_ref, f32[8,3200]{1,0:T(8,128)S(1)} %collective-permute-done.1.along_ref, ...), custom_call_target="tpu_custom_call" | custom-call | bytes 262144 | tf_op jit(solution)/shard_map/pallas_call | solution.py:645
  12.9 4.9 %all-to-all-start = ((f32[4,48,128]{2,1,0:T(8,128)}), f32[4,48,128]{2,1,0:T(8,128)S(1)}, u32[]{:S(2)}, u32[]{:S(2)}) async-start(f32[4,48,128]{2,1,0:T(8,128)} %shard_map.40), calls=%async_computation | async-start | bytes 196608 | tf_op jit(solution)/shard_map/all_to_all | solution.py:683
  17.8 4.9 %shard_map.38 = (f32[2,64,1024]{2,1,0:T(8,128)S(1)}, f32[8,96,128]{2,1,0:T(8,128)S(1)}, f32[8,96,128]{2,1,0:T(8,128)S(1)}, f32[8,96,128]{2,1,0:T(8,128)S(1)}, f3...) custom-call(f32[2,64,1024]{2,1,0:T(8,128)S(1)} %copy-done.1, ...), custom_call_target="tpu_custom_call" | custom-call | flops 6000000000 | bytes 262144 | tf_op jit(solution)/shard_map/pallas_call | solution.py:645
  22.7 0.0 copy-start.3
  22.7 0.7 %copy-done.3 = f32[8,96,128]{2,1,0:T(8,128)} copy-done((f32[8,96,128]{2,1,0:T(8,128)}, f32[8,96,128]{2,1,0:T(8,128)S(1)}, u32[]{:S(2)}) %copy-start.3) | copy-done | bytes 393240
  23.4 0.8 %copy-done.5 = f32[8,96,128]{2,1,0:T(8,128)} copy-done((f32[8,96,128]{2,1,0:T(8,128)}, f32[8,96,128]{2,1,0:T(8,128)S(1)}, u32[]{:S(2)}) %copy-start.5) | copy-done | bytes 393240
  24.2 0.8 %copy-done.7 = f32[8,96,128]{2,1,0:T(8,128)} copy-done((f32[8,96,128]{2,1,0:T(8,128)}, f32[8,96,128]{2,1,0:T(8,128)S(1)}, u32[]{:S(2)}) %copy-start.7) | copy-done | bytes 393240
  24.9 0.8 %copy-done.9 = f32[8,96,128]{2,1,0:T(8,128)} copy-done((f32[8,96,128]{2,1,0:T(8,128)}, f32[8,96,128]{2,1,0:T(8,128)S(1)}, u32[]{:S(2)}) %copy-start.9) | copy-done | bytes 393240
  25.7 0.8 %copy-done.11 = f32[8,96,128]{2,1,0:T(8,128)} copy-done((f32[8,96,128]{2,1,0:T(8,128)}, f32[8,96,128]{2,1,0:T(8,128)S(1)}, u32[]{:S(2)}) %copy-start.11) | copy-done | bytes 393240
  26.4 0.8 %copy-done.13 = f32[8,96,128]{2,1,0:T(8,128)} copy-done((f32[8,96,128]{2,1,0:T(8,128)}, f32[8,96,128]{2,1,0:T(8,128)S(1)}, u32[]{:S(2)}) %copy-start.13) | copy-done | bytes 393240
  27.2 0.7 %copy-done.15 = f32[8,96,128]{2,1,0:T(8,128)} copy-done((f32[8,96,128]{2,1,0:T(8,128)}, f32[8,96,128]{2,1,0:T(8,128)S(1)}, u32[]{:S(2)}) %copy-start.15) | copy-done | bytes 393240
  28.0 0.8 %copy-done.17 = f32[8,96,128]{2,1,0:T(8,128)} copy-done((f32[8,96,128]{2,1,0:T(8,128)}, f32[8,96,128]{2,1,0:T(8,128)S(1)}, u32[]{:S(2)}) %copy-start.17) | copy-done | bytes 393240
  28.7 0.0 all-to-all-done.got_ref
  28.7 0.2 shard_map.41
  29.0 0.1 collective-permute-start.4
  29.1 0.0 copy-start.4
  29.1 0.0 copy-start.6
  29.1 0.0 copy-start.8
  29.1 0.0 copy-start.10
  29.1 0.0 copy-start.12
  29.1 0.0 copy-start.14
  29.1 0.0 copy-start.16
  29.1 0.0 copy-start.18
  29.1 1.2 %shard_map.43 = (f32[2,64,128]{2,1,0:T(8,128)S(1)}, f32[1,96,128]{2,1,0:T(8,128)S(1)}, f32[1,96,128]{2,1,0:T(8,128)S(1)}, f32[1,96,128]{2,1,0:T(8,128)S(1)}, f32...) custom-call(f32[2,64,1024]{2,1,0:T(8,128)S(1)} %copy-done.1, ...), custom_call_target="tpu_custom_call" | custom-call | flops 1000000000 | bytes 262144 | tf_op jit(solution)/shard_map/pallas_call | solution.py:645
  30.4 0.0 collective-permute-done.4.core_sums_ref
  30.4 0.6 %collective-permute-start.5 = (f32[80,128]{1,0:T(8,128)S(1)}, f32[80,128]{1,0:T(8,128)S(1)}, u32[]{:S(2)}, u32[]{:S(2)}) collective-permute-start(f32[80,128]{1,0:T(8,128)S(1)} %shard_map.44.relay_ref), channel_id=1, source_target_pairs={{0,16},{16,0},{1,17},{17,1},{2,18},{18,2},{3,19},{19,3},{4,20},{20... | collective-permute-start | bytes 122888 | tf_op jit(solution)/shard_map/ppermute | solution.py:705
  31.1 0.0 collective-permute-done.3.swap_ref
  31.1 0.0 copy-done.6
  31.1 0.0 copy-done.8
  31.1 0.0 copy-done.10
  31.1 0.0 copy-done.12
  31.1 0.0 copy-done.14
  31.1 0.0 copy-done.16
  31.1 0.0 copy-done.18
  31.1 1.5 %shard_map.42.other_ref = f32[2,64,1024]{2,1,0:T(8,128)S(1)} custom-call(f32[136,1024]{1,0:T(8,128)S(1)} %collective-permute-done.3.swap_ref, f32[8,3200]{1,0:T(8,128)S(1)} %collective-permute-done.1.along_ref, f32[8,128]{1,0:T(8,128)S(1)} %get-tuple-element.36.sums_ref, f32[8,96,128]{2,1,0:T(8,128)S(1)} %copy-done.4, f32[8,96,128]{2,1,0:T(8,128)S(1)} %copy-done.6, ...), custom_call_target="tpu_custom_call" | custom-call | flops 2000000000 | bytes 262144 | tf_op jit(solution)/shard_map/pallas_call | solution.py:645
  32.6 1.9 %collective-permute-done.5.partner_relay_ref = f32[80,128]{1,0:T(8,128)S(1)} collective-permute-done((f32[80,128]{1,0:T(8,128)S(1)}, f32[80,128]{1,0:T(8,128)S(1)}, u32[]{:S(2)}, u32[]{:S(2)}) %collective-permute-start.5) | collective-permute-done | bytes 40992 | tf_op jit(solution)/shard_map/ppermute | solution.py:705
  34.5 1.4 %shard_map.45 = f32[2,64,1024]{2,1,0:T(8,128)} custom-call(f32[2,64,1024]{2,1,0:T(8,128)S(1)} %get-tuple-element.35.own_ref, f32[2,64,1024]{2,1,0:T(8,128)S(1)} %shard_map.42.other_ref, f32[2,64,128]{2,1,0:T(8,128)S(1)} %get-tuple-element.47.own_patch_ref, f32[136,1024]{1,0:T(8,128)S(1)} %collective-permute-done.3.swap_ref, ...), custom_call_target="tpu_custom_call" | custom-call | bytes 262144 | tf_op jit(solution)/shard_map/pallas_call | solution.py:645
  (13 shorter events, 0.1 us)
Async XLA Ops:
  0.0 10.6 %copy-start = (bf16[2,1,128,1024]{3,2,1,0:T(8,128)(2,1)S(1)}, bf16[2,1,128,1024]{3,2,1,0:T(8,128)(2,1)}, u32[]{:S(2)}) copy-start(bf16[2,1,128,1024]{3,2,1,0:T(8,128)(2,1)} %measured_ref.9) | copy-start | bytes 1572868
  2.1 10.0 %collective-permute-start.1 = (f32[8,3200]{1,0:T(8,128)}, f32[8,3200]{1,0:T(8,128)S(1)}, u32[]{:S(2)}, u32[]{:S(2)}) collective-permute-start(f32[8,3200]{1,0:T(8,128)} %get-tuple-element.33), channel_id=1, source_target_pairs={{16,4},{4,16},{20,8},{8,20},{24,12},{12,24},{28,0},{0,28},{17,5},{... | collective-permute-start | bytes 307208 | tf_op jit(solution)/shard_map/ppermute | solution.py:676
  5.5 5.0 %collective-permute-start = (f32[8,2176]{1,0:T(8,128)}, f32[8,2176]{1,0:T(8,128)S(1)}, u32[]{:S(2)}, u32[]{:S(2)}) collective-permute-start(f32[8,2176]{1,0:T(8,128)} %get-tuple-element.32), channel_id=1, source_target_pairs={{0,16},{16,0},{1,17},{17,1},{2,18},{18,2},{3,19},{19,3},{4,20},{20... | collective-permute-start | bytes 208904 | tf_op jit(solution)/shard_map/ppermute | solution.py:677
  5.5 6.6 %copy-start.1 = (f32[2,64,1024]{2,1,0:T(8,128)S(1)}, f32[2,64,1024]{2,1,0:T(8,128)}, u32[]{:S(2)}) copy-start(f32[2,64,1024]{2,1,0:T(8,128)} %phase_ref.7) | copy-start | bytes 1572868
  5.5 6.6 %collective-permute-start.2 = (f32[8,1152]{1,0:T(8,128)}, f32[8,1152]{1,0:T(8,128)S(1)}, u32[]{:S(2)}, u32[]{:S(2)}) collective-permute-start(f32[8,1152]{1,0:T(8,128)} %get-tuple-element.34), channel_id=1, source_target_pairs={{0,4},{4,8},{8,12},{12,0},{20,16},{24,20},{28,24},{16,28},{1,5},{5... | collective-permute-start | bytes 110600 | tf_op jit(solution)/shard_map/ppermute | solution.py:678
  10.6 1.6 %copy-start.2 = (f32[8,128]{1,0:T(8,128)S(1)}, f32[8,128]{1,0:T(8,128)}, u32[]{:S(2)}) copy-start(f32[8,128]{1,0:T(8,128)} %get-tuple-element.31.known_ref) | copy-start | bytes 12292
  10.6 20.4 %collective-permute-start.3 = (f32[136,1024]{1,0:T(8,128)S(1)}, f32[136,1024]{1,0:T(8,128)S(1)}, u32[]{:S(2)}, u32[]{:S(2)}) collective-permute-start(f32[136,1024]{1,0:T(8,128)S(1)} %shard_map.39), channel_id=1, source_target_pairs={{0,16},{16,0},{1,17},{17,1},{2,18},{18,2},{3,19},{19,3},{4,20},{20... | collective-permute-start | bytes 1671176 | tf_op jit(solution)/shard_map/ppermute | solution.py:680
  12.9 15.8 %all-to-all-start = ((f32[4,48,128]{2,1,0:T(8,128)}), f32[4,48,128]{2,1,0:T(8,128)S(1)}, u32[]{:S(2)}, u32[]{:S(2)}) async-start(f32[4,48,128]{2,1,0:T(8,128)} %shard_map.40), calls=%async_computation | async-start | bytes 196608 | tf_op jit(solution)/shard_map/all_to_all | solution.py:683
  22.7 0.7 %copy-start.3 = (f32[8,96,128]{2,1,0:T(8,128)}, f32[8,96,128]{2,1,0:T(8,128)S(1)}, u32[]{:S(2)}) copy-start(f32[8,96,128]{2,1,0:T(8,128)S(1)} %get-tuple-element.37.w0r) | copy-start | bytes 1179652
  23.4 0.8 %copy-start.5 = (f32[8,96,128]{2,1,0:T(8,128)}, f32[8,96,128]{2,1,0:T(8,128)S(1)}, u32[]{:S(2)}) copy-start(f32[8,96,128]{2,1,0:T(8,128)S(1)} %get-tuple-element.38.w0i) | copy-start | bytes 1179652
  24.2 0.8 %copy-start.7 = (f32[8,96,128]{2,1,0:T(8,128)}, f32[8,96,128]{2,1,0:T(8,128)S(1)}, u32[]{:S(2)}) copy-start(f32[8,96,128]{2,1,0:T(8,128)S(1)} %get-tuple-element.39.w1r) | copy-start | bytes 1179652
  24.9 0.8 %copy-start.9 = (f32[8,96,128]{2,1,0:T(8,128)}, f32[8,96,128]{2,1,0:T(8,128)S(1)}, u32[]{:S(2)}) copy-start(f32[8,96,128]{2,1,0:T(8,128)S(1)} %get-tuple-element.40.w1i) | copy-start | bytes 1179652
  25.7 0.8 %copy-start.11 = (f32[8,96,128]{2,1,0:T(8,128)}, f32[8,96,128]{2,1,0:T(8,128)S(1)}, u32[]{:S(2)}) copy-start(f32[8,96,128]{2,1,0:T(8,128)S(1)} %get-tuple-element.41.ur_ref) | copy-start | bytes 1179652
  26.4 0.8 %copy-start.13 = (f32[8,96,128]{2,1,0:T(8,128)}, f32[8,96,128]{2,1,0:T(8,128)S(1)}, u32[]{:S(2)}) copy-start(f32[8,96,128]{2,1,0:T(8,128)S(1)} %get-tuple-element.42.ui_ref) | copy-start | bytes 1179652
  27.2 0.7 %copy-start.15 = (f32[8,96,128]{2,1,0:T(8,128)}, f32[8,96,128]{2,1,0:T(8,128)S(1)}, u32[]{:S(2)}) copy-start(f32[8,96,128]{2,1,0:T(8,128)S(1)} %get-tuple-element.43.c1) | copy-start | bytes 1179652
  28.0 0.8 %copy-start.17 = (f32[8,96,128]{2,1,0:T(8,128)}, f32[8,96,128]{2,1,0:T(8,128)S(1)}, u32[]{:S(2)}) copy-start(f32[8,96,128]{2,1,0:T(8,128)S(1)} %get-tuple-element.44.s1) | copy-start | bytes 1179652
  29.0 1.4 %collective-permute-start.4 = (f32[8,128]{1,0:T(8,128)S(1)}, f32[8,128]{1,0:T(8,128)S(1)}, u32[]{:S(2)}, u32[]{:S(2)}) collective-permute-start(f32[8,128]{1,0:T(8,128)S(1)} %get-tuple-element.36.sums_ref), channel_id=1, source_target_pairs={{0,4},{4,0},{8,12},{12,8},{1,5},{5,1},{9,13},{13,9},{2,6},{6,2},{1... | collective-permute-start | bytes 12296 | tf_op jit(solution)/shard_map/ppermute | solution.py:699
  29.1 2.0 %copy-start.4 = (f32[8,96,128]{2,1,0:T(8,128)S(1)}, f32[8,96,128]{2,1,0:T(8,128)}, u32[]{:S(2)}) copy-start(f32[8,96,128]{2,1,0:T(8,128)} %copy-done.3) | copy-start | bytes 1179652
  29.1 2.0 %copy-start.6 = (f32[8,96,128]{2,1,0:T(8,128)S(1)}, f32[8,96,128]{2,1,0:T(8,128)}, u32[]{:S(2)}) copy-start(f32[8,96,128]{2,1,0:T(8,128)} %copy-done.5) | copy-start | bytes 1179652
  29.1 2.0 %copy-start.8 = (f32[8,96,128]{2,1,0:T(8,128)S(1)}, f32[8,96,128]{2,1,0:T(8,128)}, u32[]{:S(2)}) copy-start(f32[8,96,128]{2,1,0:T(8,128)} %copy-done.7) | copy-start | bytes 1179652
  29.1 2.0 %copy-start.10 = (f32[8,96,128]{2,1,0:T(8,128)S(1)}, f32[8,96,128]{2,1,0:T(8,128)}, u32[]{:S(2)}) copy-start(f32[8,96,128]{2,1,0:T(8,128)} %copy-done.9) | copy-start | bytes 1179652
  29.1 2.0 %copy-start.12 = (f32[8,96,128]{2,1,0:T(8,128)S(1)}, f32[8,96,128]{2,1,0:T(8,128)}, u32[]{:S(2)}) copy-start(f32[8,96,128]{2,1,0:T(8,128)} %copy-done.11) | copy-start | bytes 1179652
  29.1 2.0 %copy-start.14 = (f32[8,96,128]{2,1,0:T(8,128)S(1)}, f32[8,96,128]{2,1,0:T(8,128)}, u32[]{:S(2)}) copy-start(f32[8,96,128]{2,1,0:T(8,128)} %copy-done.13) | copy-start | bytes 1179652
  29.1 2.0 %copy-start.16 = (f32[8,96,128]{2,1,0:T(8,128)S(1)}, f32[8,96,128]{2,1,0:T(8,128)}, u32[]{:S(2)}) copy-start(f32[8,96,128]{2,1,0:T(8,128)} %copy-done.15) | copy-start | bytes 1179652
  29.1 2.0 %copy-start.18 = (f32[8,96,128]{2,1,0:T(8,128)S(1)}, f32[8,96,128]{2,1,0:T(8,128)}, u32[]{:S(2)}) copy-start(f32[8,96,128]{2,1,0:T(8,128)} %copy-done.17) | copy-start | bytes 1179652
  30.4 4.1 %collective-permute-start.5 = (f32[80,128]{1,0:T(8,128)S(1)}, f32[80,128]{1,0:T(8,128)S(1)}, u32[]{:S(2)}, u32[]{:S(2)}) collective-permute-start(f32[80,128]{1,0:T(8,128)S(1)} %shard_map.44.relay_ref), channel_id=1, source_target_pairs={{0,16},{16,0},{1,17},{17,1},{2,18},{18,2},{3,19},{19,3},{4,20},{20... | collective-permute-start | bytes 122888 | tf_op jit(solution)/shard_map/ppermute | solution.py:705

commit v5 on v4

--- a/solution.py
+++ b/solution.py
@@ -287,7 +287,7 @@
     known_ref[...] = note
 
 
-def swap_kernel(measured_ref, partner_ref, swap_ref):
+def swap_kernel(measured_ref, same_ref, swap_ref):
     stripe = measured_ref.shape[2] // 2
     illum, _, _ = place()
     other = pl.multiple_of((1 - illum) * stripe, 16)
@@ -300,67 +300,73 @@
     swap_ref[2 * stripe :, :] = jnp.where(illum == 0, above, below)
 
 
-def rim_pack_kernel(phase_ref, measured_ref, known_ref, partner_ref, along_ref, same_ref, out_ref):
+def rim_pack_kernel(phase_ref, measured_ref, known_ref, partner_ref, along_ref, same_ref, first_ref, second_ref, note_ref):
     stripe, width = phase_ref.shape[1:]
     rows = 2 * stripe
     illum, _, col = place()
     low_illum = illum == 0
-    cols = out_ref.shape[0]
+    even = lax.rem(col, 2) == 0
     lane = lane_ids((8, LANES))
     known = jnp.maximum(known_ref[...], partner_ref[:, 2 * width :])
     known = jnp.maximum(jnp.maximum(known, same_ref[:, width:]), along_ref[:, 3 * width :])
-    for c in range(cols):
-        out_ref[c, out_ref.shape[1] - 8 :, :] = known
-
-    for east in (True, False):
+    note_ref[...] = known
+    first_ref[first_ref.shape[0] - 8 :, :] = known
+
+    def packed(east):
         edge = slice(width - LANES, width) if east else slice(0, LANES)
         base = LANES - RIM if east else 0
-
-        @pl.when(col < cols - 1 if east else col > 0)
-        def _():
-            to = col + 1 if east else col - 1
-            groups = []
-            for j in range(stripe // 8 + 2):
-                items = []
-                for k in range(2):
-                    tile = slice(k * width + edge.start, k * width + edge.stop)
-                    if j == 0:
-                        items.append(jnp.where(low_illum, along_ref[:, tile], partner_ref[:, tile]))
-                    elif j == stripe // 8 + 1:
-                        items.append(jnp.where(low_illum, partner_ref[:, tile], along_ref[:, tile]))
-                    else:
-                        items.append(phase_ref[k, 8 * (j - 1) : 8 * j, edge])
-                groups.append(items)
-            while len(groups) < rows // 8 + 1:
-                groups.append([None, None])
-            for r in range(0, rows, 16):
-                both = [measured_ref[p, 0, r : r + 16, edge].astype(F32) for p in range(2)]
-                for h in range(2):
-                    groups[r // 8 + h] += [b[8 * h : 8 * h + 8] for b in both]
-            groups[rows // 8] += [same_ref[:, edge], along_ref[:, 2 * width + edge.start : 2 * width + edge.stop]]
-            for g in range(0, len(groups), 4):
-                acc = jnp.zeros((8, LANES), F32)
-                for q, items in enumerate(groups[g : g + 4]):
-                    for k, item in enumerate(items):
-                        if item is not None:
-                            slot = 4 * q + k
-                            shift = (8 * slot - base) % LANES
-                            moved = pltpu.roll(item, shift, 1) if shift else item
-                            acc = jnp.where((lane >= 8 * slot) & (lane < 8 * slot + 8), moved, acc)
-                out_ref[to, 2 * g : 2 * g + 8, :] = acc
-
-
-def rim_unpack_kernel(got_ref, phase_rim_ref, rim_ref, relay_ref, sums_ref):
-    cols, depth = got_ref.shape[:2]
+        groups = []
+        for j in range(stripe // 8 + 2):
+            items = []
+            for k in range(2):
+                tile = slice(k * width + edge.start, k * width + edge.stop)
+                if j == 0:
+                    items.append(jnp.where(low_illum, along_ref[:, tile], partner_ref[:, tile]))
+                elif j == stripe // 8 + 1:
+                    items.append(jnp.where(low_illum, partner_ref[:, tile], along_ref[:, tile]))
+                else:
+                    items.append(phase_ref[k, 8 * (j - 1) : 8 * j, edge])
+            groups.append(items)
+        while len(groups) < rows // 8 + 1:
+            groups.append([None, None])
+        for r in range(0, rows, 16):
+            both = [measured_ref[p, 0, r : r + 16, edge].astype(F32) for p in range(2)]
+            for h in range(2):
+                groups[r // 8 + h] += [b[8 * h : 8 * h + 8] for b in both]
+        groups[rows // 8] += [same_ref[:, edge], along_ref[:, 2 * width + edge.start : 2 * width + edge.stop]]
+        for g in range(0, len(groups), 4):
+            acc = jnp.zeros((8, LANES), F32)
+            for q, items in enumerate(groups[g : g + 4]):
+                for k, item in enumerate(items):
+                    if item is not None:
+                        slot = 4 * q + k
+                        shift = (8 * slot - base) % LANES
+                        moved = pltpu.roll(item, shift, 1) if shift else item
+                        acc = jnp.where((lane >= 8 * slot) & (lane < 8 * slot + 8), moved, acc)
+            yield 2 * g, acc
+
+    for (at, east), (_, west) in zip(packed(True), packed(False)):
+        first_ref[at : at + 8, :] = jnp.where(even, east, west)
+        second_ref[at : at + 8, :] = jnp.where(even, west, east)
+
+
+def second_kernel(packed_ref, note_ref, first_ref, out_ref):
+    rims = packed_ref.shape[0]
+    out_ref[:rims, :] = packed_ref[...]
+    out_ref[rims:, :] = note_ref[...] + first_ref[rims:, :]
+
+
+def rim_unpack_kernel(first_ref, second_ref, note_ref, phase_rim_ref, rim_ref, relay_ref, sums_ref):
     stripe = phase_rim_ref.shape[1] - 2 * RIM
-    rows = 2 * stripe
+    rims, rows = first_ref.shape[0] - 8, 2 * stripe
     illum, _, col = place()
-    west, east = jnp.maximum(col - 1, 0), jnp.minimum(col + 1, cols - 1)
+    even = lax.rem(col, 2) == 0
     lane = lane_ids((8, LANES))
     in_west = (lane >= LANES - RIM) & (col > 0)
-    in_east = (lane < RIM) & (col < cols - 1)
+    in_east = (lane < RIM) & (col < lax.axis_size("col") - 1)
     for g in range(0, rows // 8 + 1, 4):
-        a, b = got_ref[west, 2 * g : 2 * g + 8, :], got_ref[east, 2 * g : 2 * g + 8, :]
+        first, second = first_ref[2 * g : 2 * g + 8, :], second_ref[2 * g : 2 * g + 8, :]
+        a, b = jnp.where(even, second, first), jnp.where(even, first, second)
         for j in range(g, min(g + 4, rows // 8 + 1)):
             for k in range(4):
                 if k < 2 and j >= stripe // 8 + 2:
@@ -375,15 +381,7 @@
     for r in range(0, stripe + 8, 8):
         at = pl.ds(pl.multiple_of(other + r, 8) if r < stripe else near, 8)
         relay_ref[r : r + 8, :] = rim_ref[0, at, :] + pltpu.roll(rim_ref[1, at, :], LANES // 2, 1)
-    total = got_ref[0, depth - 8 :, :]
-    for c in range(1, cols):
-        total = total + got_ref[c, depth - 8 :, :]
-    sums_ref[...] = total
-
-
-def relay_kernel(relay_ref, sums_ref, core_sums_ref, out_ref):
-    out_ref[: relay_ref.shape[0], :] = relay_ref[...]
-    out_ref[relay_ref.shape[0] :, :] = jnp.maximum(sums_ref[...], core_sums_ref[...])
+    sums_ref[...] = note_ref[...] + first_ref[rims:, :] + second_ref[rims:, :]
 
 
 def fill_target(tile, target, low_illum, middle, near, far):
@@ -412,14 +410,13 @@
     return [jnp.sum(jnp.where(lane == n, note, 0.0)[:1], axis=1, keepdims=True) for n in (16, 17)]
 
 
-def forward_both(tile, notes, columns, row_first, totals, trig, half, tables, fields, uses):
-    for note, columns_of, (w0, w1), use in zip(notes, (columns, columns), fields, uses):
-        incident_tables(tile, tilts_of(note), row_first, columns_of, *totals, tables)
-        enter(tile, tables, trig[0], w0)
-        first_half(tile, w0, half, 1.0, tile.blocks)
-        second_half(tile, w0, half, tile.blocks, modulate_into(trig[1], w1))
-        first_half(tile, w1, half, 1.0, tile.blocks)
-        second_half(tile, w1, half, tile.blocks, use)
+def forward(tile, note, columns, row_first, totals, trig, half, tables, w0, w1, use):
+    incident_tables(tile, tilts_of(note), row_first, columns, *totals, tables)
+    enter(tile, tables, trig[0], w0)
+    first_half(tile, w0, half, 1.0, tile.blocks)
+    second_half(tile, w0, half, tile.blocks, modulate_into(trig[1], w1))
+    first_half(tile, w1, half, 1.0, tile.blocks)
+    second_half(tile, w1, half, tile.blocks, use)
 
 
 def keep_in(field):
@@ -481,21 +478,46 @@
     return jnp.where(lane < 16, west, jnp.where(lane >= LANES - RIM, rim, moved))
 
 
-def forward_kernel(sizes, phase_ref, measured_ref, known_ref, partner_ref, along_ref, same_ref,
-                   own_ref, o0r, o0i, o1r, o1i, o2r, o2i, c1, s1,
-                   c0, s0, w0r, w0i, w1r, w1i, gr, gi, hr, hi, mr, mi, row_r, row_i, col_r, col_i):
+def trig_kernel(phase_ref, c0, s0, c1, s1):
+    for t in range(c0.shape[0]):
+        for k, (c, s) in enumerate(((c0, s0), (c1, s1))):
+            for r in range(0, c.shape[1], 16):
+                s[t, r : r + 16, :], c[t, r : r + 16, :] = sine_cosine(phase_ref[k, r : r + 16, own_columns(t)])
+
+
+def ahead_kernel(sizes, own_c0, own_s0, own_c1, own_s1, partner_ref, along_ref,
+                 c0, s0, c1, s1, w0r, w0i, w1r, w1i, ur_ref, ui_ref, hr, hi, row_r, row_i, col_r, col_i):
     stripe, tiles, total_rows, total_cols = sizes
     tile, row_first, col_first = main_tile(sizes)
     illum, _, _ = place()
     low_illum = illum == 0
-    blank_rims((w0r, w0i, w1r, w1i, gr, gi, hr, hi, o0r, o0i, o1r, o1i), tile)
+    blank_rims((w0r, w0i, w1r, w1i, hr, hi), tile)
     trig = (c0, s0), (c1, s1)
-    fill_trig(
-        tile, trig, low_illum,
-        lambda k, t, r: phase_ref[k, r : r + 16, own_columns(t)],
-        lambda k, t: partner_ref[:, own_columns(t + k * tiles)],
-        lambda k, t: along_ref[:, own_columns(t + k * tiles)],
-    )
+    end = 2 * RIM + stripe
+    for t in range(tiles):
+        for k, (mine, here) in enumerate((((own_c0, own_s0), trig[0]), ((own_c1, own_s1), trig[1]))):
+            far, near = along_ref[:, own_columns(t + k * tiles)], partner_ref[:, own_columns(t + k * tiles)]
+            above = sine_cosine(jnp.where(low_illum, far, near))
+            below = sine_cosine(jnp.where(low_illum, near, far))
+            for part in range(2):
+                here[part][t, 2 * RIM : end, :] = mine[part][t]
+                here[part][t, RIM : 2 * RIM, :] = above[1 - part]
+                here[part][t, end : end + RIM, :] = below[1 - part]
+    forward(
+        tile, partner_ref[:, 2 * tiles * LANES :], rim_columns(tile, col_first, col_r.shape), row_first,
+        (total_rows, total_cols), trig, (hr, hi), (row_r, row_i, col_r, col_i),
+        (w0r, w0i), (w1r, w1i), keep_in((ur_ref, ui_ref)),
+    )
+
+
+def own_kernel(sizes, c0, s0, c1, s1, measured_ref, known_ref, same_ref,
+               own_ref, w0r, w0i, w1r, w1i, gr, gi, hr, hi, mr, mi, row_r, row_i, col_r, col_i):
+    stripe, tiles, total_rows, total_cols = sizes
+    tile, row_first, col_first = main_tile(sizes)
+    illum, _, _ = place()
+    low_illum = illum == 0
+    blank_rims((w0r, w0i, w1r, w1i, gr, gi, hr, hi), tile)
+    trig = (c0, s0), (c1, s1)
     mine = illum * stripe
     near_base = pl.multiple_of(stripe - 16 * illum, 16)
 
@@ -507,14 +529,12 @@
         return [jnp.where(low_illum, x[:8], x[8:]) for x in both]
 
     fill_target(tile, (mr, mi), low_illum, middle, near, lambda t: same_ref[:, own_columns(t)])
-    half = hr, hi
-    forward_both(
-        tile, (partner_ref[:, 2 * tiles * LANES :], known_ref[...]), rim_columns(tile, col_first, col_r.shape), row_first,
-        (total_rows, total_cols), trig, half, (row_r, row_i, col_r, col_i),
-        (((o0r, o0i), (o1r, o1i)), ((w0r, w0i), (w1r, w1i))),
-        (keep_in((o2r, o2i)), residual_in((gr, gi), (mr, mi))),
-    )
-    backward(tile, (gr, gi), half, (w0r, w0i), (w1r, w1i), trig[1], put_in(own_ref))
+    forward(
+        tile, known_ref[...], rim_columns(tile, col_first, col_r.shape), row_first,
+        (total_rows, total_cols), trig, (hr, hi), (row_r, row_i, col_r, col_i),
+        (w0r, w0i), (w1r, w1i), residual_in((gr, gi), (mr, mi)),
+    )
+    backward(tile, (gr, gi), (hr, hi), (w0r, w0i), (w1r, w1i), trig[1], put_in(own_ref))
 
 
 def other_near(swap_ref, stripe, low_illum, columns):
@@ -585,16 +605,19 @@
 
     fill_target(tile, (mr, mi), low_illum, middle, near, far)
     half = hr, hi
-    forward_both(
-        tile, (partner_ref[:, 2 * tiles * LANES :], known_ref[...]), columns, row_first,
-        (total_rows, total_cols), trig, half, (row_r, row_i, col_r, col_i),
-        (((o0r, o0i), (o1r, o1i)), ((w0r, w0i), (w1r, w1i))),
-        (keep_in((o2r, o2i)), residual_in((gr, gi), (mr, mi))),
+    totals, tables = (total_rows, total_cols), (row_r, row_i, col_r, col_i)
+    forward(
+        tile, partner_ref[:, 2 * tiles * LANES :], columns, row_first, totals, trig, half, tables,
+        (o0r, o0i), (o1r, o1i), keep_in((o2r, o2i)),
+    )
+    forward(
+        tile, known_ref[...], columns, row_first, totals, trig, half, tables,
+        (w0r, w0i), (w1r, w1i), residual_in((gr, gi), (mr, mi)),
     )
     backward(tile, (gr, gi), half, (w0r, w0i), (w1r, w1i), trig[1], put_in(own_ref))
 
 
-def finish_kernel(sizes, own_ref, other_ref, own_patch_ref, swap_ref, along_ref, rim_ref, relay_ref, partner_relay_ref,
+def finish_kernel(sizes, own_ref, other_ref, own_patch_ref, swap_ref, along_ref, rim_ref, sums_ref, far_sums_ref, partner_relay_ref,
                   w0r, w0i, w1r, w1i, ur_ref, ui_ref, c1, s1, out_ref, other_patch, gr, gi, hr, hi, mr, mi):
     stripe, tiles, total_rows, total_cols = sizes
     tile, _, _ = patch_tile(sizes)
@@ -603,7 +626,7 @@
     blank_rims((gr, gi, hr, hi), tile)
 
     lane = lane_ids((8, LANES))
-    sums = jnp.maximum(relay_ref[stripe + 8 :, :], partner_relay_ref[stripe + 8 :, :])
+    sums = jnp.maximum(sums_ref[...], far_sums_ref[...])
     scales = []
     for which in range(2):
         here = jnp.where((lane >= 4 * which) & (lane < 4 * which + 4), sums, 0.0)
@@ -641,10 +664,15 @@
         out_ref[k, :, last] = jnp.where(on >= LANES - RIM, pltpu.roll(patch, 56, 1), out_ref[k, :, last])
 
 
-def call(kernel, outs, *args, scratch=(), in_place=0, flops=0, mib=8):
+def like(x, held):
+    shape, dtype = (x, F32) if isinstance(x, tuple) else (x.shape, x.dtype)
+    return pltpu.VMEM(shape, dtype) if held else jax.ShapeDtypeStruct(shape, dtype)
+
+
+def call(kernel, outs, *args, scratch=(), in_place=0, flops=0, mib=8, held=()):
     return pl.pallas_call(
         kernel,
-        out_shape=[jax.ShapeDtypeStruct(shape, F32) for shape in outs],
+        out_shape=[like(x, n in held) for n, x in enumerate(outs)],
         in_specs=[pl.BlockSpec(memory_space=pltpu.HBM)] * in_place
         + [pl.BlockSpec(memory_space=pltpu.VMEM)] * (len(args) - in_place),
         out_specs=[pl.BlockSpec(memory_space=pltpu.VMEM)] * len(outs),
@@ -665,22 +693,26 @@
         along += [(rows + r, (r + 1) % rows), ((r + 1) % rows, rows + r)]
     same = [(r, (r + 1) % rows) for r in range(rows)] + [(rows + (r + 1) % rows, rows + r) for r in range(rows)]
 
-    partner_out, along_out, same_out, known = call(
-        open_kernel, [(8, 2 * width + LANES), (8, 3 * width + LANES), (8, width + LANES), (8, LANES)],
-        phase_delay, measured, angles, in_place=3, mib=62,
+    partner_out, along_out, same_out, known, measured = call(
+        open_kernel, [(8, 2 * width + LANES), (8, 3 * width + LANES), (8, width + LANES), (8, LANES), measured],
+        phase_delay, measured, angles, in_place=3, mib=62, held=(4,),
         scratch=[
-            pltpu.VMEM(measured.shape, measured.dtype), (2, slices, 8, width),
+            (2, slices, 8, width),
             pltpu.VMEM(angles.shape, angles.dtype), pltpu.SemaphoreType.DMA((4,)),
         ],
     )
     along_in = lax.ppermute(along_out, ("illum", "row"), along)
     partner_in = lax.ppermute(partner_out, "illum", swap)
     same_in = lax.ppermute(same_out, ("illum", "row"), same)
-    (swap_out,) = call(swap_kernel, [(2 * stripe + 8, width)], measured, partner_in)
+    (swap_out,) = call(swap_kernel, [(2 * stripe + 8, width)], measured, same_in)
     swap_in = lax.ppermute(swap_out, "illum", swap)
-    depth = 8 * (-(-(stripe // 4 + 1) // 4)) + 8
-    (rims_out,) = call(rim_pack_kernel, [(cols, depth, LANES)], phase_delay, measured, known, partner_in, along_in, same_in)
-    rims_in = lax.all_to_all(rims_out, "col", 0, 0, tiled=True)
+    rims = 8 * (-(-(stripe // 4 + 1) // 4))
+    first_out, second_packed, note = call(
+        rim_pack_kernel, [(rims + 8, LANES), (rims, LANES), (8, LANES)], phase_delay, measured, known, partner_in, along_in, same_in
+    )
+    first_in = lax.ppermute(first_out, "col", [(c, c ^ 1) for c in range(cols)])
+    (second_out,) = call(second_kernel, [(rims + 8, LANES)], second_packed, note, first_in)
+    second_in = lax.ppermute(second_out, "col", [(c, cols - 1 - c) for c in range(cols)])
 
     def fields(count):
         return [(count, stripe + 4 * RIM, LANES)]
@@ -689,27 +721,31 @@
         return [(stripe + 2 * RIM, LANES)] * 2 + [(-(-count // 8) * 8, LANES)] * 2
 
     rows_in = phase_delay, measured, known, partner_in, along_in, same_in
-    own, *kept = call(
-        functools.partial(forward_kernel, sizes), [phase_delay.shape] + fields(tiles) * 8, *rows_in,
-        scratch=fields(tiles) * 12 + tables(tiles), flops=6 * 10**9, mib=16,
+    own_trig = call(trig_kernel, [(tiles, stripe, LANES)] * 4, phase_delay, flops=10**9)
+    kept = call(
+        functools.partial(ahead_kernel, sizes), fields(tiles) * 10, *own_trig, partner_in, along_in,
+        scratch=fields(tiles) * 2 + tables(tiles), flops=15*10**8, mib=16,
+    )
+    (own,) = call(
+        functools.partial(own_kernel, sizes), [phase_delay.shape], *kept[:4], measured, known, same_in,
+        scratch=fields(tiles) * 10 + tables(tiles), flops=3*10**9, mib=16,
     )
     phase_rim, rim, relay, sums = call(
-        rim_unpack_kernel, [(2, stripe + 2 * RIM, LANES), (2, 2 * stripe + 8, LANES), (stripe + 8, LANES), (8, LANES)], rims_in
-    )
-    core_sums = lax.ppermute(sums, "row", [(r, r ^ 1) for r in range(rows)])
+        rim_unpack_kernel, [(2, stripe + 2 * RIM, LANES), (2, 2 * stripe + 8, LANES), (stripe + 8, LANES), (8, LANES)], first_in, second_in, note
+    )
+    partner_relay = lax.ppermute(relay, "illum", swap)
+    far_sums = lax.ppermute(sums, "row", [(r, r ^ 2) for r in range(rows)])
     (other,) = call(
-        functools.partial(other_kernel, sizes), [phase_delay.shape], swap_in, along_in, sums, *kept,
-        scratch=fields(tiles) * 6, flops=2 * 10**9, mib=12,
-    )
-    (relay,) = call(relay_kernel, [(stripe + 16, LANES)], relay, sums, core_sums)
-    partner_relay = lax.ppermute(relay, "illum", swap)
+        functools.partial(other_kernel, sizes), [phase_delay.shape], swap_in, along_in, sums, *kept[4:], *kept[2:4],
+        scratch=fields(tiles) * 6, flops=10**9, mib=12,
+    )
     own_patch, *patch_kept = call(
         functools.partial(patch_kernel, sizes), [(slices, stripe, LANES)] + fields(1) * 8, *rows_in, phase_rim, rim,
         scratch=fields(1) * 12 + tables(1), flops=10**9,
     )
     (out,) = call(
         functools.partial(finish_kernel, sizes), [phase_delay.shape],
-        own, other, own_patch, swap_in, along_in, rim, relay, partner_relay, *patch_kept,
+        own, other, own_patch, swap_in, along_in, rim, sums, far_sums, partner_relay, *patch_kept,
         scratch=[(slices, stripe, LANES)] + fields(1) * 6,
     )
     return out
@@ -740,7 +776,7 @@
 
 def per_device(phase_delay, angles, measured):
     illums = lax.axis_size("illum")
-    if illums == 2 and lax.axis_size("row") == 4:
+    if (illums, lax.axis_size("row"), lax.axis_size("col")) == (2, 4, 4):
         return paired(phase_delay, angles, measured)
     slices, stripe, width = phase_delay.shape
     tile_rows = measured.shape[2]

time: 36.1 us -> 29.3 us (0.81)
  local copies, waits for them, and re-layouts: 6.12 us -> 0.01 us
  waiting for transfers between devices: 6.01 us -> 4.02 us
  starting transfers between devices: 11.4 us -> 13.3 us
  Pallas kernels: 12.1 us -> 11.7 us
    unnamed x38 -> x4, local copies, waits for them, and re-layouts: 6.12 us -> 0.01 us
    ppermute x1 -> x3, starting transfers between devices: 0.07 us -> 5.72 us  [the longest x1 3.6 us: paired(): lax.ppermute(second_out, 'col', [(c, cols - 1 - c) for c in range(cols)])]
    all_to_all x1 -> x0, starting transfers between devices: 4.87 us -> none  [paired(): rims_in = lax.all_to_all(rims_out, 'col', 0, 0, tiled=True)]
    ppermute x1, waiting for transfers between devices: 1.89 us -> 0.01 us  [paired(): partner_relay = lax.ppermute(relay, 'illum', swap)]
    ppermute x1, starting transfers between devices: 0.64 us -> 1.39 us  [paired(): partner_relay = lax.ppermute(relay, 'illum', swap)]
    ppermute x1, starting transfers between devices: 0.01 us -> 0.7 us  [paired(): partner_in = lax.ppermute(partner_out, 'illum', swap)]
    ppermute x1, waiting for transfers between devices: 4.11 us -> 3.54 us  [paired(): partner_in = lax.ppermute(partner_out, 'illum', swap)]
    ppermute x1 -> x3, waiting for transfers between devices: 0.01 us -> 0.47 us  [the longest x1 0.47 us: paired(): first_in = lax.ppermute(first_out, 'col', [(c, c ^ 1) for c in range(cols)])]
  transfers between devices with their start and end apart: 7 -> 8, of which waited for: 2 -> 2; matrix products, arithmetic and copies ran while one was open for 0% -> 0% of each run, Pallas kernels for 24% -> 28%
where the time goes in v5:
time: 29.3 us; the launch traced here: 29.2 us
  starting transfers between devices  13.3 us (45%)
  Pallas kernels  11.7 us (40%)
  waiting for transfers between devices  4.02 us (14%)
    pallas_call x11, Pallas kernels, call(): pl.pallas_call(kernel, out_shape=[like(x, n in held) for n, x in enumerat...  11.7 us
    ppermute x1, starting transfers between devices, paired(): lax.ppermute(second_out, 'col', [(c, cols - 1 - c) for c in range(cols)])  3.6 us
    ppermute x1, starting transfers between devices, paired(): along_in = lax.ppermute(along_out, ('illum', 'row'), along)  3.56 us
    ppermute x1, waiting for transfers between devices, paired(): partner_in = lax.ppermute(partner_out, 'illum', swap)  3.54 us
    ppermute x1, starting transfers between devices, paired(): first_in = lax.ppermute(first_out, 'col', [(c, c ^ 1) for c in range(cols)])  1.64 us
    ppermute x1, starting transfers between devices, paired(): swap_in = lax.ppermute(swap_out, 'illum', swap)  1.41 us
    ppermute x1, starting transfers between devices, paired(): partner_relay = lax.ppermute(relay, 'illum', swap)  1.39 us
    ppermute x1, starting transfers between devices, paired(): partner_in = lax.ppermute(partner_out, 'illum', swap)  0.7 us
  transfers between devices with their start and end apart: 8, of which 2 were waited for; matrix products, arithmetic and copies ran while one was open for 0% of the time, Pallas kernels for 28%

profile of v5, /device:TPU:0, one launch (start us, length us, event | category | flops | bytes accessed | tf_op | source)
XLA Modules:
  0.0 29.2 jit_solution(11262077936861947214)
XLA Ops:
  0.0 2.1 %shard_map.38 = (f32[8,2176]{1,0:T(8,128)}, f32[8,3200]{1,0:T(8,128)}, f32[8,1152]{1,0:T(8,128)}, f32[8,128]{1,0:T(8,128)}, bf16[2,1,128,1024]{3,2,1,0:T(8,128)(2,1)S(1)}) custom-call(f32[2,64,1024]{2,1,0:T(8,128)} %phase_ref.7, bf16[2,1,128,1024]{3,2,1,0:T(8,128)(2,1)} %measured_ref.1, s32[1,2]{1,0:T(1,128)} %tilt_ref.1), custom_call_target="tpu_custom_call" | custom-call | bytes 262144 | tf_op jit(solution)/shard_map/pallas_call | solution.py:673
  2.1 0.5 %collective-permute-start.2 = (f32[8,1152]{1,0:T(8,128)}, f32[8,1152]{1,0:T(8,128)S(1)}, u32[]{:S(2)}, u32[]{:S(2)}) collective-permute-start(f32[8,1152]{1,0:T(8,128)} %get-tuple-element.52), channel_id=1, source_target_pairs={{0,4},{4,8},{8,12},{12,0},{20,16},{24,20},{28,24},{16,28},{1,5},{5... | collective-permute-start | bytes 110600 | tf_op jit(solution)/shard_map/ppermute | solution.py:706
  2.6 3.6 %collective-permute-start.1 = (f32[8,3200]{1,0:T(8,128)}, f32[8,3200]{1,0:T(8,128)S(1)}, u32[]{:S(2)}, u32[]{:S(2)}) collective-permute-start(f32[8,3200]{1,0:T(8,128)} %get-tuple-element.45), channel_id=1, source_target_pairs={{16,4},{4,16},{20,8},{8,20},{24,12},{12,24},{28,0},{0,28},{17,5},{... | collective-permute-start | bytes 307208 | tf_op jit(solution)/shard_map/ppermute | solution.py:704
  6.1 0.7 %collective-permute-start = (f32[8,2176]{1,0:T(8,128)}, f32[8,2176]{1,0:T(8,128)S(1)}, u32[]{:S(2)}, u32[]{:S(2)}) collective-permute-start(f32[8,2176]{1,0:T(8,128)} %get-tuple-element.44), channel_id=1, source_target_pairs={{0,16},{16,0},{1,17},{17,1},{2,18},{18,2},{3,19},{19,3},{4,20},{20... | collective-permute-start | bytes 208904 | tf_op jit(solution)/shard_map/ppermute | solution.py:705
  6.8 0.0 collective-permute-done.2.same_ref
  6.8 0.0 copy-start
  6.9 1.4 %collective-permute-start.3 = (f32[136,1024]{1,0:T(8,128)S(1)}, f32[136,1024]{1,0:T(8,128)S(1)}, u32[]{:S(2)}, u32[]{:S(2)}) collective-permute-start(f32[136,1024]{1,0:T(8,128)S(1)} %shard_map.41), channel_id=1, source_target_pairs={{0,16},{16,0},{1,17},{17,1},{2,18},{18,2},{3,19},{19,3},{4,20},{20... | collective-permute-start | bytes 1671176 | tf_op jit(solution)/shard_map/ppermute | solution.py:708
  8.3 0.0 copy-done
  8.3 0.0 copy-start.1
  8.3 0.4 %shard_map.37 = (f32[8,64,128]{2,1,0:T(8,128)S(1)}, f32[8,64,128]{2,1,0:T(8,128)S(1)}, f32[8,64,128]{2,1,0:T(8,128)S(1)}, f32[8,64,128]{2,1,0:T(8,128)S(1)}) custom-call(f32[2,64,1024]{2,1,0:T(8,128)S(1)} %copy-done), custom_call_target="tpu_custom_call" | custom-call | flops 1000000000 | bytes 262144 | tf_op jit(solution)/shard_map/pallas_call | solution.py:673
  8.7 3.5 %collective-permute-done.partner_ref = f32[8,2176]{1,0:T(8,128)S(1)} collective-permute-done((f32[8,2176]{1,0:T(8,128)}, f32[8,2176]{1,0:T(8,128)S(1)}, u32[]{:S(2)}, u32[]{:S(2)}) %collective-permute-start) | collective-permute-done | bytes 69664 | tf_op jit(solution)/shard_map/ppermute | solution.py:705
  12.2 0.0 collective-permute-done.1.along_ref
  12.2 0.0 copy-done.1
  12.2 0.1 shard_map.42
  12.4 1.6 %collective-permute-start.4 = (f32[48,128]{1,0:T(8,128)S(1)}, f32[48,128]{1,0:T(8,128)S(1)}, u32[]{:S(2)}, u32[]{:S(2)}) collective-permute-start(f32[48,128]{1,0:T(8,128)S(1)} %get-tuple-element.53), channel_id=1, source_target_pairs={{0,1},{1,0},{2,3},{3,2},{4,5},{5,4},{6,7},{7,6},{8,9},{9,8},{10,11... | collective-permute-start | bytes 73736 | tf_op jit(solution)/shard_map/ppermute | solution.py:713
  14.0 1.8 %shard_map.39 = (f32[8,96,128]{2,1,0:T(8,128)S(1)}, f32[8,96,128]{2,1,0:T(8,128)S(1)}, f32[8,96,128]{2,1,0:T(8,128)S(1)}, f32[8,96,128]{2,1,0:T(8,128)S(1)}, f32...) custom-call(f32[8,64,128]{2,1,0:T(8,128)S(1)} %get-tuple-element.40., ...), custom_call_target="tpu_custom_call" | custom-call | flops 1500000000 | bytes 262144 | tf_op jit(solution)/shard_map/pallas_call | solution.py:673
  15.8 0.5 %collective-permute-done.4.first_ref = f32[48,128]{1,0:T(8,128)S(1)} collective-permute-done((f32[48,128]{1,0:T(8,128)S(1)}, f32[48,128]{1,0:T(8,128)S(1)}, u32[]{:S(2)}, u32[]{:S(2)}) %collective-permute-start.4) | collective-permute-done | bytes 24608 | tf_op jit(solution)/shard_map/ppermute | solution.py:713
  16.3 3.6 %collective-permute-start.5 = (f32[48,128]{1,0:T(8,128)S(1)}, f32[48,128]{1,0:T(8,128)S(1)}, u32[]{:S(2)}, u32[]{:S(2)}) collective-permute-start(f32[48,128]{1,0:T(8,128)S(1)} %shard_map.43), channel_id=1, source_target_pairs={{0,3},{1,2},{2,1},{3,0},{4,7},{5,6},{6,5},{7,4},{8,11},{9,10},{10,... | collective-permute-start | bytes 73736 | tf_op jit(solution)/shard_map/ppermute | solution.py:715
  19.9 3.0 %shard_map.40.own_ref = f32[2,64,1024]{2,1,0:T(8,128)S(1)} custom-call(f32[8,96,128]{2,1,0:T(8,128)S(1)} %get-tuple-element.46.c0, f32[8,96,128]{2,1,0:T(8,128)S(1)} %get-tuple-element.47.s0, f32[8,96,128]{2,1,0:T(8,128)S(1)} %get-tuple-element.48.c1, f32[8,96,128]{2,1,0:T(8,128)S(1)} %get-tuple-element.49.s1, ...), custom_call_target="tpu_custom_call" | custom-call | flops 3000000000 | bytes 262144 | tf_op jit(solution)/shard_map/pallas_call | solution.py:673
  22.9 0.0 collective-permute-done.5.second_ref
  22.9 0.2 shard_map.44
  23.1 0.5 %collective-permute-start.6 = (f32[8,128]{1,0:T(8,128)S(1)}, f32[8,128]{1,0:T(8,128)S(1)}, u32[]{:S(2)}, u32[]{:S(2)}) collective-permute-start(f32[8,128]{1,0:T(8,128)S(1)} %get-tuple-element.56.sums_ref), channel_id=1, source_target_pairs={{0,8},{4,12},{8,0},{12,4},{1,9},{5,13},{9,1},{13,5},{2,10},{6,14},... | collective-permute-start | bytes 12296 | tf_op jit(solution)/shard_map/ppermute | solution.py:737
  23.6 1.4 %collective-permute-start.7 = (f32[72,128]{1,0:T(8,128)S(1)}, f32[72,128]{1,0:T(8,128)S(1)}, u32[]{:S(2)}, u32[]{:S(2)}) collective-permute-start(f32[72,128]{1,0:T(8,128)S(1)} %get-tuple-element.66), channel_id=1, source_target_pairs={{0,16},{16,0},{1,17},{17,1},{2,18},{18,2},{3,19},{19,3},{4,20},{20... | collective-permute-start | bytes 110600 | tf_op jit(solution)/shard_map/ppermute | solution.py:736
  25.0 1.2 %shard_map.46 = (f32[2,64,128]{2,1,0:T(8,128)S(1)}, f32[1,96,128]{2,1,0:T(8,128)S(1)}, f32[1,96,128]{2,1,0:T(8,128)S(1)}, f32[1,96,128]{2,1,0:T(8,128)S(1)}, f32...) custom-call(f32[2,64,1024]{2,1,0:T(8,128)S(1)} %copy-done, ...), custom_call_target="tpu_custom_call" | custom-call | flops 1000000000 | bytes 262144 | tf_op jit(solution)/shard_map/pallas_call | solution.py:673
  26.3 0.0 collective-permute-done.3.swap_ref
  26.3 1.5 %shard_map.45.other_ref = f32[2,64,1024]{2,1,0:T(8,128)S(1)} custom-call(f32[136,1024]{1,0:T(8,128)S(1)} %collective-permute-done.3.swap_ref, f32[8,3200]{1,0:T(8,128)S(1)} %collective-permute-done.1.along_ref, f32[8,128]{1,0:T(8,128)S(1)} %get-tuple-element.56.sums_ref, f32[8,96,128]{2,1,0:T(8,128)S(1)} %get-tuple-element.57.w0r, ...), custom_call_target="tpu_custom_call" | custom-call | flops 1000000000 | bytes 262144 | tf_op jit(solution)/shard_map/pallas_call | solution.py:673
  27.7 0.0 collective-permute-done.6.far_sums_ref
  27.8 0.0 collective-permute-done.7.partner_relay_ref
  27.8 1.4 %shard_map.47 = f32[2,64,1024]{2,1,0:T(8,128)} custom-call(f32[2,64,1024]{2,1,0:T(8,128)S(1)} %shard_map.40.own_ref, f32[2,64,1024]{2,1,0:T(8,128)S(1)} %shard_map.45.other_ref, f32[2,64,128]{2,1,0:T(8,128)S(1)} %get-tuple-element.65.own_patch_ref, f32[136,1024]{1,0:T(8,128)S(1)} %collective-permute-done.3.swap_ref, ...), custom_call_target="tpu_custom_call" | custom-call | bytes 262144 | tf_op jit(solution)/shard_map/pallas_call | solution.py:673
  (2 shorter events, 0.1 us)
Async XLA Ops:
  2.1 4.8 %collective-permute-start.2 = (f32[8,1152]{1,0:T(8,128)}, f32[8,1152]{1,0:T(8,128)S(1)}, u32[]{:S(2)}, u32[]{:S(2)}) collective-permute-start(f32[8,1152]{1,0:T(8,128)} %get-tuple-element.52), channel_id=1, source_target_pairs={{0,4},{4,8},{8,12},{12,0},{20,16},{24,20},{28,24},{16,28},{1,5},{5... | collective-permute-start | bytes 110600 | tf_op jit(solution)/shard_map/ppermute | solution.py:706
  2.6 9.7 %collective-permute-start.1 = (f32[8,3200]{1,0:T(8,128)}, f32[8,3200]{1,0:T(8,128)S(1)}, u32[]{:S(2)}, u32[]{:S(2)}) collective-permute-start(f32[8,3200]{1,0:T(8,128)} %get-tuple-element.45), channel_id=1, source_target_pairs={{16,4},{4,16},{20,8},{8,20},{24,12},{12,24},{28,0},{0,28},{17,5},{... | collective-permute-start | bytes 307208 | tf_op jit(solution)/shard_map/ppermute | solution.py:704
  6.1 6.1 %collective-permute-start = (f32[8,2176]{1,0:T(8,128)}, f32[8,2176]{1,0:T(8,128)S(1)}, u32[]{:S(2)}, u32[]{:S(2)}) collective-permute-start(f32[8,2176]{1,0:T(8,128)} %get-tuple-element.44), channel_id=1, source_target_pairs={{0,16},{16,0},{1,17},{17,1},{2,18},{18,2},{3,19},{19,3},{4,20},{20... | collective-permute-start | bytes 208904 | tf_op jit(solution)/shard_map/ppermute | solution.py:705
  6.8 1.5 %copy-start = (f32[2,64,1024]{2,1,0:T(8,128)S(1)}, f32[2,64,1024]{2,1,0:T(8,128)}, u32[]{:S(2)}) copy-start(f32[2,64,1024]{2,1,0:T(8,128)} %phase_ref.7) | copy-start | bytes 1572868
  6.9 19.4 %collective-permute-start.3 = (f32[136,1024]{1,0:T(8,128)S(1)}, f32[136,1024]{1,0:T(8,128)S(1)}, u32[]{:S(2)}, u32[]{:S(2)}) collective-permute-start(f32[136,1024]{1,0:T(8,128)S(1)} %shard_map.41), channel_id=1, source_target_pairs={{0,16},{16,0},{1,17},{17,1},{2,18},{18,2},{3,19},{19,3},{4,20},{20... | collective-permute-start | bytes 1671176 | tf_op jit(solution)/shard_map/ppermute | solution.py:708
  8.3 3.9 %copy-start.1 = (f32[8,128]{1,0:T(8,128)S(1)}, f32[8,128]{1,0:T(8,128)}, u32[]{:S(2)}) copy-start(f32[8,128]{1,0:T(8,128)} %get-tuple-element.51.known_ref) | copy-start | bytes 12292
  12.4 3.9 %collective-permute-start.4 = (f32[48,128]{1,0:T(8,128)S(1)}, f32[48,128]{1,0:T(8,128)S(1)}, u32[]{:S(2)}, u32[]{:S(2)}) collective-permute-start(f32[48,128]{1,0:T(8,128)S(1)} %get-tuple-element.53), channel_id=1, source_target_pairs={{0,1},{1,0},{2,3},{3,2},{4,5},{5,4},{6,7},{7,6},{8,9},{9,8},{10,11... | collective-permute-start | bytes 73736 | tf_op jit(solution)/shard_map/ppermute | solution.py:713
  16.3 6.6 %collective-permute-start.5 = (f32[48,128]{1,0:T(8,128)S(1)}, f32[48,128]{1,0:T(8,128)S(1)}, u32[]{:S(2)}, u32[]{:S(2)}) collective-permute-start(f32[48,128]{1,0:T(8,128)S(1)} %shard_map.43), channel_id=1, source_target_pairs={{0,3},{1,2},{2,1},{3,0},{4,7},{5,6},{6,5},{7,4},{8,11},{9,10},{10,... | collective-permute-start | bytes 73736 | tf_op jit(solution)/shard_map/ppermute | solution.py:715
  23.1 4.6 %collective-permute-start.6 = (f32[8,128]{1,0:T(8,128)S(1)}, f32[8,128]{1,0:T(8,128)S(1)}, u32[]{:S(2)}, u32[]{:S(2)}) collective-permute-start(f32[8,128]{1,0:T(8,128)S(1)} %get-tuple-element.56.sums_ref), channel_id=1, source_target_pairs={{0,8},{4,12},{8,0},{12,4},{1,9},{5,13},{9,1},{13,5},{2,10},{6,14},... | collective-permute-start | bytes 12296 | tf_op jit(solution)/shard_map/ppermute | solution.py:737
  23.6 4.1 %collective-permute-start.7 = (f32[72,128]{1,0:T(8,128)S(1)}, f32[72,128]{1,0:T(8,128)S(1)}, u32[]{:S(2)}, u32[]{:S(2)}) collective-permute-start(f32[72,128]{1,0:T(8,128)S(1)} %get-tuple-element.66), channel_id=1, source_target_pairs={{0,16},{16,0},{1,17},{17,1},{2,18},{18,2},{3,19},{19,3},{4,20},{20... | collective-permute-start | bytes 110600 | tf_op jit(solution)/shard_map/ppermute | solution.py:736

commit v6 on v5

--- a/solution.py
+++ b/solution.py
@@ -42,11 +42,12 @@
 
 
 class Tile:
-    def __init__(self, stripe, tiles, top, bottom, lanes=None, rim=None):
+    def __init__(self, stripe, tiles, top, bottom, lanes=None, rim=None, alone=()):
         self.stripe, self.tiles = stripe, tiles
         self.rows = stripe + 2 * RIM
         self.top, self.bottom, self.lanes, self.rim = top, bottom, lanes, rim
-        self.owned = tiles - 1 if rim else tiles
+        self.alone = alone
+        self.owned = tiles if rim in alone or rim is None else tiles - 1
         step = 32 if stripe % 32 == 0 else 8
         self.inner = [(2 * RIM + r, step, None) for r in range(0, stripe, step)]
         self.blocks = [(RIM, RIM, top)] + self.inner + [(2 * RIM + stripe, RIM, bottom)]
@@ -57,12 +58,12 @@
             held = {}
 
             def load(ref, t, rows=rows, held=held):
-                key = id(ref), t % self.tiles
+                key = id(ref), t
                 if key not in held:
-                    held[key] = ref[t % self.tiles, rows, :]
+                    held[key] = ref[t, rows, :]
                 return held[key]
 
-            for t in range(self.tiles):
+            for t in [*self.alone, *range(self.tiles - len(self.alone))]:
 
                 def mask(x, factor=factor, lanes=self.lanes if t == self.rim else None):
                     x = x if factor is None else x * factor
@@ -75,10 +76,11 @@
         below = pl.ds(rows.start + 1, rows.size)
         here = load(ref, t)
         west = east = here
-        if self.tiles > 1:
+        if t not in self.alone:
+            ring = self.tiles - len(self.alone)
             lane = lane_ids(here.shape)
-            west = jnp.where(lane == LANES - 1, load(ref, t - 1), here)
-            east = jnp.where(lane == 0, load(ref, t + 1), here)
+            west = jnp.where(lane == LANES - 1, load(ref, (t - 1) % ring), here)
+            east = jnp.where(lane == 0, load(ref, (t + 1) % ring), here)
         west, east = pltpu.roll(west, 1, 1), pltpu.roll(east, LANES - 1, 1)
         return here, (ref[t, above, :] + ref[t, below, :]) + (west + east)
 
@@ -145,8 +147,9 @@
     return use
 
 
-def backward(tile, adjoint, half, w0, w1, trig1, put):
-    gr, gi = adjoint
+def backward(tile, adjoint, half, w0, w1, trig1, put, between=None, on_middle=None):
+    between = between or adjoint
+    gr, gi = between
     inner = [first for first, _, _ in tile.inner]
 
     def back(t, rows, mask, ur, ui):
@@ -162,8 +165,10 @@
 
     first_half(tile, adjoint, half, -1.0, tile.blocks)
     second_half(tile, adjoint, half, tile.blocks, back)
-    first_half(tile, adjoint, half, -1.0, tile.blocks)
-    second_half(tile, adjoint, half, tile.inner, last)
+    if on_middle:
+        on_middle()
+    first_half(tile, between, half, -1.0, tile.blocks)
+    second_half(tile, between, half, tile.inner, last)
 
 
 def own_columns(t):
@@ -245,10 +250,10 @@
     return [measured_ref[p, 0, base : base + 16, :].astype(F32)[at : at + 8] for p in range(2)]
 
 
-def open_kernel(phase_ref, measured_ref, tilt_ref, partner_ref, along_ref, same_ref, known_ref, held, edge, tilt, sems):
+def open_kernel(phase_ref, measured_ref, tilt_ref, partner_ref, along_ref, same_ref, known_ref, note_ref, held, edge, tilt, sems):
     stripe, width = phase_ref.shape[1:]
     rows = 2 * stripe
-    illum, row, _ = place()
+    illum, _, _ = place()
     field_copy = pltpu.make_async_copy(measured_ref, held, sems.at[0])
     tilt_copy = pltpu.make_async_copy(tilt_ref, tilt, sems.at[3])
     edge_copies = [
@@ -267,8 +272,8 @@
         partner_ref[:, k * width : (k + 1) * width] = jnp.where(illum == 0, bottom, top)
     field_copy.wait()
     top, bottom = pack_rows(*edge_blocks(held, 0), True), pack_rows(*edge_blocks(held, rows - 8), False)
-    along_ref[:, 2 * width : 3 * width] = jnp.where(illum == 0, top, bottom)
-    same_ref[:, :width] = jnp.where(illum == 0, bottom, top)
+    along_ref[:, 2 * width :] = jnp.where(illum == 0, top, bottom)
+    same_ref[...] = jnp.where(illum == 0, bottom, top)
     total = jnp.zeros((8, width), F32)
     for p in range(2):
         for r in range(0, rows, 16):
@@ -277,9 +282,8 @@
             total = total + (x[:8] + x[8:])
     energy = jnp.sum(jnp.sum(total, axis=1, keepdims=True), axis=0, keepdims=True)
     lane = lane_ids((8, LANES))
-    note = jnp.where(lane == illum * 4 + row, energy, 0.0)
-    along_ref[:, 3 * width :] = note
-    same_ref[:, width:] = note
+    note_ref[...] = jnp.where(lane == illum, energy, 0.0)
+    note = jnp.zeros((8, LANES), F32)
     tilt_copy.wait()
     for n in range(2):
         note = jnp.where(lane == 16 + n, tilt[:, n : n + 1].astype(F32), note)
@@ -300,17 +304,16 @@
     swap_ref[2 * stripe :, :] = jnp.where(illum == 0, above, below)
 
 
-def rim_pack_kernel(phase_ref, measured_ref, known_ref, partner_ref, along_ref, same_ref, first_ref, second_ref, note_ref):
+def rim_pack_kernel(phase_ref, measured_ref, pair_ref, far_ref, partner_ref, along_ref, same_ref, first_ref, second_ref, note_ref):
     stripe, width = phase_ref.shape[1:]
     rows = 2 * stripe
     illum, _, col = place()
     low_illum = illum == 0
     even = lax.rem(col, 2) == 0
     lane = lane_ids((8, LANES))
-    known = jnp.maximum(known_ref[...], partner_ref[:, 2 * width :])
-    known = jnp.maximum(jnp.maximum(known, same_ref[:, width:]), along_ref[:, 3 * width :])
-    note_ref[...] = known
-    first_ref[first_ref.shape[0] - 8 :, :] = known
+    note = pair_ref[...] + far_ref[...]
+    note_ref[...] = note
+    first_ref[first_ref.shape[0] - 8 :, :] = note
 
     def packed(east):
         edge = slice(width - LANES, width) if east else slice(0, LANES)
@@ -356,7 +359,7 @@
     out_ref[rims:, :] = note_ref[...] + first_ref[rims:, :]
 
 
-def rim_unpack_kernel(first_ref, second_ref, note_ref, phase_rim_ref, rim_ref, relay_ref, sums_ref):
+def rim_unpack_kernel(first_ref, second_ref, note_ref, phase_rim_ref, rim_ref, relay_ref):
     stripe = phase_rim_ref.shape[1] - 2 * RIM
     rims, rows = first_ref.shape[0] - 8, 2 * stripe
     illum, _, col = place()
@@ -381,7 +384,7 @@
     for r in range(0, stripe + 8, 8):
         at = pl.ds(pl.multiple_of(other + r, 8) if r < stripe else near, 8)
         relay_ref[r : r + 8, :] = rim_ref[0, at, :] + pltpu.roll(rim_ref[1, at, :], LANES // 2, 1)
-    sums_ref[...] = note_ref[...] + first_ref[rims:, :] + second_ref[rims:, :]
+    relay_ref[stripe + 8 :, :] = note_ref[...] + first_ref[rims:, :] + second_ref[rims:, :]
 
 
 def fill_target(tile, target, low_illum, middle, near, far):
@@ -410,8 +413,8 @@
     return [jnp.sum(jnp.where(lane == n, note, 0.0)[:1], axis=1, keepdims=True) for n in (16, 17)]
 
 
-def forward(tile, note, columns, row_first, totals, trig, half, tables, w0, w1, use):
-    incident_tables(tile, tilts_of(note), row_first, columns, *totals, tables)
+def forward(tile, tilts, columns, row_first, totals, trig, half, tables, w0, w1, use):
+    incident_tables(tile, tilts, row_first, columns, *totals, tables)
     enter(tile, tables, trig[0], w0)
     first_half(tile, w0, half, 1.0, tile.blocks)
     second_half(tile, w0, half, tile.blocks, modulate_into(trig[1], w1))
@@ -458,24 +461,35 @@
     return Tile(stripe, tiles, top, bottom), row_first, col * tiles * LANES
 
 
-def patch_tile(sizes):
+OTHER = 28
+
+
+def patch_lanes():
+    lane = lane_ids((1, LANES))
+    other = ((lane >= OTHER - RIM) & (lane < OTHER + 16)) | ((lane >= 56 + OTHER) & (lane < 80 + OTHER))
+    return other, jnp.where(other, (lane + (LANES - OTHER)) % LANES, lane)
+
+
+def patch_held(sizes):
     stripe, tiles, total_rows, total_cols = sizes
-    _, row_first, col_first = main_tile(sizes)
+    _, _, col_first = main_tile(sizes)
     width = tiles * LANES
-    top, bottom, _ = edges_of(row_first, 0, stripe, tiles + 1, total_rows, total_cols)
-    lane = lane_ids((1, LANES))
-    held = (lane < 16) | ((lane >= 56) & (lane < 72))
-    held = held | ((lane >= 72) & (lane < 80) & (col_first + width < total_cols))
-    held = held | ((lane >= LANES - RIM) & (col_first > 0))
-    columns = jnp.where(lane < 16, lane, jnp.where(lane < 80, lane - 72 + width, lane - LANES)) + col_first
-    tile = Tile(stripe, 1, top, bottom, jnp.where(held, 1.0, 0.0).astype(F32), 0)
-    return tile, row_first, jnp.broadcast_to(columns, (8, LANES))
+    _, at = patch_lanes()
+    held = (at < 16) | ((at >= 56) & (at < 72))
+    held = held | ((at >= 72) & (at < 80) & (col_first + width < total_cols))
+    held = held | ((at >= LANES - RIM) & (col_first > 0))
+    columns = jnp.where(at < 16, at, jnp.where(at < 80, at - 72 + width, at - LANES)) + col_first
+    return jnp.where(held, 1.0, 0.0).astype(F32), jnp.broadcast_to(columns, (8, LANES))
 
 
 def join_edges(west, east, rim):
     lane = lane_ids(west.shape)
     moved = pltpu.roll(jnp.where(lane < RIM, rim, east), 72, 1)
     return jnp.where(lane < 16, west, jnp.where(lane >= LANES - RIM, rim, moved))
+
+
+def join_illums(own, other):
+    return jnp.where(patch_lanes()[0], pltpu.roll(other, OTHER, 1), own)
 
 
 def trig_kernel(phase_ref, c0, s0, c1, s1):
@@ -504,14 +518,14 @@
                 here[part][t, RIM : 2 * RIM, :] = above[1 - part]
                 here[part][t, end : end + RIM, :] = below[1 - part]
     forward(
-        tile, partner_ref[:, 2 * tiles * LANES :], rim_columns(tile, col_first, col_r.shape), row_first,
+        tile, tilts_of(partner_ref[:, 2 * tiles * LANES :]), rim_columns(tile, col_first, col_r.shape), row_first,
         (total_rows, total_cols), trig, (hr, hi), (row_r, row_i, col_r, col_i),
         (w0r, w0i), (w1r, w1i), keep_in((ur_ref, ui_ref)),
     )
 
 
 def own_kernel(sizes, c0, s0, c1, s1, measured_ref, known_ref, same_ref,
-               own_ref, w0r, w0i, w1r, w1i, gr, gi, hr, hi, mr, mi, row_r, row_i, col_r, col_i):
+               w0r, w0i, w1r, w1i, gr, gi, hr, hi, mr, mi, row_r, row_i, col_r, col_i):
     stripe, tiles, total_rows, total_cols = sizes
     tile, row_first, col_first = main_tile(sizes)
     illum, _, _ = place()
@@ -530,11 +544,16 @@
 
     fill_target(tile, (mr, mi), low_illum, middle, near, lambda t: same_ref[:, own_columns(t)])
     forward(
-        tile, known_ref[...], rim_columns(tile, col_first, col_r.shape), row_first,
+        tile, tilts_of(known_ref[...]), rim_columns(tile, col_first, col_r.shape), row_first,
         (total_rows, total_cols), trig, (hr, hi), (row_r, row_i, col_r, col_i),
         (w0r, w0i), (w1r, w1i), residual_in((gr, gi), (mr, mi)),
     )
-    backward(tile, (gr, gi), (hr, hi), (w0r, w0i), (w1r, w1i), trig[1], put_in(own_ref))
+
+
+def back_kernel(sizes, c1, s1, w0r, w0i, w1r, w1i, gr, gi, own_ref, ar, ai, hr, hi):
+    tile, _, _ = main_tile(sizes)
+    blank_rims((ar, ai, hr, hi), tile)
+    backward(tile, (gr, gi), (hr, hi), (w0r, w0i), (w1r, w1i), (c1, s1), put_in(own_ref), (ar, ai))
 
 
 def other_near(swap_ref, stripe, low_illum, columns):
@@ -543,36 +562,21 @@
     return [jnp.where(low_illum, low[part], high[part]) for part in range(2)]
 
 
-def other_kernel(sizes, swap_ref, along_ref, sums_ref, w0r, w0i, w1r, w1i, ur_ref, ui_ref, c1, s1, out_ref, gr, gi, hr, hi, mr, mi):
-    stripe, tiles, _, _ = sizes
-    tile, _, _ = main_tile(sizes)
-    illum, _, _ = place()
-    blank_rims((gr, gi, hr, hi), tile)
-    fill_target(
-        tile, (mr, mi), illum == 0,
-        lambda part, t, r: swap_ref[part * stripe + r : part * stripe + r + 16, own_columns(t)],
-        lambda t: other_near(swap_ref, stripe, illum == 0, own_columns(t)),
-        lambda t: along_ref[:, own_columns(t + 2 * tiles)],
-    )
-    residual_of(tile, (gr, gi), (ur_ref, ui_ref), (mr, mi))
-    backward(tile, (gr, gi), (hr, hi), (w0r, w0i), (w1r, w1i), (c1, s1), put_in(out_ref))
-
-
-def patch_kernel(sizes, phase_ref, measured_ref, known_ref, partner_ref, along_ref, same_ref, phase_rim_ref, rim_ref,
-                 own_ref, o0r, o0i, o1r, o1i, o2r, o2i, c1, s1,
-                 c0, s0, w0r, w0i, w1r, w1i, gr, gi, hr, hi, mr, mi, row_r, row_i, col_r, col_i):
+def patch_kernel(sizes, phase_ref, known_ref, partner_ref, along_ref, phase_rim_ref,
+                 w0r, w0i, w1r, w1i, ur_ref, ui_ref, c1, s1, c0, s0, hr, hi, row_r, row_i, col_r, col_i):
     stripe, tiles, total_rows, total_cols = sizes
-    tile, row_first, columns = patch_tile(sizes)
-    illum, _, _ = place()
-    low_illum = illum == 0
-    blank_rims((w0r, w0i, w1r, w1i, gr, gi, hr, hi, o0r, o0i, o1r, o1i), tile)
+    main, row_first, _ = main_tile(sizes)
+    held, columns = patch_held(sizes)
+    tile = Tile(stripe, 1, main.top, main.bottom, held, 0, (0,))
+    low_illum = place()[0] == 0
+    blank_rims((w0r, w0i, w1r, w1i, hr, hi), tile)
     trig = (c0, s0), (c1, s1)
-    first, last = 0, tiles - 1
+    end = stripe + RIM
 
     def joined(get, rim):
-        return join_edges(get(first), get(last), rim)
-
-    end = stripe + RIM
+        x = join_edges(get(0), get(tiles - 1), rim)
+        return join_illums(x, x)
+
     fill_trig(
         tile, trig, low_illum,
         lambda k, t, r: joined(lambda e: phase_ref[k, r : r + 16, own_columns(e)], phase_rim_ref[k, RIM + r : RIM + r + 16, :]),
@@ -585,83 +589,106 @@
             jnp.where(low_illum, phase_rim_ref[k, :RIM, :], phase_rim_ref[k, end:, :]),
         ),
     )
-    mine = illum * stripe
-    near_base = pl.multiple_of(stripe - 16 * illum, 16)
-    near_rim = pl.multiple_of(stripe - 8 * illum, 8)
-
-    def middle(part, t, r):
-        at = pl.ds(pl.multiple_of(mine + r, 16), 16)
-        return joined(lambda e: measured_ref[part, 0, at, own_columns(e)].astype(F32), rim_ref[part, at, :])
-
-    def near(t):
-        def rows(part, e):
-            x = measured_ref[part, 0, pl.ds(near_base, 16), own_columns(e)].astype(F32)
-            return jnp.where(low_illum, x[:8], x[8:])
-
-        return [joined(lambda e: rows(part, e), rim_ref[part, pl.ds(near_rim, 8), :]) for part in range(2)]
-
-    def far(t):
-        return joined(lambda e: same_ref[:, own_columns(e)], rim_ref[0, 2 * stripe :, :])
-
-    fill_target(tile, (mr, mi), low_illum, middle, near, far)
-    half = hr, hi
-    totals, tables = (total_rows, total_cols), (row_r, row_i, col_r, col_i)
+    note = jnp.where(patch_lanes()[0], 0.0, 1.0)
+    tilts = [a * note + b * (1.0 - note) for a, b in zip(tilts_of(known_ref[...]), tilts_of(partner_ref[:, 2 * tiles * LANES :]))]
     forward(
-        tile, partner_ref[:, 2 * tiles * LANES :], columns, row_first, totals, trig, half, tables,
-        (o0r, o0i), (o1r, o1i), keep_in((o2r, o2i)),
-    )
-    forward(
-        tile, known_ref[...], columns, row_first, totals, trig, half, tables,
-        (w0r, w0i), (w1r, w1i), residual_in((gr, gi), (mr, mi)),
-    )
-    backward(tile, (gr, gi), half, (w0r, w0i), (w1r, w1i), trig[1], put_in(own_ref))
-
-
-def finish_kernel(sizes, own_ref, other_ref, own_patch_ref, swap_ref, along_ref, rim_ref, sums_ref, far_sums_ref, partner_relay_ref,
-                  w0r, w0i, w1r, w1i, ur_ref, ui_ref, c1, s1, out_ref, other_patch, gr, gi, hr, hi, mr, mi):
+        tile, tilts, columns, row_first, (total_rows, total_cols), trig, (hr, hi), (row_r, row_i, col_r, col_i),
+        (w0r, w0i), (w1r, w1i), keep_in((ur_ref, ui_ref)),
+    )
+
+
+def sum_kernel(a_ref, b_ref, out_ref):
+    out_ref[...] = a_ref[...] + b_ref[...]
+
+
+class Joined:
+    def __init__(self, main, patch):
+        self.main, self.patch, self.tiles = main, patch, main.shape[0]
+
+    def __getitem__(self, at):
+        return self.main[at] if at[0] < self.tiles else self.patch[(0,) + at[1:]]
+
+
+def finish_kernel(sizes, own_ref, measured_ref, swap_ref, along_ref, same_ref, rim_ref, relay_ref, partner_relay_ref,
+                  *rest):
+    main_fields, patch_fields, rest = rest[:8], rest[8:16], rest[16:]
+    out_ref, patch, gr, gi, hr, hi, mr, mi, full, sems = rest
+    w0r, w0i, w1r, w1i, ur, ui, c1, s1 = [Joined(a, b) for a, b in zip(main_fields, patch_fields)]
     stripe, tiles, total_rows, total_cols = sizes
-    tile, _, _ = patch_tile(sizes)
+    main, _, _ = main_tile(sizes)
+    tile = Tile(stripe, tiles + 1, main.top, main.bottom, patch_held(sizes)[0], tiles, (tiles,))
     illum, _, _ = place()
     low_illum = illum == 0
     blank_rims((gr, gi, hr, hi), tile)
 
     lane = lane_ids((8, LANES))
-    sums = jnp.maximum(sums_ref[...], far_sums_ref[...])
+    sums = jnp.maximum(relay_ref[stripe + 8 :, :], partner_relay_ref[stripe + 8 :, :])
     scales = []
     for which in range(2):
-        here = jnp.where((lane >= 4 * which) & (lane < 4 * which + 4), sums, 0.0)
+        here = jnp.where(lane == which, sums, 0.0)
         energy = jnp.sum(here[:1], axis=1, keepdims=True) / (total_rows * total_cols) + EPS_ENERGY
         scales.append(2.0 / energy)
     mine = jnp.where(low_illum, scales[0], scales[1])
     others = jnp.where(low_illum, scales[1], scales[0])
+
     first, last = own_columns(0), own_columns(tiles - 1)
+    own_first = illum * stripe
+    near_base = pl.multiple_of(stripe - 16 * illum, 16)
+    near_rim = pl.multiple_of(stripe - 8 * illum, 8)
 
     def middle(part, t, r):
+        at = slice(part * stripe + r, part * stripe + r + 16)
+        if t < tiles:
+            return swap_ref[at, own_columns(t)]
         rim = partner_relay_ref[r : r + 16, :]
-        at = slice(part * stripe + r, part * stripe + r + 16)
-        return join_edges(swap_ref[at, first], swap_ref[at, last], pltpu.roll(rim, LANES // 2, 1) if part else rim)
+        other = join_edges(swap_ref[at, first], swap_ref[at, last], pltpu.roll(rim, LANES // 2, 1) if part else rim)
+        at = pl.ds(pl.multiple_of(own_first + r, 16), 16)
+        own = join_edges(*[measured_ref[part, 0, at, e].astype(F32) for e in (first, last)], rim_ref[part, at, :])
+        return join_illums(own, other)
 
     def near(t):
+        if t < tiles:
+            return other_near(swap_ref, stripe, low_illum, own_columns(t))
         rim = partner_relay_ref[stripe : stripe + 8, :]
         rims = [rim, pltpu.roll(rim, LANES // 2, 1)]
         west, east = [other_near(swap_ref, stripe, low_illum, at) for at in (first, last)]
-        return [join_edges(*x) for x in zip(west, east, rims)]
+        other = [join_edges(*x) for x in zip(west, east, rims)]
+
+        def rows(part, at):
+            x = measured_ref[part, 0, pl.ds(near_base, 16), at].astype(F32)
+            return jnp.where(low_illum, x[:8], x[8:])
+
+        own = [join_edges(rows(part, first), rows(part, last), rim_ref[part, pl.ds(near_rim, 8), :]) for part in range(2)]
+        return [join_illums(*x) for x in zip(own, other)]
 
     def far(t):
-        west, east = [along_ref[:, own_columns(e + 2 * tiles)] for e in (0, tiles - 1)]
-        return join_edges(west, east, rim_ref[1, 2 * stripe :, :])
+        if t < tiles:
+            return along_ref[:, own_columns(t + 2 * tiles)]
+        other = join_edges(*[along_ref[:, own_columns(e + 2 * tiles)] for e in (0, tiles - 1)], rim_ref[1, 2 * stripe :, :])
+        own = join_edges(same_ref[:, first], same_ref[:, last], rim_ref[0, 2 * stripe :, :])
+        return join_illums(own, other)
 
     fill_target(tile, (mr, mi), low_illum, middle, near, far)
-    residual_of(tile, (gr, gi), (ur_ref, ui_ref), (mr, mi))
-    backward(tile, (gr, gi), (hr, hi), (w0r, w0i), (w1r, w1i), (c1, s1), put_in(other_patch))
-
-    for k in range(2):
-        for t in range(tiles):
-            out_ref[k, :, own_columns(t)] = own_ref[k, :, own_columns(t)] * mine + other_ref[k, :, own_columns(t)] * others
-        patch = own_patch_ref[k] * mine + other_patch[k] * others
-        on = lane_ids(patch.shape)
-        out_ref[k, :, first] = jnp.where(on < RIM, patch, out_ref[k, :, first])
-        out_ref[k, :, last] = jnp.where(on >= LANES - RIM, pltpu.roll(patch, 56, 1), out_ref[k, :, last])
+    residual_of(tile, (gr, gi), (ur, ui), (mr, mi))
+
+    def put(k, t, rows, value):
+        rows = own_rows(rows)
+        if t == tiles:
+            patch[k, rows, :] = value * mine + pltpu.roll(value, LANES - OTHER, 1) * others
+            return
+        value = own_ref[k, rows, own_columns(t)] * mine + value * others
+        on = lane_ids(value.shape)
+        if t == 0:
+            value = jnp.where(on < RIM, patch[k, rows, :], value)
+        if t == tiles - 1:
+            value = jnp.where(on >= LANES - RIM, pltpu.roll(patch[k, rows, :], 56, 1), value)
+        full[k, rows, own_columns(t)] = value
+
+    copies = [pltpu.make_async_copy(full.at[k], out_ref.at[k], sems.at[k]) for k in range(2)]
+    backward(tile, (gr, gi), (hr, hi), (w0r, w0i), (w1r, w1i), (c1, s1), put, on_middle=copies[1].start)
+    copies[0].start()
+    for copy in copies:
+        copy.wait()
 
 
 def like(x, held):
@@ -669,13 +696,24 @@
     return pltpu.VMEM(shape, dtype) if held else jax.ShapeDtypeStruct(shape, dtype)
 
 
-def call(kernel, outs, *args, scratch=(), in_place=0, flops=0, mib=8, held=()):
+def after(kernel, *refs):
+    count = len(refs)
+
+    def ordered(*args):
+        return kernel(*args[count:])
+
+    return ordered
+
+
+def call(kernel, outs, *args, behind=(), scratch=(), in_place=0, flops=0, mib=8, held=(), far=0):
+    kernel, args = after(kernel, *behind), (*behind, *args)
+    in_place_specs = [pl.BlockSpec(memory_space=pltpu.HBM)] * in_place
     return pl.pallas_call(
         kernel,
         out_shape=[like(x, n in held) for n, x in enumerate(outs)],
-        in_specs=[pl.BlockSpec(memory_space=pltpu.HBM)] * in_place
+        in_specs=in_place_specs
         + [pl.BlockSpec(memory_space=pltpu.VMEM)] * (len(args) - in_place),
-        out_specs=[pl.BlockSpec(memory_space=pltpu.VMEM)] * len(outs),
+        out_specs=[pl.BlockSpec(memory_space=pltpu.VMEM)] * (len(outs) - far) + [pl.BlockSpec(memory_space=pltpu.HBM)] * far,
         scratch_shapes=[pltpu.VMEM(s, F32) if isinstance(s, tuple) else s for s in scratch],
         compiler_params=pltpu.CompilerParams(vmem_limit_bytes=int(mib * 2**20)),
         cost_estimate=pl.CostEstimate(flops=flops, bytes_accessed=2**18, transcendentals=0),
@@ -693,60 +731,63 @@
         along += [(rows + r, (r + 1) % rows), ((r + 1) % rows, rows + r)]
     same = [(r, (r + 1) % rows) for r in range(rows)] + [(rows + (r + 1) % rows, rows + r) for r in range(rows)]
 
-    partner_out, along_out, same_out, known, measured = call(
-        open_kernel, [(8, 2 * width + LANES), (8, 3 * width + LANES), (8, width + LANES), (8, LANES), measured],
-        phase_delay, measured, angles, in_place=3, mib=62, held=(4,),
+    partner_out, along_out, same_out, known, note, measured = call(
+        open_kernel, [(8, 2 * width + LANES), (8, 3 * width), (8, width), (8, LANES), (8, LANES), measured],
+        phase_delay, measured, angles, in_place=3, mib=62, held=(5,),
         scratch=[
-            (2, slices, 8, width),
-            pltpu.VMEM(angles.shape, angles.dtype), pltpu.SemaphoreType.DMA((4,)),
+            (2, slices, 8, width), pltpu.VMEM(angles.shape, angles.dtype), pltpu.SemaphoreType.DMA((4,)),
         ],
     )
     along_in = lax.ppermute(along_out, ("illum", "row"), along)
     partner_in = lax.ppermute(partner_out, "illum", swap)
     same_in = lax.ppermute(same_out, ("illum", "row"), same)
-    (swap_out,) = call(swap_kernel, [(2 * stripe + 8, width)], measured, same_in)
+    core_note = lax.ppermute(note, "row", [(r, r ^ 1) for r in range(rows)])
+    (pair,) = call(sum_kernel, [(8, LANES)], note, core_note)
+    far = lax.ppermute(pair, "row", [(r, r ^ 2) for r in range(rows)])
+    (swap_out,) = call(swap_kernel, [(2 * stripe + 8, width)], measured, core_note)
     swap_in = lax.ppermute(swap_out, "illum", swap)
+    def fields(count):
+        return [(count, stripe + 4 * RIM, LANES)]
+
+    def tables(count):
+        return [(stripe + 2 * RIM, LANES)] * 2 + [(-(-count // 8) * 8, LANES)] * 2
+
+    own_trig = call(trig_kernel, [(tiles, stripe, LANES)] * 4, phase_delay, flops=10**9)
     rims = 8 * (-(-(stripe // 4 + 1) // 4))
     first_out, second_packed, note = call(
-        rim_pack_kernel, [(rims + 8, LANES), (rims, LANES), (8, LANES)], phase_delay, measured, known, partner_in, along_in, same_in
+        rim_pack_kernel, [(rims + 8, LANES), (rims, LANES), (8, LANES)], phase_delay, measured, pair, far, partner_in, along_in, same_in,
+        behind=own_trig[:1],
     )
     first_in = lax.ppermute(first_out, "col", [(c, c ^ 1) for c in range(cols)])
-    (second_out,) = call(second_kernel, [(rims + 8, LANES)], second_packed, note, first_in)
-    second_in = lax.ppermute(second_out, "col", [(c, cols - 1 - c) for c in range(cols)])
-
-    def fields(count):
-        return [(count, stripe + 4 * RIM, LANES)]
-
-    def tables(count):
-        return [(stripe + 2 * RIM, LANES)] * 2 + [(-(-count // 8) * 8, LANES)] * 2
-
-    rows_in = phase_delay, measured, known, partner_in, along_in, same_in
-    own_trig = call(trig_kernel, [(tiles, stripe, LANES)] * 4, phase_delay, flops=10**9)
     kept = call(
         functools.partial(ahead_kernel, sizes), fields(tiles) * 10, *own_trig, partner_in, along_in,
         scratch=fields(tiles) * 2 + tables(tiles), flops=15*10**8, mib=16,
     )
+    (second_out,) = call(second_kernel, [(rims + 8, LANES)], second_packed, note, first_in, behind=kept[:1])
+    second_in = lax.ppermute(second_out, "col", [(c, cols - 1 - c) for c in range(cols)])
+
+    own_kept = call(
+        functools.partial(own_kernel, sizes), fields(tiles) * 6, *kept[:4], measured, known, same_in,
+        scratch=fields(tiles) * 4 + tables(tiles), flops=15*10**8, mib=16,
+    )
+    phase_rim, rim, relay = call(
+        rim_unpack_kernel, [(2, stripe + 2 * RIM, LANES), (2, 2 * stripe + 8, LANES), (stripe + 16, LANES)],
+        first_in, second_in, note,
+        behind=own_kept[:1],
+    )
+    partner_relay = lax.ppermute(relay, "illum", swap)
     (own,) = call(
-        functools.partial(own_kernel, sizes), [phase_delay.shape], *kept[:4], measured, known, same_in,
-        scratch=fields(tiles) * 10 + tables(tiles), flops=3*10**9, mib=16,
-    )
-    phase_rim, rim, relay, sums = call(
-        rim_unpack_kernel, [(2, stripe + 2 * RIM, LANES), (2, 2 * stripe + 8, LANES), (stripe + 8, LANES), (8, LANES)], first_in, second_in, note
-    )
-    partner_relay = lax.ppermute(relay, "illum", swap)
-    far_sums = lax.ppermute(sums, "row", [(r, r ^ 2) for r in range(rows)])
-    (other,) = call(
-        functools.partial(other_kernel, sizes), [phase_delay.shape], swap_in, along_in, sums, *kept[4:], *kept[2:4],
-        scratch=fields(tiles) * 6, flops=10**9, mib=12,
-    )
-    own_patch, *patch_kept = call(
-        functools.partial(patch_kernel, sizes), [(slices, stripe, LANES)] + fields(1) * 8, *rows_in, phase_rim, rim,
-        scratch=fields(1) * 12 + tables(1), flops=10**9,
+        functools.partial(back_kernel, sizes), [phase_delay.shape], *kept[2:4], *own_kept,
+        scratch=fields(tiles) * 4, flops=10**9, mib=12, behind=[relay],
+    )
+    patch_kept = call(
+        functools.partial(patch_kernel, sizes), fields(1) * 8, phase_delay, known, partner_in, along_in, phase_rim,
+        scratch=fields(1) * 4 + tables(1), flops=10**9, behind=[own],
     )
     (out,) = call(
         functools.partial(finish_kernel, sizes), [phase_delay.shape],
-        own, other, own_patch, swap_in, along_in, rim, sums, far_sums, partner_relay, *patch_kept,
-        scratch=[(slices, stripe, LANES)] + fields(1) * 6,
+        own, measured, swap_in, along_in, same_in, rim, relay, partner_relay, *kept[4:], *kept[2:4], *patch_kept,
+        scratch=[(slices, stripe, LANES)] + fields(tiles + 1) * 6 + [phase_delay.shape, pltpu.SemaphoreType.DMA((slices,))], mib=12, flops=0, far=1,
     )
     return out
 

time: 29.3 us -> 27.4 us (0.935)
  waiting for transfers between devices: 4.02 us -> 1.84 us
  starting transfers between devices: 13.3 us -> 14 us
  Pallas kernels: 11.7 us -> 11.3 us
    ppermute x1, waiting for transfers between devices: 3.54 us -> 0.01 us  [paired(): partner_in = lax.ppermute(partner_out, 'illum', swap)]
    ppermute x1 -> x2, waiting for transfers between devices: 0.01 us -> 0.68 us  [the longest x1 0.52 us: paired(): far = lax.ppermute(pair, 'row', [(r, r ^ 2) for r in range(rows)])]
    ppermute x1, starting transfers between devices: 0.7 us -> 1.21 us  [paired(): partner_in = lax.ppermute(partner_out, 'illum', swap)]
    ppermute x1, starting transfers between devices: 0.5 us -> 0.01 us  [paired(): same_in = lax.ppermute(same_out, ('illum', 'row'), same)]
    ppermute x1 -> x2, starting transfers between devices: 0.47 us -> 0.9 us  [the longest x1 0.9 us: paired(): far = lax.ppermute(pair, 'row', [(r, r ^ 2) for r in range(rows)])]
    pallas_call x11 -> x12, Pallas kernels: 11.7 us -> 11.3 us  [call(): pl.pallas_call(kernel, out_shape=[like(x, n in held) for n, x in enumerat...]
    ppermute x1, waiting for transfers between devices: 0.01 us -> 0.38 us  [paired(): partner_relay = lax.ppermute(relay, 'illum', swap)]
    ppermute x1, starting transfers between devices: 1.41 us -> 1.75 us  [paired(): swap_in = lax.ppermute(swap_out, 'illum', swap)]
  transfers between devices with their start and end apart: 8 -> 9, of which waited for: 2 -> 5; matrix products, arithmetic and copies ran while one was open for 0% -> 0% of each run, Pallas kernels for 28% -> 24%
where the time goes in v6:
time: 27.4 us; the launch traced here: 27.3 us
  starting transfers between devices  14 us (51%)
  Pallas kernels  11.3 us (41%)
  waiting for transfers between devices  1.84 us (7%)
    pallas_call x12, Pallas kernels, call(): pl.pallas_call(kernel, out_shape=[like(x, n in held) for n, x in enumerat...  11.3 us
    ppermute x1, starting transfers between devices, paired(): lax.ppermute(second_out, 'col', [(c, cols - 1 - c) for c in range(cols)])  3.6 us
    ppermute x1, starting transfers between devices, paired(): along_in = lax.ppermute(along_out, ('illum', 'row'), along)  3.4 us
    ppermute x1, starting transfers between devices, paired(): swap_in = lax.ppermute(swap_out, 'illum', swap)  1.75 us
    ppermute x1, starting transfers between devices, paired(): first_in = lax.ppermute(first_out, 'col', [(c, c ^ 1) for c in range(cols)])  1.64 us
    ppermute x1, starting transfers between devices, paired(): partner_relay = lax.ppermute(relay, 'illum', swap)  1.51 us
    ppermute x1, starting transfers between devices, paired(): partner_in = lax.ppermute(partner_out, 'illum', swap)  1.21 us
    ppermute x1, starting transfers between devices, paired(): far = lax.ppermute(pair, 'row', [(r, r ^ 2) for r in range(rows)])  0.9 us
  transfers between devices with their start and end apart: 9, of which 5 were waited for; matrix products, arithmetic and copies ran while one was open for 0% of the time, Pallas kernels for 24%

profile of v6, /device:TPU:0, one launch (start us, length us, event | category | flops | bytes accessed | tf_op | source)
XLA Modules:
  0.0 27.3 jit_solution(16375575609126847893)
XLA Ops:
  0.0 2.1 %shard_map.38 = (f32[8,2176]{1,0:T(8,128)}, f32[8,3072]{1,0:T(8,128)}, f32[8,1024]{1,0:T(8,128)}, f32[8,128]{1,0:T(8,128)}, f32[8,128]{1,0:T(8,128)}, /*index=5*/bf16[2,1,128,1024]{3,2,1,0:T(8,128)(2,1)S(1)}) custom-call(f32[2,64,1024]{2,1,0:T(8,128)} %args_1_.8, bf16[2,1,128,1024]{3,2,1,0:T(8,128)(2,1)} %args_1_.6, s32[1,2]{1,0:T(1,128)} %args_2_.4), custom_call_target="tpu_custom_call" | custom-call | bytes 262144 | tf_op jit(solution)/shard_map/pallas_call | solution.py:711
  2.1 0.0 copy-start.1
  2.1 3.4 %collective-permute-start.1 = (f32[8,3072]{1,0:T(8,128)}, f32[8,3072]{1,0:T(8,128)S(1)}, u32[]{:S(2)}, u32[]{:S(2)}) collective-permute-start(f32[8,3072]{1,0:T(8,128)} %get-tuple-element.50), channel_id=1, source_target_pairs={{16,4},{4,16},{20,8},{8,20},{24,12},{12,24},{28,0},{0,28},{17,5},{... | collective-permute-start | bytes 294920 | tf_op jit(solution)/shard_map/ppermute | solution.py:741
  5.5 0.0 collective-permute-start.3
  5.5 1.2 %collective-permute-start = (f32[8,2176]{1,0:T(8,128)}, f32[8,2176]{1,0:T(8,128)S(1)}, u32[]{:S(2)}, u32[]{:S(2)}) collective-permute-start(f32[8,2176]{1,0:T(8,128)} %get-tuple-element.49), channel_id=1, source_target_pairs={{0,16},{16,0},{1,17},{17,1},{2,18},{18,2},{3,19},{19,3},{4,20},{20... | collective-permute-start | bytes 208904 | tf_op jit(solution)/shard_map/ppermute | solution.py:742
  6.7 0.0 collective-permute-start.2
  6.7 0.2 collective-permute-done.3.args_1_
  6.9 0.0 copy-done.1
  6.9 0.9 %collective-permute-start.4 = (f32[8,128]{1,0:T(8,128)S(1)}, f32[8,128]{1,0:T(8,128)S(1)}, u32[]{:S(2)}, u32[]{:S(2)}) collective-permute-start(f32[8,128]{1,0:T(8,128)S(1)} %shard_map.41.args_3_), channel_id=1, source_target_pairs={{0,8},{4,12},{8,0},{12,4},{1,9},{5,13},{9,1},{13,5},{2,10},{6,14},... | collective-permute-start | bytes 12296 | tf_op jit(solution)/shard_map/ppermute | solution.py:746
  7.8 0.0 copy-start
  7.8 1.7 %collective-permute-start.7 = (f32[136,1024]{1,0:T(8,128)S(1)}, f32[136,1024]{1,0:T(8,128)S(1)}, u32[]{:S(2)}, u32[]{:S(2)}) collective-permute-start(f32[136,1024]{1,0:T(8,128)S(1)} %shard_map.46), channel_id=1, source_target_pairs={{0,16},{16,0},{1,17},{17,1},{2,18},{18,2},{3,19},{19,3},{4,20},{20... | collective-permute-start | bytes 1671176 | tf_op jit(solution)/shard_map/ppermute | solution.py:748
  9.6 0.0 copy-done
  9.6 0.4 %shard_map.37 = (f32[8,64,128]{2,1,0:T(8,128)S(1)}, f32[8,64,128]{2,1,0:T(8,128)S(1)}, f32[8,64,128]{2,1,0:T(8,128)S(1)}, f32[8,64,128]{2,1,0:T(8,128)S(1)}) custom-call(f32[2,64,1024]{2,1,0:T(8,128)S(1)} %copy-done), custom_call_target="tpu_custom_call" | custom-call | flops 1000000000 | bytes 262144 | tf_op jit(solution)/shard_map/pallas_call | solution.py:711
  10.0 0.5 %collective-permute-done.4.args_4_ = f32[8,128]{1,0:T(8,128)S(1)} collective-permute-done((f32[8,128]{1,0:T(8,128)S(1)}, f32[8,128]{1,0:T(8,128)S(1)}, u32[]{:S(2)}, u32[]{:S(2)}) %collective-permute-start.4) | collective-permute-done | bytes 4128 | tf_op jit(solution)/shard_map/ppermute | solution.py:746
  10.5 0.0 collective-permute-done.2.args_6_.args_7_.args_4_
  10.5 0.0 collective-permute-done.args_4_.args_5_.args_3_
  10.5 0.0 collective-permute-done.1.args_5_.args_6_.args_4_.args_3_
  10.5 0.1 shard_map.42
  10.7 1.6 %collective-permute-start.5 = (f32[48,128]{1,0:T(8,128)S(1)}, f32[48,128]{1,0:T(8,128)S(1)}, u32[]{:S(2)}, u32[]{:S(2)}) collective-permute-start(f32[48,128]{1,0:T(8,128)S(1)} %get-tuple-element.60), channel_id=1, source_target_pairs={{0,1},{1,0},{2,3},{3,2},{4,5},{5,4},{6,7},{7,6},{8,9},{9,8},{10,11... | collective-permute-start | bytes 73736 | tf_op jit(solution)/shard_map/ppermute | solution.py:761
  12.3 1.8 %shard_map.39 = (f32[8,96,128]{2,1,0:T(8,128)S(1)}, f32[8,96,128]{2,1,0:T(8,128)S(1)}, f32[8,96,128]{2,1,0:T(8,128)S(1)}, f32[8,96,128]{2,1,0:T(8,128)S(1)}, f32...) custom-call(f32[8,64,128]{2,1,0:T(8,128)S(1)} %get-tuple-element.45., ...), custom_call_target="tpu_custom_call" | custom-call | flops 1500000000 | bytes 262144 | tf_op jit(solution)/shard_map/pallas_call | solution.py:711
  14.1 0.5 %collective-permute-done.5.args_3_.args_1_ = f32[48,128]{1,0:T(8,128)S(1)} collective-permute-done((f32[48,128]{1,0:T(8,128)S(1)}, f32[48,128]{1,0:T(8,128)S(1)}, u32[]{:S(2)}, u32[]{:S(2)}) %collective-permute-start.5) | collective-permute-done | bytes 24608 | tf_op jit(solution)/shard_map/ppermute | solution.py:761
  14.6 0.0 copy-start.2
  14.6 3.6 %collective-permute-start.6 = (f32[48,128]{1,0:T(8,128)S(1)}, f32[48,128]{1,0:T(8,128)S(1)}, u32[]{:S(2)}, u32[]{:S(2)}) collective-permute-start(f32[48,128]{1,0:T(8,128)S(1)} %shard_map.43), channel_id=1, source_target_pairs={{0,3},{1,2},{2,1},{3,0},{4,7},{5,6},{6,5},{7,4},{8,11},{9,10},{10,... | collective-permute-start | bytes 73736 | tf_op jit(solution)/shard_map/ppermute | solution.py:767
  18.2 0.0 copy-done.2
  18.2 1.7 %shard_map.40 = (f32[8,96,128]{2,1,0:T(8,128)S(1)}, f32[8,96,128]{2,1,0:T(8,128)S(1)}, f32[8,96,128]{2,1,0:T(8,128)S(1)}, f32[8,96,128]{2,1,0:T(8,128)S(1)}, f32...) custom-call(f32[8,96,128]{2,1,0:T(8,128)S(1)} %get-tuple-element.51.args_0_, ...), custom_call_target="tpu_custom_call" | custom-call | flops 1500000000 | bytes 262144 | tf_op jit(solution)/shard_map/pallas_call | solution.py:711
  19.9 0.3 %collective-permute-done.6.args_2_ = f32[48,128]{1,0:T(8,128)S(1)} collective-permute-done((f32[48,128]{1,0:T(8,128)S(1)}, f32[48,128]{1,0:T(8,128)S(1)}, u32[]{:S(2)}, u32[]{:S(2)}) %collective-permute-start.6) | collective-permute-done | bytes 24608 | tf_op jit(solution)/shard_map/ppermute | solution.py:767
  20.2 0.2 shard_map.44
  20.4 1.5 %collective-permute-start.8 = (f32[80,128]{1,0:T(8,128)S(1)}, f32[80,128]{1,0:T(8,128)S(1)}, u32[]{:S(2)}, u32[]{:S(2)}) collective-permute-start(f32[80,128]{1,0:T(8,128)S(1)} %get-tuple-element.63.args_0_.args_6_), channel_id=1, source_target_pairs={{0,16},{16,0},{1,17},{17,1},{2,18},{18,2},{3,19},{19,3},{4,20},{20... | collective-permute-start | bytes 122888 | tf_op jit(solution)/shard_map/ppermute | solution.py:778
  21.9 1.4 %shard_map.45.args_0_ = f32[2,64,1024]{2,1,0:T(8,128)S(1)} custom-call(f32[80,128]{1,0:T(8,128)S(1)} %get-tuple-element.63.args_0_.args_6_, f32[8,96,128]{2,1,0:T(8,128)S(1)} %get-tuple-element.53.args_2_.args_1_.args_14_, f32[8,96,128]{2,1,0:T(8,128)S(1)} %get-tuple-element.54.args_3_.args_2_.args_15_, f32[8,96,128]{2,1,0:T(8,128)S(1)} %get-tuple-element.58.args_0_.args_3_, ...), custom_call_target="tpu_custom_call" | custom-call | flops 1000000000 | bytes 262144 | tf_op jit(solution)/shard_map/pallas_call | solution.py:711
  23.3 0.8 %shard_map.47 = (f32[1,96,128]{2,1,0:T(8,128)S(1)}, f32[1,96,128]{2,1,0:T(8,128)S(1)}, f32[1,96,128]{2,1,0:T(8,128)S(1)}, f32[1,96,128]{2,1,0:T(8,128)S(1)}, f32...) custom-call(f32[2,64,1024]{2,1,0:T(8,128)S(1)} %shard_map.45.args_0_,, ...), custom_call_target="tpu_custom_call" | custom-call | flops 1000000000 | bytes 262144 | tf_op jit(solution)/shard_map/pallas_call | solution.py:711
  24.1 0.4 %collective-permute-done.8.args_7_ = f32[80,128]{1,0:T(8,128)S(1)} collective-permute-done((f32[80,128]{1,0:T(8,128)S(1)}, f32[80,128]{1,0:T(8,128)S(1)}, u32[]{:S(2)}, u32[]{:S(2)}) %collective-permute-start.8) | collective-permute-done | bytes 40992 | tf_op jit(solution)/shard_map/ppermute | solution.py:778
  24.5 0.0 collective-permute-done.7.args_2_
  24.5 2.8 %shard_map.48 = f32[2,64,1024]{2,1,0:T(8,128)} custom-call(f32[2,64,1024]{2,1,0:T(8,128)S(1)} %shard_map.45.args_0_, bf16[2,1,128,1024]{3,2,1,0:T(8,128)(2,1)S(1)} %get-tuple-element.55.args_4_.args_2_.args_0_.args_1_, f32[136,1024]{1,0:T(8,128)S(1)} %collective-permute-done.7.args_2_, f32[8,3072]{1,0:T(8,128)S(1)} %collective-permute-done.1.args_5_.args_6_.args_4_.args_3_, ...), custom_call_target="tpu_custom_call" | custom-call | bytes 262144 | tf_op jit(solution)/shard_map/pallas_call | solution.py:711
  (3 shorter events, 0.1 us)
Async XLA Ops:
  2.1 4.8 %copy-start.1 = (f32[8,128]{1,0:T(8,128)S(1)}, f32[8,128]{1,0:T(8,128)}, u32[]{:S(2)}) copy-start(f32[8,128]{1,0:T(8,128)} %get-tuple-element.59.args_0_) | copy-start | bytes 12292
  2.1 8.4 %collective-permute-start.1 = (f32[8,3072]{1,0:T(8,128)}, f32[8,3072]{1,0:T(8,128)S(1)}, u32[]{:S(2)}, u32[]{:S(2)}) collective-permute-start(f32[8,3072]{1,0:T(8,128)} %get-tuple-element.50), channel_id=1, source_target_pairs={{16,4},{4,16},{20,8},{8,20},{24,12},{12,24},{28,0},{0,28},{17,5},{... | collective-permute-start | bytes 294920 | tf_op jit(solution)/shard_map/ppermute | solution.py:741
  5.5 1.4 %collective-permute-start.3 = (f32[8,128]{1,0:T(8,128)}, f32[8,128]{1,0:T(8,128)S(1)}, u32[]{:S(2)}, u32[]{:S(2)}) collective-permute-start(f32[8,128]{1,0:T(8,128)} %get-tuple-element.59.args_0_), channel_id=1, source_target_pairs={{0,4},{4,0},{8,12},{12,8},{1,5},{5,1},{9,13},{13,9},{2,6},{6,2},{1... | collective-permute-start | bytes 12296 | tf_op jit(solution)/shard_map/ppermute | solution.py:744
  5.5 5.0 %collective-permute-start = (f32[8,2176]{1,0:T(8,128)}, f32[8,2176]{1,0:T(8,128)S(1)}, u32[]{:S(2)}, u32[]{:S(2)}) collective-permute-start(f32[8,2176]{1,0:T(8,128)} %get-tuple-element.49), channel_id=1, source_target_pairs={{0,16},{16,0},{1,17},{17,1},{2,18},{18,2},{3,19},{19,3},{4,20},{20... | collective-permute-start | bytes 208904 | tf_op jit(solution)/shard_map/ppermute | solution.py:742
  6.7 3.8 %collective-permute-start.2 = (f32[8,1024]{1,0:T(8,128)}, f32[8,1024]{1,0:T(8,128)S(1)}, u32[]{:S(2)}, u32[]{:S(2)}) collective-permute-start(f32[8,1024]{1,0:T(8,128)} %get-tuple-element.57), channel_id=1, source_target_pairs={{0,4},{4,8},{8,12},{12,0},{20,16},{24,20},{28,24},{16,28},{1,5},{5... | collective-permute-start | bytes 98312 | tf_op jit(solution)/shard_map/ppermute | solution.py:743
  6.9 3.6 %collective-permute-start.4 = (f32[8,128]{1,0:T(8,128)S(1)}, f32[8,128]{1,0:T(8,128)S(1)}, u32[]{:S(2)}, u32[]{:S(2)}) collective-permute-start(f32[8,128]{1,0:T(8,128)S(1)} %shard_map.41.args_3_), channel_id=1, source_target_pairs={{0,8},{4,12},{8,0},{12,4},{1,9},{5,13},{9,1},{13,5},{2,10},{6,14},... | collective-permute-start | bytes 12296 | tf_op jit(solution)/shard_map/ppermute | solution.py:746
  7.8 1.8 %copy-start = (f32[2,64,1024]{2,1,0:T(8,128)S(1)}, f32[2,64,1024]{2,1,0:T(8,128)}, u32[]{:S(2)}) copy-start(f32[2,64,1024]{2,1,0:T(8,128)} %args_1_.8) | copy-start | bytes 1572868
  7.8 16.6 %collective-permute-start.7 = (f32[136,1024]{1,0:T(8,128)S(1)}, f32[136,1024]{1,0:T(8,128)S(1)}, u32[]{:S(2)}, u32[]{:S(2)}) collective-permute-start(f32[136,1024]{1,0:T(8,128)S(1)} %shard_map.46), channel_id=1, source_target_pairs={{0,16},{16,0},{1,17},{17,1},{2,18},{18,2},{3,19},{19,3},{4,20},{20... | collective-permute-start | bytes 1671176 | tf_op jit(solution)/shard_map/ppermute | solution.py:748
  10.7 3.9 %collective-permute-start.5 = (f32[48,128]{1,0:T(8,128)S(1)}, f32[48,128]{1,0:T(8,128)S(1)}, u32[]{:S(2)}, u32[]{:S(2)}) collective-permute-start(f32[48,128]{1,0:T(8,128)S(1)} %get-tuple-element.60), channel_id=1, source_target_pairs={{0,1},{1,0},{2,3},{3,2},{4,5},{5,4},{6,7},{7,6},{8,9},{9,8},{10,11... | collective-permute-start | bytes 73736 | tf_op jit(solution)/shard_map/ppermute | solution.py:761
  14.6 3.6 %copy-start.2 = (f32[8,128]{1,0:T(8,128)S(1)}, f32[8,128]{1,0:T(8,128)}, u32[]{:S(2)}) copy-start(f32[8,128]{1,0:T(8,128)} %get-tuple-element.56.args_5_.args_2_) | copy-start | bytes 12292
  14.6 5.6 %collective-permute-start.6 = (f32[48,128]{1,0:T(8,128)S(1)}, f32[48,128]{1,0:T(8,128)S(1)}, u32[]{:S(2)}, u32[]{:S(2)}) collective-permute-start(f32[48,128]{1,0:T(8,128)S(1)} %shard_map.43), channel_id=1, source_target_pairs={{0,3},{1,2},{2,1},{3,0},{4,7},{5,6},{6,5},{7,4},{8,11},{9,10},{10,... | collective-permute-start | bytes 73736 | tf_op jit(solution)/shard_map/ppermute | solution.py:767
  20.4 4.1 %collective-permute-start.8 = (f32[80,128]{1,0:T(8,128)S(1)}, f32[80,128]{1,0:T(8,128)S(1)}, u32[]{:S(2)}, u32[]{:S(2)}) collective-permute-start(f32[80,128]{1,0:T(8,128)S(1)} %get-tuple-element.63.args_0_.args_6_), channel_id=1, source_target_pairs={{0,16},{16,0},{1,17},{17,1},{2,18},{18,2},{3,19},{19,3},{4,20},{20... | collective-permute-start | bytes 122888 | tf_op jit(solution)/shard_map/ppermute | solution.py:778

commit v7 on v6

--- a/solution.py
+++ b/solution.py
@@ -47,6 +47,7 @@
         self.rows = stripe + 2 * RIM
         self.top, self.bottom, self.lanes, self.rim = top, bottom, lanes, rim
         self.alone = alone
+        self.order = [*alone, *range(1, tiles - len(alone)), *([0] if tiles > len(alone) else [])]
         self.owned = tiles if rim in alone or rim is None else tiles - 1
         step = 32 if stripe % 32 == 0 else 8
         self.inner = [(2 * RIM + r, step, None) for r in range(0, stripe, step)]
@@ -63,7 +64,7 @@
                     held[key] = ref[t, rows, :]
                 return held[key]
 
-            for t in [*self.alone, *range(self.tiles - len(self.alone))]:
+            for t in self.order:
 
                 def mask(x, factor=factor, lanes=self.lanes if t == self.rim else None):
                     x = x if factor is None else x * factor
@@ -147,7 +148,7 @@
     return use
 
 
-def backward(tile, adjoint, half, w0, w1, trig1, put, between=None, on_middle=None):
+def backward(tile, adjoint, half, w0, w1, trig1, put, between=None, on_middle=None, on_rows=None):
     between = between or adjoint
     gr, gi = between
     inner = [first for first, _, _ in tile.inner]
@@ -168,7 +169,10 @@
     if on_middle:
         on_middle()
     first_half(tile, between, half, -1.0, tile.blocks)
-    second_half(tile, between, half, tile.inner, last)
+    for block in tile.inner if on_rows is None else [(r, 16, None) for r in range(2 * RIM, 2 * RIM + tile.stripe, 16)]:
+        second_half(tile, between, half, [block], last)
+        if on_rows:
+            on_rows(block[0] - 2 * RIM)
 
 
 def own_columns(t):
@@ -291,16 +295,16 @@
     known_ref[...] = note
 
 
-def swap_kernel(measured_ref, same_ref, swap_ref):
+def swap_kernel(columns, measured_ref, swap_ref):
     stripe = measured_ref.shape[2] // 2
     illum, _, _ = place()
     other = pl.multiple_of((1 - illum) * stripe, 16)
     for p in range(2):
         for r in range(0, stripe, 16):
             at = pl.ds(pl.multiple_of(other + r, 16), 16)
-            swap_ref[p * stripe + r : p * stripe + r + 16, :] = measured_ref[p, 0, at, :].astype(F32)
-    above = pack_rows(*edge_blocks(measured_ref, stripe - 8), False)
-    below = pack_rows(*edge_blocks(measured_ref, stripe), True)
+            swap_ref[p * stripe + r : p * stripe + r + 16, :] = measured_ref[p, 0, at, columns].astype(F32)
+    above = pack_rows(*[x[:, columns] for x in edge_blocks(measured_ref, stripe - 8)], False)
+    below = pack_rows(*[x[:, columns] for x in edge_blocks(measured_ref, stripe)], True)
     swap_ref[2 * stripe :, :] = jnp.where(illum == 0, above, below)
 
 
@@ -349,8 +353,8 @@
             yield 2 * g, acc
 
     for (at, east), (_, west) in zip(packed(True), packed(False)):
-        first_ref[at : at + 8, :] = jnp.where(even, east, west)
-        second_ref[at : at + 8, :] = jnp.where(even, west, east)
+        first_ref[at : at + 8, :] = jnp.where(even, west, east)
+        second_ref[at : at + 8, :] = jnp.where(even, east, west)
 
 
 def second_kernel(packed_ref, note_ref, first_ref, out_ref):
@@ -369,7 +373,7 @@
     in_east = (lane < RIM) & (col < lax.axis_size("col") - 1)
     for g in range(0, rows // 8 + 1, 4):
         first, second = first_ref[2 * g : 2 * g + 8, :], second_ref[2 * g : 2 * g + 8, :]
-        a, b = jnp.where(even, second, first), jnp.where(even, first, second)
+        a, b = jnp.where(even, first, second), jnp.where(even, second, first)
         for j in range(g, min(g + 4, rows // 8 + 1)):
             for k in range(4):
                 if k < 2 and j >= stripe // 8 + 2:
@@ -381,18 +385,23 @@
                 (phase_rim_ref if k < 2 else rim_ref)[k % 2, 8 * j : 8 * j + 8, :] = item
     other = pl.multiple_of((1 - illum) * stripe, 8)
     near = pl.multiple_of(stripe - 8 + 8 * illum, 8)
-    for r in range(0, stripe + 8, 8):
-        at = pl.ds(pl.multiple_of(other + r, 8) if r < stripe else near, 8)
-        relay_ref[r : r + 8, :] = rim_ref[0, at, :] + pltpu.roll(rim_ref[1, at, :], LANES // 2, 1)
-    relay_ref[stripe + 8 :, :] = note_ref[...] + first_ref[rims:, :] + second_ref[rims:, :]
-
-
-def fill_target(tile, target, low_illum, middle, near, far):
+    blocks = [pl.multiple_of(other + r, 8) for r in range(0, stripe, 8)] + [near]
+    for g in range(0, len(blocks), 4):
+        packed = jnp.zeros((8, LANES), F32)
+        for q, first in enumerate(blocks[g : g + 4]):
+            at = pl.ds(first, 8)
+            x = rim_ref[0, at, :] + pltpu.roll(rim_ref[1, at, :], LANES // 2, 1)
+            packed = packed + (pltpu.roll(x, 2 * RIM * q, 1) if q else x)
+        relay_ref[2 * g : 2 * g + 8, :] = packed
+    relay_ref[relay_ref.shape[0] - 8 :, :] = note_ref[...] + first_ref[rims:, :] + second_ref[rims:, :]
+
+
+def fill_target(tile, target, low_illum, middle, near, far, plain=()):
     end = 2 * RIM + tile.stripe
     for t in range(tile.tiles):
         beside_rows, packed = near(t), far(t)
         for part, ref in enumerate(target):
-            for r in range(0, tile.stripe, 16):
+            for r in range(0, tile.stripe, 16) if t not in plain else ():
                 ref[t, 2 * RIM + r : 2 * RIM + r + 16, :] = middle(part, t, r)
             ref[t, RIM : 2 * RIM, :] = jnp.where(low_illum, unpack_rows(packed, False)[part], beside_rows[part])
             ref[t, end : end + RIM, :] = jnp.where(low_illum, beside_rows[part], unpack_rows(packed, True)[part])
@@ -415,6 +424,10 @@
 
 def forward(tile, tilts, columns, row_first, totals, trig, half, tables, w0, w1, use):
     incident_tables(tile, tilts, row_first, columns, *totals, tables)
+    propagate(tile, tables, trig, half, w0, w1, use)
+
+
+def propagate(tile, tables, trig, half, w0, w1, use):
     enter(tile, tables, trig[0], w0)
     first_half(tile, w0, half, 1.0, tile.blocks)
     second_half(tile, w0, half, tile.blocks, modulate_into(trig[1], w1))
@@ -440,8 +453,8 @@
 
 def residual_of(tile, field, exit_field, target):
     def body(t, rows, mask, _):
-        for g, u, m in zip(field, exit_field, target):
-            g[t, rows, :] = mask(u[t, rows, :] - m[t, rows, :])
+        for part, (g, u) in enumerate(zip(field, exit_field)):
+            g[t, rows, :] = mask(u[t, rows, :] - target(part, t, rows))
 
     tile.sweep(body, tile.blocks)
 
@@ -492,7 +505,18 @@
     return jnp.where(patch_lanes()[0], pltpu.roll(other, OTHER, 1), own)
 
 
-def trig_kernel(phase_ref, c0, s0, c1, s1):
+def trig_kernel(sizes, phase_ref, measured_ref, known_ref, c0, s0, c1, s1, mr, mi, row_r, row_i, col_r, col_i):
+    stripe, tiles, total_rows, total_cols = sizes
+    tile, row_first, col_first = main_tile(sizes)
+    illum, _, _ = place()
+    columns = rim_columns(tile, col_first, col_r.shape)
+    tables = (row_r, row_i, col_r, col_i)
+    incident_tables(tile, tilts_of(known_ref[...]), row_first, columns, total_rows, total_cols, tables)
+    for part, m in enumerate((mr, mi)):
+        for t in range(tiles):
+            for r in range(0, stripe, 16):
+                at = pl.ds(pl.multiple_of(illum * stripe + r, 16), 16)
+                m[t, r : r + 16, :] = measured_ref[part, 0, at, own_columns(t)].astype(F32)
     for t in range(c0.shape[0]):
         for k, (c, s) in enumerate(((c0, s0), (c1, s1))):
             for r in range(0, c.shape[1], 16):
@@ -524,30 +548,34 @@
     )
 
 
-def own_kernel(sizes, c0, s0, c1, s1, measured_ref, known_ref, same_ref,
-               w0r, w0i, w1r, w1i, gr, gi, hr, hi, mr, mi, row_r, row_i, col_r, col_i):
+def own_kernel(sizes, c0, s0, c1, s1, mr, mi, row_r, row_i, col_r, col_i, measured_ref, same_ref,
+               w0r, w0i, w1r, w1i, gr, gi, hr, hi, above, below):
     stripe, tiles, total_rows, total_cols = sizes
     tile, row_first, col_first = main_tile(sizes)
     illum, _, _ = place()
     low_illum = illum == 0
     blank_rims((w0r, w0i, w1r, w1i, gr, gi, hr, hi), tile)
     trig = (c0, s0), (c1, s1)
-    mine = illum * stripe
     near_base = pl.multiple_of(stripe - 16 * illum, 16)
-
-    def middle(part, t, r):
-        return measured_ref[part, 0, pl.ds(pl.multiple_of(mine + r, 16), 16), own_columns(t)].astype(F32)
-
-    def near(t):
+    for t in range(tiles):
         both = [measured_ref[part, 0, pl.ds(near_base, 16), own_columns(t)].astype(F32) for part in range(2)]
-        return [jnp.where(low_illum, x[:8], x[8:]) for x in both]
-
-    fill_target(tile, (mr, mi), low_illum, middle, near, lambda t: same_ref[:, own_columns(t)])
-    forward(
-        tile, tilts_of(known_ref[...]), rim_columns(tile, col_first, col_r.shape), row_first,
-        (total_rows, total_cols), trig, (hr, hi), (row_r, row_i, col_r, col_i),
-        (w0r, w0i), (w1r, w1i), residual_in((gr, gi), (mr, mi)),
-    )
+        near = [jnp.where(low_illum, x[:8], x[8:]) for x in both]
+        far = same_ref[:, own_columns(t)]
+        for part in range(2):
+            above[part, t] = jnp.where(low_illum, unpack_rows(far, False)[part], near[part])
+            below[part, t] = jnp.where(low_illum, near[part], unpack_rows(far, True)[part])
+
+    def residual(t, rows, mask, ur, ui):
+        for part, (g, u, m) in enumerate(((gr, ur, mr), (gi, ui, mi))):
+            if rows.start == RIM:
+                target = above[part, t]
+            elif rows.start == 2 * RIM + stripe:
+                target = below[part, t]
+            else:
+                target = m[t, own_rows(rows), :]
+            g[t, rows, :] = mask(u - target)
+
+    propagate(tile, (row_r, row_i, col_r, col_i), trig, (hr, hi), (w0r, w0i), (w1r, w1i), residual)
 
 
 def back_kernel(sizes, c1, s1, w0r, w0i, w1r, w1i, gr, gi, own_ref, ar, ai, hr, hi):
@@ -601,28 +629,59 @@
     out_ref[...] = a_ref[...] + b_ref[...]
 
 
+def left_kernel(sizes, swap_ref, along_ref, w0r, w0i, w1r, w1i, ur, ui, c1, s1, left_ref, gr, gi, hr, hi, mr, mi):
+    stripe, tiles, _, _ = sizes
+    main, _, _ = main_tile(sizes)
+    tile = Tile(stripe, swap_ref.shape[1] // LANES, main.top, main.bottom)
+    low_illum = place()[0] == 0
+    blank_rims((gr, gi, hr, hi), tile)
+    fill_target(
+        tile, (mr, mi), low_illum, None,
+        lambda t: other_near(swap_ref, stripe, low_illum, own_columns(t)),
+        lambda t: along_ref[:, own_columns(t + 2 * tiles)],
+        range(tile.tiles),
+    )
+    residual_of(tile, (gr, gi), (ur, ui), other_target(tile, lambda rows, t: swap_ref[rows, own_columns(t)], (mr, mi)))
+    backward(tile, (gr, gi), (hr, hi), (w0r, w0i), (w1r, w1i), (c1, s1), put_in(left_ref))
+
+
+def other_target(tile, swapped, edges, patch=None):
+    def target(part, t, rows):
+        if t != patch and 2 * RIM <= rows.start < 2 * RIM + tile.stripe:
+            at = own_rows(rows)
+            return swapped(slice(part * tile.stripe + at.start, part * tile.stripe + at.stop), t)
+        return edges[part][t, rows, :]
+
+    return target
+
+
 class Joined:
-    def __init__(self, main, patch):
-        self.main, self.patch, self.tiles = main, patch, main.shape[0]
+    def __init__(self, main, patch, first):
+        self.main, self.patch, self.first = main, patch, first
 
     def __getitem__(self, at):
-        return self.main[at] if at[0] < self.tiles else self.patch[(0,) + at[1:]]
-
-
-def finish_kernel(sizes, own_ref, measured_ref, swap_ref, along_ref, same_ref, rim_ref, relay_ref, partner_relay_ref,
-                  *rest):
+        t = at[0] + self.first
+        return self.main[(t,) + at[1:]] if t < self.main.shape[0] else self.patch[(0,) + at[1:]]
+
+
+def finish_kernel(sizes, own_ref, left_ref, measured_ref, swap_ref, swap_rest_ref, along_ref, same_ref, rim_ref, relay_ref,
+                  partner_relay_ref, *rest):
     main_fields, patch_fields, rest = rest[:8], rest[8:16], rest[16:]
     out_ref, patch, gr, gi, hr, hi, mr, mi, full, sems = rest
-    w0r, w0i, w1r, w1i, ur, ui, c1, s1 = [Joined(a, b) for a, b in zip(main_fields, patch_fields)]
     stripe, tiles, total_rows, total_cols = sizes
+    left_tiles = swap_ref.shape[1] // LANES
+    begin = left_tiles - 1
+    lone = tiles - begin
+    w0r, w0i, w1r, w1i, ur, ui, c1, s1 = [Joined(a, b, begin) for a, b in zip(main_fields, patch_fields)]
     main, _, _ = main_tile(sizes)
-    tile = Tile(stripe, tiles + 1, main.top, main.bottom, patch_held(sizes)[0], tiles, (tiles,))
+    tile = Tile(stripe, lone + 1, main.top, main.bottom, patch_held(sizes)[0], lone, (lone,))
     illum, _, _ = place()
     low_illum = illum == 0
     blank_rims((gr, gi, hr, hi), tile)
 
     lane = lane_ids((8, LANES))
-    sums = jnp.maximum(relay_ref[stripe + 8 :, :], partner_relay_ref[stripe + 8 :, :])
+    last_rows = relay_ref.shape[0] - 8
+    sums = jnp.maximum(relay_ref[last_rows:, :], partner_relay_ref[last_rows:, :])
     scales = []
     for which in range(2):
         here = jnp.where(lane == which, sums, 0.0)
@@ -636,23 +695,33 @@
     near_base = pl.multiple_of(stripe - 16 * illum, 16)
     near_rim = pl.multiple_of(stripe - 8 * illum, 8)
 
+    def swapped(rows, t):
+        t = t + begin
+        return swap_ref[rows, own_columns(t)] if t < left_tiles else swap_rest_ref[rows, own_columns(t - left_tiles)]
+
+    def other_rim(part, block):
+        x = partner_relay_ref[2 * (block // 4 * 4) : 2 * (block // 4 * 4) + 8, :]
+        shift = (LANES - 2 * RIM * (block % 4) + part * (LANES // 2)) % LANES
+        return pltpu.roll(x, shift, 1) if shift else x
+
     def middle(part, t, r):
         at = slice(part * stripe + r, part * stripe + r + 16)
-        if t < tiles:
-            return swap_ref[at, own_columns(t)]
-        rim = partner_relay_ref[r : r + 16, :]
-        other = join_edges(swap_ref[at, first], swap_ref[at, last], pltpu.roll(rim, LANES // 2, 1) if part else rim)
+        rim = jnp.concatenate([other_rim(part, r // 8), other_rim(part, r // 8 + 1)], axis=0)
+        other = join_edges(swap_ref[at, first], swapped(at, lone - 1), rim)
         at = pl.ds(pl.multiple_of(own_first + r, 16), 16)
         own = join_edges(*[measured_ref[part, 0, at, e].astype(F32) for e in (first, last)], rim_ref[part, at, :])
         return join_illums(own, other)
 
+    def near_of(t):
+        t = t + begin
+        ref, t = (swap_ref, t) if t < left_tiles else (swap_rest_ref, t - left_tiles)
+        return other_near(ref, stripe, low_illum, own_columns(t))
+
     def near(t):
-        if t < tiles:
-            return other_near(swap_ref, stripe, low_illum, own_columns(t))
-        rim = partner_relay_ref[stripe : stripe + 8, :]
-        rims = [rim, pltpu.roll(rim, LANES // 2, 1)]
-        west, east = [other_near(swap_ref, stripe, low_illum, at) for at in (first, last)]
-        other = [join_edges(*x) for x in zip(west, east, rims)]
+        if t < lone:
+            return near_of(t)
+        rims = [other_rim(part, stripe // 8) for part in range(2)]
+        other = [join_edges(*x) for x in zip(near_of(-begin), near_of(lone - 1), rims)]
 
         def rows(part, at):
             x = measured_ref[part, 0, pl.ds(near_base, 16), at].astype(F32)
@@ -662,31 +731,49 @@
         return [join_illums(*x) for x in zip(own, other)]
 
     def far(t):
-        if t < tiles:
-            return along_ref[:, own_columns(t + 2 * tiles)]
+        if t < lone:
+            return along_ref[:, own_columns(t + begin + 2 * tiles)]
         other = join_edges(*[along_ref[:, own_columns(e + 2 * tiles)] for e in (0, tiles - 1)], rim_ref[1, 2 * stripe :, :])
         own = join_edges(same_ref[:, first], same_ref[:, last], rim_ref[0, 2 * stripe :, :])
         return join_illums(own, other)
 
-    fill_target(tile, (mr, mi), low_illum, middle, near, far)
-    residual_of(tile, (gr, gi), (ur, ui), (mr, mi))
+    copies = []
+
+    def send(k, columns):
+        copies.append(pltpu.make_async_copy(full.at[k, :, columns], out_ref.at[k, :, columns], sems.at[len(copies)]))
+        copies[-1].start()
+
+    for k in range(2):
+        for t in range(left_tiles):
+            at = own_columns(t)
+            full[k, :, at] = own_ref[k, :, at] * mine + left_ref[k, :, at] * others
+        if begin > 1:
+            send(k, slice(LANES, begin * LANES))
+
+    fill_target(tile, (mr, mi), low_illum, middle, near, far, range(lone))
+    residual_of(tile, (gr, gi), (ur, ui), other_target(tile, swapped, (mr, mi), lone))
 
     def put(k, t, rows, value):
         rows = own_rows(rows)
-        if t == tiles:
+        if t == lone:
             patch[k, rows, :] = value * mine + pltpu.roll(value, LANES - OTHER, 1) * others
             return
-        value = own_ref[k, rows, own_columns(t)] * mine + value * others
-        on = lane_ids(value.shape)
+        at = own_columns(t + begin)
+        value = own_ref[k, rows, at] * mine + value * others
         if t == 0:
-            value = jnp.where(on < RIM, patch[k, rows, :], value)
-        if t == tiles - 1:
-            value = jnp.where(on >= LANES - RIM, pltpu.roll(patch[k, rows, :], 56, 1), value)
-        full[k, rows, own_columns(t)] = value
-
-    copies = [pltpu.make_async_copy(full.at[k], out_ref.at[k], sems.at[k]) for k in range(2)]
-    backward(tile, (gr, gi), (hr, hi), (w0r, w0i), (w1r, w1i), (c1, s1), put, on_middle=copies[1].start)
-    copies[0].start()
+            value = jnp.where(lane_ids(value.shape) < LANES // 2, full[k, rows, at], value)
+        full[k, rows, at] = value
+
+    def close(k):
+        on = lane_ids(patch.shape[1:])
+        full[k, :, first] = jnp.where(on < RIM, patch[k], full[k, :, first])
+        full[k, :, last] = jnp.where(on >= LANES - RIM, pltpu.roll(patch[k], 56, 1), full[k, :, last])
+        if begin > 0:
+            send(k, first)
+        send(k, slice(begin * LANES, tiles * LANES))
+
+    backward(tile, (gr, gi), (hr, hi), (w0r, w0i), (w1r, w1i), (c1, s1), put, on_middle=functools.partial(close, 1))
+    close(0)
     for copy in copies:
         copy.wait()
 
@@ -727,8 +814,11 @@
     sizes = (stripe, tiles, 2 * stripe * rows, width * cols)
     swap = [(0, 1), (1, 0)]
     along = []
-    for r in range(rows):
-        along += [(rows + r, (r + 1) % rows), ((r + 1) % rows, rows + r)]
+    for c in range(cols):
+        for r in range(rows - 1):
+            below, above = ((rows + r) * cols + c, (r + 1) * cols + c)
+            along += [(below, above), (above, below)]
+        along += [(c, c ^ 1), ((2 * rows - 1) * cols + c, (2 * rows - 1) * cols + (c ^ 1))]
     same = [(r, (r + 1) % rows) for r in range(rows)] + [(rows + (r + 1) % rows, rows + r) for r in range(rows)]
 
     partner_out, along_out, same_out, known, note, measured = call(
@@ -738,44 +828,55 @@
             (2, slices, 8, width), pltpu.VMEM(angles.shape, angles.dtype), pltpu.SemaphoreType.DMA((4,)),
         ],
     )
-    along_in = lax.ppermute(along_out, ("illum", "row"), along)
+    along_in = lax.ppermute(along_out, ("illum", "row", "col"), along)
     partner_in = lax.ppermute(partner_out, "illum", swap)
     same_in = lax.ppermute(same_out, ("illum", "row"), same)
     core_note = lax.ppermute(note, "row", [(r, r ^ 1) for r in range(rows)])
     (pair,) = call(sum_kernel, [(8, LANES)], note, core_note)
     far = lax.ppermute(pair, "row", [(r, r ^ 2) for r in range(rows)])
-    (swap_out,) = call(swap_kernel, [(2 * stripe + 8, width)], measured, core_note)
+    cut = max(tiles - 2, 1) * LANES
+    rows_swapped = 2 * stripe + 8
+    (swap_out,) = call(
+        functools.partial(swap_kernel, slice(0, cut)), [(rows_swapped, cut)], measured, behind=[core_note]
+    )
     swap_in = lax.ppermute(swap_out, "illum", swap)
+
     def fields(count):
         return [(count, stripe + 4 * RIM, LANES)]
 
     def tables(count):
         return [(stripe + 2 * RIM, LANES)] * 2 + [(-(-count // 8) * 8, LANES)] * 2
 
-    own_trig = call(trig_kernel, [(tiles, stripe, LANES)] * 4, phase_delay, flops=10**9)
+    own_trig = call(
+        functools.partial(trig_kernel, sizes), [(tiles, stripe, LANES)] * 6 + tables(tiles), phase_delay, measured, known,
+        flops=3*10**9)
     rims = 8 * (-(-(stripe // 4 + 1) // 4))
     first_out, second_packed, note = call(
         rim_pack_kernel, [(rims + 8, LANES), (rims, LANES), (8, LANES)], phase_delay, measured, pair, far, partner_in, along_in, same_in,
         behind=own_trig[:1],
     )
-    first_in = lax.ppermute(first_out, "col", [(c, c ^ 1) for c in range(cols)])
+    first_in = lax.ppermute(first_out, "col", [(c, cols - 1 - c) for c in range(cols)])
     kept = call(
-        functools.partial(ahead_kernel, sizes), fields(tiles) * 10, *own_trig, partner_in, along_in,
+        functools.partial(ahead_kernel, sizes), fields(tiles) * 10, *own_trig[:4], partner_in, along_in,
         scratch=fields(tiles) * 2 + tables(tiles), flops=15*10**8, mib=16,
     )
     (second_out,) = call(second_kernel, [(rims + 8, LANES)], second_packed, note, first_in, behind=kept[:1])
-    second_in = lax.ppermute(second_out, "col", [(c, cols - 1 - c) for c in range(cols)])
+    second_in = lax.ppermute(second_out, "col", [(c, c ^ 1) for c in range(cols)])
 
     own_kept = call(
-        functools.partial(own_kernel, sizes), fields(tiles) * 6, *kept[:4], measured, known, same_in,
-        scratch=fields(tiles) * 4 + tables(tiles), flops=15*10**8, mib=16,
+        functools.partial(own_kernel, sizes), fields(tiles) * 6, *kept[:4], *own_trig[4:], measured, same_in,
+        scratch=fields(tiles) * 2 + [(2, tiles, RIM, LANES)] * 2, flops=15*10**8, mib=16,
     )
     phase_rim, rim, relay = call(
-        rim_unpack_kernel, [(2, stripe + 2 * RIM, LANES), (2, 2 * stripe + 8, LANES), (stripe + 16, LANES)],
+        rim_unpack_kernel, [(2, stripe + 2 * RIM, LANES), (2, 2 * stripe + 8, LANES), (8 * (-(-(stripe // 8 + 1) // 4)) + 8, LANES)],
         first_in, second_in, note,
         behind=own_kept[:1],
     )
     partner_relay = lax.ppermute(relay, "illum", swap)
+    (swap_out,) = call(
+        functools.partial(swap_kernel, slice(cut, width)), [(rows_swapped, width - cut)], measured, behind=own_kept[:1]
+    )
+    swap_rest = lax.ppermute(swap_out, "illum", swap)
     (own,) = call(
         functools.partial(back_kernel, sizes), [phase_delay.shape], *kept[2:4], *own_kept,
         scratch=fields(tiles) * 4, flops=10**9, mib=12, behind=[relay],
@@ -784,10 +885,17 @@
         functools.partial(patch_kernel, sizes), fields(1) * 8, phase_delay, known, partner_in, along_in, phase_rim,
         scratch=fields(1) * 4 + tables(1), flops=10**9, behind=[own],
     )
+    (left,) = call(
+        functools.partial(left_kernel, sizes), [(slices, stripe, cut)], swap_in, along_in, *kept[4:], *kept[2:4],
+        behind=patch_kept[:1], scratch=fields(cut // LANES) * 6, flops=10**9, mib=12,
+    )
     (out,) = call(
         functools.partial(finish_kernel, sizes), [phase_delay.shape],
-        own, measured, swap_in, along_in, same_in, rim, relay, partner_relay, *kept[4:], *kept[2:4], *patch_kept,
-        scratch=[(slices, stripe, LANES)] + fields(tiles + 1) * 6 + [phase_delay.shape, pltpu.SemaphoreType.DMA((slices,))], mib=12, flops=0, far=1,
+        own, left, measured, swap_in, swap_rest, along_in, same_in, rim, relay, partner_relay,
+        *kept[4:], *kept[2:4], *patch_kept,
+        scratch=[(slices, stripe, LANES)] + fields(tiles - cut // LANES + 2) * 6
+        + [phase_delay.shape, pltpu.SemaphoreType.DMA((6,))],
+        mib=12, flops=0, far=1,
     )
     return out
 

time: 27.4 us -> 27.3 us (level)
  starting transfers between devices: 14 us -> 13.4 us
  Pallas kernels: 11.3 us -> 11.6 us
    ppermute x1, starting transfers between devices: 0.01 us -> 1.24 us  [paired(): same_in = lax.ppermute(same_out, ('illum', 'row'), same)]
    ppermute x1, starting transfers between devices: 1.21 us -> 0.01 us  [paired(): partner_in = lax.ppermute(partner_out, 'illum', swap)]
    ppermute x1, starting transfers between devices: 1.75 us -> 0.64 us  [paired(): swap_in = lax.ppermute(swap_out, 'illum', swap)]
    ppermute x1, starting transfers between devices: 0.9 us -> 1.71 us  [paired(): far = lax.ppermute(pair, 'row', [(r, r ^ 2) for r in range(rows)])]
    ppermute x3 -> x4, starting transfers between devices: 8.64 us -> 7.97 us  [the longest x1 3.89 us: paired(): lax.ppermute(first_out, 'col', [(c, cols - 1 - c) for c in range(cols)])]
    ppermute x1, starting transfers between devices: 0.01 us -> 0.52 us  [paired(): core_note = lax.ppermute(note, 'row', [(r, r ^ 1) for r in range(rows)])]
    ppermute x1, waiting for transfers between devices: 0.38 us -> 0.01 us  [paired(): partner_relay = lax.ppermute(relay, 'illum', swap)]
    ppermute x1, waiting for transfers between devices: 0.01 us -> 0.33 us  [paired(): partner_in = lax.ppermute(partner_out, 'illum', swap)]
  transfers between devices with their start and end apart: 9 -> 10, of which waited for: 5 -> 3; matrix products, arithmetic and copies ran while one was open for 0% -> 0% of each run, Pallas kernels for 24% -> 28%
where the time goes in v7:
time: 27.3 us; the launch traced here: 27.1 us
  starting transfers between devices  13.4 us (49%)
  Pallas kernels  11.6 us (42%)
  waiting for transfers between devices  1.91 us (7%)
    pallas_call x14, Pallas kernels, call(): pl.pallas_call(kernel, out_shape=[like(x, n in held) for n, x in enumerat...  11.6 us
    ppermute x1, starting transfers between devices, paired(): lax.ppermute(first_out, 'col', [(c, cols - 1 - c) for c in range(cols)])  3.89 us
    ppermute x1, starting transfers between devices, paired(): along_in = lax.ppermute(along_out, ('illum', 'row', 'col'), along)  2.65 us
    ppermute x1, starting transfers between devices, paired(): far = lax.ppermute(pair, 'row', [(r, r ^ 2) for r in range(rows)])  1.71 us
    ppermute x1, starting transfers between devices, paired(): partner_relay = lax.ppermute(relay, 'illum', swap)  1.36 us
    ppermute x1, starting transfers between devices, paired(): same_in = lax.ppermute(same_out, ('illum', 'row'), same)  1.24 us
    ppermute x1, starting transfers between devices, paired(): swap_rest = lax.ppermute(swap_out, 'illum', swap)  1.18 us
    ppermute x1, waiting for transfers between devices, paired(): lax.ppermute(second_out, 'col', [(c, c ^ 1) for c in range(cols)])  0.82 us
  transfers between devices with their start and end apart: 10, of which 3 were waited for; matrix products, arithmetic and copies ran while one was open for 0% of the time, Pallas kernels for 28%

profile of v7, /device:TPU:0, one launch (start us, length us, event | category | flops | bytes accessed | tf_op | source)
XLA Modules:
  0.0 27.1 jit_solution(2790432564637914263)
XLA Ops:
  0.0 0.0 copy-start
  0.0 2.1 %shard_map.37 = (f32[8,2176]{1,0:T(8,128)}, f32[8,3072]{1,0:T(8,128)}, f32[8,1024]{1,0:T(8,128)}, f32[8,128]{1,0:T(8,128)}, f32[8,128]{1,0:T(8,128)}, /*index=5*/bf16[2,1,128,1024]{3,2,1,0:T(8,128)(2,1)S(1)}) custom-call(f32[2,64,1024]{2,1,0:T(8,128)} %args_1_.8, bf16[2,1,128,1024]{3,2,1,0:T(8,128)(2,1)} %args_1_.6, s32[1,2]{1,0:T(1,128)} %args_2_.4), custom_call_target="tpu_custom_call" | custom-call | bytes 262144 | tf_op jit(solution)/shard_map/pallas_call | solution.py:798
  2.1 0.0 copy-start.1
  2.1 0.5 %collective-permute-start.3 = (f32[8,128]{1,0:T(8,128)}, f32[8,128]{1,0:T(8,128)S(1)}, u32[]{:S(2)}, u32[]{:S(2)}) collective-permute-start(f32[8,128]{1,0:T(8,128)} %get-tuple-element.71.args_0_), channel_id=1, source_target_pairs={{0,4},{4,0},{8,12},{12,8},{1,5},{5,1},{9,13},{13,9},{2,6},{6,2},{1... | collective-permute-start | bytes 12296 | tf_op jit(solution)/shard_map/ppermute | solution.py:834
  2.6 2.6 %collective-permute-start.1 = (f32[8,3072]{1,0:T(8,128)}, f32[8,3072]{1,0:T(8,128)S(1)}, u32[]{:S(2)}, u32[]{:S(2)}) collective-permute-start(f32[8,3072]{1,0:T(8,128)} %get-tuple-element.58), channel_id=1, source_target_pairs={{16,4},{4,16},{20,8},{8,20},{24,12},{12,24},{0,1},{28,29},{17,5},{... | collective-permute-start | bytes 294920 | tf_op jit(solution)/shard_map/ppermute | solution.py:831
  5.3 0.0 collective-permute-start
  5.3 0.0 copy-start.2
  5.3 1.2 %collective-permute-start.2 = (f32[8,1024]{1,0:T(8,128)}, f32[8,1024]{1,0:T(8,128)S(1)}, u32[]{:S(2)}, u32[]{:S(2)}) collective-permute-start(f32[8,1024]{1,0:T(8,128)} %get-tuple-element.69), channel_id=1, source_target_pairs={{0,4},{4,8},{8,12},{12,0},{20,16},{24,20},{28,24},{16,28},{1,5},{5... | collective-permute-start | bytes 98312 | tf_op jit(solution)/shard_map/ppermute | solution.py:833
  6.5 0.0 collective-permute-done.3.args_1_.args_0_
  6.5 0.0 copy-done.1
  6.5 1.7 %collective-permute-start.4 = (f32[8,128]{1,0:T(8,128)S(1)}, f32[8,128]{1,0:T(8,128)S(1)}, u32[]{:S(2)}, u32[]{:S(2)}) collective-permute-start(f32[8,128]{1,0:T(8,128)S(1)} %shard_map.41.args_3_), channel_id=1, source_target_pairs={{0,8},{4,12},{8,0},{12,4},{1,9},{5,13},{9,1},{13,5},{2,10},{6,14},... | collective-permute-start | bytes 12296 | tf_op jit(solution)/shard_map/ppermute | solution.py:836
  8.3 0.0 copy-done
  8.3 0.0 copy-done.2
  8.3 0.6 %shard_map.38 = (f32[8,64,128]{2,1,0:T(8,128)S(1)}, f32[8,64,128]{2,1,0:T(8,128)S(1)}, f32[8,64,128]{2,1,0:T(8,128)S(1)}, f32[8,64,128]{2,1,0:T(8,128)S(1)}, f32...) custom-call(f32[2,64,1024]{2,1,0:T(8,128)S(1)} %copy-done, ...), custom_call_target="tpu_custom_call" | custom-call | flops 3000000000 | bytes 262144 | tf_op jit(solution)/shard_map/pallas_call | solution.py:798
  8.9 0.6 %collective-permute-start.7 = (f32[136,768]{1,0:T(8,128)S(1)}, f32[136,768]{1,0:T(8,128)S(1)}, u32[]{:S(2)}, u32[]{:S(2)}) collective-permute-start(f32[136,768]{1,0:T(8,128)S(1)} %shard_map.47), channel_id=1, source_target_pairs={{0,16},{16,0},{1,17},{17,1},{2,18},{18,2},{3,19},{19,3},{4,20},{20... | collective-permute-start | bytes 1253384 | tf_op jit(solution)/shard_map/ppermute | solution.py:842
  9.5 0.7 %collective-permute-done.4.args_4_ = f32[8,128]{1,0:T(8,128)S(1)} collective-permute-done((f32[8,128]{1,0:T(8,128)S(1)}, f32[8,128]{1,0:T(8,128)S(1)}, u32[]{:S(2)}, u32[]{:S(2)}) %collective-permute-start.4) | collective-permute-done | bytes 4128 | tf_op jit(solution)/shard_map/ppermute | solution.py:836
  10.2 0.0 collective-permute-done.2.args_11_.args_7_.args_6_
  10.2 0.3 %collective-permute-done.args_4_.args_5_.args_3_ = f32[8,2176]{1,0:T(8,128)S(1)} collective-permute-done((f32[8,2176]{1,0:T(8,128)}, f32[8,2176]{1,0:T(8,128)S(1)}, u32[]{:S(2)}, u32[]{:S(2)}) %collective-permute-start) | collective-permute-done | bytes 69664 | tf_op jit(solution)/shard_map/ppermute | solution.py:832
  10.6 0.0 collective-permute-done.1.args_5_.args_6_.args_4_.args_2_
  10.6 0.1 shard_map.42
  10.7 3.9 %collective-permute-start.5 = (f32[48,128]{1,0:T(8,128)S(1)}, f32[48,128]{1,0:T(8,128)S(1)}, u32[]{:S(2)}, u32[]{:S(2)}) collective-permute-start(f32[48,128]{1,0:T(8,128)S(1)} %get-tuple-element.72), channel_id=1, source_target_pairs={{0,3},{1,2},{2,1},{3,0},{4,7},{5,6},{6,5},{7,4},{8,11},{9,10},{10,... | collective-permute-start | bytes 73736 | tf_op jit(solution)/shard_map/ppermute | solution.py:858
  14.6 1.8 %shard_map.39 = (f32[8,96,128]{2,1,0:T(8,128)S(1)}, f32[8,96,128]{2,1,0:T(8,128)S(1)}, f32[8,96,128]{2,1,0:T(8,128)S(1)}, f32[8,96,128]{2,1,0:T(8,128)S(1)}, f32...) custom-call(f32[8,64,128]{2,1,0:T(8,128)S(1)} %get-tuple-element.53., ...), custom_call_target="tpu_custom_call" | custom-call | flops 1500000000 | bytes 262144 | tf_op jit(solution)/shard_map/pallas_call | solution.py:798
  16.4 0.0 collective-permute-done.5.args_3_.args_1_
  16.4 0.3 collective-permute-start.6
  16.7 1.6 %shard_map.40 = (f32[8,96,128]{2,1,0:T(8,128)S(1)}, f32[8,96,128]{2,1,0:T(8,128)S(1)}, f32[8,96,128]{2,1,0:T(8,128)S(1)}, f32[8,96,128]{2,1,0:T(8,128)S(1)}, f32...) custom-call(f32[8,96,128]{2,1,0:T(8,128)S(1)} %get-tuple-element.59.args_0_, ...), custom_call_target="tpu_custom_call" | custom-call | flops 1500000000 | bytes 262144 | tf_op jit(solution)/shard_map/pallas_call | solution.py:798
  18.3 1.2 %collective-permute-start.8 = (f32[136,256]{1,0:T(8,128)S(1)}, f32[136,256]{1,0:T(8,128)S(1)}, u32[]{:S(2)}, u32[]{:S(2)}) collective-permute-start(f32[136,256]{1,0:T(8,128)S(1)} %shard_map.49), channel_id=1, source_target_pairs={{0,16},{16,0},{1,17},{17,1},{2,18},{18,2},{3,19},{19,3},{4,20},{20... | collective-permute-start | bytes 417800 | tf_op jit(solution)/shard_map/ppermute | solution.py:879
  19.5 0.8 %collective-permute-done.6.args_2_ = f32[48,128]{1,0:T(8,128)S(1)} collective-permute-done((f32[48,128]{1,0:T(8,128)S(1)}, f32[48,128]{1,0:T(8,128)S(1)}, u32[]{:S(2)}, u32[]{:S(2)}) %collective-permute-start.6) | collective-permute-done | bytes 24608 | tf_op jit(solution)/shard_map/ppermute | solution.py:864
  20.3 0.2 shard_map.44
  20.5 1.4 %collective-permute-start.9 = (f32[32,128]{1,0:T(8,128)S(1)}, f32[32,128]{1,0:T(8,128)S(1)}, u32[]{:S(2)}, u32[]{:S(2)}) collective-permute-start(f32[32,128]{1,0:T(8,128)S(1)} %get-tuple-element.75.args_0_.args_8_), channel_id=1, source_target_pairs={{0,16},{16,0},{1,17},{17,1},{2,18},{18,2},{3,19},{19,3},{4,20},{20... | collective-permute-start | bytes 49160 | tf_op jit(solution)/shard_map/ppermute | solution.py:875
  21.9 1.4 %shard_map.45.args_0_ = f32[2,64,1024]{2,1,0:T(8,128)S(1)} custom-call(f32[32,128]{1,0:T(8,128)S(1)} %get-tuple-element.75.args_0_.args_8_, f32[8,96,128]{2,1,0:T(8,128)S(1)} %get-tuple-element.61.args_2_.args_1_.args_9_.args_16_, f32[8,96,128]{2,1,0:T(8,128)S(1)} %get-tuple-element.62.args_3_.args_2_.args_10_.args_17_, ...), custom_call_target="tpu_custom_call" | custom-call | flops 1000000000 | bytes 262144 | tf_op jit(solution)/shard_map/pallas_call | solution.py:798
  23.4 0.8 %shard_map.46 = (f32[1,96,128]{2,1,0:T(8,128)S(1)}, f32[1,96,128]{2,1,0:T(8,128)S(1)}, f32[1,96,128]{2,1,0:T(8,128)S(1)}, f32[1,96,128]{2,1,0:T(8,128)S(1)}, f32...) custom-call(f32[2,64,1024]{2,1,0:T(8,128)S(1)} %shard_map.45.args_0_,, ...), custom_call_target="tpu_custom_call" | custom-call | flops 1000000000 | bytes 262144 | tf_op jit(solution)/shard_map/pallas_call | solution.py:798
  24.1 0.0 collective-permute-done.7.args_1_.args_3_
  24.1 1.1 %shard_map.48.args_1_ = f32[2,64,768]{2,1,0:T(8,128)S(1)} custom-call(f32[1,96,128]{2,1,0:T(8,128)S(1)} %get-tuple-element.82.args_0_.args_18_, f32[136,768]{1,0:T(8,128)S(1)} %collective-permute-done.7.args_1_.args_3_, f32[8,3072]{1,0:T(8,128)S(1)} %collective-permute-done.1.args_5_.args_6_.args_4_.args_2_, ...), custom_call_target="tpu_custom_call" | custom-call | flops 1000000000 | bytes 262144 | tf_op jit(solution)/shard_map/pallas_call | solution.py:798
  25.3 0.0 collective-permute-done.9.args_9_
  25.3 0.0 collective-permute-done.8.args_4_
  25.3 1.8 %shard_map.50 = f32[2,64,1024]{2,1,0:T(8,128)} custom-call(f32[2,64,1024]{2,1,0:T(8,128)S(1)} %shard_map.45.args_0_, f32[2,64,768]{2,1,0:T(8,128)S(1)} %shard_map.48.args_1_, bf16[2,1,128,1024]{3,2,1,0:T(8,128)(2,1)S(1)} %get-tuple-element.51.args_1_.args_10_.args_2_, f32[136,768]{1,0:T(8,128)S(1)} %collective-permute-done.7.args_1_.args_3_, ...), custom_call_target="tpu_custom_call" | custom-call | bytes 262144 | tf_op jit(solution)/shard_map/pallas_call | solution.py:798
  (4 shorter events, 0.1 us)
Async XLA Ops:
  0.0 8.3 %copy-start = (f32[2,64,1024]{2,1,0:T(8,128)S(1)}, f32[2,64,1024]{2,1,0:T(8,128)}, u32[]{:S(2)}) copy-start(f32[2,64,1024]{2,1,0:T(8,128)} %args_1_.8) | copy-start | bytes 1572868
  2.1 4.4 %copy-start.1 = (f32[8,128]{1,0:T(8,128)S(1)}, f32[8,128]{1,0:T(8,128)}, u32[]{:S(2)}) copy-start(f32[8,128]{1,0:T(8,128)} %get-tuple-element.71.args_0_) | copy-start | bytes 12292
  2.1 4.4 %collective-permute-start.3 = (f32[8,128]{1,0:T(8,128)}, f32[8,128]{1,0:T(8,128)S(1)}, u32[]{:S(2)}, u32[]{:S(2)}) collective-permute-start(f32[8,128]{1,0:T(8,128)} %get-tuple-element.71.args_0_), channel_id=1, source_target_pairs={{0,4},{4,0},{8,12},{12,8},{1,5},{5,1},{9,13},{13,9},{2,6},{6,2},{1... | collective-permute-start | bytes 12296 | tf_op jit(solution)/shard_map/ppermute | solution.py:834
  2.6 7.9 %collective-permute-start.1 = (f32[8,3072]{1,0:T(8,128)}, f32[8,3072]{1,0:T(8,128)S(1)}, u32[]{:S(2)}, u32[]{:S(2)}) collective-permute-start(f32[8,3072]{1,0:T(8,128)} %get-tuple-element.58), channel_id=1, source_target_pairs={{16,4},{4,16},{20,8},{8,20},{24,12},{12,24},{0,1},{28,29},{17,5},{... | collective-permute-start | bytes 294920 | tf_op jit(solution)/shard_map/ppermute | solution.py:831
  5.3 5.3 %collective-permute-start = (f32[8,2176]{1,0:T(8,128)}, f32[8,2176]{1,0:T(8,128)S(1)}, u32[]{:S(2)}, u32[]{:S(2)}) collective-permute-start(f32[8,2176]{1,0:T(8,128)} %get-tuple-element.57), channel_id=1, source_target_pairs={{0,16},{16,0},{1,17},{17,1},{2,18},{18,2},{3,19},{19,3},{4,20},{20... | collective-permute-start | bytes 208904 | tf_op jit(solution)/shard_map/ppermute | solution.py:832
  5.3 3.0 %copy-start.2 = (f32[8,128]{1,0:T(8,128)S(1)}, f32[8,128]{1,0:T(8,128)}, u32[]{:S(2)}) copy-start(f32[8,128]{1,0:T(8,128)} %get-tuple-element.52.args_2_) | copy-start | bytes 12292
  5.3 4.9 %collective-permute-start.2 = (f32[8,1024]{1,0:T(8,128)}, f32[8,1024]{1,0:T(8,128)S(1)}, u32[]{:S(2)}, u32[]{:S(2)}) collective-permute-start(f32[8,1024]{1,0:T(8,128)} %get-tuple-element.69), channel_id=1, source_target_pairs={{0,4},{4,8},{8,12},{12,0},{20,16},{24,20},{28,24},{16,28},{1,5},{5... | collective-permute-start | bytes 98312 | tf_op jit(solution)/shard_map/ppermute | solution.py:833
  6.5 3.7 %collective-permute-start.4 = (f32[8,128]{1,0:T(8,128)S(1)}, f32[8,128]{1,0:T(8,128)S(1)}, u32[]{:S(2)}, u32[]{:S(2)}) collective-permute-start(f32[8,128]{1,0:T(8,128)S(1)} %shard_map.41.args_3_), channel_id=1, source_target_pairs={{0,8},{4,12},{8,0},{12,4},{1,9},{5,13},{9,1},{13,5},{2,10},{6,14},... | collective-permute-start | bytes 12296 | tf_op jit(solution)/shard_map/ppermute | solution.py:836
  8.9 15.3 %collective-permute-start.7 = (f32[136,768]{1,0:T(8,128)S(1)}, f32[136,768]{1,0:T(8,128)S(1)}, u32[]{:S(2)}, u32[]{:S(2)}) collective-permute-start(f32[136,768]{1,0:T(8,128)S(1)} %shard_map.47), channel_id=1, source_target_pairs={{0,16},{16,0},{1,17},{17,1},{2,18},{18,2},{3,19},{19,3},{4,20},{20... | collective-permute-start | bytes 1253384 | tf_op jit(solution)/shard_map/ppermute | solution.py:842
  10.7 5.7 %collective-permute-start.5 = (f32[48,128]{1,0:T(8,128)S(1)}, f32[48,128]{1,0:T(8,128)S(1)}, u32[]{:S(2)}, u32[]{:S(2)}) collective-permute-start(f32[48,128]{1,0:T(8,128)S(1)} %get-tuple-element.72), channel_id=1, source_target_pairs={{0,3},{1,2},{2,1},{3,0},{4,7},{5,6},{6,5},{7,4},{8,11},{9,10},{10,... | collective-permute-start | bytes 73736 | tf_op jit(solution)/shard_map/ppermute | solution.py:858
  16.4 3.9 %collective-permute-start.6 = (f32[48,128]{1,0:T(8,128)S(1)}, f32[48,128]{1,0:T(8,128)S(1)}, u32[]{:S(2)}, u32[]{:S(2)}) collective-permute-start(f32[48,128]{1,0:T(8,128)S(1)} %shard_map.43), channel_id=1, source_target_pairs={{0,1},{1,0},{2,3},{3,2},{4,5},{5,4},{6,7},{7,6},{8,9},{9,8},{10,11... | collective-permute-start | bytes 73736 | tf_op jit(solution)/shard_map/ppermute | solution.py:864
  18.3 7.0 %collective-permute-start.8 = (f32[136,256]{1,0:T(8,128)S(1)}, f32[136,256]{1,0:T(8,128)S(1)}, u32[]{:S(2)}, u32[]{:S(2)}) collective-permute-start(f32[136,256]{1,0:T(8,128)S(1)} %shard_map.49), channel_id=1, source_target_pairs={{0,16},{16,0},{1,17},{17,1},{2,18},{18,2},{3,19},{19,3},{4,20},{20... | collective-permute-start | bytes 417800 | tf_op jit(solution)/shard_map/ppermute | solution.py:879
  20.5 4.7 %collective-permute-start.9 = (f32[32,128]{1,0:T(8,128)S(1)}, f32[32,128]{1,0:T(8,128)S(1)}, u32[]{:S(2)}, u32[]{:S(2)}) collective-permute-start(f32[32,128]{1,0:T(8,128)S(1)} %get-tuple-element.75.args_0_.args_8_), channel_id=1, source_target_pairs={{0,16},{16,0},{1,17},{17,1},{2,18},{18,2},{3,19},{19,3},{4,20},{20... | collective-permute-start | bytes 49160 | tf_op jit(solution)/shard_map/ppermute | solution.py:875

commit v8 on v7

--- a/solution.py
+++ b/solution.py
@@ -148,7 +148,12 @@
     return use
 
 
-def backward(tile, adjoint, half, w0, w1, trig1, put, between=None, on_middle=None, on_rows=None):
+def backward(*args, **kwargs):
+    for _ in backward_steps(*args, **kwargs):
+        pass
+
+
+def backward_steps(tile, adjoint, half, w0, w1, trig1, put, between=None, on_middle=None, on_rows=None):
     between = between or adjoint
     gr, gi = between
     inner = [first for first, _, _ in tile.inner]
@@ -165,10 +170,13 @@
             put(0, t, rows, ui * w0[0][t, rows, :] - ur * w0[1][t, rows, :])
 
     first_half(tile, adjoint, half, -1.0, tile.blocks)
+    yield
     second_half(tile, adjoint, half, tile.blocks, back)
+    yield
     if on_middle:
         on_middle()
     first_half(tile, between, half, -1.0, tile.blocks)
+    yield
     for block in tile.inner if on_rows is None else [(r, 16, None) for r in range(2 * RIM, 2 * RIM + tile.stripe, 16)]:
         second_half(tile, between, half, [block], last)
         if on_rows:
@@ -427,11 +435,19 @@
     propagate(tile, tables, trig, half, w0, w1, use)
 
 
-def propagate(tile, tables, trig, half, w0, w1, use):
+def propagate(*args):
+    for _ in propagate_steps(*args):
+        pass
+
+
+def propagate_steps(tile, tables, trig, half, w0, w1, use):
     enter(tile, tables, trig[0], w0)
     first_half(tile, w0, half, 1.0, tile.blocks)
+    yield
     second_half(tile, w0, half, tile.blocks, modulate_into(trig[1], w1))
+    yield
     first_half(tile, w1, half, 1.0, tile.blocks)
+    yield
     second_half(tile, w1, half, tile.blocks, use)
 
 
@@ -578,25 +594,22 @@
     propagate(tile, (row_r, row_i, col_r, col_i), trig, (hr, hi), (w0r, w0i), (w1r, w1i), residual)
 
 
-def back_kernel(sizes, c1, s1, w0r, w0i, w1r, w1i, gr, gi, own_ref, ar, ai, hr, hi):
-    tile, _, _ = main_tile(sizes)
-    blank_rims((ar, ai, hr, hi), tile)
-    backward(tile, (gr, gi), (hr, hi), (w0r, w0i), (w1r, w1i), (c1, s1), put_in(own_ref), (ar, ai))
-
-
 def other_near(swap_ref, stripe, low_illum, columns):
     packed = swap_ref[2 * stripe :, columns]
     high, low = unpack_rows(packed, False), unpack_rows(packed, True)
     return [jnp.where(low_illum, low[part], high[part]) for part in range(2)]
 
 
-def patch_kernel(sizes, phase_ref, known_ref, partner_ref, along_ref, phase_rim_ref,
-                 w0r, w0i, w1r, w1i, ur_ref, ui_ref, c1, s1, c0, s0, hr, hi, row_r, row_i, col_r, col_i):
+def back_kernel(sizes, main_c1, main_s1, main_w0r, main_w0i, main_w1r, main_w1i, gr, gi,
+                phase_ref, known_ref, partner_ref, along_ref, phase_rim_ref,
+                own_ref, w0r, w0i, w1r, w1i, ur_ref, ui_ref, c1, s1,
+                ar, ai, main_hr, main_hi, c0, s0, hr, hi, row_r, row_i, col_r, col_i):
     stripe, tiles, total_rows, total_cols = sizes
     main, row_first, _ = main_tile(sizes)
     held, columns = patch_held(sizes)
     tile = Tile(stripe, 1, main.top, main.bottom, held, 0, (0,))
     low_illum = place()[0] == 0
+    blank_rims((ar, ai, main_hr, main_hi), main)
     blank_rims((w0r, w0i, w1r, w1i, hr, hi), tile)
     trig = (c0, s0), (c1, s1)
     end = stripe + RIM
@@ -619,10 +632,18 @@
     )
     note = jnp.where(patch_lanes()[0], 0.0, 1.0)
     tilts = [a * note + b * (1.0 - note) for a, b in zip(tilts_of(known_ref[...]), tilts_of(partner_ref[:, 2 * tiles * LANES :]))]
-    forward(
-        tile, tilts, columns, row_first, (total_rows, total_cols), trig, (hr, hi), (row_r, row_i, col_r, col_i),
-        (w0r, w0i), (w1r, w1i), keep_in((ur_ref, ui_ref)),
-    )
+    tables = (row_r, row_i, col_r, col_i)
+    incident_tables(tile, tilts, row_first, columns, total_rows, total_cols, tables)
+    ways = [
+        propagate_steps(tile, tables, trig, (hr, hi), (w0r, w0i), (w1r, w1i), keep_in((ur_ref, ui_ref))),
+        backward_steps(
+            main, (gr, gi), (main_hr, main_hi), (main_w0r, main_w0i), (main_w1r, main_w1i), (main_c1, main_s1),
+            put_in(own_ref), (ar, ai),
+        ),
+    ]
+    for _ in range(4):
+        for way in ways:
+            next(way, None)
 
 
 def sum_kernel(a_ref, b_ref, out_ref):
@@ -823,7 +844,7 @@
 
     partner_out, along_out, same_out, known, note, measured = call(
         open_kernel, [(8, 2 * width + LANES), (8, 3 * width), (8, width), (8, LANES), (8, LANES), measured],
-        phase_delay, measured, angles, in_place=3, mib=62, held=(5,),
+        phase_delay, measured, angles, in_place=3, mib=62, held=(0, 1, 2, 3, 4, 5),
         scratch=[
             (2, slices, 8, width), pltpu.VMEM(angles.shape, angles.dtype), pltpu.SemaphoreType.DMA((4,)),
         ],
@@ -877,13 +898,10 @@
         functools.partial(swap_kernel, slice(cut, width)), [(rows_swapped, width - cut)], measured, behind=own_kept[:1]
     )
     swap_rest = lax.ppermute(swap_out, "illum", swap)
-    (own,) = call(
-        functools.partial(back_kernel, sizes), [phase_delay.shape], *kept[2:4], *own_kept,
-        scratch=fields(tiles) * 4, flops=10**9, mib=12, behind=[relay],
-    )
-    patch_kept = call(
-        functools.partial(patch_kernel, sizes), fields(1) * 8, phase_delay, known, partner_in, along_in, phase_rim,
-        scratch=fields(1) * 4 + tables(1), flops=10**9, behind=[own],
+    own, *patch_kept = call(
+        functools.partial(back_kernel, sizes), [phase_delay.shape] + fields(1) * 8, *kept[2:4], *own_kept,
+        phase_delay, known, partner_in, along_in, phase_rim,
+        behind=[relay], scratch=fields(tiles) * 4 + fields(1) * 4 + tables(1), flops=10**9, mib=12,
     )
     (left,) = call(
         functools.partial(left_kernel, sizes), [(slices, stripe, cut)], swap_in, along_in, *kept[4:], *kept[2:4],

time: 27.3 us -> 26.1 us (0.956)
  Pallas kernels: 11.6 us -> 10.6 us
    pallas_call x14 -> x13, Pallas kernels: 11.6 us -> 10.6 us  [call(): pl.pallas_call(kernel, out_shape=[like(x, n in held) for n, x in enumerat...]
where the time goes in v8:
time: 26.1 us; the launch traced here: 26 us
  starting transfers between devices  13.6 us (52%)
  Pallas kernels  10.6 us (41%)
  waiting for transfers between devices  1.64 us (6%)
    pallas_call x13, Pallas kernels, call(): pl.pallas_call(kernel, out_shape=[like(x, n in held) for n, x in enumerat...  10.6 us
    ppermute x1, starting transfers between devices, paired(): lax.ppermute(first_out, 'col', [(c, cols - 1 - c) for c in range(cols)])  3.89 us
    ppermute x1, starting transfers between devices, paired(): along_in = lax.ppermute(along_out, ('illum', 'row', 'col'), along)  2.65 us
    ppermute x1, starting transfers between devices, paired(): far = lax.ppermute(pair, 'row', [(r, r ^ 2) for r in range(rows)])  1.64 us
    ppermute x1, starting transfers between devices, paired(): partner_relay = lax.ppermute(relay, 'illum', swap)  1.48 us
    ppermute x1, starting transfers between devices, paired(): swap_rest = lax.ppermute(swap_out, 'illum', swap)  1.28 us
    ppermute x1, starting transfers between devices, paired(): same_in = lax.ppermute(same_out, ('illum', 'row'), same)  1.24 us
    ppermute x1, waiting for transfers between devices, paired(): lax.ppermute(second_out, 'col', [(c, c ^ 1) for c in range(cols)])  0.72 us
  transfers between devices with their start and end apart: 10, of which 3 were waited for; matrix products, arithmetic and copies ran while one was open for 0% of the time, Pallas kernels for 28%

profile of v8, /device:TPU:0, one launch (start us, length us, event | category | flops | bytes accessed | tf_op | source)
XLA Modules:
  0.0 26.0 jit_solution(10760208513490042077)
XLA Ops:
  0.0 1.4 %shard_map.37 = (f32[8,2176]{1,0:T(8,128)S(1)}, f32[8,3072]{1,0:T(8,128)S(1)}, f32[8,1024]{1,0:T(8,128)S(1)}, f32[8,128]{1,0:T(8,128)S(1)}, f32[8,128]{1,0:T(8,128)S(1)}, /*index=5*/bf16[2,1,128,1024]{3,2,1,0:T(8,128)(2,1)S(1)}) custom-call(f32[2,64,1024]{2,1,0:T(8,128)} %args_9_.1, bf16[2,1,128,1024]{3,2,1,0:T(8,128)(2,1)} %args_1_.5, s32[1,2]{1,0:T(1,128)} %args_2_.4), custom_call_target="tpu_custom_call" | custom-call | bytes 262144 | tf_op jit(solution)/shard_map/pallas_call | solution.py:819
  1.4 0.0 copy-start
  1.4 0.5 %collective-permute-start.3 = (f32[8,128]{1,0:T(8,128)S(1)}, f32[8,128]{1,0:T(8,128)S(1)}, u32[]{:S(2)}, u32[]{:S(2)}) collective-permute-start(f32[8,128]{1,0:T(8,128)S(1)} %get-tuple-element.72.args_0_), channel_id=1, source_target_pairs={{0,4},{4,0},{8,12},{12,8},{1,5},{5,1},{9,13},{13,9},{2,6},{6,2},{1... | collective-permute-start | bytes 12296 | tf_op jit(solution)/shard_map/ppermute | solution.py:855
  2.0 2.6 %collective-permute-start.1 = (f32[8,3072]{1,0:T(8,128)S(1)}, f32[8,3072]{1,0:T(8,128)S(1)}, u32[]{:S(2)}, u32[]{:S(2)}) collective-permute-start(f32[8,3072]{1,0:T(8,128)S(1)} %get-tuple-element.59), channel_id=1, source_target_pairs={{16,4},{4,16},{20,8},{8,20},{24,12},{12,24},{0,1},{28,29},{17,5},{... | collective-permute-start | bytes 294920 | tf_op jit(solution)/shard_map/ppermute | solution.py:852
  4.6 0.0 collective-permute-start
  4.6 1.2 %collective-permute-start.2 = (f32[8,1024]{1,0:T(8,128)S(1)}, f32[8,1024]{1,0:T(8,128)S(1)}, u32[]{:S(2)}, u32[]{:S(2)}) collective-permute-start(f32[8,1024]{1,0:T(8,128)S(1)} %get-tuple-element.70), channel_id=1, source_target_pairs={{0,4},{4,8},{8,12},{12,0},{20,16},{24,20},{28,24},{16,28},{1,5},{5... | collective-permute-start | bytes 98312 | tf_op jit(solution)/shard_map/ppermute | solution.py:854
  5.9 0.0 collective-permute-done.3.args_1_.args_0_
  5.9 1.6 %collective-permute-start.4 = (f32[8,128]{1,0:T(8,128)S(1)}, f32[8,128]{1,0:T(8,128)S(1)}, u32[]{:S(2)}, u32[]{:S(2)}) collective-permute-start(f32[8,128]{1,0:T(8,128)S(1)} %shard_map.41.args_3_), channel_id=1, source_target_pairs={{0,8},{4,12},{8,0},{12,4},{1,9},{5,13},{9,1},{13,5},{2,10},{6,14},... | collective-permute-start | bytes 12296 | tf_op jit(solution)/shard_map/ppermute | solution.py:857
  7.5 0.7 %collective-permute-start.7 = (f32[136,768]{1,0:T(8,128)S(1)}, f32[136,768]{1,0:T(8,128)S(1)}, u32[]{:S(2)}, u32[]{:S(2)}) collective-permute-start(f32[136,768]{1,0:T(8,128)S(1)} %shard_map.46), channel_id=1, source_target_pairs={{0,16},{16,0},{1,17},{17,1},{2,18},{18,2},{3,19},{19,3},{4,20},{20... | collective-permute-start | bytes 1253384 | tf_op jit(solution)/shard_map/ppermute | solution.py:863
  8.2 0.0 copy-done
  8.2 0.6 %shard_map.38 = (f32[8,64,128]{2,1,0:T(8,128)S(1)}, f32[8,64,128]{2,1,0:T(8,128)S(1)}, f32[8,64,128]{2,1,0:T(8,128)S(1)}, f32[8,64,128]{2,1,0:T(8,128)S(1)}, f32...) custom-call(f32[2,64,1024]{2,1,0:T(8,128)S(1)} %copy-done, ...), custom_call_target="tpu_custom_call" | custom-call | flops 3000000000 | bytes 262144 | tf_op jit(solution)/shard_map/pallas_call | solution.py:819
  8.8 0.7 %collective-permute-done.4.args_4_ = f32[8,128]{1,0:T(8,128)S(1)} collective-permute-done((f32[8,128]{1,0:T(8,128)S(1)}, f32[8,128]{1,0:T(8,128)S(1)}, u32[]{:S(2)}, u32[]{:S(2)}) %collective-permute-start.4) | collective-permute-done | bytes 4128 | tf_op jit(solution)/shard_map/ppermute | solution.py:857
  9.5 0.0 collective-permute-done.2.args_11_.args_7_.args_6_
  9.5 0.2 collective-permute-done.args_4_.args_5_.args_11_
  9.7 0.0 collective-permute-done.1.args_5_.args_6_.args_12_.args_2_
  9.7 0.1 shard_map.42
  9.8 3.9 %collective-permute-start.5 = (f32[48,128]{1,0:T(8,128)S(1)}, f32[48,128]{1,0:T(8,128)S(1)}, u32[]{:S(2)}, u32[]{:S(2)}) collective-permute-start(f32[48,128]{1,0:T(8,128)S(1)} %get-tuple-element.73), channel_id=1, source_target_pairs={{0,3},{1,2},{2,1},{3,0},{4,7},{5,6},{6,5},{7,4},{8,11},{9,10},{10,... | collective-permute-start | bytes 73736 | tf_op jit(solution)/shard_map/ppermute | solution.py:879
  13.7 1.8 %shard_map.39 = (f32[8,96,128]{2,1,0:T(8,128)S(1)}, f32[8,96,128]{2,1,0:T(8,128)S(1)}, f32[8,96,128]{2,1,0:T(8,128)S(1)}, f32[8,96,128]{2,1,0:T(8,128)S(1)}, f32...) custom-call(f32[8,64,128]{2,1,0:T(8,128)S(1)} %get-tuple-element.54., ...), custom_call_target="tpu_custom_call" | custom-call | flops 1500000000 | bytes 262144 | tf_op jit(solution)/shard_map/pallas_call | solution.py:819
  15.5 0.0 collective-permute-done.5.args_3_.args_1_
  15.5 0.3 collective-permute-start.6
  15.8 1.6 %shard_map.40 = (f32[8,96,128]{2,1,0:T(8,128)S(1)}, f32[8,96,128]{2,1,0:T(8,128)S(1)}, f32[8,96,128]{2,1,0:T(8,128)S(1)}, f32[8,96,128]{2,1,0:T(8,128)S(1)}, f32...) custom-call(f32[8,96,128]{2,1,0:T(8,128)S(1)} %get-tuple-element.60.args_0_, ...), custom_call_target="tpu_custom_call" | custom-call | flops 1500000000 | bytes 262144 | tf_op jit(solution)/shard_map/pallas_call | solution.py:819
  17.4 1.3 %collective-permute-start.8 = (f32[136,256]{1,0:T(8,128)S(1)}, f32[136,256]{1,0:T(8,128)S(1)}, u32[]{:S(2)}, u32[]{:S(2)}) collective-permute-start(f32[136,256]{1,0:T(8,128)S(1)} %shard_map.48), channel_id=1, source_target_pairs={{0,16},{16,0},{1,17},{17,1},{2,18},{18,2},{3,19},{19,3},{4,20},{20... | collective-permute-start | bytes 417800 | tf_op jit(solution)/shard_map/ppermute | solution.py:900
  18.7 0.7 %collective-permute-done.6.args_2_ = f32[48,128]{1,0:T(8,128)S(1)} collective-permute-done((f32[48,128]{1,0:T(8,128)S(1)}, f32[48,128]{1,0:T(8,128)S(1)}, u32[]{:S(2)}, u32[]{:S(2)}) %collective-permute-start.6) | collective-permute-done | bytes 24608 | tf_op jit(solution)/shard_map/ppermute | solution.py:885
  19.4 0.2 shard_map.44
  19.6 1.5 %collective-permute-start.9 = (f32[32,128]{1,0:T(8,128)S(1)}, f32[32,128]{1,0:T(8,128)S(1)}, u32[]{:S(2)}, u32[]{:S(2)}) collective-permute-start(f32[32,128]{1,0:T(8,128)S(1)} %get-tuple-element.76.args_0_.args_8_), channel_id=1, source_target_pairs={{0,16},{16,0},{1,17},{17,1},{2,18},{18,2},{3,19},{19,3},{4,20},{20... | collective-permute-start | bytes 49160 | tf_op jit(solution)/shard_map/ppermute | solution.py:896
  21.1 1.8 %shard_map.45 = (f32[2,64,1024]{2,1,0:T(8,128)S(1)}, f32[1,96,128]{2,1,0:T(8,128)S(1)}, f32[1,96,128]{2,1,0:T(8,128)S(1)}, f32[1,96,128]{2,1,0:T(8,128)S(1)}, f3...) custom-call(f32[32,128]{1,0:T(8,128)S(1)} %get-tuple-element.76.args, ...), custom_call_target="tpu_custom_call" | custom-call | flops 1000000000 | bytes 262144 | tf_op jit(solution)/shard_map/pallas_call | solution.py:819
  22.9 0.0 collective-permute-done.7.args_1_.args_3_
  22.9 1.1 %shard_map.47.args_1_ = f32[2,64,768]{2,1,0:T(8,128)S(1)} custom-call(f32[1,96,128]{2,1,0:T(8,128)S(1)} %get-tuple-element.84.args_0_.args_18_, f32[136,768]{1,0:T(8,128)S(1)} %collective-permute-done.7.args_1_.args_3_, f32[8,3072]{1,0:T(8,128)S(1)} %collective-permute-done.1.args_5_.args_6_.args_12_.args_2_, ...), custom_call_target="tpu_custom_call" | custom-call | flops 1000000000 | bytes 262144 | tf_op jit(solution)/shard_map/pallas_call | solution.py:819
  24.1 0.0 collective-permute-done.9.args_9_
  24.1 0.0 collective-permute-done.8.args_4_
  24.1 1.9 %shard_map.49 = f32[2,64,1024]{2,1,0:T(8,128)} custom-call(f32[2,64,1024]{2,1,0:T(8,128)S(1)} %get-tuple-element.83.args_0_, f32[2,64,768]{2,1,0:T(8,128)S(1)} %shard_map.47.args_1_, bf16[2,1,128,1024]{3,2,1,0:T(8,128)(2,1)S(1)} %get-tuple-element.52.args_1_.args_10_.args_2_, f32[136,768]{1,0:T(8,128)S(1)} %collective-permute-done.7.args_1_.args_3_, ...), custom_call_target="tpu_custom_call" | custom-call | bytes 262144 | tf_op jit(solution)/shard_map/pallas_call | solution.py:819
  (4 shorter events, 0.1 us)
Async XLA Ops:
  1.4 6.8 %copy-start = (f32[2,64,1024]{2,1,0:T(8,128)S(1)}, f32[2,64,1024]{2,1,0:T(8,128)}, u32[]{:S(2)}) copy-start(f32[2,64,1024]{2,1,0:T(8,128)} %args_9_.1) | copy-start | bytes 1572868
  1.4 4.4 %collective-permute-start.3 = (f32[8,128]{1,0:T(8,128)S(1)}, f32[8,128]{1,0:T(8,128)S(1)}, u32[]{:S(2)}, u32[]{:S(2)}) collective-permute-start(f32[8,128]{1,0:T(8,128)S(1)} %get-tuple-element.72.args_0_), channel_id=1, source_target_pairs={{0,4},{4,0},{8,12},{12,8},{1,5},{5,1},{9,13},{13,9},{2,6},{6,2},{1... | collective-permute-start | bytes 12296 | tf_op jit(solution)/shard_map/ppermute | solution.py:855
  2.0 7.7 %collective-permute-start.1 = (f32[8,3072]{1,0:T(8,128)S(1)}, f32[8,3072]{1,0:T(8,128)S(1)}, u32[]{:S(2)}, u32[]{:S(2)}) collective-permute-start(f32[8,3072]{1,0:T(8,128)S(1)} %get-tuple-element.59), channel_id=1, source_target_pairs={{16,4},{4,16},{20,8},{8,20},{24,12},{12,24},{0,1},{28,29},{17,5},{... | collective-permute-start | bytes 294920 | tf_op jit(solution)/shard_map/ppermute | solution.py:852
  4.6 5.1 %collective-permute-start = (f32[8,2176]{1,0:T(8,128)S(1)}, f32[8,2176]{1,0:T(8,128)S(1)}, u32[]{:S(2)}, u32[]{:S(2)}) collective-permute-start(f32[8,2176]{1,0:T(8,128)S(1)} %get-tuple-element.58), channel_id=1, source_target_pairs={{0,16},{16,0},{1,17},{17,1},{2,18},{18,2},{3,19},{19,3},{4,20},{20... | collective-permute-start | bytes 208904 | tf_op jit(solution)/shard_map/ppermute | solution.py:853
  4.6 4.9 %collective-permute-start.2 = (f32[8,1024]{1,0:T(8,128)S(1)}, f32[8,1024]{1,0:T(8,128)S(1)}, u32[]{:S(2)}, u32[]{:S(2)}) collective-permute-start(f32[8,1024]{1,0:T(8,128)S(1)} %get-tuple-element.70), channel_id=1, source_target_pairs={{0,4},{4,8},{8,12},{12,0},{20,16},{24,20},{28,24},{16,28},{1,5},{5... | collective-permute-start | bytes 98312 | tf_op jit(solution)/shard_map/ppermute | solution.py:854
  5.9 3.6 %collective-permute-start.4 = (f32[8,128]{1,0:T(8,128)S(1)}, f32[8,128]{1,0:T(8,128)S(1)}, u32[]{:S(2)}, u32[]{:S(2)}) collective-permute-start(f32[8,128]{1,0:T(8,128)S(1)} %shard_map.41.args_3_), channel_id=1, source_target_pairs={{0,8},{4,12},{8,0},{12,4},{1,9},{5,13},{9,1},{13,5},{2,10},{6,14},... | collective-permute-start | bytes 12296 | tf_op jit(solution)/shard_map/ppermute | solution.py:857
  7.5 15.4 %collective-permute-start.7 = (f32[136,768]{1,0:T(8,128)S(1)}, f32[136,768]{1,0:T(8,128)S(1)}, u32[]{:S(2)}, u32[]{:S(2)}) collective-permute-start(f32[136,768]{1,0:T(8,128)S(1)} %shard_map.46), channel_id=1, source_target_pairs={{0,16},{16,0},{1,17},{17,1},{2,18},{18,2},{3,19},{19,3},{4,20},{20... | collective-permute-start | bytes 1253384 | tf_op jit(solution)/shard_map/ppermute | solution.py:863
  9.8 5.7 %collective-permute-start.5 = (f32[48,128]{1,0:T(8,128)S(1)}, f32[48,128]{1,0:T(8,128)S(1)}, u32[]{:S(2)}, u32[]{:S(2)}) collective-permute-start(f32[48,128]{1,0:T(8,128)S(1)} %get-tuple-element.73), channel_id=1, source_target_pairs={{0,3},{1,2},{2,1},{3,0},{4,7},{5,6},{6,5},{7,4},{8,11},{9,10},{10,... | collective-permute-start | bytes 73736 | tf_op jit(solution)/shard_map/ppermute | solution.py:879
  15.5 3.9 %collective-permute-start.6 = (f32[48,128]{1,0:T(8,128)S(1)}, f32[48,128]{1,0:T(8,128)S(1)}, u32[]{:S(2)}, u32[]{:S(2)}) collective-permute-start(f32[48,128]{1,0:T(8,128)S(1)} %shard_map.43), channel_id=1, source_target_pairs={{0,1},{1,0},{2,3},{3,2},{4,5},{5,4},{6,7},{7,6},{8,9},{9,8},{10,11... | collective-permute-start | bytes 73736 | tf_op jit(solution)/shard_map/ppermute | solution.py:885
  17.4 6.7 %collective-permute-start.8 = (f32[136,256]{1,0:T(8,128)S(1)}, f32[136,256]{1,0:T(8,128)S(1)}, u32[]{:S(2)}, u32[]{:S(2)}) collective-permute-start(f32[136,256]{1,0:T(8,128)S(1)} %shard_map.48), channel_id=1, source_target_pairs={{0,16},{16,0},{1,17},{17,1},{2,18},{18,2},{3,19},{19,3},{4,20},{20... | collective-permute-start | bytes 417800 | tf_op jit(solution)/shard_map/ppermute | solution.py:900
  19.6 4.4 %collective-permute-start.9 = (f32[32,128]{1,0:T(8,128)S(1)}, f32[32,128]{1,0:T(8,128)S(1)}, u32[]{:S(2)}, u32[]{:S(2)}) collective-permute-start(f32[32,128]{1,0:T(8,128)S(1)} %get-tuple-element.76.args_0_.args_8_), channel_id=1, source_target_pairs={{0,16},{16,0},{1,17},{17,1},{2,18},{18,2},{3,19},{19,3},{4,20},{20... | collective-permute-start | bytes 49160 | tf_op jit(solution)/shard_map/ppermute | solution.py:896

commit v9 on v8

--- a/solution.py
+++ b/solution.py
@@ -676,6 +676,13 @@
     return target
 
 
+def back_and_left_kernel(sizes, *refs):
+    back_in, left_in, refs = refs[:13], refs[13:23], refs[23:]
+    back_out, left_out, refs = refs[:9], refs[9], refs[10:]
+    back_kernel(sizes, *back_in, *back_out, *refs[:12])
+    left_kernel(sizes, *left_in, left_out, *refs[12:])
+
+
 class Joined:
     def __init__(self, main, patch, first):
         self.main, self.patch, self.first = main, patch, first
@@ -898,14 +905,13 @@
         functools.partial(swap_kernel, slice(cut, width)), [(rows_swapped, width - cut)], measured, behind=own_kept[:1]
     )
     swap_rest = lax.ppermute(swap_out, "illum", swap)
-    own, *patch_kept = call(
-        functools.partial(back_kernel, sizes), [phase_delay.shape] + fields(1) * 8, *kept[2:4], *own_kept,
-        phase_delay, known, partner_in, along_in, phase_rim,
-        behind=[relay], scratch=fields(tiles) * 4 + fields(1) * 4 + tables(1), flops=10**9, mib=12,
-    )
-    (left,) = call(
-        functools.partial(left_kernel, sizes), [(slices, stripe, cut)], swap_in, along_in, *kept[4:], *kept[2:4],
-        behind=patch_kept[:1], scratch=fields(cut // LANES) * 6, flops=10**9, mib=12,
+    own, *patch_kept, left = call(
+        functools.partial(back_and_left_kernel, sizes),
+        [phase_delay.shape] + fields(1) * 8 + [(slices, stripe, cut)],
+        *kept[2:4], *own_kept, phase_delay, known, partner_in, along_in, phase_rim,
+        swap_in, along_in, *kept[4:], *kept[2:4],
+        behind=[relay], scratch=fields(tiles) * 4 + fields(1) * 4 + tables(1) + fields(cut // LANES) * 6,
+        flops=2*10**9, mib=16,
     )
     (out,) = call(
         functools.partial(finish_kernel, sizes), [phase_delay.shape],

time: 26.1 us -> 26 us (level)
    pallas_call x13 -> x12, Pallas kernels: 10.6 us -> 10.5 us  [call(): pl.pallas_call(kernel, out_shape=[like(x, n in held) for n, x in enumerat...]
where the time goes in v9:
time: 26 us; the launch traced here: 25.8 us
  starting transfers between devices  13.6 us (52%)
  Pallas kernels  10.5 us (40%)
  waiting for transfers between devices  1.67 us (6%)
    pallas_call x12, Pallas kernels, call(): pl.pallas_call(kernel, out_shape=[like(x, n in held) for n, x in enumerat...  10.5 us
    ppermute x1, starting transfers between devices, paired(): lax.ppermute(first_out, 'col', [(c, cols - 1 - c) for c in range(cols)])  3.89 us
    ppermute x1, starting transfers between devices, paired(): along_in = lax.ppermute(along_out, ('illum', 'row', 'col'), along)  2.65 us
    ppermute x1, starting transfers between devices, paired(): far = lax.ppermute(pair, 'row', [(r, r ^ 2) for r in range(rows)])  1.64 us
    ppermute x1, starting transfers between devices, paired(): partner_relay = lax.ppermute(relay, 'illum', swap)  1.47 us
    ppermute x1, starting transfers between devices, paired(): swap_rest = lax.ppermute(swap_out, 'illum', swap)  1.28 us
    ppermute x1, starting transfers between devices, paired(): same_in = lax.ppermute(same_out, ('illum', 'row'), same)  1.24 us
    ppermute x1, waiting for transfers between devices, paired(): lax.ppermute(second_out, 'col', [(c, c ^ 1) for c in range(cols)])  0.75 us
  transfers between devices with their start and end apart: 10, of which 3 were waited for; matrix products, arithmetic and copies ran while one was open for 0% of the time, Pallas kernels for 28%

profile of v9, /device:TPU:0, one launch (start us, length us, event | category | flops | bytes accessed | tf_op | source)
XLA Modules:
  0.0 25.8 jit_solution(792955642450377735)
XLA Ops:
  0.0 1.4 %shard_map.37 = (f32[8,2176]{1,0:T(8,128)S(1)}, f32[8,3072]{1,0:T(8,128)S(1)}, f32[8,1024]{1,0:T(8,128)S(1)}, f32[8,128]{1,0:T(8,128)S(1)}, f32[8,128]{1,0:T(8,128)S(1)}, /*index=5*/bf16[2,1,128,1024]{3,2,1,0:T(8,128)(2,1)S(1)}) custom-call(f32[2,64,1024]{2,1,0:T(8,128)} %args_9_.1, bf16[2,1,128,1024]{3,2,1,0:T(8,128)(2,1)} %args_1_.5, s32[1,2]{1,0:T(1,128)} %args_2_.4), custom_call_target="tpu_custom_call" | custom-call | bytes 262144 | tf_op jit(solution)/shard_map/pallas_call | solution.py:826
  1.4 0.0 copy-start
  1.4 0.5 %collective-permute-start.3 = (f32[8,128]{1,0:T(8,128)S(1)}, f32[8,128]{1,0:T(8,128)S(1)}, u32[]{:S(2)}, u32[]{:S(2)}) collective-permute-start(f32[8,128]{1,0:T(8,128)S(1)} %get-tuple-element.73.args_0_), channel_id=1, source_target_pairs={{0,4},{4,0},{8,12},{12,8},{1,5},{5,1},{9,13},{13,9},{2,6},{6,2},{1... | collective-permute-start | bytes 12296 | tf_op jit(solution)/shard_map/ppermute | solution.py:862
  2.0 2.6 %collective-permute-start.1 = (f32[8,3072]{1,0:T(8,128)S(1)}, f32[8,3072]{1,0:T(8,128)S(1)}, u32[]{:S(2)}, u32[]{:S(2)}) collective-permute-start(f32[8,3072]{1,0:T(8,128)S(1)} %get-tuple-element.60), channel_id=1, source_target_pairs={{16,4},{4,16},{20,8},{8,20},{24,12},{12,24},{0,1},{28,29},{17,5},{... | collective-permute-start | bytes 294920 | tf_op jit(solution)/shard_map/ppermute | solution.py:859
  4.6 0.0 collective-permute-start
  4.6 1.2 %collective-permute-start.2 = (f32[8,1024]{1,0:T(8,128)S(1)}, f32[8,1024]{1,0:T(8,128)S(1)}, u32[]{:S(2)}, u32[]{:S(2)}) collective-permute-start(f32[8,1024]{1,0:T(8,128)S(1)} %get-tuple-element.71), channel_id=1, source_target_pairs={{0,4},{4,8},{8,12},{12,0},{20,16},{24,20},{28,24},{16,28},{1,5},{5... | collective-permute-start | bytes 98312 | tf_op jit(solution)/shard_map/ppermute | solution.py:861
  5.9 0.0 collective-permute-done.3.args_1_.args_0_
  5.9 1.6 %collective-permute-start.4 = (f32[8,128]{1,0:T(8,128)S(1)}, f32[8,128]{1,0:T(8,128)S(1)}, u32[]{:S(2)}, u32[]{:S(2)}) collective-permute-start(f32[8,128]{1,0:T(8,128)S(1)} %shard_map.41.args_3_), channel_id=1, source_target_pairs={{0,8},{4,12},{8,0},{12,4},{1,9},{5,13},{9,1},{13,5},{2,10},{6,14},... | collective-permute-start | bytes 12296 | tf_op jit(solution)/shard_map/ppermute | solution.py:864
  7.5 0.7 %collective-permute-start.7 = (f32[136,768]{1,0:T(8,128)S(1)}, f32[136,768]{1,0:T(8,128)S(1)}, u32[]{:S(2)}, u32[]{:S(2)}) collective-permute-start(f32[136,768]{1,0:T(8,128)S(1)} %shard_map.45), channel_id=1, source_target_pairs={{0,16},{16,0},{1,17},{17,1},{2,18},{18,2},{3,19},{19,3},{4,20},{20... | collective-permute-start | bytes 1253384 | tf_op jit(solution)/shard_map/ppermute | solution.py:870
  8.2 0.0 copy-done
  8.2 0.6 %shard_map.38 = (f32[8,64,128]{2,1,0:T(8,128)S(1)}, f32[8,64,128]{2,1,0:T(8,128)S(1)}, f32[8,64,128]{2,1,0:T(8,128)S(1)}, f32[8,64,128]{2,1,0:T(8,128)S(1)}, f32...) custom-call(f32[2,64,1024]{2,1,0:T(8,128)S(1)} %copy-done, ...), custom_call_target="tpu_custom_call" | custom-call | flops 3000000000 | bytes 262144 | tf_op jit(solution)/shard_map/pallas_call | solution.py:826
  8.8 0.7 %collective-permute-done.4.args_4_ = f32[8,128]{1,0:T(8,128)S(1)} collective-permute-done((f32[8,128]{1,0:T(8,128)S(1)}, f32[8,128]{1,0:T(8,128)S(1)}, u32[]{:S(2)}, u32[]{:S(2)}) %collective-permute-start.4) | collective-permute-done | bytes 4128 | tf_op jit(solution)/shard_map/ppermute | solution.py:864
  9.5 0.0 collective-permute-done.2.args_11_.args_7_.args_6_
  9.5 0.2 collective-permute-done.args_4_.args_5_.args_11_
  9.7 0.0 collective-permute-done.1.args_5_.args_6_.args_12_.args_15_
  9.7 0.1 shard_map.42
  9.8 3.9 %collective-permute-start.5 = (f32[48,128]{1,0:T(8,128)S(1)}, f32[48,128]{1,0:T(8,128)S(1)}, u32[]{:S(2)}, u32[]{:S(2)}) collective-permute-start(f32[48,128]{1,0:T(8,128)S(1)} %get-tuple-element.74), channel_id=1, source_target_pairs={{0,3},{1,2},{2,1},{3,0},{4,7},{5,6},{6,5},{7,4},{8,11},{9,10},{10,... | collective-permute-start | bytes 73736 | tf_op jit(solution)/shard_map/ppermute | solution.py:886
  13.7 1.8 %shard_map.39 = (f32[8,96,128]{2,1,0:T(8,128)S(1)}, f32[8,96,128]{2,1,0:T(8,128)S(1)}, f32[8,96,128]{2,1,0:T(8,128)S(1)}, f32[8,96,128]{2,1,0:T(8,128)S(1)}, f32...) custom-call(f32[8,64,128]{2,1,0:T(8,128)S(1)} %get-tuple-element.55., ...), custom_call_target="tpu_custom_call" | custom-call | flops 1500000000 | bytes 262144 | tf_op jit(solution)/shard_map/pallas_call | solution.py:826
  15.5 0.0 collective-permute-done.5.args_3_.args_1_
  15.5 0.3 collective-permute-start.6
  15.8 1.6 %shard_map.40 = (f32[8,96,128]{2,1,0:T(8,128)S(1)}, f32[8,96,128]{2,1,0:T(8,128)S(1)}, f32[8,96,128]{2,1,0:T(8,128)S(1)}, f32[8,96,128]{2,1,0:T(8,128)S(1)}, f32...) custom-call(f32[8,96,128]{2,1,0:T(8,128)S(1)} %get-tuple-element.61.args_0_, ...), custom_call_target="tpu_custom_call" | custom-call | flops 1500000000 | bytes 262144 | tf_op jit(solution)/shard_map/pallas_call | solution.py:826
  17.4 1.3 %collective-permute-start.8 = (f32[136,256]{1,0:T(8,128)S(1)}, f32[136,256]{1,0:T(8,128)S(1)}, u32[]{:S(2)}, u32[]{:S(2)}) collective-permute-start(f32[136,256]{1,0:T(8,128)S(1)} %shard_map.47), channel_id=1, source_target_pairs={{0,16},{16,0},{1,17},{17,1},{2,18},{18,2},{3,19},{19,3},{4,20},{20... | collective-permute-start | bytes 417800 | tf_op jit(solution)/shard_map/ppermute | solution.py:907
  18.7 0.7 %collective-permute-done.6.args_2_ = f32[48,128]{1,0:T(8,128)S(1)} collective-permute-done((f32[48,128]{1,0:T(8,128)S(1)}, f32[48,128]{1,0:T(8,128)S(1)}, u32[]{:S(2)}, u32[]{:S(2)}) %collective-permute-start.6) | collective-permute-done | bytes 24608 | tf_op jit(solution)/shard_map/ppermute | solution.py:892
  19.4 0.2 shard_map.44
  19.7 1.5 %collective-permute-start.9 = (f32[32,128]{1,0:T(8,128)S(1)}, f32[32,128]{1,0:T(8,128)S(1)}, u32[]{:S(2)}, u32[]{:S(2)}) collective-permute-start(f32[32,128]{1,0:T(8,128)S(1)} %get-tuple-element.77.args_0_.args_8_), channel_id=1, source_target_pairs={{0,16},{16,0},{1,17},{17,1},{2,18},{18,2},{3,19},{19,3},{4,20},{20... | collective-permute-start | bytes 49160 | tf_op jit(solution)/shard_map/ppermute | solution.py:903
  21.1 0.0 collective-permute-done.7.args_14_.args_3_
  21.1 2.8 %shard_map.46 = (f32[2,64,1024]{2,1,0:T(8,128)S(1)}, f32[1,96,128]{2,1,0:T(8,128)S(1)}, f32[1,96,128]{2,1,0:T(8,128)S(1)}, f32[1,96,128]{2,1,0:T(8,128)S(1)}, f3...) custom-call(f32[32,128]{1,0:T(8,128)S(1)} %get-tuple-element.77.args, ...), custom_call_target="tpu_custom_call" | custom-call | flops 2000000000 | bytes 262144 | tf_op jit(solution)/shard_map/pallas_call | solution.py:826
  24.0 0.0 collective-permute-done.9.args_9_
  24.0 0.0 collective-permute-done.8.args_4_
  24.0 1.9 %shard_map.48 = f32[2,64,1024]{2,1,0:T(8,128)} custom-call(f32[2,64,1024]{2,1,0:T(8,128)S(1)} %get-tuple-element.90.args_0_, f32[2,64,768]{2,1,0:T(8,128)S(1)} %get-tuple-element.91.args_1_, bf16[2,1,128,1024]{3,2,1,0:T(8,128)(2,1)S(1)} %get-tuple-element.53.args_1_.args_10_.args_2_, f32[136,768]{1,0:T(8,128)S(1)} %collective-permute-done.7.args_14_.args_3_, ...), custom_call_target="tpu_custom_call" | custom-call | bytes 262144 | tf_op jit(solution)/shard_map/pallas_call | solution.py:826
  (4 shorter events, 0.1 us)
Async XLA Ops:
  1.4 6.8 %copy-start = (f32[2,64,1024]{2,1,0:T(8,128)S(1)}, f32[2,64,1024]{2,1,0:T(8,128)}, u32[]{:S(2)}) copy-start(f32[2,64,1024]{2,1,0:T(8,128)} %args_9_.1) | copy-start | bytes 1572868
  1.4 4.4 %collective-permute-start.3 = (f32[8,128]{1,0:T(8,128)S(1)}, f32[8,128]{1,0:T(8,128)S(1)}, u32[]{:S(2)}, u32[]{:S(2)}) collective-permute-start(f32[8,128]{1,0:T(8,128)S(1)} %get-tuple-element.73.args_0_), channel_id=1, source_target_pairs={{0,4},{4,0},{8,12},{12,8},{1,5},{5,1},{9,13},{13,9},{2,6},{6,2},{1... | collective-permute-start | bytes 12296 | tf_op jit(solution)/shard_map/ppermute | solution.py:862
  2.0 7.7 %collective-permute-start.1 = (f32[8,3072]{1,0:T(8,128)S(1)}, f32[8,3072]{1,0:T(8,128)S(1)}, u32[]{:S(2)}, u32[]{:S(2)}) collective-permute-start(f32[8,3072]{1,0:T(8,128)S(1)} %get-tuple-element.60), channel_id=1, source_target_pairs={{16,4},{4,16},{20,8},{8,20},{24,12},{12,24},{0,1},{28,29},{17,5},{... | collective-permute-start | bytes 294920 | tf_op jit(solution)/shard_map/ppermute | solution.py:859
  4.6 5.1 %collective-permute-start = (f32[8,2176]{1,0:T(8,128)S(1)}, f32[8,2176]{1,0:T(8,128)S(1)}, u32[]{:S(2)}, u32[]{:S(2)}) collective-permute-start(f32[8,2176]{1,0:T(8,128)S(1)} %get-tuple-element.59), channel_id=1, source_target_pairs={{0,16},{16,0},{1,17},{17,1},{2,18},{18,2},{3,19},{19,3},{4,20},{20... | collective-permute-start | bytes 208904 | tf_op jit(solution)/shard_map/ppermute | solution.py:860
  4.6 4.9 %collective-permute-start.2 = (f32[8,1024]{1,0:T(8,128)S(1)}, f32[8,1024]{1,0:T(8,128)S(1)}, u32[]{:S(2)}, u32[]{:S(2)}) collective-permute-start(f32[8,1024]{1,0:T(8,128)S(1)} %get-tuple-element.71), channel_id=1, source_target_pairs={{0,4},{4,8},{8,12},{12,0},{20,16},{24,20},{28,24},{16,28},{1,5},{5... | collective-permute-start | bytes 98312 | tf_op jit(solution)/shard_map/ppermute | solution.py:861
  5.9 3.6 %collective-permute-start.4 = (f32[8,128]{1,0:T(8,128)S(1)}, f32[8,128]{1,0:T(8,128)S(1)}, u32[]{:S(2)}, u32[]{:S(2)}) collective-permute-start(f32[8,128]{1,0:T(8,128)S(1)} %shard_map.41.args_3_), channel_id=1, source_target_pairs={{0,8},{4,12},{8,0},{12,4},{1,9},{5,13},{9,1},{13,5},{2,10},{6,14},... | collective-permute-start | bytes 12296 | tf_op jit(solution)/shard_map/ppermute | solution.py:864
  7.5 13.6 %collective-permute-start.7 = (f32[136,768]{1,0:T(8,128)S(1)}, f32[136,768]{1,0:T(8,128)S(1)}, u32[]{:S(2)}, u32[]{:S(2)}) collective-permute-start(f32[136,768]{1,0:T(8,128)S(1)} %shard_map.45), channel_id=1, source_target_pairs={{0,16},{16,0},{1,17},{17,1},{2,18},{18,2},{3,19},{19,3},{4,20},{20... | collective-permute-start | bytes 1253384 | tf_op jit(solution)/shard_map/ppermute | solution.py:870
  9.8 5.7 %collective-permute-start.5 = (f32[48,128]{1,0:T(8,128)S(1)}, f32[48,128]{1,0:T(8,128)S(1)}, u32[]{:S(2)}, u32[]{:S(2)}) collective-permute-start(f32[48,128]{1,0:T(8,128)S(1)} %get-tuple-element.74), channel_id=1, source_target_pairs={{0,3},{1,2},{2,1},{3,0},{4,7},{5,6},{6,5},{7,4},{8,11},{9,10},{10,... | collective-permute-start | bytes 73736 | tf_op jit(solution)/shard_map/ppermute | solution.py:886
  15.5 3.9 %collective-permute-start.6 = (f32[48,128]{1,0:T(8,128)S(1)}, f32[48,128]{1,0:T(8,128)S(1)}, u32[]{:S(2)}, u32[]{:S(2)}) collective-permute-start(f32[48,128]{1,0:T(8,128)S(1)} %shard_map.43), channel_id=1, source_target_pairs={{0,1},{1,0},{2,3},{3,2},{4,5},{5,4},{6,7},{7,6},{8,9},{9,8},{10,11... | collective-permute-start | bytes 73736 | tf_op jit(solution)/shard_map/ppermute | solution.py:892
  17.4 6.6 %collective-permute-start.8 = (f32[136,256]{1,0:T(8,128)S(1)}, f32[136,256]{1,0:T(8,128)S(1)}, u32[]{:S(2)}, u32[]{:S(2)}) collective-permute-start(f32[136,256]{1,0:T(8,128)S(1)} %shard_map.47), channel_id=1, source_target_pairs={{0,16},{16,0},{1,17},{17,1},{2,18},{18,2},{3,19},{19,3},{4,20},{20... | collective-permute-start | bytes 417800 | tf_op jit(solution)/shard_map/ppermute | solution.py:907
  19.7 4.3 %collective-permute-start.9 = (f32[32,128]{1,0:T(8,128)S(1)}, f32[32,128]{1,0:T(8,128)S(1)}, u32[]{:S(2)}, u32[]{:S(2)}) collective-permute-start(f32[32,128]{1,0:T(8,128)S(1)} %get-tuple-element.77.args_0_.args_8_), channel_id=1, source_target_pairs={{0,16},{16,0},{1,17},{17,1},{2,18},{18,2},{3,19},{19,3},{4,20},{20... | collective-permute-start | bytes 49160 | tf_op jit(solution)/shard_map/ppermute | solution.py:903
